TPU v7x, 32 devices: a whole 2x2x4 slice. The times are simulated.
32 devices in a mesh: seq: 8 (over z, x), tensor: 4 (over y, core).
Axes of the slice: x: 2, y: 2, z: 4, core: 2. Of those that a mesh axis runs over, the one named last changes fastest.
Arguments:
- tokens: bfloat16 [4096, 4096], P('seq', 'tensor'), may hold values from -6 to 6
- w_query: bfloat16 [4096, 2048], P(None, 'tensor'), may hold values from -0.09375 to 0.09375
- w_key: bfloat16 [4096, 2048], P(None, 'tensor'), may hold values from -0.09375 to 0.09375
- w_value: bfloat16 [4096, 4096], P(None, 'tensor'), may hold values from -0.09375 to 0.09375
- w_outgate: bfloat16 [4096, 4096], P(None, 'tensor'), may hold values from -0.09375 to 0.09375
- w_gates: bfloat16 [2, 4096, 8], P(None, None, 'tensor'), may hold values from -0.09375 to 0.09375
- gate_bias: float32 [2, 8], P(None, 'tensor'), may hold values from -2 to 78, as said below
- w_out: bfloat16 [4096, 4096], P('tensor'), may hold values from -0.09375 to 0.09375
- carry_matrix: float32 [8, 256, 512], P('tensor'), may hold values from -6 to 6
- carry_norm: float32 [8, 256], P('tensor'), may hold values from -6 to 6
- carry_max: float32 [8], P('tensor'), may hold values from 0 to 78
- doc_lengths: int32 [4], replicated, may hold values from 1 to 2048, 4096 in all
Outputs:
- layer_out: bfloat16 [4096, 4096], P('seq', 'tensor')
Inputs may be any that keep to these rules, and one draw needn't show every extreme that they name: `doc_lengths`: the 4 lengths sum to 4096; the longest is exactly 2048. `gate_bias`: row 0 holds the input gates' biases, row 1 the forget gates' biases.
All inputs are finite; a program needn't handle non-finite values.
Results may differ from a plain program's by a relative error of at most 0.014.
Values may be sent and summed in bfloat16 or wider, within the bound.
No kernel may reach another device: no remote copies, remote signals or barrier semaphores. Data moves between devices by JAX's collectives and lax.ppermute only.
A program may use at most 128 MiB of HBM per device.

v0:
```python
import jax
import jax.numpy as jnp
from jax import lax
from jax.sharding import PartitionSpec as P

FULL_ACCURACY = lax.Precision.HIGHEST


def shifted(x, axis, by):
    devices = lax.axis_size(axis)
    pairs = [(i, i + by) for i in range(devices) if 0 <= i + by < devices]
    return lax.ppermute(x, axis, pairs)


def segment_of(doc_lengths, positions):
    bounds = jnp.cumsum(doc_lengths)[:-1]
    return jnp.sum((positions[:, None] >= bounds[None, :]).astype(jnp.int32), axis=1)


def combine(earlier, later):
    early_c, early_n, early_m, early_g, early_r = earlier
    late_c, late_n, late_m, late_g, late_r = later
    ceiling = jnp.maximum(early_m + late_g, late_m)
    early_weight = jnp.exp(early_m + late_g - ceiling)
    late_weight = jnp.exp(late_m - ceiling)
    reset_mask = late_r > 0.5
    merged_c = jnp.where(
        reset_mask[:, None, None],
        late_c,
        early_weight[:, None, None] * early_c + late_weight[:, None, None] * late_c,
    )
    merged_n = jnp.where(
        reset_mask[:, None], late_n, early_weight[:, None] * early_n + late_weight[:, None] * late_n
    )
    merged_m = jnp.where(reset_mask, late_m, ceiling)
    return (merged_c, merged_n, merged_m, late_g, jnp.maximum(early_r, late_r))


def block_local(queries, keys, value_rows, input_pre, log_forget, segment, segment_before):
    length = segment.shape[0]
    log_decay = jnp.cumsum(log_forget, axis=0)
    position = jnp.arange(length)
    allowed = (position[:, None] >= position[None, :]) & (segment[:, None] == segment[None, :])
    exponent = log_decay.T[:, :, None] - log_decay.T[:, None, :] + input_pre.T[:, None, :]
    exponent = jnp.where(allowed[None], exponent, -jnp.inf)
    inner_max = jnp.max(exponent, axis=2)
    scores = jnp.einsum("lhk,mhk->hlm", queries, keys, preferred_element_type=jnp.float32)
    weighted = jnp.exp(exponent - inner_max[:, :, None]) * scores
    weighted_bf = weighted.astype(jnp.bfloat16)
    inner_num = jnp.einsum(
        "hlm,mhv->lhv", weighted_bf, value_rows, preferred_element_type=jnp.float32
    )
    inner_den = jnp.sum(weighted, axis=2).T
    in_last = segment == segment[-1]
    tail_expo = log_decay[-1][None, :] - log_decay + input_pre
    tail_expo = jnp.where(in_last[:, None], tail_expo, -jnp.inf)
    tail_max = jnp.max(tail_expo, axis=0)
    key_scaled_rows = (jnp.exp(tail_expo - tail_max[None, :])[:, :, None] * keys).astype(
        jnp.bfloat16
    )
    cell_state_matrix = jnp.einsum(
        "emn,emp->mnp", key_scaled_rows, value_rows, preferred_element_type=jnp.float32
    )
    state_n = jnp.sum(key_scaled_rows.astype(jnp.float32), axis=0)
    reset = (segment[-1] != segment_before).astype(jnp.float32) * jnp.ones_like(tail_max)
    summary = (cell_state_matrix, state_n, tail_max, log_decay[-1], reset)
    return (log_decay, inner_max.T, inner_num, inner_den, summary)


def block_output(
    queries, log_decay, inner_max, inner_num, inner_den, segment, segment_before, incoming
):
    cell_state_matrix, state_n, state_m = incoming
    outer = jnp.where((segment == segment_before)[:, None], log_decay + state_m[None, :], -jnp.inf)
    ceiling = jnp.maximum(inner_max, outer)
    inner_weight = jnp.exp(inner_max - ceiling)
    outer_weight = jnp.exp(outer - ceiling)
    query_single = queries.astype(jnp.float32)
    outer_numerator_sum = jnp.einsum(
        "ciy,iyo->cio", query_single, cell_state_matrix, precision=FULL_ACCURACY
    )
    outer_den = jnp.einsum("lhk,hk->lh", query_single, state_n, precision=FULL_ACCURACY)
    numerator = (
        inner_weight[:, :, None] * inner_num + outer_weight[:, :, None] * outer_numerator_sum
    )
    denominator = inner_weight * inner_den + outer_weight * outer_den
    return numerator / jnp.maximum(jnp.abs(denominator), 1.0)[:, :, None]


def local(
    tokens,
    w_query,
    w_key,
    w_value,
    w_outgate,
    w_gates,
    gate_bias,
    w_out,
    carry_matrix,
    carry_norm,
    carry_max,
    doc_lengths,
):
    length = tokens.shape[0]
    head_count = gate_bias.shape[1]
    query_size = w_query.shape[1] // head_count
    value_size = w_value.shape[1] // head_count
    matrices = (w_query, w_key, w_value, w_outgate)
    zero_init = tuple((jnp.zeros((length, matrix.shape[1]), jnp.float32) for matrix in matrices))
    zero_init = zero_init + (
        jnp.zeros((length, head_count), jnp.float32),
        jnp.zeros((length, head_count), jnp.float32),
    )
    column_block = lax.all_gather(tokens, "tensor", axis=1, tiled=True)
    updated = tuple(
        (jnp.dot(column_block, matrix, preferred_element_type=jnp.float32) for matrix in matrices)
    )
    input_sum = jnp.dot(column_block, w_gates[0], preferred_element_type=jnp.float32)
    forget_sum = jnp.dot(column_block, w_gates[1], preferred_element_type=jnp.float32)
    projected = updated + (input_sum, forget_sum)
    queries = projected[0].astype(jnp.bfloat16).reshape(length, head_count, query_size)
    keys = (
        (projected[1] * query_size ** (-0.5))
        .astype(jnp.bfloat16)
        .reshape(length, head_count, query_size)
    )
    value_rows = projected[2].astype(jnp.bfloat16).reshape(length, head_count, value_size)
    outgate = jax.nn.sigmoid(projected[3])
    input_pre = projected[4] + gate_bias[0][None, :]
    log_forget = jax.nn.log_sigmoid(projected[5] + gate_bias[1][None, :])
    offset = lax.axis_index("seq") * length
    positions = offset + jnp.arange(length, dtype=jnp.int32)
    segment = segment_of(doc_lengths, positions)
    segment_before = segment_of(doc_lengths, jnp.maximum(offset - 1, 0)[None])[0]
    log_decay, inner_max, inner_num, inner_den, summary = block_local(
        queries, keys, value_rows, input_pre, log_forget, segment, segment_before
    )
    start_state = (carry_matrix, carry_norm, carry_max)
    zero_heads = jnp.zeros((head_count,), jnp.float32)
    is_leader = lax.axis_index("seq") == 0

    def relay(iteration, current):
        leaving = combine(current + (zero_heads, zero_heads), summary)[:3]
        arrived = shifted(leaving, "seq", 1)
        return tuple(
            (
                jnp.where(is_leader, initial, received)
                for initial, received in zip(start_state, arrived)
            )
        )

    incoming = lax.fori_loop(0, lax.axis_size("seq") - 1, relay, start_state)
    mixed_heads = block_output(
        queries, log_decay, inner_max, inner_num, inner_den, segment, segment_before, incoming
    )
    hidden = (outgate * mixed_heads.reshape(length, head_count * value_size)).astype(jnp.bfloat16)
    partial_value = jnp.dot(hidden, w_out, preferred_element_type=jnp.float32)
    summed = lax.psum_scatter(
        partial_value.astype(jnp.bfloat16), "tensor", scatter_dimension=1, tiled=True
    ).astype(jnp.float32)
    return (tokens.astype(jnp.float32) + summed).astype(jnp.bfloat16)


def solution(mesh):
    return jax.shard_map(
        local,
        mesh=mesh,
        in_specs=(
            P("seq", "tensor"),
            P(None, "tensor"),
            P(None, "tensor"),
            P(None, "tensor"),
            P(None, "tensor"),
            P(None, None, "tensor"),
            P(None, "tensor"),
            P("tensor", None),
            P("tensor", None, None),
            P("tensor", None),
            P("tensor"),
            P(),
        ),
        out_specs=P("seq", "tensor"),
        check_vma=False,
    )
```

profile of v0, /device:TPU:0, one launch (start us, length us, event | category | flops | bytes accessed | tf_op | source)
XLA Modules:
  0.0 363.0 jit_solution(17765410430710623540)
XLA Ops:
  6.5 0.7 all-gather.2.cloned.1.call-update
  7.3 0.8 reduce-window.10
  8.1 0.7 copy.64
  11.4 0.7 copy.63
  12.1 1.2 copy.62
  13.3 1.3 broadcast_compare_fusion.1
  14.8 31.3 %all-gather.2.cloned.1.call-done = bf16[512,4096]{1,0:T(8,128)(2,1)} async-done(((bf16[512,1024]{1,0:T(8,128)(2,1)}), bf16[512,4096]{1,0:T(8,128)(2,1)}) %all-gather.2.cloned.1.call-update) | async-done | bytes 4194320 | tf_op jit(solution)/shard_map/all_gather | solution.py:114
  46.1 3.4 fusion.19
  50.8 3.6 %fusion.31 = (f32[2]{0:T(128)S(1)}, f32[512,2]{0,1:T(2,128)S(1)}, f32[512,2]{0,1:T(2,128)S(1)}) fusion(f32[1,2,4,128]{3,2,1,0:T(4,128)S(1)} %add_bitcast_fusion, f32[2]{0:T(128)S(1)} %slice_reduce_fusion.1, pred[512]{0:T(512)(128)(4,1)S(1)} %get-tuple-element.143, f32[2]{0:T(128)S(1)} %get-tuple-element.145, ...), kind=kOutput, calls=%fused_computation.70 | convolution fusion | flops 8393726 | bytes 4224520 | tf_op jit(solution)/shard_map/dot_general | solution.py:118
  54.5 5.4 %convert_reduce_fusion = (f32[512]{0:T(512)S(1)}, bf16[512,512]{0,1:T(8,128)(2,1)}) fusion(f32[512,2]{0,1:T(2,128)S(1)} %subtract_exponential_fusion.2, bf16[512,4096]{1,0:T(8,128)(2,1)S(1)} %copy-done, bf16[4096,512]{1,0:T(8,128)(2,1)} %param.16), kind=kOutput, calls=%fused_computation.30 | convolution fusion | flops 2149318144 | bytes 8919040 | tf_op jit(solution)/shard_map/dot_general | solution.py:116
  60.0 9.1 %convolution_convert_fusion.1 = bf16[512,1024]{1,0:T(8,128)(2,1)S(1)} fusion(bf16[512,4096]{1,0:T(8,128)(2,1)} %all-gather.2.cloned.1.call-done, bf16[4096,1024]{1,0:T(8,128)(2,1)} %param.17), kind=kOutput, calls=%fused_computation.19 | convolution fusion | flops 4295491584 | bytes 13631488 | tf_op jit(solution)/shard_map/dot_general | solution.py:116
  70.1 1.5 fusion.11
  71.6 5.9 %convolution_convert_fusion.2 = bf16[512,512]{0,1:T(8,128)(2,1)S(1)} fusion(bf16[512,4096]{1,0:T(8,128)(2,1)} %all-gather.2.cloned.1.call-done, bf16[4096,512]{1,0:T(8,128)(2,1)} %param.15), kind=kOutput, calls=%fused_computation.22 | convolution fusion | flops 2147745792 | bytes 8912896 | tf_op jit(solution)/shard_map/dot_general | solution.py:116
  77.5 1.0 fusion.32
  79.0 2.0 fusion.8
  81.0 200.5 %while.15 = (s32[]{:T(128)}, f32[2,256,512]{2,1,0:T(8,128)S(1)}, f32[2,256]{1,0:T(2,128)S(1)}, f32[2]{0:T(128)S(1)}, pred[]{:T(512)}, /*index=5*/f32[2]{0:T(128)...) while((s32[]{:T(128)}, f32[2,256,512]{2,1,0:T(8,128)S(1)}, ...), condition=%wide.region_9.10_spmd.clone, body=%wide.region_8.9_spmd.clone.sunk | while | flops 1313295 | bytes 14700984 | solution.py:152
  81.2 1.3 add_select_fusion.8
  82.5 3.4 collective-permute-start
  85.9 3.3 collective-permute-start.2
  89.3 3.4 collective-permute-start.1
  92.7 16.3 %collective-permute-done.2 = f32[2]{0:T(128)S(1)} collective-permute-done((f32[2]{0:T(128)S(1)}, f32[2]{0:T(128)S(1)}, u32[]{:S(2)}, u32[]{:S(2)}) %collective-permute-start.2) | collective-permute-done | bytes 40 | tf_op jit(solution)/shard_map/while/body/eval_jaxpr/ppermute | solution.py:12
  109.0 1.0 copy-done.2
  110.3 1.3 add_select_fusion.8
  111.5 5.6 %collective-permute-start = (f32[2,256,512]{2,1,0:T(8,128)}, f32[2,256,512]{2,1,0:T(8,128)S(1)}, u32[]{:S(2)}, u32[]{:S(2)}) collective-permute-start(f32[2,256,512]{2,1,0:T(8,128)} %add_select_fusion.8), channel_id=1, source_target_pairs={{0,4},{4,8},{8,12},{12,16},{16,20},{20,24},{24,28},{1,5},{5,9},{9,... | collective-permute-start | bytes 3145736 | tf_op jit(solution)/shard_map/while/body/eval_jaxpr/ppermute | solution.py:12
  117.2 4.2 %collective-permute-start.2 = (f32[2]{0:T(128)S(1)}, f32[2]{0:T(128)S(1)}, u32[]{:S(2)}, u32[]{:S(2)}) collective-permute-start(f32[2]{0:T(128)S(1)} %get-tuple-element.239), channel_id=1, source_target_pairs={{0,4},{4,8},{8,12},{12,16},{16,20},{20,24},{24,28},{1,5},{5,9},{9,... | collective-permute-start | bytes 32 | tf_op jit(solution)/shard_map/while/body/eval_jaxpr/ppermute | solution.py:12
  121.5 2.5 collective-permute-start.1
  123.9 15.4 %collective-permute-done.2 = f32[2]{0:T(128)S(1)} collective-permute-done((f32[2]{0:T(128)S(1)}, f32[2]{0:T(128)S(1)}, u32[]{:S(2)}, u32[]{:S(2)}) %collective-permute-start.2) | collective-permute-done | bytes 40 | tf_op jit(solution)/shard_map/while/body/eval_jaxpr/ppermute | solution.py:12
  139.4 1.0 copy-done.2
  140.6 1.3 add_select_fusion.8
  141.9 5.6 %collective-permute-start = (f32[2,256,512]{2,1,0:T(8,128)}, f32[2,256,512]{2,1,0:T(8,128)S(1)}, u32[]{:S(2)}, u32[]{:S(2)}) collective-permute-start(f32[2,256,512]{2,1,0:T(8,128)} %add_select_fusion.8), channel_id=1, source_target_pairs={{0,4},{4,8},{8,12},{12,16},{16,20},{20,24},{24,28},{1,5},{5,9},{9,... | collective-permute-start | bytes 3145736 | tf_op jit(solution)/shard_map/while/body/eval_jaxpr/ppermute | solution.py:12
  147.5 5.2 %collective-permute-start.2 = (f32[2]{0:T(128)S(1)}, f32[2]{0:T(128)S(1)}, u32[]{:S(2)}, u32[]{:S(2)}) collective-permute-start(f32[2]{0:T(128)S(1)} %get-tuple-element.239), channel_id=1, source_target_pairs={{0,4},{4,8},{8,12},{12,16},{16,20},{20,24},{24,28},{1,5},{5,9},{9,... | collective-permute-start | bytes 32 | tf_op jit(solution)/shard_map/while/body/eval_jaxpr/ppermute | solution.py:12
  152.8 1.9 collective-permute-start.1
  154.7 14.1 %collective-permute-done.2 = f32[2]{0:T(128)S(1)} collective-permute-done((f32[2]{0:T(128)S(1)}, f32[2]{0:T(128)S(1)}, u32[]{:S(2)}, u32[]{:S(2)}) %collective-permute-start.2) | collective-permute-done | bytes 40 | tf_op jit(solution)/shard_map/while/body/eval_jaxpr/ppermute | solution.py:12
  168.8 1.0 copy-done.2
  170.0 1.3 add_select_fusion.8
  171.3 6.5 %collective-permute-start = (f32[2,256,512]{2,1,0:T(8,128)}, f32[2,256,512]{2,1,0:T(8,128)S(1)}, u32[]{:S(2)}, u32[]{:S(2)}) collective-permute-start(f32[2,256,512]{2,1,0:T(8,128)} %add_select_fusion.8), channel_id=1, source_target_pairs={{0,4},{4,8},{8,12},{12,16},{16,20},{20,24},{24,28},{1,5},{5,9},{9,... | collective-permute-start | bytes 3145736 | tf_op jit(solution)/shard_map/while/body/eval_jaxpr/ppermute | solution.py:12
  177.8 5.2 %collective-permute-start.2 = (f32[2]{0:T(128)S(1)}, f32[2]{0:T(128)S(1)}, u32[]{:S(2)}, u32[]{:S(2)}) collective-permute-start(f32[2]{0:T(128)S(1)} %get-tuple-element.239), channel_id=1, source_target_pairs={{0,4},{4,8},{8,12},{12,16},{16,20},{20,24},{24,28},{1,5},{5,9},{9,... | collective-permute-start | bytes 32 | tf_op jit(solution)/shard_map/while/body/eval_jaxpr/ppermute | solution.py:12
  183.1 1.9 collective-permute-start.1
  185.0 13.1 %collective-permute-done.2 = f32[2]{0:T(128)S(1)} collective-permute-done((f32[2]{0:T(128)S(1)}, f32[2]{0:T(128)S(1)}, u32[]{:S(2)}, u32[]{:S(2)}) %collective-permute-start.2) | collective-permute-done | bytes 40 | tf_op jit(solution)/shard_map/while/body/eval_jaxpr/ppermute | solution.py:12
  198.2 1.0 copy-done.2
  199.4 1.3 add_select_fusion.8
  200.7 6.5 %collective-permute-start = (f32[2,256,512]{2,1,0:T(8,128)}, f32[2,256,512]{2,1,0:T(8,128)S(1)}, u32[]{:S(2)}, u32[]{:S(2)}) collective-permute-start(f32[2,256,512]{2,1,0:T(8,128)} %add_select_fusion.8), channel_id=1, source_target_pairs={{0,4},{4,8},{8,12},{12,16},{16,20},{20,24},{24,28},{1,5},{5,9},{9,... | collective-permute-start | bytes 3145736 | tf_op jit(solution)/shard_map/while/body/eval_jaxpr/ppermute | solution.py:12
  207.2 5.2 %collective-permute-start.2 = (f32[2]{0:T(128)S(1)}, f32[2]{0:T(128)S(1)}, u32[]{:S(2)}, u32[]{:S(2)}) collective-permute-start(f32[2]{0:T(128)S(1)} %get-tuple-element.239), channel_id=1, source_target_pairs={{0,4},{4,8},{8,12},{12,16},{16,20},{20,24},{24,28},{1,5},{5,9},{9,... | collective-permute-start | bytes 32 | tf_op jit(solution)/shard_map/while/body/eval_jaxpr/ppermute | solution.py:12
  212.4 1.9 collective-permute-start.1
  214.3 12.2 %collective-permute-done.2 = f32[2]{0:T(128)S(1)} collective-permute-done((f32[2]{0:T(128)S(1)}, f32[2]{0:T(128)S(1)}, u32[]{:S(2)}, u32[]{:S(2)}) %collective-permute-start.2) | collective-permute-done | bytes 40 | tf_op jit(solution)/shard_map/while/body/eval_jaxpr/ppermute | solution.py:12
  226.5 1.0 copy-done.2
  227.7 1.3 add_select_fusion.8
  229.0 6.5 %collective-permute-start = (f32[2,256,512]{2,1,0:T(8,128)}, f32[2,256,512]{2,1,0:T(8,128)S(1)}, u32[]{:S(2)}, u32[]{:S(2)}) collective-permute-start(f32[2,256,512]{2,1,0:T(8,128)} %add_select_fusion.8), channel_id=1, source_target_pairs={{0,4},{4,8},{8,12},{12,16},{16,20},{20,24},{24,28},{1,5},{5,9},{9,... | collective-permute-start | bytes 3145736 | tf_op jit(solution)/shard_map/while/body/eval_jaxpr/ppermute | solution.py:12
  235.5 5.2 %collective-permute-start.2 = (f32[2]{0:T(128)S(1)}, f32[2]{0:T(128)S(1)}, u32[]{:S(2)}, u32[]{:S(2)}) collective-permute-start(f32[2]{0:T(128)S(1)} %get-tuple-element.239), channel_id=1, source_target_pairs={{0,4},{4,8},{8,12},{12,16},{16,20},{20,24},{24,28},{1,5},{5,9},{9,... | collective-permute-start | bytes 32 | tf_op jit(solution)/shard_map/while/body/eval_jaxpr/ppermute | solution.py:12
  240.8 1.9 collective-permute-start.1
  242.7 11.2 %collective-permute-done.2 = f32[2]{0:T(128)S(1)} collective-permute-done((f32[2]{0:T(128)S(1)}, f32[2]{0:T(128)S(1)}, u32[]{:S(2)}, u32[]{:S(2)}) %collective-permute-start.2) | collective-permute-done | bytes 40 | tf_op jit(solution)/shard_map/while/body/eval_jaxpr/ppermute | solution.py:12
  253.9 1.0 copy-done.2
  255.1 1.3 add_select_fusion.8
  256.4 6.5 %collective-permute-start = (f32[2,256,512]{2,1,0:T(8,128)}, f32[2,256,512]{2,1,0:T(8,128)S(1)}, u32[]{:S(2)}, u32[]{:S(2)}) collective-permute-start(f32[2,256,512]{2,1,0:T(8,128)} %add_select_fusion.8), channel_id=1, source_target_pairs={{0,4},{4,8},{8,12},{12,16},{16,20},{20,24},{24,28},{1,5},{5,9},{9,... | collective-permute-start | bytes 3145736 | tf_op jit(solution)/shard_map/while/body/eval_jaxpr/ppermute | solution.py:12
  262.9 5.2 %collective-permute-start.2 = (f32[2]{0:T(128)S(1)}, f32[2]{0:T(128)S(1)}, u32[]{:S(2)}, u32[]{:S(2)}) collective-permute-start(f32[2]{0:T(128)S(1)} %get-tuple-element.239), channel_id=1, source_target_pairs={{0,4},{4,8},{8,12},{12,16},{16,20},{20,24},{24,28},{1,5},{5,9},{9,... | collective-permute-start | bytes 32 | tf_op jit(solution)/shard_map/while/body/eval_jaxpr/ppermute | solution.py:12
  268.2 1.9 collective-permute-start.1
  270.1 10.2 %collective-permute-done.2 = f32[2]{0:T(128)S(1)} collective-permute-done((f32[2]{0:T(128)S(1)}, f32[2]{0:T(128)S(1)}, u32[]{:S(2)}, u32[]{:S(2)}) %collective-permute-start.2) | collective-permute-done | bytes 40 | tf_op jit(solution)/shard_map/while/body/eval_jaxpr/ppermute | solution.py:12
  280.3 1.0 copy-done.2
  281.5 1.3 fusion.25
  282.9 3.0 fusion.3
  285.9 1.9 copy.42
  287.8 17.1 %convolution_convert_fusion = bf16[512,4096]{1,0:T(8,128)(2,1)} fusion(bf16[1024,4096]{1,0:T(8,128)(2,1)} %param.21, f32[512,1024]{1,0:T(8,128)} %copy.42, bf16[512,4096]{1,0:T(8,128)(2,1)} %all-gather.2.cloned.1.call-done, bf16[4096,1024]{1,0:T(8,128)(2,1)} %param.18), kind=kOutput, calls=%fused_computation.9 | convolution fusion | flops 8594653184 | bytes 27262976 | tf_op jit(solution)/shard_map/dot_general | solution.py:157
  305.0 48.6 %reduce-scatter.2.cloned.1.call-done = bf16[512,1024]{1,0:T(8,128)(2,1)} async-done(((bf16[512,4096]{1,0:T(8,128)(2,1)}), bf16[512,1024]{1,0:T(8,128)(2,1)}) %reduce-scatter.2.cloned.1.call-update) | async-done | bytes 1048592 | tf_op jit(solution)/shard_map/reduce_scatter | solution.py:158
  353.6 2.6 add_convert_fusion
  (99 shorter events, 6.6 us)
Async XLA Ops:
  6.5 6.8 %copy-start.11 = (f32[2,2]{1,0:T(2,128)S(1)}, f32[2,2]{1,0:T(2,128)}, u32[]{:S(2)}) copy-start(f32[2,2]{1,0:T(2,128)} %param.20) | copy-start | bytes 52
  6.5 39.6 %copy-start.9 = (bf16[2,4096,2]{1,2,0:T(2,128)(2,1)S(1)}, bf16[2,4096,2]{1,2,0:T(2,128)(2,1)}, u32[]{:S(2)}) copy-start(bf16[2,4096,2]{1,2,0:T(2,128)(2,1)} %param.19) | copy-start | bytes 98308
  6.5 39.6 %all-gather.2.cloned.1.call-start = ((), (), s32[]{:S(2)}) async-start(), calls=%async_computation.1 | async-start | bytes 5242880 | tf_op jit(solution)/shard_map/all_gather | solution.py:114
  7.3 346.3 %reduce-scatter.2.cloned.1.call-start = ((), (), s32[]{:S(2)}) async-start(), calls=%async_computation.2 | async-start | bytes 5242880 | tf_op jit(solution)/shard_map/reduce_scatter | solution.py:158
  50.8 3.7 %copy-start = (bf16[512,4096]{1,0:T(8,128)(2,1)S(1)}, bf16[512,4096]{1,0:T(8,128)(2,1)}, u32[]{:S(2)}) copy-start(bf16[512,4096]{1,0:T(8,128)(2,1)} %all-gather.2.cloned.1.call-done) | copy-start | bytes 12582916
  69.7 7.9 %copy-start.3 = (bf16[512,1024]{0,1:T(8,128)(2,1)}, bf16[512,1024]{0,1:T(8,128)(2,1)S(1)}, u32[]{:S(2)}) copy-start(bf16[512,1024]{0,1:T(8,128)(2,1)S(1)} %copy.43) | copy-start | bytes 3145732
  71.6 5.9 %copy-start.6 = (bf16[512,512]{0,1:T(8,128)(2,1)S(1)}, bf16[512,512]{0,1:T(8,128)(2,1)}, u32[]{:S(2)}) copy-start(bf16[512,512]{0,1:T(8,128)(2,1)} %get-tuple-element.150) | copy-start | bytes 1572868
  77.5 1.0 copy-start.7
  77.5 1.4 copy-start.4
  79.0 2.0 copy-start.1
  79.0 2.0 copy-start.8
  79.0 2.0 copy-start.10
  82.5 26.5 %collective-permute-start = (f32[2,256,512]{2,1,0:T(8,128)}, f32[2,256,512]{2,1,0:T(8,128)S(1)}, u32[]{:S(2)}, u32[]{:S(2)}) collective-permute-start(f32[2,256,512]{2,1,0:T(8,128)} %add_select_fusion.8), channel_id=1, source_target_pairs={{0,4},{4,8},{8,12},{12,16},{16,20},{20,24},{24,28},{1,5},{5,9},{9,... | collective-permute-start | bytes 3145736 | tf_op jit(solution)/shard_map/while/body/eval_jaxpr/ppermute | solution.py:12
  85.9 23.1 %collective-permute-start.2 = (f32[2]{0:T(128)S(1)}, f32[2]{0:T(128)S(1)}, u32[]{:S(2)}, u32[]{:S(2)}) collective-permute-start(f32[2]{0:T(128)S(1)} %get-tuple-element.239), channel_id=1, source_target_pairs={{0,4},{4,8},{8,12},{12,16},{16,20},{20,24},{24,28},{1,5},{5,9},{9,... | collective-permute-start | bytes 32 | tf_op jit(solution)/shard_map/while/body/eval_jaxpr/ppermute | solution.py:12
  89.3 19.7 %collective-permute-start.1 = (f32[2,256]{1,0:T(2,128)S(1)}, f32[2,256]{1,0:T(2,128)S(1)}, u32[]{:S(2)}, u32[]{:S(2)}) collective-permute-start(f32[2,256]{1,0:T(2,128)S(1)} %add_select_fusion.9), channel_id=1, source_target_pairs={{0,4},{4,8},{8,12},{12,16},{16,20},{20,24},{24,28},{1,5},{5,9},{9,... | collective-permute-start | bytes 6152 | tf_op jit(solution)/shard_map/while/body/eval_jaxpr/ppermute | solution.py:12
  109.0 1.0 copy-start.2
  111.5 27.9 %collective-permute-start = (f32[2,256,512]{2,1,0:T(8,128)}, f32[2,256,512]{2,1,0:T(8,128)S(1)}, u32[]{:S(2)}, u32[]{:S(2)}) collective-permute-start(f32[2,256,512]{2,1,0:T(8,128)} %add_select_fusion.8), channel_id=1, source_target_pairs={{0,4},{4,8},{8,12},{12,16},{16,20},{20,24},{24,28},{1,5},{5,9},{9,... | collective-permute-start | bytes 3145736 | tf_op jit(solution)/shard_map/while/body/eval_jaxpr/ppermute | solution.py:12
  117.2 22.2 %collective-permute-start.2 = (f32[2]{0:T(128)S(1)}, f32[2]{0:T(128)S(1)}, u32[]{:S(2)}, u32[]{:S(2)}) collective-permute-start(f32[2]{0:T(128)S(1)} %get-tuple-element.239), channel_id=1, source_target_pairs={{0,4},{4,8},{8,12},{12,16},{16,20},{20,24},{24,28},{1,5},{5,9},{9,... | collective-permute-start | bytes 32 | tf_op jit(solution)/shard_map/while/body/eval_jaxpr/ppermute | solution.py:12
  121.5 17.9 %collective-permute-start.1 = (f32[2,256]{1,0:T(2,128)S(1)}, f32[2,256]{1,0:T(2,128)S(1)}, u32[]{:S(2)}, u32[]{:S(2)}) collective-permute-start(f32[2,256]{1,0:T(2,128)S(1)} %add_select_fusion.9), channel_id=1, source_target_pairs={{0,4},{4,8},{8,12},{12,16},{16,20},{20,24},{24,28},{1,5},{5,9},{9,... | collective-permute-start | bytes 6152 | tf_op jit(solution)/shard_map/while/body/eval_jaxpr/ppermute | solution.py:12
  139.4 1.0 copy-start.2
  141.9 26.9 %collective-permute-start = (f32[2,256,512]{2,1,0:T(8,128)}, f32[2,256,512]{2,1,0:T(8,128)S(1)}, u32[]{:S(2)}, u32[]{:S(2)}) collective-permute-start(f32[2,256,512]{2,1,0:T(8,128)} %add_select_fusion.8), channel_id=1, source_target_pairs={{0,4},{4,8},{8,12},{12,16},{16,20},{20,24},{24,28},{1,5},{5,9},{9,... | collective-permute-start | bytes 3145736 | tf_op jit(solution)/shard_map/while/body/eval_jaxpr/ppermute | solution.py:12
  147.5 21.3 %collective-permute-start.2 = (f32[2]{0:T(128)S(1)}, f32[2]{0:T(128)S(1)}, u32[]{:S(2)}, u32[]{:S(2)}) collective-permute-start(f32[2]{0:T(128)S(1)} %get-tuple-element.239), channel_id=1, source_target_pairs={{0,4},{4,8},{8,12},{12,16},{16,20},{20,24},{24,28},{1,5},{5,9},{9,... | collective-permute-start | bytes 32 | tf_op jit(solution)/shard_map/while/body/eval_jaxpr/ppermute | solution.py:12
  152.8 16.0 %collective-permute-start.1 = (f32[2,256]{1,0:T(2,128)S(1)}, f32[2,256]{1,0:T(2,128)S(1)}, u32[]{:S(2)}, u32[]{:S(2)}) collective-permute-start(f32[2,256]{1,0:T(2,128)S(1)} %add_select_fusion.9), channel_id=1, source_target_pairs={{0,4},{4,8},{8,12},{12,16},{16,20},{20,24},{24,28},{1,5},{5,9},{9,... | collective-permute-start | bytes 6152 | tf_op jit(solution)/shard_map/while/body/eval_jaxpr/ppermute | solution.py:12
  168.8 1.0 copy-start.2
  171.3 26.8 %collective-permute-start = (f32[2,256,512]{2,1,0:T(8,128)}, f32[2,256,512]{2,1,0:T(8,128)S(1)}, u32[]{:S(2)}, u32[]{:S(2)}) collective-permute-start(f32[2,256,512]{2,1,0:T(8,128)} %add_select_fusion.8), channel_id=1, source_target_pairs={{0,4},{4,8},{8,12},{12,16},{16,20},{20,24},{24,28},{1,5},{5,9},{9,... | collective-permute-start | bytes 3145736 | tf_op jit(solution)/shard_map/while/body/eval_jaxpr/ppermute | solution.py:12
  177.8 20.3 %collective-permute-start.2 = (f32[2]{0:T(128)S(1)}, f32[2]{0:T(128)S(1)}, u32[]{:S(2)}, u32[]{:S(2)}) collective-permute-start(f32[2]{0:T(128)S(1)} %get-tuple-element.239), channel_id=1, source_target_pairs={{0,4},{4,8},{8,12},{12,16},{16,20},{20,24},{24,28},{1,5},{5,9},{9,... | collective-permute-start | bytes 32 | tf_op jit(solution)/shard_map/while/body/eval_jaxpr/ppermute | solution.py:12
  183.1 15.1 %collective-permute-start.1 = (f32[2,256]{1,0:T(2,128)S(1)}, f32[2,256]{1,0:T(2,128)S(1)}, u32[]{:S(2)}, u32[]{:S(2)}) collective-permute-start(f32[2,256]{1,0:T(2,128)S(1)} %add_select_fusion.9), channel_id=1, source_target_pairs={{0,4},{4,8},{8,12},{12,16},{16,20},{20,24},{24,28},{1,5},{5,9},{9,... | collective-permute-start | bytes 6152 | tf_op jit(solution)/shard_map/while/body/eval_jaxpr/ppermute | solution.py:12
  198.2 1.0 copy-start.2
  200.7 25.9 %collective-permute-start = (f32[2,256,512]{2,1,0:T(8,128)}, f32[2,256,512]{2,1,0:T(8,128)S(1)}, u32[]{:S(2)}, u32[]{:S(2)}) collective-permute-start(f32[2,256,512]{2,1,0:T(8,128)} %add_select_fusion.8), channel_id=1, source_target_pairs={{0,4},{4,8},{8,12},{12,16},{16,20},{20,24},{24,28},{1,5},{5,9},{9,... | collective-permute-start | bytes 3145736 | tf_op jit(solution)/shard_map/while/body/eval_jaxpr/ppermute | solution.py:12
  207.2 19.3 %collective-permute-start.2 = (f32[2]{0:T(128)S(1)}, f32[2]{0:T(128)S(1)}, u32[]{:S(2)}, u32[]{:S(2)}) collective-permute-start(f32[2]{0:T(128)S(1)} %get-tuple-element.239), channel_id=1, source_target_pairs={{0,4},{4,8},{8,12},{12,16},{16,20},{20,24},{24,28},{1,5},{5,9},{9,... | collective-permute-start | bytes 32 | tf_op jit(solution)/shard_map/while/body/eval_jaxpr/ppermute | solution.py:12
  212.4 14.1 %collective-permute-start.1 = (f32[2,256]{1,0:T(2,128)S(1)}, f32[2,256]{1,0:T(2,128)S(1)}, u32[]{:S(2)}, u32[]{:S(2)}) collective-permute-start(f32[2,256]{1,0:T(2,128)S(1)} %add_select_fusion.9), channel_id=1, source_target_pairs={{0,4},{4,8},{8,12},{12,16},{16,20},{20,24},{24,28},{1,5},{5,9},{9,... | collective-permute-start | bytes 6152 | tf_op jit(solution)/shard_map/while/body/eval_jaxpr/ppermute | solution.py:12
  226.5 1.0 copy-start.2
  229.0 24.9 %collective-permute-start = (f32[2,256,512]{2,1,0:T(8,128)}, f32[2,256,512]{2,1,0:T(8,128)S(1)}, u32[]{:S(2)}, u32[]{:S(2)}) collective-permute-start(f32[2,256,512]{2,1,0:T(8,128)} %add_select_fusion.8), channel_id=1, source_target_pairs={{0,4},{4,8},{8,12},{12,16},{16,20},{20,24},{24,28},{1,5},{5,9},{9,... | collective-permute-start | bytes 3145736 | tf_op jit(solution)/shard_map/while/body/eval_jaxpr/ppermute | solution.py:12
  235.5 18.4 %collective-permute-start.2 = (f32[2]{0:T(128)S(1)}, f32[2]{0:T(128)S(1)}, u32[]{:S(2)}, u32[]{:S(2)}) collective-permute-start(f32[2]{0:T(128)S(1)} %get-tuple-element.239), channel_id=1, source_target_pairs={{0,4},{4,8},{8,12},{12,16},{16,20},{20,24},{24,28},{1,5},{5,9},{9,... | collective-permute-start | bytes 32 | tf_op jit(solution)/shard_map/while/body/eval_jaxpr/ppermute | solution.py:12
  240.8 13.1 %collective-permute-start.1 = (f32[2,256]{1,0:T(2,128)S(1)}, f32[2,256]{1,0:T(2,128)S(1)}, u32[]{:S(2)}, u32[]{:S(2)}) collective-permute-start(f32[2,256]{1,0:T(2,128)S(1)} %add_select_fusion.9), channel_id=1, source_target_pairs={{0,4},{4,8},{8,12},{12,16},{16,20},{20,24},{24,28},{1,5},{5,9},{9,... | collective-permute-start | bytes 6152 | tf_op jit(solution)/shard_map/while/body/eval_jaxpr/ppermute | solution.py:12
  253.9 1.0 copy-start.2
  256.4 23.9 %collective-permute-start = (f32[2,256,512]{2,1,0:T(8,128)}, f32[2,256,512]{2,1,0:T(8,128)S(1)}, u32[]{:S(2)}, u32[]{:S(2)}) collective-permute-start(f32[2,256,512]{2,1,0:T(8,128)} %add_select_fusion.8), channel_id=1, source_target_pairs={{0,4},{4,8},{8,12},{12,16},{16,20},{20,24},{24,28},{1,5},{5,9},{9,... | collective-permute-start | bytes 3145736 | tf_op jit(solution)/shard_map/while/body/eval_jaxpr/ppermute | solution.py:12
  262.9 17.4 %collective-permute-start.2 = (f32[2]{0:T(128)S(1)}, f32[2]{0:T(128)S(1)}, u32[]{:S(2)}, u32[]{:S(2)}) collective-permute-start(f32[2]{0:T(128)S(1)} %get-tuple-element.239), channel_id=1, source_target_pairs={{0,4},{4,8},{8,12},{12,16},{16,20},{20,24},{24,28},{1,5},{5,9},{9,... | collective-permute-start | bytes 32 | tf_op jit(solution)/shard_map/while/body/eval_jaxpr/ppermute | solution.py:12
  268.2 12.1 %collective-permute-start.1 = (f32[2,256]{1,0:T(2,128)S(1)}, f32[2,256]{1,0:T(2,128)S(1)}, u32[]{:S(2)}, u32[]{:S(2)}) collective-permute-start(f32[2,256]{1,0:T(2,128)S(1)} %add_select_fusion.9), channel_id=1, source_target_pairs={{0,4},{4,8},{8,12},{12,16},{16,20},{20,24},{24,28},{1,5},{5,9},{9,... | collective-permute-start | bytes 6152 | tf_op jit(solution)/shard_map/while/body/eval_jaxpr/ppermute | solution.py:12
  280.3 1.0 copy-start.2
  304.9 48.6 %copy-start.5 = (bf16[512,1024]{1,0:T(8,128)(2,1)S(1)}, bf16[512,1024]{1,0:T(8,128)(2,1)}, u32[]{:S(2)}) copy-start(bf16[512,1024]{1,0:T(8,128)(2,1)} %param.14) | copy-start | bytes 3145732
Sparse Core Ops, SparseCore 0:
  8.9 37.1 all-gather.1
  305.1 48.4 reduce-scatter.1
where the time goes:
time: 364 us; the launch traced here: 363 us
  waiting for transfers between devices  173 us (48%)
  starting transfers between devices  89.5 us (25%)
  matrix products  53.4 us (15%)
  other arithmetic  18.1 us (5%)
  between operations  14.9 us (4%)
  local copies, waits for them, and re-layouts  13.2 us (4%)
    ppermute x21, waiting for transfers between devices, shifted(): return lax.ppermute(x, axis, pairs)  92.6 us
    ppermute x21, starting transfers between devices, shifted(): return lax.ppermute(x, axis, pairs)  89.4 us
    reduce_scatter x1, waiting for transfers between devices, local(): lax.psum_scatter(partial_value.astype(jnp.bfloat16), 'tensor', scatter_di...  48.6 us
    all_gather x1, waiting for transfers between devices, local(): column_block = lax.all_gather(tokens, 'tensor', axis=1, tiled=True)  31.3 us
    dot_general x3, matrix products, local(): jnp.dot(column_block, matrix, preferred_element_type=jnp.float32)  20.4 us
    dot_general x1, matrix products, local(): partial_value = jnp.dot(hidden, w_out, preferred_element_type=jnp.float32)  17.1 us
    select_n x7, other arithmetic, combine(): jnp.where(reset_mask[:, None, None], late_c, early_weight[:, None, None]...  8.92 us
  transfers between devices with their start and end apart: 23, of which 9 were waited for; matrix products, arithmetic and copies ran while one was open for 2% of the time, Pallas kernels for 0%

commit v1 on v0

--- a/solution.py
+++ b/solution.py
@@ -1,12 +1,561 @@
+import functools
+
 import jax
 import jax.numpy as jnp
 from jax import lax
+from jax.experimental import pallas as pl
+from jax.experimental.pallas import tpu as pltpu
 from jax.sharding import PartitionSpec as P
 
+BF = jnp.bfloat16
+F32 = jnp.float32
+MIB = 1024 * 1024
+TOKEN_CHUNKS = (512, 512)
+OUT_CHUNKS = (256, 256, 256, 256)
+
+
+def params(mib):
+    return pltpu.CompilerParams(vmem_limit_bytes=mib * MIB)
+
+
+def cost(flops, moved):
+    return pl.CostEstimate(flops=int(flops), bytes_accessed=int(moved), transcendentals=0)
+
+
+def swapped(x, axis, mask):
+    size = lax.axis_size(axis)
+    return lax.ppermute(x, axis, [(i, i ^ mask) for i in range(size)])
+
+
+def shifted(x, axis, by):
+    size = lax.axis_size(axis)
+    return lax.ppermute(x, axis, [(i, i + by) for i in range(size - by)])
+
+
+def project_kernel(pieces, with_sum, finish, _, *refs):
+    xs, ws = refs[:pieces], refs[pieces : 2 * pieces]
+    total = None
+    for x, w in zip(xs, ws):
+        part = jnp.dot(x[...], w[...], preferred_element_type=F32)
+        total = part if total is None else total + part
+    if with_sum:
+        total = total + refs[2 * pieces][...]
+    refs[-1][...] = finish(total).astype(refs[-1].dtype)
+
+
+def project(xs, rows, weight, summed=None, finish=lambda x: x, kind=F32):
+    length, columns = xs[0].shape[0], weight.shape[1]
+    wide = min(512, columns)
+    depth = sum(x.shape[1] for x in xs)
+    specs = [pl.BlockSpec(x.shape, lambda j, r: (0, 0)) for x in xs]
+    specs += [
+        pl.BlockSpec((x.shape[1], wide), functools.partial(lambda i, j, r: (r[i], j), i))
+        for i, x in enumerate(xs)
+    ]
+    block = pl.BlockSpec((length, wide), lambda j, r: (0, j))
+    operands = list(xs) + [weight] * len(xs)
+    if summed is not None:
+        specs.append(block)
+        operands.append(summed)
+    return pl.pallas_call(
+        functools.partial(project_kernel, len(xs), summed is not None, finish),
+        out_shape=jax.ShapeDtypeStruct((length, columns), kind),
+        grid_spec=pltpu.PrefetchScalarGridSpec(
+            num_scalar_prefetch=1,
+            grid=(columns // wide,),
+            in_specs=specs,
+            out_specs=block,
+        ),
+        compiler_params=params(24),
+        cost_estimate=cost(
+            2 * length * depth * columns,
+            2 * depth * (columns + length) + 8 * length * columns,
+        ),
+    )(jnp.stack(rows).astype(jnp.int32), *operands)
+
+
+def segments(docs, positions):
+    total = jnp.zeros_like(positions)
+    bound = jnp.int32(0)
+    for j in range(docs.shape[0] - 1):
+        bound = bound + docs[j]
+        total = total + (positions >= bound).astype(jnp.int32)
+    return total
+
+
+def gates_kernel(heads, place, docs, bias, sums, u_out, weight_out, stats_out):
+    length = sums.shape[1]
+    offset = place[0]
+    row = lax.broadcasted_iota(jnp.int32, (heads, length), 0)
+    lane = lax.broadcasted_iota(jnp.int32, (heads, length), 1)
+    input_bias = jnp.zeros((heads, length), F32)
+    forget_bias = jnp.zeros((heads, length), F32)
+    for h in range(heads):
+        input_bias = jnp.where(row == h, bias[0, h], input_bias)
+        forget_bias = jnp.where(row == h, bias[1, h], forget_bias)
+    both = sums[...]
+    input_pre = both[:heads] + input_bias
+    forget = both[heads:] + forget_bias
+    decay = jnp.minimum(forget, 0.0) - jnp.log1p(jnp.exp(-jnp.abs(forget)))
+    step = 1
+    while step < length:
+        decay = decay + jnp.where(lane >= step, pltpu.roll(decay, step, 1), 0.0)
+        step *= 2
+    u = input_pre - decay
+    segment = segments(docs, lane + offset)
+    last = segments(docs, lane * 0 + (offset + length - 1))
+    open_rows = segment == last
+    top = jnp.max(jnp.where(open_rows, u, -jnp.inf), axis=1, keepdims=True)
+    weight = jnp.where(open_rows, jnp.exp(u - top), 0.0)
+    total = decay[:, length - 1 : length]
+    u_out[...] = u
+    spare = jnp.zeros((128 - heads, length), F32)
+    weight_out[...] = jnp.concatenate([weight, spare], axis=0).T
+    narrow = lax.broadcasted_iota(jnp.int32, (heads, 128), 1)
+    stats_out[...] = jnp.where(narrow == 0, total + top, jnp.where(narrow == 1, total, 0.0))
+
+
+def gate_rows(sums, bias, docs, offset):
+    heads, length = sums.shape[0] // 2, sums.shape[1]
+    smem = pl.BlockSpec(memory_space=pltpu.SMEM)
+    vmem = pl.BlockSpec(memory_space=pltpu.VMEM)
+    return pl.pallas_call(
+        functools.partial(gates_kernel, heads),
+        out_shape=(
+            jax.ShapeDtypeStruct((heads, length), F32),
+            jax.ShapeDtypeStruct((length, 128), F32),
+            jax.ShapeDtypeStruct((heads, 128), F32),
+        ),
+        in_specs=[smem, smem, smem, vmem],
+        out_specs=(vmem, vmem, vmem),
+        compiler_params=params(8),
+        cost_estimate=cost(1e6, 1e6),
+    )(offset[None], docs, bias, sums)
+
+
+def summary_kernel(pieces, scale, info, *refs):
+    xs = refs[:pieces]
+    key_ws = refs[pieces : 2 * pieces]
+    value_ws = refs[2 * pieces : 3 * pieces]
+    key_sum, value_sum, weight = refs[3 * pieces : 3 * pieces + 3]
+    key_out, value_out, keep_out, send_out, norm_out, state = refs[3 * pieces + 3 :]
+    head = pl.program_id(0)
+    key, value = key_sum[...], value_sum[...]
+    for x, key_w, value_w in zip(xs, key_ws, value_ws):
+        key = key + jnp.dot(x[...], key_w[...], preferred_element_type=F32)
+        value = value + jnp.dot(x[...], value_w[...], preferred_element_type=F32)
+    key = (key * scale).astype(BF)
+    value = value.astype(BF)
+    key_out[...] = key
+    value_out[...] = value
+    lanes = lax.broadcasted_iota(jnp.int32, weight.shape, 1)
+    column = jnp.sum(jnp.where(lanes == head, weight[...], 0.0), axis=1, keepdims=True)
+    scaled = (column * key.astype(F32)).astype(BF)
+    norm_out[0] = jnp.sum(scaled.astype(F32), axis=0, keepdims=True)
+    state[...] = lax.dot_general(
+        scaled, value, (((0,), (0,)), ((), ())), preferred_element_type=F32
+    )
+    half = keep_out.shape[1]
+    side = info[pieces]
+    keep_out[0] = state[pl.ds(pl.multiple_of(side * half, half), half)].astype(BF)
+    send_out[0] = state[pl.ds(pl.multiple_of((1 - side) * half, half), half)].astype(BF)
+
+
+def block_summary(xs, rows, side, w_key, w_value, key_sum, value_sum, weight, heads):
+    length = xs[0].shape[0]
+    size, wide = w_key.shape[1] // heads, w_value.shape[1] // heads
+    pieces = len(xs)
+    depth = sum(x.shape[1] for x in xs)
+
+    def weight_spec(i, columns):
+        return pl.BlockSpec((xs[i].shape[1], columns), lambda h, r: (r[i], h))
+
+    specs = [pl.BlockSpec(x.shape, lambda h, r: (0, 0)) for x in xs]
+    specs += [weight_spec(i, size) for i in range(pieces)]
+    specs += [weight_spec(i, wide) for i in range(pieces)]
+    by_head = lambda columns: pl.BlockSpec((length, columns), lambda h, r: (0, h))
+    specs += [by_head(size), by_head(wide), pl.BlockSpec(weight.shape, lambda h, r: (0, 0))]
+    half = pl.BlockSpec((1, size // 2, wide), lambda h, r: (h, 0, 0))
+    return pl.pallas_call(
+        functools.partial(summary_kernel, pieces, size ** (-0.5)),
+        out_shape=(
+            jax.ShapeDtypeStruct((length, heads * size), BF),
+            jax.ShapeDtypeStruct((length, heads * wide), BF),
+            jax.ShapeDtypeStruct((heads, size // 2, wide), BF),
+            jax.ShapeDtypeStruct((heads, size // 2, wide), BF),
+            jax.ShapeDtypeStruct((heads, 1, size), F32),
+        ),
+        grid_spec=pltpu.PrefetchScalarGridSpec(
+            num_scalar_prefetch=1,
+            grid=(heads,),
+            in_specs=specs,
+            out_specs=(
+                by_head(size),
+                by_head(wide),
+                half,
+                half,
+                pl.BlockSpec((1, 1, size), lambda h, r: (h, 0, 0)),
+            ),
+            scratch_shapes=[pltpu.VMEM((size, wide), F32)],
+        ),
+        compiler_params=params(32),
+        cost_estimate=cost(
+            2 * length * heads * (depth * (size + wide) + size * wide),
+            2 * depth * heads * (size + wide) + 6 * length * heads * (size + wide),
+        ),
+    )(
+        jnp.stack(list(rows) + [side]).astype(jnp.int32),
+        *xs,
+        *([w_key] * pieces),
+        *([w_value] * pieces),
+        key_sum,
+        value_sum,
+        weight,
+    )
+
+
+def inner_kernel(place, docs, top_in, query, key, value, u, norm, gate, base_out, slope_out):
+    head = pl.program_id(0)
+    length = query.shape[0]
+    offset = place[0]
+    heads = u.shape[0]
+    rows_u = lax.broadcasted_iota(jnp.int32, u.shape, 0)
+    u_row = jnp.max(jnp.where(rows_u == head, u[...], -jnp.inf), axis=0, keepdims=True)
+    top = top_in[head]
+    norm_row = norm[0]
+    chunk = 128
+    one = jnp.zeros((chunk, 1), jnp.int32)
+    before = segments(docs, one + jnp.maximum(offset - 1, 0))
+    for low in range(0, length, chunk):
+        high = low + chunk
+        position_t = lax.broadcasted_iota(jnp.int32, (chunk, 1), 0) + low
+        position_s = lax.broadcasted_iota(jnp.int32, (1, high), 1)
+        segment_t = segments(docs, position_t + offset)
+        segment_s = segments(docs, position_s + offset)
+        allowed = (position_s <= position_t) & (segment_s == segment_t)
+        expo = jnp.where(allowed, u_row[:, :high], -jnp.inf)
+        peak = jnp.max(expo, axis=1, keepdims=True)
+        q = query[low:high]
+        scores = lax.dot_general(
+            q, key[:high], (((1,), (1,)), ((), ())), preferred_element_type=F32
+        )
+        weighted = jnp.exp(expo - peak) * scores
+        num = jnp.dot(weighted.astype(BF), value[:high], preferred_element_type=F32)
+        den = jnp.sum(weighted, axis=1, keepdims=True)
+        carried = segment_t == before
+        ceiling = jnp.where(carried, jnp.maximum(peak, top), peak)
+        inner_weight = jnp.exp(peak - ceiling)
+        outer_weight = jnp.where(carried, jnp.exp(jnp.minimum(top - ceiling, 0.0)), 0.0)
+        outer_den = jnp.sum(q.astype(F32) * norm_row, axis=1, keepdims=True)
+        full = inner_weight * den + outer_weight * outer_den
+        inverse = 1.0 / jnp.maximum(jnp.abs(full), 1.0)
+        g = gate[low:high]
+        base_out[low:high] = g * (num * (inner_weight * inverse))
+        slope_out[low:high] = g * (outer_weight * inverse)
+
+
+def inner(query, key, value, u, norm, gate, top, docs, offset, heads):
+    length = query.shape[0]
+    size, wide = query.shape[1] // heads, value.shape[1] // heads
+    by_head = lambda columns: pl.BlockSpec((length, columns), lambda h: (0, h))
+    smem = pl.BlockSpec(memory_space=pltpu.SMEM)
+    return pl.pallas_call(
+        inner_kernel,
+        out_shape=(
+            jax.ShapeDtypeStruct((length, heads * wide), F32),
+            jax.ShapeDtypeStruct((length, heads * wide), F32),
+        ),
+        grid=(heads,),
+        in_specs=[
+            smem,
+            smem,
+            smem,
+            by_head(size),
+            by_head(size),
+            by_head(wide),
+            pl.BlockSpec(u.shape, lambda h: (0, 0)),
+            pl.BlockSpec((1, 1, size), lambda h: (h, 0, 0)),
+            by_head(wide),
+        ],
+        out_specs=(by_head(wide), by_head(wide)),
+        compiler_params=params(32),
+        cost_estimate=cost(
+            2 * length * length * heads * (size + wide),
+            length * heads * (4 * size + 14 * wide),
+        ),
+    )(offset[None], docs, top, query, key, value, u, norm, gate)
+
+
+def hidden_kernel(heads, info, query, own, other, base, slope, w, hidden, send, keep, state):
+    step = pl.program_id(0)
+
+    @pl.when(step == 0)
+    def _():
+        half = own.shape[1]
+        side = info[4]
+        size, wide = 2 * half, own.shape[2]
+        for h in range(heads):
+            state[pl.ds(pl.multiple_of(side * half, half), half)] = own[h]
+            state[pl.ds(pl.multiple_of((1 - side) * half, half), half)] = other[h]
+            outer = jnp.dot(
+                query[:, h * size : (h + 1) * size], state[...], preferred_element_type=F32
+            )
+            columns = slice(h * wide, (h + 1) * wide)
+            hidden[:, columns] = (base[:, columns] + slope[:, columns] * outer).astype(BF)
+
+    part = jnp.dot(hidden[...], w[...], preferred_element_type=F32).astype(BF)
+
+    @pl.when(step < 2)
+    def _():
+        send[...] = part
+
+    @pl.when(step >= 2)
+    def _():
+        keep[...] = part
+
+
+def out_specs_of(length, wide):
+    return (
+        pl.BlockSpec((length, wide), lambda j, r: (0, jnp.minimum(j, 1))),
+        pl.BlockSpec((length, wide), lambda j, r: (0, jnp.maximum(j - 2, 0))),
+    )
+
+
+def out_shapes_of(length, wide):
+    return (
+        jax.ShapeDtypeStruct((length, 2 * wide), BF),
+        jax.ShapeDtypeStruct((length, 2 * wide), BF),
+    )
+
+
+def hidden_and_first(query, own, other, base, slope, w_out, quarters, side, wide, start, heads):
+    length, depth = base.shape
+    per = w_out.shape[1] // 4 // wide
+    whole = lambda x: pl.BlockSpec(x.shape, lambda j, r: (0,) * x.ndim)
+    info = jnp.stack([q * per + start // wide for q in quarters] + [side]).astype(jnp.int32)
+    return pl.pallas_call(
+        functools.partial(hidden_kernel, heads),
+        out_shape=(jax.ShapeDtypeStruct((length, depth), BF),) + out_shapes_of(length, wide),
+        grid_spec=pltpu.PrefetchScalarGridSpec(
+            num_scalar_prefetch=1,
+            grid=(4,),
+            in_specs=[whole(x) for x in (query, own, other, base, slope)]
+            + [pl.BlockSpec((depth, wide), lambda j, r: (0, r[j]))],
+            out_specs=(pl.BlockSpec((length, depth), lambda j, r: (0, 0)),)
+            + out_specs_of(length, wide),
+            scratch_shapes=[pltpu.VMEM((2 * own.shape[1], own.shape[2]), BF)],
+        ),
+        compiler_params=params(32),
+        cost_estimate=cost(
+            2 * length * depth * (4 * wide + query.shape[1] // heads),
+            length * depth * 12 + depth * wide * 8,
+        ),
+    )(info, query, own, other, base, slope, w_out)
+
+
+def columns_kernel(info, hidden, w, send, keep):
+    step = pl.program_id(0)
+    part = jnp.dot(hidden[...], w[...], preferred_element_type=F32).astype(BF)
+
+    @pl.when(step < 2)
+    def _():
+        send[...] = part
+
+    @pl.when(step >= 2)
+    def _():
+        keep[...] = part
+
+
+def next_columns(hidden, w_out, quarters, wide, start):
+    length, depth = hidden.shape
+    per = w_out.shape[1] // 4 // wide
+    info = jnp.stack([q * per + start // wide for q in quarters]).astype(jnp.int32)
+    return pl.pallas_call(
+        columns_kernel,
+        out_shape=out_shapes_of(length, wide),
+        grid_spec=pltpu.PrefetchScalarGridSpec(
+            num_scalar_prefetch=1,
+            grid=(4,),
+            in_specs=[
+                pl.BlockSpec((length, depth), lambda j, r: (0, 0)),
+                pl.BlockSpec((depth, wide), lambda j, r: (0, r[j])),
+            ],
+            out_specs=out_specs_of(length, wide),
+        ),
+        compiler_params=params(24),
+        cost_estimate=cost(
+            8 * length * depth * wide, 2 * length * depth + depth * wide * 8 + length * wide * 8
+        ),
+    )(info, hidden, w_out)
+
+
+def pick(flag, a, b):
+    return jnp.where(flag, a, b)
+
+
+def local(
+    tokens,
+    w_query,
+    w_key,
+    w_value,
+    w_outgate,
+    w_gates,
+    gate_bias,
+    w_out,
+    carry_matrix,
+    carry_norm,
+    carry_max,
+    doc_lengths,
+):
+    length, share = tokens.shape
+    heads = gate_bias.shape[1]
+    size = w_query.shape[1] // heads
+    place = lax.axis_index("tensor")
+    block = lax.axis_index("seq")
+    blocks = lax.axis_size("seq")
+    offset = (block * length).astype(jnp.int32)
+    tensor = lambda x, mask: swapped(x, "tensor", mask)
+    pair = lambda x: swapped(x, "seq", 1)
+    down = lambda x: shifted(x, "seq", 2)
+
+    gate_rows_w = w_gates.transpose(0, 2, 1).reshape(2 * heads, 4 * share)
+    mine = [
+        lax.dynamic_slice(gate_rows_w, (0, (place ^ k) * share), (2 * heads, share))
+        for k in range(4)
+    ]
+    mine = [mine[0]] + [tensor(mine[k], k) for k in (1, 2, 3)]
+    starts = [sum(TOKEN_CHUNKS[:i]) for i in range(len(TOKEN_CHUNKS))]
+    across = [
+        tensor(tokens[:, s : s + c], 2) for s, c in zip(starts, TOKEN_CHUNKS)
+    ]
+    beside = tensor(tokens, 1)
+    gate_part = lax.dot_general(
+        jnp.concatenate(mine, axis=0),
+        tokens,
+        (((1,), (1,)), ((), ())),
+        preferred_element_type=F32,
+    )
+    gate_part = [gate_part[2 * heads * k : 2 * heads * (k + 1)] for k in range(4)]
+    gate_sum = gate_part[0] + sum(tensor(gate_part[k], k) for k in (1, 2, 3))
+    u, key_weight, stats = gate_rows(gate_sum, gate_bias, doc_lengths, offset)
+
+    side = (block % 2).astype(jnp.int32)
+    even = side == 0
+    z = block // 2
+    reach = blocks // 4
+    mg = jnp.stack([stats[:, 0], stats[:, 1]])
+    mg_other = pair(mg)
+    m_even, g_even = pick(even, mg, mg_other)
+    m_odd, g_odd = pick(even, mg_other, mg)
+
+    def segment_at(position):
+        return segments(doc_lengths, position)
+
+    def reset(index):
+        first = jnp.maximum(index * length - 1, 0)
+        return segment_at((index + 1) * length - 1) != segment_at(first)
+
+    reset_even, reset_odd = reset(2 * z), reset(2 * z + 1)
+    m_pair = jnp.maximum(pick(reset_odd, -jnp.inf, m_even + g_odd), m_odd)
+    pair_even = pick(reset_odd, 0.0, jnp.exp(jnp.minimum(m_even + g_odd - m_pair, 0.0)))
+    pair_odd = jnp.exp(m_odd - m_pair)
+    travelling = jnp.stack([m_pair, g_even + g_odd])
+    expos = []
+    passed = jnp.zeros_like(m_pair)
+    unbroken = jnp.bool_(True)
+    for k in range(1, reach + 1):
+        travelling = down(travelling)
+        there = z >= k
+        expos.append(pick(there & unbroken, travelling[0] + passed, -jnp.inf))
+        passed = passed + pick(there, travelling[1], 0.0)
+        broken = there & (reset(2 * (z - k)) | reset(2 * (z - k) + 1))
+        unbroken = unbroken & ~broken
+    expos.append(pick((z <= reach) & unbroken, carry_max + passed, -jnp.inf))
+    expos = jnp.stack(expos)
+    top_even = jnp.max(expos, axis=0)
+    expos_odd = pick(reset_even, -jnp.inf, expos + g_even)
+    top_odd = jnp.maximum(jnp.max(expos_odd, axis=0), m_even)
+    weights_even = jnp.exp(expos - top_even)
+    weights_odd = jnp.exp(expos_odd - top_odd)
+    direct = jnp.exp(m_even - top_odd)
+    weights_own = pick(even, weights_even, weights_odd)
+    weights_other = pick(even, weights_odd, weights_even)
+    direct_own = pick(even, 0.0, direct)
+    direct_other = pick(even, direct, 0.0)
+    top_own = pick(even, top_even, top_odd)
+    pair_own = pick(even, pair_even, pair_odd)
+    pair_other = pick(even, pair_odd, pair_even)
+
+    near = ([tokens, beside], [place, place ^ 1])
+    far = []
+    for s, c, x in zip(starts, TOKEN_CHUNKS, across):
+        rows = [((place ^ 2) * share + s) // c, ((place ^ 3) * share + s) // c]
+        far.append(([x, tensor(x, 1)], rows))
+    sums = [project(*near, w) for w in (w_key, w_value, w_query, w_outgate)]
+    for group in far[:-1]:
+        sums = [
+            project(*group, w, total)
+            for w, total in zip((w_key, w_value, w_query, w_outgate), sums)
+        ]
+    keys, values, kept, sent, norm = block_summary(
+        *far[-1], side, w_key, w_value, sums[0], sums[1], key_weight, heads
+    )
+    queries = project(*far[-1], w_query, sums[2], kind=BF)
+    gate = project(*far[-1], w_outgate, sums[3], jax.nn.sigmoid)
+
+    spread = lambda w: w[:, None, None]
+    norm_other = pair(norm)
+    norm_even = pick(even, norm, norm_other)
+    norm_pair = spread(pair_own) * norm + spread(pair_other) * norm_other
+    norm_in = spread(direct_own) * norm_even
+    for k in range(reach):
+        norm_pair = down(norm_pair)
+        norm_in = norm_in + spread(weights_own[k]) * norm_pair
+    norm_in = norm_in + spread(weights_own[reach]) * carry_norm[:, None, :]
+
+    got = pair(sent)
+    kept, got = kept.astype(F32), got.astype(F32)
+    state_even = pick(even, kept, got)
+    state_pair = (spread(pair_own) * kept + spread(pair_other) * got).astype(BF)
+    carried = lax.dynamic_slice(
+        carry_matrix, (0, side * (size // 2), 0), (heads, size // 2, carry_matrix.shape[2])
+    )
+    state_own = spread(weights_own[reach]) * carried + spread(direct_own) * state_even
+    state_other = spread(weights_other[reach]) * carried + spread(direct_other) * state_even
+    for k in range(reach):
+        state_pair = down(state_pair)
+        wide = state_pair.astype(F32)
+        state_own = state_own + spread(weights_own[k]) * wide
+        state_other = state_other + spread(weights_other[k]) * wide
+    state_got = pair(state_other.astype(BF))
+
+    base, slope = inner(
+        queries, keys, values, u, norm_in, gate, top_own, doc_lengths, offset, heads
+    )
+
+    quarters = [place ^ 1, place ^ 3, place, place ^ 2]
+    outs = []
+    start = 0
+    for wide in OUT_CHUNKS:
+        if start == 0:
+            hidden, send, keep = hidden_and_first(
+                queries, state_own.astype(BF), state_got, base, slope, w_out, quarters, side,
+                wide, start, heads,
+            )
+        else:
+            send, keep = next_columns(hidden, w_out, quarters, wide, start)
+        both = keep.astype(F32) + tensor(send, 1).astype(F32)
+        came = tensor(both[:, wide:].astype(BF), 2)
+        summed = both[:, :wide] + came.astype(F32)
+        outs.append((tokens[:, start : start + wide].astype(F32) + summed).astype(BF))
+        start += wide
+    return jnp.concatenate(outs, axis=1)
+
+
 FULL_ACCURACY = lax.Precision.HIGHEST
 
 
-def shifted(x, axis, by):
+def plain_shifted(x, axis, by):
     devices = lax.axis_size(axis)
     pairs = [(i, i + by) for i in range(devices) if 0 <= i + by < devices]
     return lax.ppermute(x, axis, pairs)
@@ -87,7 +636,7 @@
     return numerator / jnp.maximum(jnp.abs(denominator), 1.0)[:, :, None]
 
 
-def local(
+def plain_local(
     tokens,
     w_query,
     w_key,
@@ -141,7 +690,7 @@
 
     def relay(iteration, current):
         leaving = combine(current + (zero_heads, zero_heads), summary)[:3]
-        arrived = shifted(leaving, "seq", 1)
+        arrived = plain_shifted(leaving, "seq", 1)
         return tuple(
             (
                 jnp.where(is_leader, initial, received)
@@ -162,8 +711,9 @@
 
 
 def solution(mesh):
+    fast = mesh.shape["tensor"] == 4 and mesh.shape["seq"] % 4 == 0
     return jax.shard_map(
-        local,
+        local if fast else plain_local,
         mesh=mesh,
         in_specs=(
             P("seq", "tensor"),

time: 364 us -> 152 us (0.42)
  waiting for transfers between devices: 173 us -> 36.6 us
  matrix products: 53.4 us -> 0.38 us
  starting transfers between devices: 89.5 us -> 43.8 us
  Pallas kernels: 0 us -> 42.3 us
  other arithmetic: 18.1 us -> 3.6 us
  between operations: 14.9 us -> 10.8 us
    ppermute x21 -> x29, waiting for transfers between devices: 92.6 us -> 36.6 us  [the longest x23 34 us: swapped(): return lax.ppermute(x, axis, [(i, i ^ mask) for i in range(size)])]
    dot_general x11 -> x1, matrix products: 53.4 us -> 0.38 us  [local(): lax.dot_general(jnp.concatenate(mine, axis=0), tokens, (((1,), (1,)), (()...]
    reduce_scatter x1 -> x0, waiting for transfers between devices: 48.6 us -> none  [local(): lax.psum_scatter(partial_value.astype(jnp.bfloat16), 'tensor', scatter_di...]
    ppermute x21 -> x29, starting transfers between devices: 89.4 us -> 43.8 us  [the longest x6 23.4 us: shifted(): return lax.ppermute(x, axis, [(i, i + by) for i in range(size - by)])]
    pallas_call x0 -> x17, Pallas kernels: none -> 42.3 us  [the longest x10 21.8 us: project(): pl.pallas_call(functools.partial(project_kernel, len(xs), summed is not N...]
    all_gather x1 -> x0, waiting for transfers between devices: 31.3 us -> none  [local(): column_block = lax.all_gather(tokens, 'tensor', axis=1, tiled=True)]
    select_n x42 -> x4, other arithmetic: 11 us -> 0.05 us  [pick(): return jnp.where(flag, a, b)]
    unnamed x26 -> x54, local copies, waits for them, and re-layouts: 3.01 us -> 10.7 us
  transfers between devices with their start and end apart: 23 -> 29, of which waited for: 9 -> 11; matrix products, arithmetic and copies ran while one was open for 2% -> 4% of each run, Pallas kernels for 0% -> 23%
where the time goes in v1:
time: 152 us; the launch traced here: 151 us
  starting transfers between devices  43.8 us (29%)
  Pallas kernels  42.3 us (28%)
  waiting for transfers between devices  36.6 us (24%)
  local copies, waits for them, and re-layouts  13.9 us (9%)
  between operations  10.8 us (7%)
  other arithmetic  3.6 us (2%)
    ppermute x23, waiting for transfers between devices, swapped(): return lax.ppermute(x, axis, [(i, i ^ mask) for i in range(size)])  34 us
    ppermute x6, starting transfers between devices, shifted(): return lax.ppermute(x, axis, [(i, i + by) for i in range(size - by)])  23.4 us
    pallas_call x10, Pallas kernels, project(): pl.pallas_call(functools.partial(project_kernel, len(xs), summed is not N...  21.8 us
    ppermute x23, starting transfers between devices, swapped(): return lax.ppermute(x, axis, [(i, i ^ mask) for i in range(size)])  20.4 us
    unnamed x54, local copies, waits for them, and re-layouts  10.7 us
    pallas_call x3, Pallas kernels, next_columns(): pl.pallas_call(columns_kernel, out_shape=out_shapes_of(length, wide), gri...  8.75 us
    pallas_call x1, Pallas kernels, block_summary(): pl.pallas_call(functools.partial(summary_kernel, pieces, size ** (-0.5)),...  3.96 us
    pallas_call x1, Pallas kernels, hidden_and_first(): pl.pallas_call(functools.partial(hidden_kernel, heads), out_shape=(jax.Sh...  3.39 us
  transfers between devices with their start and end apart: 29, of which 11 were waited for; matrix products, arithmetic and copies ran while one was open for 4% of the time, Pallas kernels for 23%

profile of v1, /device:TPU:0, one launch (start us, length us, event | category | flops | bytes accessed | tf_op | source)
XLA Modules:
  0.0 151.3 jit_solution(2208609817514828588)
XLA Ops:
  0.0 0.5 collective-permute-start.4
  0.6 2.1 %fusion.40 = (bf16[512,512]{1,0:T(8,128)(2,1)}, bf16[512,512]{1,0:T(8,128)(2,1)S(1)}) fusion(bf16[512,1024]{1,0:T(8,128)(2,1)} %refs_0_.7), kind=kLoop, calls=%fused_computation.113 | loop fusion | bytes 2097152 | tf_op jit(solution)/shard_map/slice | solution.py:429
  2.6 2.6 %collective-permute-start = (bf16[512,512]{1,0:T(8,128)(2,1)S(1)}, bf16[512,512]{1,0:T(8,128)(2,1)S(1)}, u32[]{:S(2)}, u32[]{:S(2)}) collective-permute-start(bf16[512,512]{1,0:T(8,128)(2,1)S(1)} %get-tuple-element.59), channel_id=1, source_target_pairs={{0,2},{1,3},{2,0},{3,1},{4,6},{5,7},{6,4},{7,5},{8,10},{9,11},{10,... | collective-permute-start | bytes 1572872 | tf_op jit(solution)/shard_map/ppermute | solution.py:27
  5.4 1.8 %collective-permute-start.6 = (bf16[4,1024]{1,0:T(4,128)(2,1)S(1)}, bf16[4,1024]{1,0:T(4,128)(2,1)S(1)}, u32[]{:S(2)}, u32[]{:S(2)}) collective-permute-start(bf16[4,1024]{1,0:T(4,128)(2,1)S(1)} %get-tuple-element.65), channel_id=1, source_target_pairs={{0,2},{1,3},{2,0},{3,1},{4,6},{5,7},{6,4},{7,5},{8,10},{9,11},{10,... | collective-permute-start | bytes 24584 | tf_op jit(solution)/shard_map/ppermute | solution.py:27
  7.4 0.7 fusion.42
  10.9 6.8 %collective-permute-done.7 = bf16[4,1024]{1,0:T(4,128)(2,1)S(1)} collective-permute-done((bf16[4,1024]{1,0:T(4,128)(2,1)S(1)}, bf16[4,1024]{1,0:T(4,128)(2,1)S(1)}, u32[]{:S(2)}, u32[]{:S(2)}) %collective-permute-start.7) | collective-permute-done | bytes 8224 | tf_op jit(solution)/shard_map/ppermute | solution.py:27
  17.6 0.5 collective-permute-done.6
  18.1 0.4 fusion.16
  18.5 1.4 collective-permute-start.10
  19.9 0.6 collective-permute-start.8
  28.4 1.8 %collective-permute-start.2 = (bf16[512,512]{1,0:T(8,128)(2,1)}, bf16[512,512]{1,0:T(8,128)(2,1)S(1)}, u32[]{:S(2)}, u32[]{:S(2)}) collective-permute-start(bf16[512,512]{1,0:T(8,128)(2,1)} %get-tuple-element.58), channel_id=1, source_target_pairs={{0,2},{1,3},{2,0},{3,1},{4,6},{5,7},{6,4},{7,5},{8,10},{9,11},{10,... | collective-permute-start | bytes 1572872 | tf_op jit(solution)/shard_map/ppermute | solution.py:27
  30.2 1.4 shard_map.121
  31.6 0.7 copy-done.13
  32.4 1.6 %collective-permute-start.11 = (f32[2,2]{1,0:T(2,128)S(1)}, f32[2,2]{1,0:T(2,128)S(1)}, u32[]{:S(2)}, u32[]{:S(2)}) collective-permute-start(f32[2,2]{1,0:T(2,128)S(1)} %pad_maximum_fusion.2), channel_id=1, source_target_pairs={{0,4},{4,0},{8,12},{12,8},{16,20},{20,16},{24,28},{28,24},{1,5},{5... | collective-permute-start | bytes 56 | tf_op jit(solution)/shard_map/ppermute | solution.py:27
  34.0 2.1 %collective-permute-done.11 = f32[2,2]{1,0:T(2,128)S(1)} collective-permute-done((f32[2,2]{1,0:T(2,128)S(1)}, f32[2,2]{1,0:T(2,128)S(1)}, u32[]{:S(2)}, u32[]{:S(2)}) %collective-permute-start.11) | collective-permute-done | bytes 48 | tf_op jit(solution)/shard_map/ppermute | solution.py:27
  36.1 3.5 %collective-permute-start.12 = (f32[2,2]{1,0:T(2,128)S(1)}, f32[2,2]{1,0:T(2,128)S(1)}, u32[]{:S(2)}, u32[]{:S(2)}) collective-permute-start(f32[2,2]{1,0:T(2,128)S(1)} %pad_maximum_fusion.3), channel_id=1, source_target_pairs={{0,8},{4,12},{8,16},{12,20},{16,24},{20,28},{1,9},{5,13},{9,17},{1... | collective-permute-start | bytes 56 | tf_op jit(solution)/shard_map/ppermute | solution.py:32
  39.6 1.3 collective-permute-done.12
  40.9 4.2 %collective-permute-start.13 = (f32[2,2]{1,0:T(2,128)S(1)}, f32[2,2]{1,0:T(2,128)S(1)}, u32[]{:S(2)}, u32[]{:S(2)}) collective-permute-start(f32[2,2]{1,0:T(2,128)S(1)} %collective-permute-done.12), channel_id=1, source_target_pairs={{0,8},{4,12},{8,16},{12,20},{16,24},{20,28},{1,9},{5,13},{9,17},{1... | collective-permute-start | bytes 56 | tf_op jit(solution)/shard_map/ppermute | solution.py:32
  45.1 1.3 collective-permute-done.13
  46.6 0.5 collective-permute-start.1
  47.1 1.0 copy-done.5
  48.1 2.2 %copy-done.2 = bf16[4096,512]{1,0:T(8,128)(2,1)S(1)} copy-done((bf16[4096,512]{1,0:T(8,128)(2,1)S(1)}, bf16[4096,512]{1,0:T(8,128)(2,1)}, u32[]{:S(2)}) %copy-start.2) | copy-done | bytes 4194328
  50.3 1.2 copy-done.6
  51.5 1.8 %shard_map.122.refs_4_ = f32[512,512]{1,0:T(8,128)S(1)} custom-call(s32[2]{0:T(128)S(1)} %pad_add_fusion.2._, bf16[512,1024]{1,0:T(8,128)(2,1)S(1)} %copy-done.4, bf16[512,1024]{1,0:T(8,128)(2,1)S(1)} %copy-done.6, bf16[4096,512]{1,0:T(8,128)(2,1)S(1)} %copy-done.2, bf16[4096,512]{1,0:T(8,128)(2,1)S(1)} %copy-done.2), custom_call_target="tpu_custom_call" | custom-call | flops 1073741824 | bytes 6291456 | tf_op jit(solution)/shard_map/pallas_call | solution.py:60
  53.4 0.3 copy-done.3
  53.7 1.2 shard_map.123.refs_6_
  55.0 1.4 slice-done.3
  56.6 3.5 %shard_map.124.refs_4_ = f32[512,1024]{1,0:T(8,128)S(1)} custom-call(s32[2]{0:T(128)S(1)} %pad_add_fusion.2._, bf16[512,1024]{1,0:T(8,128)(2,1)S(1)} %copy-done.4, bf16[512,1024]{1,0:T(8,128)(2,1)S(1)} %copy-done.7, bf16[4096,1024]{1,0:T(8,128)(2,1)S(1)} %bitcast.108, bf16[4096,1024]{1,0:T(8,128)(2,1)S(1)} %bitcast.108), custom_call_target="tpu_custom_call" | custom-call | flops 2147483648 | bytes 10485760 | tf_op jit(solution)/shard_map/pallas_call | solution.py:60
  60.1 2.5 %shard_map.125.refs_7_ = f32[512,1024]{1,0:T(8,128)S(1)} custom-call(s32[2]{0:T(128)S(1)} %pad_add_fusion.1._, bf16[512,512]{1,0:T(8,128)(2,1)S(1)} %collective-permute-done.2.refs_0_, bf16[512,512]{1,0:T(8,128)(2,1)S(1)} %collective-permute-done.3.refs_1_, bf16[4096,1024]{1,0:T(8,128)(2,1)S(1)} %bitcast.108, bf16[4096,1024]{1,0:T(8,128)(2,1)S(1)} %bitcast.108, ...), custom_call_target="tpu_custom_call" | custom-call | flops 1073741824 | bytes 7340032 | tf_op jit(solution)/shard_map/pallas_call | solution.py:60
  62.6 3.5 %copy-done = bf16[4096,1024]{1,0:T(8,128)(2,1)S(1)} copy-done((bf16[4096,1024]{1,0:T(8,128)(2,1)S(1)}, bf16[4096,1024]{1,0:T(8,128)(2,1)}, u32[]{:S(2)}) %copy-start) | copy-done | bytes 8388632
  66.2 4.0 %shard_map.126 = (bf16[512,512]{1,0:T(8,128)(2,1)S(1)}, bf16[512,1024]{1,0:T(8,128)(2,1)S(1)}, bf16[2,128,512]{2,1,0:T(8,128)(2,1)S(1)}, bf16[2,128,512]{2,1,0:T(8,128)(2,1)S(1)}, f32[2,1,256]{2,1,0:T(1,128)S(1)}) custom-call(s32[3]{0:T(128)S(1)} %pad_add_fusion.3.info, bf16[512,512]{1,0:T(8,128)(2,1)S(1)} %collective-permute-done.refs_0_, ...), custom_call_target="tpu_custom_call" | custom-call | flops 1879048192 | bytes 7864320 | tf_op jit(solution)/shard_map/pallas_call | solution.py:179
  70.2 1.6 %collective-permute-start.14 = (bf16[2,128,512]{2,1,0:T(8,128)(2,1)S(1)}, bf16[2,128,512]{2,1,0:T(8,128)(2,1)S(1)}, u32[]{:S(2)}, u32[]{:S(2)}) collective-permute-start(bf16[2,128,512]{2,1,0:T(8,128)(2,1)S(1)} %get-tuple-element.27), channel_id=1, source_target_pairs={{0,4},{4,0},{8,12},{12,8},{16,20},{20,16},{24,28},{28,24},{1,5},{5... | collective-permute-start | bytes 786440 | tf_op jit(solution)/shard_map/ppermute | solution.py:27
  71.7 0.5 collective-permute-start.18
  72.3 3.5 %shard_map.127.refs_4_ = f32[512,1024]{1,0:T(8,128)S(1)} custom-call(s32[2]{0:T(128)S(1)} %pad_add_fusion.2._, bf16[512,1024]{1,0:T(8,128)(2,1)S(1)} %copy-done.4, bf16[512,1024]{1,0:T(8,128)(2,1)S(1)} %copy-done.8, bf16[4096,1024]{1,0:T(8,128)(2,1)S(1)} %bitcast.106, bf16[4096,1024]{1,0:T(8,128)(2,1)S(1)} %bitcast.106), custom_call_target="tpu_custom_call" | custom-call | flops 2147483648 | bytes 10485760 | tf_op jit(solution)/shard_map/pallas_call | solution.py:60
  75.8 2.7 %collective-permute-done.14 = bf16[2,128,512]{2,1,0:T(8,128)(2,1)S(1)} collective-permute-done((bf16[2,128,512]{2,1,0:T(8,128)(2,1)S(1)}, bf16[2,128,512]{2,1,0:T(8,128)(2,1)S(1)}, u32[]{:S(2)}, u32[]{:S(2)}) %collective-permute-start.14) | collective-permute-done | bytes 262176 | tf_op jit(solution)/shard_map/ppermute | solution.py:27
  78.7 4.2 %collective-permute-start.15 = (bf16[2,128,512]{2,1,0:T(8,128)(2,1)S(1)}, bf16[2,128,512]{2,1,0:T(8,128)(2,1)S(1)}, u32[]{:S(2)}, u32[]{:S(2)}) collective-permute-start(bf16[2,128,512]{2,1,0:T(8,128)(2,1)S(1)} %fusion.1), channel_id=1, source_target_pairs={{0,8},{4,12},{8,16},{12,20},{16,24},{20,28},{1,9},{5,13},{9,17},{1... | collective-permute-start | bytes 786440 | tf_op jit(solution)/shard_map/ppermute | solution.py:32
  82.9 1.8 %shard_map.118.refs_4_ = f32[512,512]{1,0:T(8,128)S(1)} custom-call(s32[2]{0:T(128)S(1)} %pad_add_fusion.2._, bf16[512,1024]{1,0:T(8,128)(2,1)S(1)} %copy-done.4, bf16[512,1024]{1,0:T(8,128)(2,1)S(1)} %copy-done.8, bf16[4096,512]{1,0:T(8,128)(2,1)S(1)} %copy-done.1, bf16[4096,512]{1,0:T(8,128)(2,1)S(1)} %copy-done.1), custom_call_target="tpu_custom_call" | custom-call | flops 1073741824 | bytes 6291456 | tf_op jit(solution)/shard_map/pallas_call | solution.py:60
  84.7 2.5 %shard_map.128.refs_4_ = f32[512,1024]{1,0:T(8,128)S(1)} custom-call(s32[2]{0:T(128)S(1)} %pad_add_fusion.1._, bf16[512,512]{1,0:T(8,128)(2,1)S(1)} %collective-permute-done.2.refs_0_, bf16[512,512]{1,0:T(8,128)(2,1)S(1)} %collective-permute-done.3.refs_1_, bf16[4096,1024]{1,0:T(8,128)(2,1)S(1)} %bitcast.106, bf16[4096,1024]{1,0:T(8,128)(2,1)S(1)} %bitcast.106, ...), custom_call_target="tpu_custom_call" | custom-call | flops 1073741824 | bytes 7340032 | tf_op jit(solution)/shard_map/pallas_call | solution.py:60
  87.1 2.5 %shard_map.129.gate = f32[512,1024]{1,0:T(8,128)S(1)} custom-call(s32[2]{0:T(128)S(1)} %pad_add_fusion._, bf16[512,512]{1,0:T(8,128)(2,1)S(1)} %collective-permute-done.refs_0_, bf16[512,512]{1,0:T(8,128)(2,1)S(1)} %collective-permute-done.1.refs_1_, bf16[4096,1024]{1,0:T(8,128)(2,1)S(1)} %bitcast.106, bf16[4096,1024]{1,0:T(8,128)(2,1)S(1)} %bitcast.106, ...), custom_call_target="tpu_custom_call" | custom-call | flops 1073741824 | bytes 7340032 | tf_op jit(solution)/shard_map/pallas_call | solution.py:60
  89.6 1.3 shard_map.119.refs_4_
  90.9 3.5 %collective-permute-start.16 = (bf16[2,128,512]{2,1,0:T(8,128)(2,1)S(1)}, bf16[2,128,512]{2,1,0:T(8,128)(2,1)S(1)}, u32[]{:S(2)}, u32[]{:S(2)}) collective-permute-start(bf16[2,128,512]{2,1,0:T(8,128)(2,1)S(1)} %collective-permute-done.15), channel_id=1, source_target_pairs={{0,8},{4,12},{8,16},{12,20},{16,24},{20,28},{1,9},{5,13},{9,17},{1... | collective-permute-start | bytes 786440 | tf_op jit(solution)/shard_map/ppermute | solution.py:32
  94.5 3.7 %collective-permute-start.19 = (f32[2,1,256]{2,1,0:T(1,128)S(1)}, f32[2,1,256]{2,1,0:T(1,128)S(1)}, u32[]{:S(2)}, u32[]{:S(2)}) collective-permute-start(f32[2,1,256]{2,1,0:T(1,128)S(1)} %multiply_add_fusion), channel_id=1, source_target_pairs={{0,8},{4,12},{8,16},{12,20},{16,24},{20,28},{1,9},{5,13},{9,17},{1... | collective-permute-start | bytes 6152 | tf_op jit(solution)/shard_map/ppermute | solution.py:32
  98.2 1.3 shard_map.120.query
  99.5 4.3 %collective-permute-start.20 = (f32[2,1,256]{2,1,0:T(1,128)S(1)}, f32[2,1,256]{2,1,0:T(1,128)S(1)}, u32[]{:S(2)}, u32[]{:S(2)}) collective-permute-start(f32[2,1,256]{2,1,0:T(1,128)S(1)} %collective-permute-done.19), channel_id=1, source_target_pairs={{0,8},{4,12},{8,16},{12,20},{16,24},{20,28},{1,9},{5,13},{9,17},{1... | collective-permute-start | bytes 6152 | tf_op jit(solution)/shard_map/ppermute | solution.py:32
  103.9 0.4 fusion.7
  104.3 1.6 %collective-permute-start.17 = (bf16[2,128,512]{2,1,0:T(8,128)(2,1)S(1)}, bf16[2,128,512]{2,1,0:T(8,128)(2,1)S(1)}, u32[]{:S(2)}, u32[]{:S(2)}) collective-permute-start(bf16[2,128,512]{2,1,0:T(8,128)(2,1)S(1)} %get-tuple-element.52), channel_id=1, source_target_pairs={{0,4},{4,0},{8,12},{12,8},{16,20},{20,16},{24,28},{28,24},{1,5},{5... | collective-permute-start | bytes 786440 | tf_op jit(solution)/shard_map/ppermute | solution.py:27
  106.0 3.0 %shard_map.130 = (f32[512,1024]{1,0:T(8,128)S(1)}, f32[512,1024]{1,0:T(8,128)S(1)}) custom-call(s32[1]{0:T(128)} %bitcast.14.place, s32[4]{0:T(128)S(1)} %copy-done.15, f32[2]{0:T(128)S(1)} %get-tuple-element.79.top_in, bf16[512,512]{1,0:T(8,128)(2,1)S(1)} %shard_map.120.query, bf16[512,512]{1,0:T(8,128)(2,1)S(1)} %copy-done.12, ...), custom_call_target="tpu_custom_call" | custom-call | flops 805306368 | bytes 8388608 | tf_op jit(solution)/shard_map/pallas_call | solution.py:262
  109.0 1.8 %collective-permute-done.17.other = bf16[2,128,512]{2,1,0:T(8,128)(2,1)S(1)} collective-permute-done((bf16[2,128,512]{2,1,0:T(8,128)(2,1)S(1)}, bf16[2,128,512]{2,1,0:T(8,128)(2,1)S(1)}, u32[]{:S(2)}, u32[]{:S(2)}) %collective-permute-start.17) | collective-permute-done | bytes 262176 | tf_op jit(solution)/shard_map/ppermute | solution.py:27
  110.8 3.4 %shard_map.131 = (bf16[512,1024]{1,0:T(8,128)(2,1)S(1)}, bf16[512,512]{1,0:T(8,128)(2,1)S(1)}, bf16[512,512]{1,0:T(8,128)(2,1)S(1)}) custom-call(s32[5]{0:T(128)S(1)} %stack.138.info, bf16[512,512]{1,0:T(8,128)(2,1)S(1)} %shard_map.120.query, bf16[2,128,512]{2,1,0:T(8,128)(2,1)S(1)} %get-tuple-element.53.own, ...), custom_call_target="tpu_custom_call" | custom-call | flops 1342177280 | bytes 8388608 | tf_op jit(solution)/shard_map/pallas_call | solution.py:336
  114.3 2.9 %shard_map.132 = (bf16[512,512]{1,0:T(8,128)(2,1)S(1)}, bf16[512,512]{1,0:T(8,128)(2,1)S(1)}) custom-call(s32[4]{0:T(128)S(1)} %get-tuple-element.89.info, bf16[512,1024]{1,0:T(8,128)(2,1)S(1)} %get-tuple-element.36.hidden, bf16[1024,4096]{1,0:T(8,128)(2,1)S(1)} %bitcast.110), custom_call_target="tpu_custom_call" | custom-call | flops 1073741824 | bytes 4194304 | tf_op jit(solution)/shard_map/pallas_call | solution.py:373
  117.2 0.6 collective-permute-start.23
  117.9 2.9 %shard_map.134 = (bf16[512,512]{1,0:T(8,128)(2,1)S(1)}, bf16[512,512]{1,0:T(8,128)(2,1)S(1)}) custom-call(s32[4]{0:T(128)S(1)} %pad_add_fusion.6.info, bf16[512,1024]{1,0:T(8,128)(2,1)S(1)} %get-tuple-element.36.hidden, bf16[1024,4096]{1,0:T(8,128)(2,1)S(1)} %bitcast.110), custom_call_target="tpu_custom_call" | custom-call | flops 1073741824 | bytes 4194304 | tf_op jit(solution)/shard_map/pallas_call | solution.py:373
  120.9 2.9 %shard_map.133 = (bf16[512,512]{1,0:T(8,128)(2,1)S(1)}, bf16[512,512]{1,0:T(8,128)(2,1)S(1)}) custom-call(s32[4]{0:T(128)S(1)} %get-tuple-element.90.info, bf16[512,1024]{1,0:T(8,128)(2,1)S(1)} %get-tuple-element.36.hidden, bf16[1024,4096]{1,0:T(8,128)(2,1)S(1)} %bitcast.110), custom_call_target="tpu_custom_call" | custom-call | flops 1073741824 | bytes 4194304 | tf_op jit(solution)/shard_map/pallas_call | solution.py:373
  123.8 0.6 collective-permute-start.25
  124.6 0.6 collective-permute-start.22
  125.4 1.6 %collective-permute-start.24 = (bf16[512,256]{1,0:T(8,128)(2,1)S(1)}, bf16[512,256]{1,0:T(8,128)(2,1)S(1)}, u32[]{:S(2)}, u32[]{:S(2)}) collective-permute-start(bf16[512,256]{1,0:T(8,128)(2,1)S(1)} %slice.231), channel_id=1, source_target_pairs={{0,2},{1,3},{2,0},{3,1},{4,6},{5,7},{6,4},{7,5},{8,10},{9,11},{10,... | collective-permute-start | bytes 786440 | tf_op jit(solution)/shard_map/ppermute | solution.py:27
  127.1 0.6 collective-permute-start.28
  127.9 1.6 %collective-permute-start.26 = (bf16[512,256]{1,0:T(8,128)(2,1)S(1)}, bf16[512,256]{1,0:T(8,128)(2,1)S(1)}, u32[]{:S(2)}, u32[]{:S(2)}) collective-permute-start(bf16[512,256]{1,0:T(8,128)(2,1)S(1)} %slice.230), channel_id=1, source_target_pairs={{0,2},{1,3},{2,0},{3,1},{4,6},{5,7},{6,4},{7,5},{8,10},{9,11},{10,... | collective-permute-start | bytes 786440 | tf_op jit(solution)/shard_map/ppermute | solution.py:27
  129.5 4.3 %collective-permute-done.22 = bf16[512,256]{1,0:T(8,128)(2,1)S(1)} collective-permute-done((bf16[512,256]{1,0:T(8,128)(2,1)S(1)}, bf16[512,256]{1,0:T(8,128)(2,1)S(1)}, u32[]{:S(2)}, u32[]{:S(2)}) %collective-permute-start.22) | collective-permute-done | bytes 262176 | tf_op jit(solution)/shard_map/ppermute | solution.py:27
  133.8 5.6 %collective-permute-done.24 = bf16[512,256]{1,0:T(8,128)(2,1)S(1)} collective-permute-done((bf16[512,256]{1,0:T(8,128)(2,1)S(1)}, bf16[512,256]{1,0:T(8,128)(2,1)S(1)}, u32[]{:S(2)}, u32[]{:S(2)}) %collective-permute-start.24) | collective-permute-done | bytes 262176 | tf_op jit(solution)/shard_map/ppermute | solution.py:27
  139.4 5.6 %collective-permute-done.28 = bf16[512,256]{1,0:T(8,128)(2,1)S(1)} collective-permute-done((bf16[512,256]{1,0:T(8,128)(2,1)S(1)}, bf16[512,256]{1,0:T(8,128)(2,1)S(1)}, u32[]{:S(2)}, u32[]{:S(2)}) %collective-permute-start.28) | collective-permute-done | bytes 262176 | tf_op jit(solution)/shard_map/ppermute | solution.py:27
  145.0 4.7 %collective-permute-done.26 = bf16[512,256]{1,0:T(8,128)(2,1)S(1)} collective-permute-done((bf16[512,256]{1,0:T(8,128)(2,1)S(1)}, bf16[512,256]{1,0:T(8,128)(2,1)S(1)}, u32[]{:S(2)}, u32[]{:S(2)}) %collective-permute-start.26) | collective-permute-done | bytes 262176 | tf_op jit(solution)/shard_map/ppermute | solution.py:27
  149.7 0.5 fusion.15
  150.2 1.1 pad_maximum_fusion
  (110 shorter events, 3.1 us)
Async XLA Ops:
  0.0 18.1 %copy-start.4 = (bf16[512,1024]{1,0:T(8,128)(2,1)S(1)}, bf16[512,1024]{1,0:T(8,128)(2,1)}, u32[]{:S(2)}) copy-start(bf16[512,1024]{1,0:T(8,128)(2,1)} %refs_0_.7) | copy-start | bytes 3145732
  0.0 5.2 %copy-start.18 = (bf16[2,4096,2]{1,2,0:T(2,128)(2,1)S(1)}, bf16[2,4096,2]{1,2,0:T(2,128)(2,1)}, u32[]{:S(2)}) copy-start(bf16[2,4096,2]{1,2,0:T(2,128)(2,1)} %param.17) | copy-start | bytes 98308
  0.0 7.4 %copy-start.15 = (s32[4]{0:T(128)S(1)}, s32[4]{0:T(128)}, u32[]{:S(2)}) copy-start(s32[4]{0:T(128)} %docs.3) | copy-start | bytes 52
  0.0 30.1 %copy-start.16 = (f32[2,2]{1,0:T(2,128)S(1)}, f32[2,2]{1,0:T(2,128)}, u32[]{:S(2)}) copy-start(f32[2,2]{1,0:T(2,128)} %bias.1) | copy-start | bytes 52
  0.0 46.3 %copy-start.20 = (f32[2]{0:T(128)S(1)}, f32[2]{0:T(128)}, u32[]{:S(2)}) copy-start(f32[2]{0:T(128)} %param.22) | copy-start | bytes 28
  0.0 46.5 %copy-start.19 = (f32[2,256]{1,0:T(2,128)S(1)}, f32[2,256]{1,0:T(2,128)}, u32[]{:S(2)}) copy-start(f32[2,256]{1,0:T(2,128)} %param.21) | copy-start | bytes 6148
  0.0 47.1 %collective-permute-start.4 = (bf16[512,1024]{1,0:T(8,128)(2,1)}, bf16[512,1024]{1,0:T(8,128)(2,1)S(1)}, u32[]{:S(2)}, u32[]{:S(2)}) collective-permute-start(bf16[512,1024]{1,0:T(8,128)(2,1)} %refs_0_.7), channel_id=1, source_target_pairs={{0,1},{1,0},{2,3},{3,2},{4,5},{5,4},{6,7},{7,6},{8,9},{9,8},{10,11... | collective-permute-start | bytes 3145736 | tf_op jit(solution)/shard_map/ppermute | solution.py:27
  2.6 44.0 %collective-permute-start = (bf16[512,512]{1,0:T(8,128)(2,1)S(1)}, bf16[512,512]{1,0:T(8,128)(2,1)S(1)}, u32[]{:S(2)}, u32[]{:S(2)}) collective-permute-start(bf16[512,512]{1,0:T(8,128)(2,1)S(1)} %get-tuple-element.59), channel_id=1, source_target_pairs={{0,2},{1,3},{2,0},{3,1},{4,6},{5,7},{6,4},{7,5},{8,10},{9,11},{10,... | collective-permute-start | bytes 1572872 | tf_op jit(solution)/shard_map/ppermute | solution.py:27
  5.3 12.3 %collective-permute-start.7 = (bf16[4,1024]{1,0:T(4,128)(2,1)S(1)}, bf16[4,1024]{1,0:T(4,128)(2,1)S(1)}, u32[]{:S(2)}, u32[]{:S(2)}) collective-permute-start(bf16[4,1024]{1,0:T(4,128)(2,1)S(1)} %get-tuple-element.64), channel_id=1, source_target_pairs={{0,3},{1,2},{2,1},{3,0},{4,7},{5,6},{6,5},{7,4},{8,11},{9,10},{10,... | collective-permute-start | bytes 24584 | tf_op jit(solution)/shard_map/ppermute | solution.py:27
  5.4 12.7 %collective-permute-start.6 = (bf16[4,1024]{1,0:T(4,128)(2,1)S(1)}, bf16[4,1024]{1,0:T(4,128)(2,1)S(1)}, u32[]{:S(2)}, u32[]{:S(2)}) collective-permute-start(bf16[4,1024]{1,0:T(4,128)(2,1)S(1)} %get-tuple-element.65), channel_id=1, source_target_pairs={{0,2},{1,3},{2,0},{3,1},{4,6},{5,7},{6,4},{7,5},{8,10},{9,11},{10,... | collective-permute-start | bytes 24584 | tf_op jit(solution)/shard_map/ppermute | solution.py:27
  7.2 10.9 %collective-permute-start.5 = (bf16[4,1024]{1,0:T(4,128)(2,1)S(1)}, bf16[4,1024]{1,0:T(4,128)(2,1)S(1)}, u32[]{:S(2)}, u32[]{:S(2)}) collective-permute-start(bf16[4,1024]{1,0:T(4,128)(2,1)S(1)} %get-tuple-element.66), channel_id=1, source_target_pairs={{0,1},{1,0},{2,3},{3,2},{4,5},{5,4},{6,7},{7,6},{8,9},{9,8},{10,11... | collective-permute-start | bytes 24584 | tf_op jit(solution)/shard_map/ppermute | solution.py:27
  18.5 9.9 %collective-permute-start.10 = (f32[4,512]{1,0:T(4,128)S(1)}, f32[4,512]{1,0:T(4,128)S(1)}, u32[]{:S(2)}, u32[]{:S(2)}) collective-permute-start(f32[4,512]{1,0:T(4,128)S(1)} %get-tuple-element.61), channel_id=1, source_target_pairs={{0,3},{1,2},{2,1},{3,0},{4,7},{5,6},{6,5},{7,4},{8,11},{9,10},{10,... | collective-permute-start | bytes 24584 | tf_op jit(solution)/shard_map/ppermute | solution.py:27
  19.9 10.3 %collective-permute-start.8 = (f32[4,512]{1,0:T(4,128)S(1)}, f32[4,512]{1,0:T(4,128)S(1)}, u32[]{:S(2)}, u32[]{:S(2)}) collective-permute-start(f32[4,512]{1,0:T(4,128)S(1)} %get-tuple-element.62), channel_id=1, source_target_pairs={{0,1},{1,0},{2,3},{3,2},{4,5},{5,4},{6,7},{7,6},{8,9},{9,8},{10,11... | collective-permute-start | bytes 24584 | tf_op jit(solution)/shard_map/ppermute | solution.py:27
  20.4 9.7 %collective-permute-start.9 = (f32[4,512]{1,0:T(4,128)S(1)}, f32[4,512]{1,0:T(4,128)S(1)}, u32[]{:S(2)}, u32[]{:S(2)}) collective-permute-start(f32[4,512]{1,0:T(4,128)S(1)} %get-tuple-element.60), channel_id=1, source_target_pairs={{0,2},{1,3},{2,0},{3,1},{4,6},{5,7},{6,4},{7,5},{8,10},{9,11},{10,... | collective-permute-start | bytes 24584 | tf_op jit(solution)/shard_map/ppermute | solution.py:27
  28.4 18.1 %collective-permute-start.2 = (bf16[512,512]{1,0:T(8,128)(2,1)}, bf16[512,512]{1,0:T(8,128)(2,1)S(1)}, u32[]{:S(2)}, u32[]{:S(2)}) collective-permute-start(bf16[512,512]{1,0:T(8,128)(2,1)} %get-tuple-element.58), channel_id=1, source_target_pairs={{0,2},{1,3},{2,0},{3,1},{4,6},{5,7},{6,4},{7,5},{8,10},{9,11},{10,... | collective-permute-start | bytes 1572872 | tf_op jit(solution)/shard_map/ppermute | solution.py:27
  31.5 0.7 copy-start.13
  32.4 3.6 %collective-permute-start.11 = (f32[2,2]{1,0:T(2,128)S(1)}, f32[2,2]{1,0:T(2,128)S(1)}, u32[]{:S(2)}, u32[]{:S(2)}) collective-permute-start(f32[2,2]{1,0:T(2,128)S(1)} %pad_maximum_fusion.2), channel_id=1, source_target_pairs={{0,4},{4,0},{8,12},{12,8},{16,20},{20,16},{24,28},{28,24},{1,5},{5... | collective-permute-start | bytes 56 | tf_op jit(solution)/shard_map/ppermute | solution.py:27
  36.1 4.8 %collective-permute-start.12 = (f32[2,2]{1,0:T(2,128)S(1)}, f32[2,2]{1,0:T(2,128)S(1)}, u32[]{:S(2)}, u32[]{:S(2)}) collective-permute-start(f32[2,2]{1,0:T(2,128)S(1)} %pad_maximum_fusion.3), channel_id=1, source_target_pairs={{0,8},{4,12},{8,16},{12,20},{16,24},{20,28},{1,9},{5,13},{9,17},{1... | collective-permute-start | bytes 56 | tf_op jit(solution)/shard_map/ppermute | solution.py:32
  40.9 5.5 %collective-permute-start.13 = (f32[2,2]{1,0:T(2,128)S(1)}, f32[2,2]{1,0:T(2,128)S(1)}, u32[]{:S(2)}, u32[]{:S(2)}) collective-permute-start(f32[2,2]{1,0:T(2,128)S(1)} %collective-permute-done.12), channel_id=1, source_target_pairs={{0,8},{4,12},{8,16},{12,20},{16,24},{20,28},{1,9},{5,13},{9,17},{1... | collective-permute-start | bytes 56 | tf_op jit(solution)/shard_map/ppermute | solution.py:32
  46.5 6.9 %collective-permute-start.3 = (bf16[512,512]{1,0:T(8,128)(2,1)S(1)}, bf16[512,512]{1,0:T(8,128)(2,1)S(1)}, u32[]{:S(2)}, u32[]{:S(2)}) collective-permute-start(bf16[512,512]{1,0:T(8,128)(2,1)S(1)} %collective-permute-done.2.refs_0_), channel_id=1, source_target_pairs={{0,1},{1,0},{2,3},{3,2},{4,5},{5,4},{6,7},{7,6},{8,9},{9,8},{10,11... | collective-permute-start | bytes 1572872 | tf_op jit(solution)/shard_map/ppermute | solution.py:27
  46.6 16.0 %collective-permute-start.1 = (bf16[512,512]{1,0:T(8,128)(2,1)S(1)}, bf16[512,512]{1,0:T(8,128)(2,1)S(1)}, u32[]{:S(2)}, u32[]{:S(2)}) collective-permute-start(bf16[512,512]{1,0:T(8,128)(2,1)S(1)} %collective-permute-done.refs_0_), channel_id=1, source_target_pairs={{0,1},{1,0},{2,3},{3,2},{4,5},{5,4},{6,7},{7,6},{8,9},{9,8},{10,11... | collective-permute-start | bytes 1572872 | tf_op jit(solution)/shard_map/ppermute | solution.py:27
  47.1 1.0 copy-start.5
  48.1 2.2 %copy-start.2 = (bf16[4096,512]{1,0:T(8,128)(2,1)S(1)}, bf16[4096,512]{1,0:T(8,128)(2,1)}, u32[]{:S(2)}) copy-start(bf16[4096,512]{1,0:T(8,128)(2,1)} %refs_3_.18) | copy-start | bytes 12582916
  50.3 1.2 copy-start.6
  51.5 2.2 %copy-start.3 = (bf16[4096,512]{1,0:T(8,128)(2,1)S(1)}, bf16[4096,512]{1,0:T(8,128)(2,1)}, u32[]{:S(2)}) copy-start(bf16[4096,512]{1,0:T(8,128)(2,1)} %refs_3_.18) | copy-start | bytes 12582916
  51.5 3.5 %slice-start.2 = ((s8[8388608]{0:T(1024)(128)(4,1)}), s8[4194304]{0:T(1024)(128)(4,1)S(1)}, s32[]{:S(2)}) async-start(s8[8388608]{0:T(1024)(128)(4,1)} %bitcast.107), calls=%async_computation.2 | async-start | bytes 8388608
  53.3 3.1 %slice-start.3 = ((s8[8388608]{0:T(1024)(128)(4,1)}), s8[4194304]{0:T(1024)(128)(4,1)S(1)}, s32[]{:S(2)}) async-start(s8[8388608]{0:T(1024)(128)(4,1)} %bitcast.107), calls=%async_computation.3 | async-start | bytes 8388608
  53.3 3.3 %copy-start.7 = (bf16[512,1024]{1,0:T(8,128)(2,1)S(1)}, bf16[512,1024]{1,0:T(8,128)(2,1)}, u32[]{:S(2)}) copy-start(bf16[512,1024]{1,0:T(8,128)(2,1)} %copy-done.5) | copy-start | bytes 3145732
  60.1 2.5 %copy-start.14 = (f32[512,128]{1,0:T(8,128)S(1)}, f32[512,128]{1,0:T(8,128)}, u32[]{:S(2)}) copy-start(f32[512,128]{1,0:T(8,128)} %copy-done.13) | copy-start | bytes 786436
  62.6 9.7 %slice-start = ((s8[8388608]{0:T(1024)(128)(4,1)}), s8[4194304]{0:T(1024)(128)(4,1)S(1)}, s32[]{:S(2)}) async-start(s8[8388608]{0:T(1024)(128)(4,1)} %bitcast.105), calls=%async_computation | async-start | bytes 8388608
  62.6 3.5 %copy-start = (bf16[4096,1024]{1,0:T(8,128)(2,1)S(1)}, bf16[4096,1024]{1,0:T(8,128)(2,1)}, u32[]{:S(2)}) copy-start(bf16[4096,1024]{1,0:T(8,128)(2,1)} %refs_5_.1) | copy-start | bytes 25165828
  66.2 6.1 %slice-start.1 = ((s8[8388608]{0:T(1024)(128)(4,1)}), s8[4194304]{0:T(1024)(128)(4,1)S(1)}, s32[]{:S(2)}) async-start(s8[8388608]{0:T(1024)(128)(4,1)} %bitcast.105), calls=%async_computation.1 | async-start | bytes 8388608
  66.2 6.1 %copy-start.8 = (bf16[512,1024]{1,0:T(8,128)(2,1)S(1)}, bf16[512,1024]{1,0:T(8,128)(2,1)}, u32[]{:S(2)}) copy-start(bf16[512,1024]{1,0:T(8,128)(2,1)} %copy-done.5) | copy-start | bytes 3145732
  70.1 5.7 %copy-start.9 = (bf16[512,1024]{1,0:T(8,128)(2,1)}, bf16[512,1024]{1,0:T(8,128)(2,1)S(1)}, u32[]{:S(2)}) copy-start(bf16[512,1024]{1,0:T(8,128)(2,1)S(1)} %get-tuple-element.29.value) | copy-start | bytes 3145732
  70.2 5.7 %copy-start.11 = (bf16[512,512]{1,0:T(8,128)(2,1)}, bf16[512,512]{1,0:T(8,128)(2,1)S(1)}, u32[]{:S(2)}) copy-start(bf16[512,512]{1,0:T(8,128)(2,1)S(1)} %get-tuple-element.28.key) | copy-start | bytes 1572868
  70.2 8.3 %collective-permute-start.14 = (bf16[2,128,512]{2,1,0:T(8,128)(2,1)S(1)}, bf16[2,128,512]{2,1,0:T(8,128)(2,1)S(1)}, u32[]{:S(2)}, u32[]{:S(2)}) collective-permute-start(bf16[2,128,512]{2,1,0:T(8,128)(2,1)S(1)} %get-tuple-element.27), channel_id=1, source_target_pairs={{0,4},{4,0},{8,12},{12,8},{16,20},{20,16},{24,28},{28,24},{1,5},{5... | collective-permute-start | bytes 786440 | tf_op jit(solution)/shard_map/ppermute | solution.py:27
  71.7 22.7 %collective-permute-start.18 = (f32[2,1,256]{2,1,0:T(1,128)S(1)}, f32[2,1,256]{2,1,0:T(1,128)S(1)}, u32[]{:S(2)}, u32[]{:S(2)}) collective-permute-start(f32[2,1,256]{2,1,0:T(1,128)S(1)} %get-tuple-element.31), channel_id=1, source_target_pairs={{0,4},{4,0},{8,12},{12,8},{16,20},{20,16},{24,28},{28,24},{1,5},{5... | collective-permute-start | bytes 6152 | tf_op jit(solution)/shard_map/ppermute | solution.py:27
  72.3 10.6 %copy-start.1 = (bf16[4096,512]{1,0:T(8,128)(2,1)S(1)}, bf16[4096,512]{1,0:T(8,128)(2,1)}, u32[]{:S(2)}) copy-start(bf16[4096,512]{1,0:T(8,128)(2,1)} %refs_3_.13) | copy-start | bytes 12582916
  78.7 12.2 %collective-permute-start.15 = (bf16[2,128,512]{2,1,0:T(8,128)(2,1)S(1)}, bf16[2,128,512]{2,1,0:T(8,128)(2,1)S(1)}, u32[]{:S(2)}, u32[]{:S(2)}) collective-permute-start(bf16[2,128,512]{2,1,0:T(8,128)(2,1)S(1)} %fusion.1), channel_id=1, source_target_pairs={{0,8},{4,12},{8,16},{12,20},{16,24},{20,28},{1,9},{5,13},{9,17},{1... | collective-permute-start | bytes 786440 | tf_op jit(solution)/shard_map/ppermute | solution.py:32
  89.6 21.1 %slice-start.4 = ((s8[8388608]{0:T(1024)(128)(4,1)}), s8[4194304]{0:T(1024)(128)(4,1)S(1)}, s32[]{:S(2)}) async-start(s8[8388608]{0:T(1024)(128)(4,1)} %bitcast.109), calls=%async_computation.4 | async-start | bytes 8388608
  90.9 13.0 %collective-permute-start.16 = (bf16[2,128,512]{2,1,0:T(8,128)(2,1)S(1)}, bf16[2,128,512]{2,1,0:T(8,128)(2,1)S(1)}, u32[]{:S(2)}, u32[]{:S(2)}) collective-permute-start(bf16[2,128,512]{2,1,0:T(8,128)(2,1)S(1)} %collective-permute-done.15), channel_id=1, source_target_pairs={{0,8},{4,12},{8,16},{12,20},{16,24},{20,28},{1,9},{5,13},{9,17},{1... | collective-permute-start | bytes 786440 | tf_op jit(solution)/shard_map/ppermute | solution.py:32
  94.5 9.4 %copy-start.17 = (f32[2,256,512]{2,1,0:T(8,128)S(1)}, f32[2,256,512]{2,1,0:T(8,128)}, u32[]{:S(2)}) copy-start(f32[2,256,512]{2,1,0:T(8,128)} %param.20) | copy-start | bytes 3145732
  94.5 16.3 %slice-start.5 = ((s8[8388608]{0:T(1024)(128)(4,1)}), s8[4194304]{0:T(1024)(128)(4,1)S(1)}, s32[]{:S(2)}) async-start(s8[8388608]{0:T(1024)(128)(4,1)} %bitcast.109), calls=%async_computation.5 | async-start | bytes 8388608
  94.5 5.0 %collective-permute-start.19 = (f32[2,1,256]{2,1,0:T(1,128)S(1)}, f32[2,1,256]{2,1,0:T(1,128)S(1)}, u32[]{:S(2)}, u32[]{:S(2)}) collective-permute-start(f32[2,1,256]{2,1,0:T(1,128)S(1)} %multiply_add_fusion), channel_id=1, source_target_pairs={{0,8},{4,12},{8,16},{12,20},{16,24},{20,28},{1,9},{5,13},{9,17},{1... | collective-permute-start | bytes 6152 | tf_op jit(solution)/shard_map/ppermute | solution.py:32
  99.5 6.5 %copy-start.10 = (bf16[512,1024]{1,0:T(8,128)(2,1)S(1)}, bf16[512,1024]{1,0:T(8,128)(2,1)}, u32[]{:S(2)}) copy-start(bf16[512,1024]{1,0:T(8,128)(2,1)} %copy-done.9) | copy-start | bytes 3145732
  99.5 6.5 %copy-start.12 = (bf16[512,512]{1,0:T(8,128)(2,1)S(1)}, bf16[512,512]{1,0:T(8,128)(2,1)}, u32[]{:S(2)}) copy-start(bf16[512,512]{1,0:T(8,128)(2,1)} %copy-done.11) | copy-start | bytes 1572868
  99.5 6.4 %collective-permute-start.20 = (f32[2,1,256]{2,1,0:T(1,128)S(1)}, f32[2,1,256]{2,1,0:T(1,128)S(1)}, u32[]{:S(2)}, u32[]{:S(2)}) collective-permute-start(f32[2,1,256]{2,1,0:T(1,128)S(1)} %collective-permute-done.19), channel_id=1, source_target_pairs={{0,8},{4,12},{8,16},{12,20},{16,24},{20,28},{1,9},{5,13},{9,17},{1... | collective-permute-start | bytes 6152 | tf_op jit(solution)/shard_map/ppermute | solution.py:32
  104.3 6.4 %collective-permute-start.17 = (bf16[2,128,512]{2,1,0:T(8,128)(2,1)S(1)}, bf16[2,128,512]{2,1,0:T(8,128)(2,1)S(1)}, u32[]{:S(2)}, u32[]{:S(2)}) collective-permute-start(bf16[2,128,512]{2,1,0:T(8,128)(2,1)S(1)} %get-tuple-element.52), channel_id=1, source_target_pairs={{0,4},{4,0},{8,12},{12,8},{16,20},{20,16},{24,28},{28,24},{1,5},{5... | collective-permute-start | bytes 786440 | tf_op jit(solution)/shard_map/ppermute | solution.py:27
  114.2 10.2 %collective-permute-start.21 = (bf16[512,512]{1,0:T(8,128)(2,1)S(1)}, bf16[512,512]{1,0:T(8,128)(2,1)S(1)}, u32[]{:S(2)}, u32[]{:S(2)}) collective-permute-start(bf16[512,512]{1,0:T(8,128)(2,1)S(1)} %get-tuple-element.35), channel_id=1, source_target_pairs={{0,1},{1,0},{2,3},{3,2},{4,5},{5,4},{6,7},{7,6},{8,9},{9,8},{10,11... | collective-permute-start | bytes 1572872 | tf_op jit(solution)/shard_map/ppermute | solution.py:27
  117.2 7.9 %collective-permute-start.23 = (bf16[512,512]{1,0:T(8,128)(2,1)S(1)}, bf16[512,512]{1,0:T(8,128)(2,1)S(1)}, u32[]{:S(2)}, u32[]{:S(2)}) collective-permute-start(bf16[512,512]{1,0:T(8,128)(2,1)S(1)} %get-tuple-element.38), channel_id=1, source_target_pairs={{0,1},{1,0},{2,3},{3,2},{4,5},{5,4},{6,7},{7,6},{8,9},{9,8},{10,11... | collective-permute-start | bytes 1572872 | tf_op jit(solution)/shard_map/ppermute | solution.py:27
  120.8 6.1 %collective-permute-start.27 = (bf16[512,512]{1,0:T(8,128)(2,1)S(1)}, bf16[512,512]{1,0:T(8,128)(2,1)S(1)}, u32[]{:S(2)}, u32[]{:S(2)}) collective-permute-start(bf16[512,512]{1,0:T(8,128)(2,1)S(1)} %get-tuple-element.42), channel_id=1, source_target_pairs={{0,1},{1,0},{2,3},{3,2},{4,5},{5,4},{6,7},{7,6},{8,9},{9,8},{10,11... | collective-permute-start | bytes 1572872 | tf_op jit(solution)/shard_map/ppermute | solution.py:27
  123.8 3.9 %collective-permute-start.25 = (bf16[512,512]{1,0:T(8,128)(2,1)S(1)}, bf16[512,512]{1,0:T(8,128)(2,1)S(1)}, u32[]{:S(2)}, u32[]{:S(2)}) collective-permute-start(bf16[512,512]{1,0:T(8,128)(2,1)S(1)} %get-tuple-element.40), channel_id=1, source_target_pairs={{0,1},{1,0},{2,3},{3,2},{4,5},{5,4},{6,7},{7,6},{8,9},{9,8},{10,11... | collective-permute-start | bytes 1572872 | tf_op jit(solution)/shard_map/ppermute | solution.py:27
  124.6 9.2 %collective-permute-start.22 = (bf16[512,256]{1,0:T(8,128)(2,1)S(1)}, bf16[512,256]{1,0:T(8,128)(2,1)S(1)}, u32[]{:S(2)}, u32[]{:S(2)}) collective-permute-start(bf16[512,256]{1,0:T(8,128)(2,1)S(1)} %slice.232), channel_id=1, source_target_pairs={{0,2},{1,3},{2,0},{3,1},{4,6},{5,7},{6,4},{7,5},{8,10},{9,11},{10,... | collective-permute-start | bytes 786440 | tf_op jit(solution)/shard_map/ppermute | solution.py:27
  125.4 14.1 %collective-permute-start.24 = (bf16[512,256]{1,0:T(8,128)(2,1)S(1)}, bf16[512,256]{1,0:T(8,128)(2,1)S(1)}, u32[]{:S(2)}, u32[]{:S(2)}) collective-permute-start(bf16[512,256]{1,0:T(8,128)(2,1)S(1)} %slice.231), channel_id=1, source_target_pairs={{0,2},{1,3},{2,0},{3,1},{4,6},{5,7},{6,4},{7,5},{8,10},{9,11},{10,... | collective-permute-start | bytes 786440 | tf_op jit(solution)/shard_map/ppermute | solution.py:27
  127.1 17.9 %collective-permute-start.28 = (bf16[512,256]{1,0:T(8,128)(2,1)S(1)}, bf16[512,256]{1,0:T(8,128)(2,1)S(1)}, u32[]{:S(2)}, u32[]{:S(2)}) collective-permute-start(bf16[512,256]{1,0:T(8,128)(2,1)S(1)} %slice.229), channel_id=1, source_target_pairs={{0,2},{1,3},{2,0},{3,1},{4,6},{5,7},{6,4},{7,5},{8,10},{9,11},{10,... | collective-permute-start | bytes 786440 | tf_op jit(solution)/shard_map/ppermute | solution.py:27
  127.9 21.8 %collective-permute-start.26 = (bf16[512,256]{1,0:T(8,128)(2,1)S(1)}, bf16[512,256]{1,0:T(8,128)(2,1)S(1)}, u32[]{:S(2)}, u32[]{:S(2)}) collective-permute-start(bf16[512,256]{1,0:T(8,128)(2,1)S(1)} %slice.230), channel_id=1, source_target_pairs={{0,2},{1,3},{2,0},{3,1},{4,6},{5,7},{6,4},{7,5},{8,10},{9,11},{10,... | collective-permute-start | bytes 786440 | tf_op jit(solution)/shard_map/ppermute | solution.py:27

commit v2 on v1

--- a/solution.py
+++ b/solution.py
@@ -10,7 +10,7 @@
 BF = jnp.bfloat16
 F32 = jnp.float32
 MIB = 1024 * 1024
-TOKEN_CHUNKS = (512, 512)
+TOKEN_CHUNKS = ((256, 256), (512,))
 OUT_CHUNKS = (256, 256, 256, 256)
 
 
@@ -29,21 +29,45 @@
 
 def shifted(x, axis, by):
     size = lax.axis_size(axis)
-    return lax.ppermute(x, axis, [(i, i + by) for i in range(size - by)])
-
-
-def project_kernel(pieces, with_sum, finish, _, *refs):
+    return lax.ppermute(x, axis, [(i, (i + by) % size) for i in range(size)])
+
+
+def after(first, *others):
+    out = lax.optimization_barrier((first,) + others)[1:]
+    return out[0] if len(out) == 1 else out
+
+
+def project_kernel(pieces, with_sum, gated, finish, _, *refs):
     xs, ws = refs[:pieces], refs[pieces : 2 * pieces]
+    rest = refs[2 * pieces :]
     total = None
     for x, w in zip(xs, ws):
         part = jnp.dot(x[...], w[...], preferred_element_type=F32)
         total = part if total is None else total + part
     if with_sum:
-        total = total + refs[2 * pieces][...]
-    refs[-1][...] = finish(total).astype(refs[-1].dtype)
-
-
-def project(xs, rows, weight, summed=None, finish=lambda x: x, kind=F32):
+        total = total + rest[0][...]
+        rest = rest[1:]
+    if not gated:
+        (out,) = rest
+    else:
+        gate_ws, rest = rest[:pieces], rest[pieces:]
+        out, gate_out = rest[-2:]
+
+        @pl.when(pl.program_id(0) == 0)
+        def _():
+            gates = rest[0][...] if with_sum else 0.0
+            for x, w in zip(xs, gate_ws):
+                gates = gates + across_tokens(w[...], x[...])
+            gate_out[...] = gates
+
+    out[...] = finish(total).astype(out.dtype)
+
+
+def across_tokens(w, x):
+    return lax.dot_general(w, x, (((1,), (1,)), ((), ())), preferred_element_type=F32)
+
+
+def project(xs, rows, weight, summed=None, finish=lambda x: x, kind=F32, gate_w=None, gates=None):
     length, columns = xs[0].shape[0], weight.shape[1]
     wide = min(512, columns)
     depth = sum(x.shape[1] for x in xs)
@@ -57,20 +81,31 @@
     if summed is not None:
         specs.append(block)
         operands.append(summed)
+    shapes, outs = jax.ShapeDtypeStruct((length, columns), kind), block
+    if gate_w is not None:
+        count = gate_w.shape[0]
+        specs += [
+            pl.BlockSpec((count, x.shape[1]), functools.partial(lambda i, j, r: (0, r[i]), i))
+            for i, x in enumerate(xs)
+        ]
+        operands += [gate_w] * len(xs)
+        small = pl.BlockSpec((count, length), lambda j, r: (0, 0))
+        if summed is not None:
+            specs.append(small)
+            operands.append(gates)
+        shapes = (shapes, jax.ShapeDtypeStruct((count, length), F32))
+        outs = (block, small)
     return pl.pallas_call(
-        functools.partial(project_kernel, len(xs), summed is not None, finish),
-        out_shape=jax.ShapeDtypeStruct((length, columns), kind),
+        functools.partial(project_kernel, len(xs), summed is not None, gate_w is not None, finish),
+        out_shape=shapes,
         grid_spec=pltpu.PrefetchScalarGridSpec(
             num_scalar_prefetch=1,
             grid=(columns // wide,),
             in_specs=specs,
-            out_specs=block,
-        ),
-        compiler_params=params(24),
-        cost_estimate=cost(
-            2 * length * depth * columns,
-            2 * depth * (columns + length) + 8 * length * columns,
-        ),
+            out_specs=outs,
+        ),
+        compiler_params=params(60),
+        cost_estimate=cost(1e6, 1e5),
     )(jnp.stack(rows).astype(jnp.int32), *operands)
 
 
@@ -83,9 +118,8 @@
     return total
 
 
-def gates_kernel(heads, place, docs, bias, sums, u_out, weight_out, stats_out):
-    length = sums.shape[1]
-    offset = place[0]
+def gate_rows(both, offset, docs, bias):
+    heads, length = both.shape[0] // 2, both.shape[1]
     row = lax.broadcasted_iota(jnp.int32, (heads, length), 0)
     lane = lax.broadcasted_iota(jnp.int32, (heads, length), 1)
     input_bias = jnp.zeros((heads, length), F32)
@@ -93,7 +127,6 @@
     for h in range(heads):
         input_bias = jnp.where(row == h, bias[0, h], input_bias)
         forget_bias = jnp.where(row == h, bias[1, h], forget_bias)
-    both = sums[...]
     input_pre = both[:heads] + input_bias
     forget = both[heads:] + forget_bias
     decay = jnp.minimum(forget, 0.0) - jnp.log1p(jnp.exp(-jnp.abs(forget)))
@@ -108,38 +141,34 @@
     top = jnp.max(jnp.where(open_rows, u, -jnp.inf), axis=1, keepdims=True)
     weight = jnp.where(open_rows, jnp.exp(u - top), 0.0)
     total = decay[:, length - 1 : length]
-    u_out[...] = u
-    spare = jnp.zeros((128 - heads, length), F32)
-    weight_out[...] = jnp.concatenate([weight, spare], axis=0).T
     narrow = lax.broadcasted_iota(jnp.int32, (heads, 128), 1)
-    stats_out[...] = jnp.where(narrow == 0, total + top, jnp.where(narrow == 1, total, 0.0))
-
-
-def gate_rows(sums, bias, docs, offset):
-    heads, length = sums.shape[0] // 2, sums.shape[1]
-    smem = pl.BlockSpec(memory_space=pltpu.SMEM)
-    vmem = pl.BlockSpec(memory_space=pltpu.VMEM)
-    return pl.pallas_call(
-        functools.partial(gates_kernel, heads),
-        out_shape=(
-            jax.ShapeDtypeStruct((heads, length), F32),
-            jax.ShapeDtypeStruct((length, 128), F32),
-            jax.ShapeDtypeStruct((heads, 128), F32),
-        ),
-        in_specs=[smem, smem, smem, vmem],
-        out_specs=(vmem, vmem, vmem),
-        compiler_params=params(8),
-        cost_estimate=cost(1e6, 1e6),
-    )(offset[None], docs, bias, sums)
-
-
-def summary_kernel(pieces, scale, info, *refs):
+    stats = jnp.where(narrow == 0, total + top, jnp.where(narrow == 1, total, 0.0))
+    return u, weight, stats
+
+
+def summary_kernel(pieces, scale, info, docs, bias, *refs):
     xs = refs[:pieces]
     key_ws = refs[pieces : 2 * pieces]
     value_ws = refs[2 * pieces : 3 * pieces]
-    key_sum, value_sum, weight = refs[3 * pieces : 3 * pieces + 3]
-    key_out, value_out, keep_out, send_out, norm_out, state = refs[3 * pieces + 3 :]
+    gate_ws = refs[3 * pieces : 4 * pieces]
+    key_sum, value_sum, gate_sum = refs[4 * pieces : 4 * pieces + 3]
+    key_out, value_out, keep_out, send_out, small_out, u_out, weights, state = refs[
+        4 * pieces + 3 :
+    ]
     head = pl.program_id(0)
+    size = key_sum.shape[1]
+
+    @pl.when(head == 0)
+    def _():
+        gates = gate_sum[...]
+        for x, w in zip(xs, gate_ws):
+            gates = gates + across_tokens(w[...], x[...])
+        u, weight, stats = gate_rows(gates, info[pieces + 1], docs, bias)
+        u_out[...] = u
+        small_out[:, size:] = stats
+        spare = jnp.zeros((128 - weight.shape[0], weight.shape[1]), F32)
+        weights[...] = jnp.concatenate([weight, spare], axis=0).T
+
     key, value = key_sum[...], value_sum[...]
     for x, key_w, value_w in zip(xs, key_ws, value_ws):
         key = key + jnp.dot(x[...], key_w[...], preferred_element_type=F32)
@@ -148,10 +177,10 @@
     value = value.astype(BF)
     key_out[...] = key
     value_out[...] = value
-    lanes = lax.broadcasted_iota(jnp.int32, weight.shape, 1)
-    column = jnp.sum(jnp.where(lanes == head, weight[...], 0.0), axis=1, keepdims=True)
+    lanes = lax.broadcasted_iota(jnp.int32, weights.shape, 1)
+    column = jnp.sum(jnp.where(lanes == head, weights[...], 0.0), axis=1, keepdims=True)
     scaled = (column * key.astype(F32)).astype(BF)
-    norm_out[0] = jnp.sum(scaled.astype(F32), axis=0, keepdims=True)
+    small_out[pl.ds(head, 1), :size] = jnp.sum(scaled.astype(F32), axis=0, keepdims=True)
     state[...] = lax.dot_general(
         scaled, value, (((0,), (0,)), ((), ())), preferred_element_type=F32
     )
@@ -161,7 +190,9 @@
     send_out[0] = state[pl.ds(pl.multiple_of((1 - side) * half, half), half)].astype(BF)
 
 
-def block_summary(xs, rows, side, w_key, w_value, key_sum, value_sum, weight, heads):
+def block_summary(
+    xs, rows, side, offset, docs, bias, w_key, w_value, gate_w, key_sum, value_sum, gates, heads
+):
     length = xs[0].shape[0]
     size, wide = w_key.shape[1] // heads, w_value.shape[1] // heads
     pieces = len(xs)
@@ -170,11 +201,17 @@
     def weight_spec(i, columns):
         return pl.BlockSpec((xs[i].shape[1], columns), lambda h, r: (r[i], h))
 
-    specs = [pl.BlockSpec(x.shape, lambda h, r: (0, 0)) for x in xs]
+    def gate_spec(i):
+        return pl.BlockSpec((2 * heads, xs[i].shape[1]), lambda h, r: (0, r[i]))
+
+    whole = lambda shape: pl.BlockSpec(shape, lambda h, r: (0,) * len(shape))
+    smem = pl.BlockSpec(memory_space=pltpu.SMEM)
+    specs = [smem, smem] + [whole(x.shape) for x in xs]
     specs += [weight_spec(i, size) for i in range(pieces)]
     specs += [weight_spec(i, wide) for i in range(pieces)]
+    specs += [gate_spec(i) for i in range(pieces)]
     by_head = lambda columns: pl.BlockSpec((length, columns), lambda h, r: (0, h))
-    specs += [by_head(size), by_head(wide), pl.BlockSpec(weight.shape, lambda h, r: (0, 0))]
+    specs += [by_head(size), by_head(wide), whole(gates.shape)]
     half = pl.BlockSpec((1, size // 2, wide), lambda h, r: (h, 0, 0))
     return pl.pallas_call(
         functools.partial(summary_kernel, pieces, size ** (-0.5)),
@@ -183,7 +220,8 @@
             jax.ShapeDtypeStruct((length, heads * wide), BF),
             jax.ShapeDtypeStruct((heads, size // 2, wide), BF),
             jax.ShapeDtypeStruct((heads, size // 2, wide), BF),
-            jax.ShapeDtypeStruct((heads, 1, size), F32),
+            jax.ShapeDtypeStruct((heads, size + 128), F32),
+            jax.ShapeDtypeStruct((heads, length), F32),
         ),
         grid_spec=pltpu.PrefetchScalarGridSpec(
             num_scalar_prefetch=1,
@@ -194,23 +232,27 @@
                 by_head(wide),
                 half,
                 half,
-                pl.BlockSpec((1, 1, size), lambda h, r: (h, 0, 0)),
+                whole((heads, size + 128)),
+                whole((heads, length)),
             ),
-            scratch_shapes=[pltpu.VMEM((size, wide), F32)],
-        ),
-        compiler_params=params(32),
+            scratch_shapes=[pltpu.VMEM((length, 128), F32), pltpu.VMEM((size, wide), F32)],
+        ),
+        compiler_params=params(60),
         cost_estimate=cost(
             2 * length * heads * (depth * (size + wide) + size * wide),
             2 * depth * heads * (size + wide) + 6 * length * heads * (size + wide),
         ),
     )(
-        jnp.stack(list(rows) + [side]).astype(jnp.int32),
+        jnp.stack(list(rows) + [side, offset]).astype(jnp.int32),
+        docs,
+        bias,
         *xs,
         *([w_key] * pieces),
         *([w_value] * pieces),
+        *([gate_w] * pieces),
         key_sum,
         value_sum,
-        weight,
+        gates,
     )
 
 
@@ -278,7 +320,7 @@
             by_head(wide),
         ],
         out_specs=(by_head(wide), by_head(wide)),
-        compiler_params=params(32),
+        compiler_params=params(60),
         cost_estimate=cost(
             2 * length * length * heads * (size + wide),
             length * heads * (4 * size + 14 * wide),
@@ -345,7 +387,7 @@
             + out_specs_of(length, wide),
             scratch_shapes=[pltpu.VMEM((2 * own.shape[1], own.shape[2]), BF)],
         ),
-        compiler_params=params(32),
+        compiler_params=params(60),
         cost_estimate=cost(
             2 * length * depth * (4 * wide + query.shape[1] // heads),
             length * depth * 12 + depth * wide * 8,
@@ -382,7 +424,7 @@
             ],
             out_specs=out_specs_of(length, wide),
         ),
-        compiler_params=params(24),
+        compiler_params=params(60),
         cost_estimate=cost(
             8 * length * depth * wide, 2 * length * depth + depth * wide * 8 + length * wide * 8
         ),
@@ -418,35 +460,52 @@
     pair = lambda x: swapped(x, "seq", 1)
     down = lambda x: shifted(x, "seq", 2)
 
-    gate_rows_w = w_gates.transpose(0, 2, 1).reshape(2 * heads, 4 * share)
-    mine = [
-        lax.dynamic_slice(gate_rows_w, (0, (place ^ k) * share), (2 * heads, share))
-        for k in range(4)
-    ]
-    mine = [mine[0]] + [tensor(mine[k], k) for k in (1, 2, 3)]
-    starts = [sum(TOKEN_CHUNKS[:i]) for i in range(len(TOKEN_CHUNKS))]
-    across = [
-        tensor(tokens[:, s : s + c], 2) for s, c in zip(starts, TOKEN_CHUNKS)
-    ]
+    groups, source, start = [], tokens, 0
+    for chunks in TOKEN_CHUNKS:
+        group = []
+        for c in chunks:
+            piece = source[:, start : start + c]
+            group.append((start, c, tensor(piece, 2)))
+            source = after(piece, source)
+            start += c
+        groups.append(group)
     beside = tensor(tokens, 1)
-    gate_part = lax.dot_general(
-        jnp.concatenate(mine, axis=0),
-        tokens,
-        (((1,), (1,)), ((), ())),
-        preferred_element_type=F32,
-    )
-    gate_part = [gate_part[2 * heads * k : 2 * heads * (k + 1)] for k in range(4)]
-    gate_sum = gate_part[0] + sum(tensor(gate_part[k], k) for k in (1, 2, 3))
-    u, key_weight, stats = gate_rows(gate_sum, gate_bias, doc_lengths, offset)
+    gate_w = w_gates.transpose(0, 2, 1).reshape(2 * heads, 4 * share)
+
+    weights_qg = (w_query, w_outgate)
+    near = ([source, beside], [place, place ^ 1])
+    key_sum, gates = project(*near, w_key, gate_w=gate_w)
+    value_sum = project(*near, w_value)
+    sums = [project(*near, w) for w in weights_qg]
+    for group in groups:
+        xs = [x for _, _, x in group]
+        *xs, key_sum, value_sum, sums[0], sums[1] = lax.optimization_barrier(
+            (*xs, key_sum, value_sum, *sums)
+        )
+        rows = []
+        for s, c, _ in group:
+            rows += [((place ^ 2) * share + s) // c, ((place ^ 3) * share + s) // c]
+        far = ([y for x in xs for y in (x, tensor(x, 1))], rows)
+        if group is groups[-1]:
+            break
+        key_sum, gates = project(*far, w_key, key_sum, gate_w=gate_w, gates=gates)
+        value_sum = project(*far, w_value, value_sum)
+        sums = [project(*far, w, total) for w, total in zip(weights_qg, sums)]
 
     side = (block % 2).astype(jnp.int32)
+    keys, values, kept, sent, small, u = block_summary(
+        *far, side, offset, doc_lengths, gate_bias, w_key, w_value, gate_w,
+        key_sum, value_sum, gates, heads,
+    )
+
     even = side == 0
     z = block // 2
     reach = blocks // 4
-    mg = jnp.stack([stats[:, 0], stats[:, 1]])
-    mg_other = pair(mg)
-    m_even, g_even = pick(even, mg, mg_other)
-    m_odd, g_odd = pick(even, mg_other, mg)
+    small_other = pair(small)
+    got = pair(sent)
+    small_other, got = lax.optimization_barrier((small_other, got))
+    last_xs = after(keys, *far[0])
+    queries = project(last_xs, far[1], w_query, sums[0], kind=BF)
 
     def segment_at(position):
         return segments(doc_lengths, position)
@@ -455,19 +514,48 @@
         first = jnp.maximum(index * length - 1, 0)
         return segment_at((index + 1) * length - 1) != segment_at(first)
 
+    def packed(norm, m, g):
+        return jnp.concatenate(
+            [norm, m[:, None], g[:, None], jnp.zeros((heads, 126), F32)], axis=1
+        )
+
+    def unpacked(x):
+        return x[:, :size], x[:, size], x[:, size + 1]
+
+    norm_own, m_own, g_own = unpacked(small)
+    norm_other, m_other, g_other = unpacked(small_other)
+    m_even, g_even = pick(even, m_own, m_other), pick(even, g_own, g_other)
+    m_odd, g_odd = pick(even, m_other, m_own), pick(even, g_other, g_own)
     reset_even, reset_odd = reset(2 * z), reset(2 * z + 1)
     m_pair = jnp.maximum(pick(reset_odd, -jnp.inf, m_even + g_odd), m_odd)
     pair_even = pick(reset_odd, 0.0, jnp.exp(jnp.minimum(m_even + g_odd - m_pair, 0.0)))
     pair_odd = jnp.exp(m_odd - m_pair)
-    travelling = jnp.stack([m_pair, g_even + g_odd])
+    pair_own = pick(even, pair_even, pair_odd)
+    pair_other = pick(even, pair_odd, pair_even)
+
+    spread = lambda w: w[:, None, None]
+    norm_pair = pair_own[:, None] * norm_own + pair_other[:, None] * norm_other
+    norm_even = pick(even, norm_own, norm_other)
+    kept, got = kept.astype(F32), got.astype(F32)
+    state_even = pick(even, kept, got)
+    state_pair = (spread(pair_own) * kept + spread(pair_other) * got).astype(BF)
+
+    travel = packed(norm_pair, m_pair, g_even + g_odd)
+    smalls, states = [], []
+    for k in range(reach):
+        travel, state_pair = lax.optimization_barrier((down(travel), down(state_pair)))
+        if k == 0:
+            last_xs = after(got, *last_xs)
+            gate = project(last_xs, far[1], w_outgate, sums[1], jax.nn.sigmoid)
+        smalls.append(unpacked(travel))
+        states.append(state_pair)
     expos = []
     passed = jnp.zeros_like(m_pair)
     unbroken = jnp.bool_(True)
     for k in range(1, reach + 1):
-        travelling = down(travelling)
         there = z >= k
-        expos.append(pick(there & unbroken, travelling[0] + passed, -jnp.inf))
-        passed = passed + pick(there, travelling[1], 0.0)
+        expos.append(pick(there & unbroken, smalls[k - 1][1] + passed, -jnp.inf))
+        passed = passed + pick(there, smalls[k - 1][2], 0.0)
         broken = there & (reset(2 * (z - k)) | reset(2 * (z - k) + 1))
         unbroken = unbroken & ~broken
     expos.append(pick((z <= reach) & unbroken, carry_max + passed, -jnp.inf))
@@ -483,59 +571,26 @@
     direct_own = pick(even, 0.0, direct)
     direct_other = pick(even, direct, 0.0)
     top_own = pick(even, top_even, top_odd)
-    pair_own = pick(even, pair_even, pair_odd)
-    pair_other = pick(even, pair_odd, pair_even)
-
-    near = ([tokens, beside], [place, place ^ 1])
-    far = []
-    for s, c, x in zip(starts, TOKEN_CHUNKS, across):
-        rows = [((place ^ 2) * share + s) // c, ((place ^ 3) * share + s) // c]
-        far.append(([x, tensor(x, 1)], rows))
-    sums = [project(*near, w) for w in (w_key, w_value, w_query, w_outgate)]
-    for group in far[:-1]:
-        sums = [
-            project(*group, w, total)
-            for w, total in zip((w_key, w_value, w_query, w_outgate), sums)
-        ]
-    keys, values, kept, sent, norm = block_summary(
-        *far[-1], side, w_key, w_value, sums[0], sums[1], key_weight, heads
-    )
-    queries = project(*far[-1], w_query, sums[2], kind=BF)
-    gate = project(*far[-1], w_outgate, sums[3], jax.nn.sigmoid)
-
-    spread = lambda w: w[:, None, None]
-    norm_other = pair(norm)
-    norm_even = pick(even, norm, norm_other)
-    norm_pair = spread(pair_own) * norm + spread(pair_other) * norm_other
-    norm_in = spread(direct_own) * norm_even
-    for k in range(reach):
-        norm_pair = down(norm_pair)
-        norm_in = norm_in + spread(weights_own[k]) * norm_pair
-    norm_in = norm_in + spread(weights_own[reach]) * carry_norm[:, None, :]
-
-    got = pair(sent)
-    kept, got = kept.astype(F32), got.astype(F32)
-    state_even = pick(even, kept, got)
-    state_pair = (spread(pair_own) * kept + spread(pair_other) * got).astype(BF)
+
+    norm_in = direct_own[:, None] * norm_even + weights_own[reach][:, None] * carry_norm
     carried = lax.dynamic_slice(
         carry_matrix, (0, side * (size // 2), 0), (heads, size // 2, carry_matrix.shape[2])
     )
     state_own = spread(weights_own[reach]) * carried + spread(direct_own) * state_even
     state_other = spread(weights_other[reach]) * carried + spread(direct_other) * state_even
     for k in range(reach):
-        state_pair = down(state_pair)
-        wide = state_pair.astype(F32)
-        state_own = state_own + spread(weights_own[k]) * wide
-        state_other = state_other + spread(weights_other[k]) * wide
+        norm_in = norm_in + weights_own[k][:, None] * smalls[k][0]
+        state_own = state_own + spread(weights_own[k]) * states[k].astype(F32)
+        state_other = state_other + spread(weights_other[k]) * states[k].astype(F32)
     state_got = pair(state_other.astype(BF))
-
     base, slope = inner(
-        queries, keys, values, u, norm_in, gate, top_own, doc_lengths, offset, heads
+        queries, keys, values, u, norm_in[:, None, :], gate, top_own, doc_lengths, offset, heads
     )
 
     quarters = [place ^ 1, place ^ 3, place, place ^ 2]
-    outs = []
+    out = tokens
     start = 0
+    leaving = []
     for wide in OUT_CHUNKS:
         if start == 0:
             hidden, send, keep = hidden_and_first(
@@ -543,13 +598,16 @@
                 wide, start, heads,
             )
         else:
-            send, keep = next_columns(hidden, w_out, quarters, wide, start)
+            now = after(leaving[-2], hidden) if len(leaving) > 1 else hidden
+            send, keep = next_columns(now, w_out, quarters, wide, start)
         both = keep.astype(F32) + tensor(send, 1).astype(F32)
-        came = tensor(both[:, wide:].astype(BF), 2)
+        leaving.append(both[:, wide:].astype(BF))
+        came = tensor(leaving[-1], 2)
         summed = both[:, :wide] + came.astype(F32)
-        outs.append((tokens[:, start : start + wide].astype(F32) + summed).astype(BF))
+        columns = slice(start, start + wide)
+        out = out.at[:, columns].set((tokens[:, columns].astype(F32) + summed).astype(BF))
         start += wide
-    return jnp.concatenate(outs, axis=1)
+    return out
 
 
 FULL_ACCURACY = lax.Precision.HIGHEST

time: 152 us -> 172 us (1.13)
  Pallas kernels: 42.3 us -> 89.1 us
  starting transfers between devices: 43.8 us -> 19.1 us
  waiting for transfers between devices: 36.6 us -> 20.9 us
  other arithmetic: 3.6 us -> 19.1 us
    pallas_call x10, Pallas kernels: 21.8 us -> 51.3 us  [project(): pl.pallas_call(functools.partial(project_kernel, len(xs), summed is not N...]
    ppermute x6 -> x4, starting transfers between devices: 23.4 us -> 4.5 us  [shifted(): return lax.ppermute(x, axis, [(i, (i + by) % size) for i in range(size)])]
    ppermute x23 -> x18, waiting for transfers between devices: 34 us -> 15.4 us  [swapped(): return lax.ppermute(x, axis, [(i, i ^ mask) for i in range(size)])]
    pallas_call x3, Pallas kernels: 8.75 us -> 17 us  [next_columns(): pl.pallas_call(columns_kernel, out_shape=out_shapes_of(length, wide), gri...]
    ppermute x23 -> x18, starting transfers between devices: 20.4 us -> 14.6 us  [swapped(): return lax.ppermute(x, axis, [(i, i ^ mask) for i in range(size)])]
    unnamed x54 -> x45, local copies, waits for them, and re-layouts: 10.7 us -> 5.45 us
    scatter x0 -> x4, other arithmetic: none -> 4.44 us  [local(): out.at[:, columns].set((tokens[:, columns].astype(F32) + summed).astype(BF))]
    pallas_call x1, Pallas kernels: 3.39 us -> 7.77 us  [hidden_and_first(): pl.pallas_call(functools.partial(hidden_kernel, heads), out_shape=(jax.Sh...]
  transfers between devices with their start and end apart: 29 -> 22, of which waited for: 11 -> 7; matrix products, arithmetic and copies ran while one was open for 4% -> 12% of each run, Pallas kernels for 23% -> 43%
where the time goes in v2:
time: 172 us; the launch traced here: 171 us
  Pallas kernels  89.1 us (52%)
  waiting for transfers between devices  20.9 us (12%)
  starting transfers between devices  19.1 us (11%)
  other arithmetic  19.1 us (11%)
  local copies, waits for them, and re-layouts  12.7 us (7%)
  between operations  9.81 us (6%)
    pallas_call x10, Pallas kernels, project(): pl.pallas_call(functools.partial(project_kernel, len(xs), summed is not N...  51.3 us
    pallas_call x3, Pallas kernels, next_columns(): pl.pallas_call(columns_kernel, out_shape=out_shapes_of(length, wide), gri...  17 us
    ppermute x18, waiting for transfers between devices, swapped(): return lax.ppermute(x, axis, [(i, i ^ mask) for i in range(size)])  15.4 us
    ppermute x18, starting transfers between devices, swapped(): return lax.ppermute(x, axis, [(i, i ^ mask) for i in range(size)])  14.6 us
    pallas_call x1, Pallas kernels, block_summary(): pl.pallas_call(functools.partial(summary_kernel, pieces, size ** (-0.5)),...  8.16 us
    pallas_call x1, Pallas kernels, hidden_and_first(): pl.pallas_call(functools.partial(hidden_kernel, heads), out_shape=(jax.Sh...  7.77 us
    unnamed x45, local copies, waits for them, and re-layouts  5.45 us
    ppermute x4, waiting for transfers between devices, shifted(): return lax.ppermute(x, axis, [(i, (i + by) % size) for i in range(size)])  5.43 us
  transfers between devices with their start and end apart: 22, of which 7 were waited for; matrix products, arithmetic and copies ran while one was open for 12% of the time, Pallas kernels for 43%

profile of v2, /device:TPU:0, one launch (start us, length us, event | category | flops | bytes accessed | tf_op | source)
XLA Modules:
  0.0 170.7 jit_solution(17893797750987134873)
XLA Ops:
  0.5 1.0 slice.218
  1.4 1.0 slice.219
  2.4 2.6 %collective-permute-start.2 = (bf16[512,256]{1,0:T(8,128)(2,1)S(1)}, bf16[512,256]{1,0:T(8,128)(2,1)S(1)}, u32[]{:S(2)}, u32[]{:S(2)}) collective-permute-start(bf16[512,256]{1,0:T(8,128)(2,1)S(1)} %slice.219), channel_id=1, source_target_pairs={{0,2},{1,3},{2,0},{3,1},{4,6},{5,7},{6,4},{7,5},{8,10},{9,11},{10,... | collective-permute-start | bytes 786440 | tf_op jit(solution)/shard_map/ppermute | solution.py:27
  5.1 1.1 slice.220
  6.2 2.0 %collective-permute-start = (bf16[512,512]{1,0:T(8,128)(2,1)S(1)}, bf16[512,512]{1,0:T(8,128)(2,1)S(1)}, u32[]{:S(2)}, u32[]{:S(2)}) collective-permute-start(bf16[512,512]{1,0:T(8,128)(2,1)S(1)} %slice.220), channel_id=1, source_target_pairs={{0,2},{1,3},{2,0},{3,1},{4,6},{5,7},{6,4},{7,5},{8,10},{9,11},{10,... | collective-permute-start | bytes 1572872 | tf_op jit(solution)/shard_map/ppermute | solution.py:27
  8.2 0.6 reshape.281.refs_4_.refs_5_.refs_9_.refs_10_.refs_11_.refs_12_.refs_6_.refs_7_
  9.4 1.0 copy-done.1
  10.3 6.4 %shard_map.119.refs_8_ = f32[512,1024]{1,0:T(8,128)} custom-call(s32[2]{0:T(128)} %pad_add_fusion.3._, bf16[512,1024]{1,0:T(8,128)(2,1)} %refs_0_.3, bf16[512,1024]{1,0:T(8,128)(2,1)} %copy-done.1, bf16[4096,1024]{1,0:T(8,128)(2,1)} %refs_5_.9, bf16[4096,1024]{1,0:T(8,128)(2,1)} %refs_5_.9), custom_call_target="tpu_custom_call" | custom-call | flops 1000000 | bytes 100000 | tf_op jit(solution)/shard_map/pallas_call | solution.py:98
  16.7 6.4 %shard_map.121.refs_8_ = f32[512,1024]{1,0:T(8,128)} custom-call(s32[2]{0:T(128)} %pad_add_fusion.3._, bf16[512,1024]{1,0:T(8,128)(2,1)} %refs_0_.3, bf16[512,1024]{1,0:T(8,128)(2,1)} %copy-done.1, bf16[4096,1024]{1,0:T(8,128)(2,1)} %refs_3_.13, bf16[4096,1024]{1,0:T(8,128)(2,1)} %refs_3_.13), custom_call_target="tpu_custom_call" | custom-call | flops 1000000 | bytes 100000 | tf_op jit(solution)/shard_map/pallas_call | solution.py:98
  23.1 5.1 %shard_map.120.refs_8_ = f32[512,512]{1,0:T(8,128)} custom-call(s32[2]{0:T(128)} %pad_add_fusion.3._, bf16[512,1024]{1,0:T(8,128)(2,1)} %refs_0_.3, bf16[512,1024]{1,0:T(8,128)(2,1)} %copy-done.1, bf16[4096,512]{1,0:T(8,128)(2,1)} %refs_3_.12, bf16[4096,512]{1,0:T(8,128)(2,1)} %refs_3_.12), custom_call_target="tpu_custom_call" | custom-call | flops 1000000 | bytes 100000 | tf_op jit(solution)/shard_map/pallas_call | solution.py:98
  28.2 5.2 %shard_map.118 = (f32[512,512]{1,0:T(8,128)}, f32[4,512]{1,0:T(4,128)}) custom-call(s32[2]{0:T(128)} %pad_add_fusion.3._, bf16[512,1024]{1,0:T(8,128)(2,1)} %refs_0_.3, bf16[512,1024]{1,0:T(8,128)(2,1)} %copy-done.1, bf16[4096,512]{1,0:T(8,128)(2,1)} %refs_3_.11, bf16[4096,512]{1,0:T(8,128)(2,1)} %refs_3_.11, ...), custom_call_target="tpu_custom_call" | custom-call | flops 1000000 | bytes 100000 | tf_op jit(solution)/shard_map/pallas_call | solution.py:98
  34.0 0.6 pad_add_fusion.2._
  35.8 0.7 copy-done.7
  36.4 5.2 %shard_map.125.refs_4_ = f32[512,1024]{1,0:T(8,128)} custom-call(s32[4]{0:T(128)} %pad_add_fusion.2._, bf16[512,256]{1,0:T(8,128)(2,1)} %copy-done.5, bf16[512,256]{1,0:T(8,128)(2,1)} %copy-done.6, bf16[512,256]{1,0:T(8,128)(2,1)} %copy-done.4, bf16[512,256]{1,0:T(8,128)(2,1)} %copy-done.7, bf16[4096,1024]{1,0:T(8,128)(2,1)} %refs_3_.13, ...), custom_call_target="tpu_custom_call" | custom-call | flops 1000000 | bytes 100000 | tf_op jit(solution)/shard_map/pallas_call | solution.py:98
  41.7 4.2 %shard_map.124.refs_4_ = f32[512,512]{1,0:T(8,128)} custom-call(s32[4]{0:T(128)} %pad_add_fusion.2._, bf16[512,256]{1,0:T(8,128)(2,1)} %copy-done.5, bf16[512,256]{1,0:T(8,128)(2,1)} %copy-done.6, bf16[512,256]{1,0:T(8,128)(2,1)} %copy-done.4, bf16[512,256]{1,0:T(8,128)(2,1)} %copy-done.7, bf16[4096,512]{1,0:T(8,128)(2,1)} %refs_3_.12, ...), custom_call_target="tpu_custom_call" | custom-call | flops 1000000 | bytes 100000 | tf_op jit(solution)/shard_map/pallas_call | solution.py:98
  45.9 5.2 %shard_map.123.refs_9_ = f32[512,1024]{1,0:T(8,128)} custom-call(s32[4]{0:T(128)} %pad_add_fusion.2._, bf16[512,256]{1,0:T(8,128)(2,1)} %copy-done.5, bf16[512,256]{1,0:T(8,128)(2,1)} %copy-done.6, bf16[512,256]{1,0:T(8,128)(2,1)} %copy-done.4, bf16[512,256]{1,0:T(8,128)(2,1)} %copy-done.7, bf16[4096,1024]{1,0:T(8,128)(2,1)} %refs_5_.9, ...), custom_call_target="tpu_custom_call" | custom-call | flops 1000000 | bytes 100000 | tf_op jit(solution)/shard_map/pallas_call | solution.py:98
  51.0 4.2 %shard_map.122 = (f32[512,512]{1,0:T(8,128)}, f32[4,512]{1,0:T(4,128)}) custom-call(s32[4]{0:T(128)} %pad_add_fusion.2._, bf16[512,256]{1,0:T(8,128)(2,1)} %copy-done.5, bf16[512,256]{1,0:T(8,128)(2,1)} %copy-done.6, bf16[512,256]{1,0:T(8,128)(2,1)} %copy-done.4, bf16[512,256]{1,0:T(8,128)(2,1)} %copy-done.7, bf16[4096,512]{1,0:T(8,128)(2,1)} %refs_3_.11, ...), custom_call_target="tpu_custom_call" | custom-call | flops 1000000 | bytes 100000 | tf_op jit(solution)/shard_map/pallas_call | solution.py:98
  55.5 0.6 pad_add_fusion.1.info
  56.1 1.2 collective-permute-done.6.refs_1_
  57.3 0.8 copy-done.3
  58.1 8.2 %shard_map.126 = (bf16[512,512]{1,0:T(8,128)(2,1)}, bf16[512,1024]{1,0:T(8,128)(2,1)}, bf16[2,128,512]{2,1,0:T(8,128)(2,1)}, bf16[2,128,512]{2,1,0:T(8,128)(2,1)}, f32[2,384]{1,0:T(2,128)}, /*index=5*/f32[2,512]{1,0:T(2,128)}) custom-call(s32[4]{0:T(128)} %pad_add_fusion.1.info, s32[4]{0:T(128)} %docs.3, f32[2,2]{1,0:T(2,128)} %bias.1, ...), custom_call_target="tpu_custom_call" | custom-call | flops 1879048192 | bytes 7864320 | tf_op jit(solution)/shard_map/pallas_call | solution.py:216
  66.3 1.6 collective-permute-start.8
  68.4 0.6 fusion.39
  72.3 2.6 %collective-permute-done.7 = f32[2,384]{1,0:T(2,128)S(1)} collective-permute-done((f32[2,384]{1,0:T(2,128)}, f32[2,384]{1,0:T(2,128)S(1)}, u32[]{:S(2)}, u32[]{:S(2)}) %collective-permute-start.7) | collective-permute-done | bytes 3104 | tf_op jit(solution)/shard_map/ppermute | solution.py:27
  74.9 1.0 fusion.38
  75.9 1.0 select_reduce_fusion.1
  76.9 1.1 fusion.1
  78.0 1.6 collective-permute-start.10
  79.6 0.7 multiply_add_fusion.1
  80.5 1.6 collective-permute-start.9
  82.0 5.4 %collective-permute-done.9 = f32[2,384]{1,0:T(2,128)S(1)} collective-permute-done((f32[2,384]{1,0:T(2,128)S(1)}, f32[2,384]{1,0:T(2,128)S(1)}, u32[]{:S(2)}, u32[]{:S(2)}) %collective-permute-start.9) | collective-permute-done | bytes 3104 | tf_op jit(solution)/shard_map/ppermute | solution.py:32
  93.8 0.7 pad_add_fusion._
  94.5 1.3 collective-permute-start.11
  95.7 0.6 stack.145.info
  96.4 4.1 %shard_map.127.query = bf16[512,512]{1,0:T(8,128)(2,1)} custom-call(s32[2]{0:T(128)} %pad_add_fusion._, bf16[512,512]{1,0:T(8,128)(2,1)} %copy-done.2, bf16[512,512]{1,0:T(8,128)(2,1)} %copy-done.3, bf16[4096,512]{1,0:T(8,128)(2,1)} %refs_3_.12, bf16[4096,512]{1,0:T(8,128)(2,1)} %refs_3_.12, f32[512,512]{1,0:T(8,128)} %shard_map.124.refs_4_), custom_call_target="tpu_custom_call" | custom-call | flops 1000000 | bytes 100000 | tf_op jit(solution)/shard_map/pallas_call | solution.py:98
  100.4 5.3 %shard_map.128.gate = f32[512,1024]{1,0:T(8,128)} custom-call(s32[2]{0:T(128)} %pad_add_fusion._, bf16[512,512]{1,0:T(8,128)(2,1)} %copy-done.2, bf16[512,512]{1,0:T(8,128)(2,1)} %copy-done.3, bf16[4096,1024]{1,0:T(8,128)(2,1)} %refs_3_.13, bf16[4096,1024]{1,0:T(8,128)(2,1)} %refs_3_.13, f32[512,1024]{1,0:T(8,128)} %shard_map.125.refs_4_), custom_call_target="tpu_custom_call" | custom-call | flops 1000000 | bytes 100000 | tf_op jit(solution)/shard_map/pallas_call | solution.py:98
  106.3 0.6 broadcast_select_fusion.3
  106.9 1.1 fusion.7
  108.0 1.5 collective-permute-start.13
  110.2 4.9 %shard_map.129 = (f32[512,1024]{1,0:T(8,128)}, f32[512,1024]{1,0:T(8,128)}) custom-call(s32[1]{0:T(128)} %bitcast.7.place, s32[4]{0:T(128)} %docs.3, f32[2]{0:T(128)} %get-tuple-element.154.top_in, bf16[512,512]{1,0:T(8,128)(2,1)} %shard_map.127.query, bf16[512,512]{1,0:T(8,128)(2,1)} %get-tuple-element.116.key, bf16[512,1024]{1,0:T(8,128)(2,1)} %get-tuple-element.129.value, ...), custom_call_target="tpu_custom_call" | custom-call | flops 805306368 | bytes 8388608 | tf_op jit(solution)/shard_map/pallas_call | solution.py:304
  115.1 0.7 copy-done.15
  115.8 7.8 %shard_map.130 = (bf16[512,1024]{1,0:T(8,128)(2,1)}, bf16[512,512]{1,0:T(8,128)(2,1)}, bf16[512,512]{1,0:T(8,128)(2,1)}) custom-call(s32[5]{0:T(128)} %stack.145.info, bf16[512,512]{1,0:T(8,128)(2,1)} %shard_map.127.query, bf16[2,128,512]{2,1,0:T(8,128)(2,1)} %get-tuple-element.167.own, bf16[2,128,512]{2,1,0:T(8,128)(2,1)} %copy-done.15, ...), custom_call_target="tpu_custom_call" | custom-call | flops 1342177280 | bytes 8388608 | tf_op jit(solution)/shard_map/pallas_call | solution.py:378
  123.6 0.6 pad_add_fusion.4.info
  124.2 5.8 %shard_map.131 = (bf16[512,512]{1,0:T(8,128)(2,1)}, bf16[512,512]{1,0:T(8,128)(2,1)}) custom-call(s32[4]{0:T(128)} %pad_add_fusion.4.info, bf16[512,1024]{1,0:T(8,128)(2,1)} %get-tuple-element.144.hidden, bf16[1024,4096]{1,0:T(8,128)(2,1)} %w.7), custom_call_target="tpu_custom_call" | custom-call | flops 1073741824 | bytes 4194304 | tf_op jit(solution)/shard_map/pallas_call | solution.py:415
  130.5 0.6 compare_reduce_fusion.2
  131.2 0.7 compare_reduce_fusion.1
  131.9 0.7 compare_reduce_fusion
  132.6 0.7 pad_add_fusion.5
  133.2 0.8 copy-done.11
  134.0 1.3 convert_add_fusion.3
  135.4 0.8 slice.360
  136.6 1.2 convert_add_fusion.2
  137.8 1.0 copy-done.9
  138.8 0.7 slice.359
  139.5 1.5 collective-permute-start.17
  141.1 5.6 %shard_map.132 = (bf16[512,512]{1,0:T(8,128)(2,1)}, bf16[512,512]{1,0:T(8,128)(2,1)}) custom-call(s32[4]{0:T(128)} %get-tuple-element.185.info, bf16[512,1024]{1,0:T(8,128)(2,1)} %get-tuple-element.144.hidden, bf16[1024,4096]{1,0:T(8,128)(2,1)} %w.7), custom_call_target="tpu_custom_call" | custom-call | flops 1073741824 | bytes 4194304 | tf_op jit(solution)/shard_map/pallas_call | solution.py:415
  146.7 5.7 %shard_map.133 = (bf16[512,512]{1,0:T(8,128)(2,1)}, bf16[512,512]{1,0:T(8,128)(2,1)}) custom-call(s32[4]{0:T(128)} %get-tuple-element.186.info, bf16[512,1024]{1,0:T(8,128)(2,1)} %get-tuple-element.144.hidden, bf16[1024,4096]{1,0:T(8,128)(2,1)} %w.7), custom_call_target="tpu_custom_call" | custom-call | flops 1073741824 | bytes 4194304 | tf_op jit(solution)/shard_map/pallas_call | solution.py:415
  152.9 0.7 fusion.17
  153.6 2.1 %fusion.19 = bf16[512,1024]{1,0:T(8,128)(2,1)S(1)} fusion(bf16[512,1024]{1,0:T(8,128)(2,1)S(1)} %fusion.17, bf16[512,256]{1,0:T(8,128)(2,1)} %collective-permute-done.17, f32[512,512]{1,0:T(8,128)} %copy-done.9, bf16[512,1024]{1,0:T(8,128)(2,1)S(1)} %copy-done, pred[]{:T(512)} %compare_reduce_fusion.1), kind=kLoop, calls=%fused_computation.37 | loop fusion | flops 786432 | bytes 1572865 | tf_op jit(solution)/shard_map/scatter | solution.py:608
  156.7 1.6 collective-permute-start.21
  158.3 6.9 %collective-permute-done.19 = bf16[512,256]{1,0:T(8,128)(2,1)S(1)} collective-permute-done((bf16[512,256]{1,0:T(8,128)(2,1)S(1)}, bf16[512,256]{1,0:T(8,128)(2,1)S(1)}, u32[]{:S(2)}, u32[]{:S(2)}) %collective-permute-start.19) | collective-permute-done | bytes 262176 | tf_op jit(solution)/shard_map/ppermute | solution.py:27
  165.1 0.8 fusion.21
  166.0 3.9 %collective-permute-done.21 = bf16[512,256]{1,0:T(8,128)(2,1)S(1)} collective-permute-done((bf16[512,256]{1,0:T(8,128)(2,1)S(1)}, bf16[512,256]{1,0:T(8,128)(2,1)S(1)}, u32[]{:S(2)}, u32[]{:S(2)}) %collective-permute-start.21) | collective-permute-done | bytes 262176 | tf_op jit(solution)/shard_map/ppermute | solution.py:27
  169.9 0.8 fusion.22
  (90 shorter events, 7.4 us)
Async XLA Ops:
  0.0 8.2 %copy-start.17 = (bf16[2,4096,2]{1,2,0:T(2,128)(2,1)S(1)}, bf16[2,4096,2]{1,2,0:T(2,128)(2,1)}, u32[]{:S(2)}) copy-start(bf16[2,4096,2]{1,2,0:T(2,128)(2,1)} %param.25) | copy-start | bytes 98308
  0.0 9.4 %collective-permute-start.3 = (bf16[512,1024]{1,0:T(8,128)(2,1)}, bf16[512,1024]{1,0:T(8,128)(2,1)S(1)}, u32[]{:S(2)}, u32[]{:S(2)}) collective-permute-start(bf16[512,1024]{1,0:T(8,128)(2,1)} %refs_0_.3), channel_id=1, source_target_pairs={{0,1},{1,0},{2,3},{3,2},{4,5},{5,4},{6,7},{7,6},{8,9},{9,8},{10,11... | collective-permute-start | bytes 3145736 | tf_op jit(solution)/shard_map/ppermute | solution.py:27
  2.4 31.0 %collective-permute-start.2 = (bf16[512,256]{1,0:T(8,128)(2,1)S(1)}, bf16[512,256]{1,0:T(8,128)(2,1)S(1)}, u32[]{:S(2)}, u32[]{:S(2)}) collective-permute-start(bf16[512,256]{1,0:T(8,128)(2,1)S(1)} %slice.219), channel_id=1, source_target_pairs={{0,2},{1,3},{2,0},{3,1},{4,6},{5,7},{6,4},{7,5},{8,10},{9,11},{10,... | collective-permute-start | bytes 786440 | tf_op jit(solution)/shard_map/ppermute | solution.py:27
  5.0 28.4 %collective-permute-start.1 = (bf16[512,256]{1,0:T(8,128)(2,1)S(1)}, bf16[512,256]{1,0:T(8,128)(2,1)S(1)}, u32[]{:S(2)}, u32[]{:S(2)}) collective-permute-start(bf16[512,256]{1,0:T(8,128)(2,1)S(1)} %slice.218), channel_id=1, source_target_pairs={{0,2},{1,3},{2,0},{3,1},{4,6},{5,7},{6,4},{7,5},{8,10},{9,11},{10,... | collective-permute-start | bytes 786440 | tf_op jit(solution)/shard_map/ppermute | solution.py:27
  6.2 49.1 %collective-permute-start = (bf16[512,512]{1,0:T(8,128)(2,1)S(1)}, bf16[512,512]{1,0:T(8,128)(2,1)S(1)}, u32[]{:S(2)}, u32[]{:S(2)}) collective-permute-start(bf16[512,512]{1,0:T(8,128)(2,1)S(1)} %slice.220), channel_id=1, source_target_pairs={{0,2},{1,3},{2,0},{3,1},{4,6},{5,7},{6,4},{7,5},{8,10},{9,11},{10,... | collective-permute-start | bytes 1572872 | tf_op jit(solution)/shard_map/ppermute | solution.py:27
  9.4 1.0 copy-start.1
  33.4 2.0 %copy-start.4 = (bf16[512,256]{1,0:T(8,128)(2,1)}, bf16[512,256]{1,0:T(8,128)(2,1)S(1)}, u32[]{:S(2)}) copy-start(bf16[512,256]{1,0:T(8,128)(2,1)S(1)} %collective-permute-done.2.refs_2_) | copy-start | bytes 786436
  33.4 2.0 %copy-start.5 = (bf16[512,256]{1,0:T(8,128)(2,1)}, bf16[512,256]{1,0:T(8,128)(2,1)S(1)}, u32[]{:S(2)}) copy-start(bf16[512,256]{1,0:T(8,128)(2,1)S(1)} %collective-permute-done.1.refs_0_) | copy-start | bytes 786436
  33.4 1.6 collective-permute-start.4
  33.5 1.9 %collective-permute-start.5 = (bf16[512,256]{1,0:T(8,128)(2,1)S(1)}, bf16[512,256]{1,0:T(8,128)(2,1)S(1)}, u32[]{:S(2)}, u32[]{:S(2)}) collective-permute-start(bf16[512,256]{1,0:T(8,128)(2,1)S(1)} %collective-permute-done.2.refs_2_), channel_id=1, source_target_pairs={{0,1},{1,0},{2,3},{3,2},{4,5},{5,4},{6,7},{7,6},{8,9},{9,8},{10,11... | collective-permute-start | bytes 786440 | tf_op jit(solution)/shard_map/ppermute | solution.py:27
  35.0 0.7 copy-start.6
  35.8 0.7 copy-start.7
  55.3 2.0 %copy-start.2 = (bf16[512,512]{1,0:T(8,128)(2,1)}, bf16[512,512]{1,0:T(8,128)(2,1)S(1)}, u32[]{:S(2)}) copy-start(bf16[512,512]{1,0:T(8,128)(2,1)S(1)} %collective-permute-done.refs_0_) | copy-start | bytes 1572868
  55.3 2.0 %collective-permute-start.6 = (bf16[512,512]{1,0:T(8,128)(2,1)S(1)}, bf16[512,512]{1,0:T(8,128)(2,1)S(1)}, u32[]{:S(2)}, u32[]{:S(2)}) collective-permute-start(bf16[512,512]{1,0:T(8,128)(2,1)S(1)} %collective-permute-done.refs_0_), channel_id=1, source_target_pairs={{0,1},{1,0},{2,3},{3,2},{4,5},{5,4},{6,7},{7,6},{8,9},{9,8},{10,11... | collective-permute-start | bytes 1572872 | tf_op jit(solution)/shard_map/ppermute | solution.py:27
  57.3 0.8 copy-start.3
  58.1 10.3 %copy-start.19 = (s32[4]{0:T(128)S(1)}, s32[4]{0:T(128)}, u32[]{:S(2)}) copy-start(s32[4]{0:T(128)} %docs.3) | copy-start | bytes 52
  66.3 8.7 %collective-permute-start.8 = (bf16[2,128,512]{2,1,0:T(8,128)(2,1)}, bf16[2,128,512]{2,1,0:T(8,128)(2,1)S(1)}, u32[]{:S(2)}, u32[]{:S(2)}) collective-permute-start(bf16[2,128,512]{2,1,0:T(8,128)(2,1)} %get-tuple-element.121), channel_id=1, source_target_pairs={{0,4},{4,0},{8,12},{12,8},{16,20},{20,16},{24,28},{28,24},{1,5},{5... | collective-permute-start | bytes 786440 | tf_op jit(solution)/shard_map/ppermute | solution.py:27
  67.8 7.1 %collective-permute-start.7 = (f32[2,384]{1,0:T(2,128)}, f32[2,384]{1,0:T(2,128)S(1)}, u32[]{:S(2)}, u32[]{:S(2)}) collective-permute-start(f32[2,384]{1,0:T(2,128)} %get-tuple-element.120), channel_id=1, source_target_pairs={{0,4},{4,0},{8,12},{12,8},{16,20},{20,16},{24,28},{28,24},{1,5},{5... | collective-permute-start | bytes 9224 | tf_op jit(solution)/shard_map/ppermute | solution.py:27
  78.0 9.5 %collective-permute-start.10 = (bf16[2,128,512]{2,1,0:T(8,128)(2,1)S(1)}, bf16[2,128,512]{2,1,0:T(8,128)(2,1)S(1)}, u32[]{:S(2)}, u32[]{:S(2)}) collective-permute-start(bf16[2,128,512]{2,1,0:T(8,128)(2,1)S(1)} %fusion.1), channel_id=1, source_target_pairs={{0,8},{4,12},{8,16},{12,20},{16,24},{20,28},{24,0},{28,4},{1,9},{5... | collective-permute-start | bytes 786440 | tf_op jit(solution)/shard_map/ppermute | solution.py:32
  80.5 7.0 %collective-permute-start.9 = (f32[2,384]{1,0:T(2,128)S(1)}, f32[2,384]{1,0:T(2,128)S(1)}, u32[]{:S(2)}, u32[]{:S(2)}) collective-permute-start(f32[2,384]{1,0:T(2,128)S(1)} %maximum_maximum_fusion), channel_id=1, source_target_pairs={{0,8},{4,12},{8,16},{12,20},{16,24},{20,28},{24,0},{28,4},{1,9},{5... | collective-permute-start | bytes 9224 | tf_op jit(solution)/shard_map/ppermute | solution.py:32
  87.5 18.3 %collective-permute-start.12 = (bf16[2,128,512]{2,1,0:T(8,128)(2,1)S(1)}, bf16[2,128,512]{2,1,0:T(8,128)(2,1)S(1)}, u32[]{:S(2)}, u32[]{:S(2)}) collective-permute-start(bf16[2,128,512]{2,1,0:T(8,128)(2,1)S(1)} %collective-permute-done.10), channel_id=1, source_target_pairs={{0,8},{4,12},{8,16},{12,20},{16,24},{20,28},{24,0},{28,4},{1,9},{5... | collective-permute-start | bytes 786440 | tf_op jit(solution)/shard_map/ppermute | solution.py:32
  94.5 11.3 %collective-permute-start.11 = (f32[2,384]{1,0:T(2,128)S(1)}, f32[2,384]{1,0:T(2,128)S(1)}, u32[]{:S(2)}, u32[]{:S(2)}) collective-permute-start(f32[2,384]{1,0:T(2,128)S(1)} %collective-permute-done.9), channel_id=1, source_target_pairs={{0,8},{4,12},{8,16},{12,20},{16,24},{20,28},{24,0},{28,4},{1,9},{5... | collective-permute-start | bytes 9224 | tf_op jit(solution)/shard_map/ppermute | solution.py:32
  100.4 5.5 %copy-start.20 = (f32[2]{0:T(128)S(1)}, f32[2]{0:T(128)}, u32[]{:S(2)}) copy-start(f32[2]{0:T(128)} %param.30) | copy-start | bytes 28
  100.4 6.5 %copy-start.10 = (bf16[2,128,512]{2,1,0:T(8,128)(2,1)S(1)}, bf16[2,128,512]{2,1,0:T(8,128)(2,1)}, u32[]{:S(2)}) copy-start(bf16[2,128,512]{2,1,0:T(8,128)(2,1)} %get-tuple-element.123) | copy-start | bytes 786436
  100.4 6.5 %copy-start.16 = (f32[2,256,512]{2,1,0:T(8,128)S(1)}, f32[2,256,512]{2,1,0:T(8,128)}, u32[]{:S(2)}) copy-start(f32[2,256,512]{2,1,0:T(8,128)} %param.28) | copy-start | bytes 3145732
  105.7 3.8 %copy-start.18 = (f32[2,384]{1,0:T(2,128)S(1)}, f32[2,384]{1,0:T(2,128)}, u32[]{:S(2)}) copy-start(f32[2,384]{1,0:T(2,128)} %get-tuple-element.120) | copy-start | bytes 9220
  105.7 3.8 %copy-start.21 = (f32[2,256]{1,0:T(2,128)S(1)}, f32[2,256]{1,0:T(2,128)}, u32[]{:S(2)}) copy-start(f32[2,256]{1,0:T(2,128)} %param.29) | copy-start | bytes 6148
  108.0 7.0 %collective-permute-start.13 = (bf16[2,128,512]{2,1,0:T(8,128)(2,1)S(1)}, bf16[2,128,512]{2,1,0:T(8,128)(2,1)S(1)}, u32[]{:S(2)}, u32[]{:S(2)}) collective-permute-start(bf16[2,128,512]{2,1,0:T(8,128)(2,1)S(1)} %get-tuple-element.166), channel_id=1, source_target_pairs={{0,4},{4,0},{8,12},{12,8},{16,20},{20,16},{24,28},{28,24},{1,5},{5... | collective-permute-start | bytes 786440 | tf_op jit(solution)/shard_map/ppermute | solution.py:27
  115.1 0.7 copy-start.15
  123.6 9.6 %collective-permute-start.14 = (bf16[512,512]{1,0:T(8,128)(2,1)}, bf16[512,512]{1,0:T(8,128)(2,1)S(1)}, u32[]{:S(2)}, u32[]{:S(2)}) collective-permute-start(bf16[512,512]{1,0:T(8,128)(2,1)} %get-tuple-element.137), channel_id=1, source_target_pairs={{0,1},{1,0},{2,3},{3,2},{4,5},{5,4},{6,7},{7,6},{8,9},{9,8},{10,11... | collective-permute-start | bytes 1572872 | tf_op jit(solution)/shard_map/ppermute | solution.py:27
  124.2 6.3 %copy-start = (bf16[512,1024]{1,0:T(8,128)(2,1)S(1)}, bf16[512,1024]{1,0:T(8,128)(2,1)}, u32[]{:S(2)}) copy-start(bf16[512,1024]{1,0:T(8,128)(2,1)} %refs_0_.3) | copy-start | bytes 3145732
  130.0 6.7 %collective-permute-start.16 = (bf16[512,512]{1,0:T(8,128)(2,1)}, bf16[512,512]{1,0:T(8,128)(2,1)}, u32[]{:S(2)}, u32[]{:S(2)}) collective-permute-start(bf16[512,512]{1,0:T(8,128)(2,1)} %get-tuple-element.140), channel_id=1, source_target_pairs={{0,1},{1,0},{2,3},{3,2},{4,5},{5,4},{6,7},{7,6},{8,9},{9,8},{10,11... | collective-permute-start | bytes 1572872 | tf_op jit(solution)/shard_map/ppermute | solution.py:27
  130.5 6.2 %copy-start.12 = (bf16[512,512]{1,0:T(8,128)(2,1)S(1)}, bf16[512,512]{1,0:T(8,128)(2,1)}, u32[]{:S(2)}) copy-start(bf16[512,512]{1,0:T(8,128)(2,1)} %get-tuple-element.139) | copy-start | bytes 1572868
  133.2 0.8 copy-start.11
  136.1 16.7 %collective-permute-start.15 = (bf16[512,256]{1,0:T(8,128)(2,1)}, bf16[512,256]{1,0:T(8,128)(2,1)S(1)}, u32[]{:S(2)}, u32[]{:S(2)}) collective-permute-start(bf16[512,256]{1,0:T(8,128)(2,1)} %slice.360), channel_id=1, source_target_pairs={{0,2},{1,3},{2,0},{3,1},{4,6},{5,7},{6,4},{7,5},{8,10},{9,11},{10,... | collective-permute-start | bytes 786440 | tf_op jit(solution)/shard_map/ppermute | solution.py:27
  137.8 1.0 copy-start.9
  139.5 14.1 %collective-permute-start.17 = (bf16[512,256]{1,0:T(8,128)(2,1)}, bf16[512,256]{1,0:T(8,128)(2,1)}, u32[]{:S(2)}, u32[]{:S(2)}) collective-permute-start(bf16[512,256]{1,0:T(8,128)(2,1)} %slice.359), channel_id=1, source_target_pairs={{0,2},{1,3},{2,0},{3,1},{4,6},{5,7},{6,4},{7,5},{8,10},{9,11},{10,... | collective-permute-start | bytes 786440 | tf_op jit(solution)/shard_map/ppermute | solution.py:27
  146.7 9.0 %collective-permute-start.18 = (bf16[512,512]{1,0:T(8,128)(2,1)}, bf16[512,512]{1,0:T(8,128)(2,1)S(1)}, u32[]{:S(2)}, u32[]{:S(2)}) collective-permute-start(bf16[512,512]{1,0:T(8,128)(2,1)} %get-tuple-element.143), channel_id=1, source_target_pairs={{0,1},{1,0},{2,3},{3,2},{4,5},{5,4},{6,7},{7,6},{8,9},{9,8},{10,11... | collective-permute-start | bytes 1572872 | tf_op jit(solution)/shard_map/ppermute | solution.py:27
  152.4 3.4 %copy-start.14 = (bf16[512,512]{1,0:T(8,128)(2,1)S(1)}, bf16[512,512]{1,0:T(8,128)(2,1)}, u32[]{:S(2)}) copy-start(bf16[512,512]{1,0:T(8,128)(2,1)} %get-tuple-element.142) | copy-start | bytes 1572868
  152.4 4.1 %collective-permute-start.20 = (bf16[512,512]{1,0:T(8,128)(2,1)}, bf16[512,512]{1,0:T(8,128)(2,1)S(1)}, u32[]{:S(2)}, u32[]{:S(2)}) collective-permute-start(bf16[512,512]{1,0:T(8,128)(2,1)} %get-tuple-element.146), channel_id=1, source_target_pairs={{0,1},{1,0},{2,3},{3,2},{4,5},{5,4},{6,7},{7,6},{8,9},{9,8},{10,11... | collective-permute-start | bytes 1572872 | tf_op jit(solution)/shard_map/ppermute | solution.py:27
  153.6 2.9 %copy-start.13 = (bf16[512,512]{1,0:T(8,128)(2,1)S(1)}, bf16[512,512]{1,0:T(8,128)(2,1)}, u32[]{:S(2)}) copy-start(bf16[512,512]{1,0:T(8,128)(2,1)} %get-tuple-element.145) | copy-start | bytes 1572868
  155.9 9.2 %collective-permute-start.19 = (bf16[512,256]{1,0:T(8,128)(2,1)S(1)}, bf16[512,256]{1,0:T(8,128)(2,1)S(1)}, u32[]{:S(2)}, u32[]{:S(2)}) collective-permute-start(bf16[512,256]{1,0:T(8,128)(2,1)S(1)} %slice.358), channel_id=1, source_target_pairs={{0,2},{1,3},{2,0},{3,1},{4,6},{5,7},{6,4},{7,5},{8,10},{9,11},{10,... | collective-permute-start | bytes 786440 | tf_op jit(solution)/shard_map/ppermute | solution.py:27
  156.7 13.2 %collective-permute-start.21 = (bf16[512,256]{1,0:T(8,128)(2,1)S(1)}, bf16[512,256]{1,0:T(8,128)(2,1)S(1)}, u32[]{:S(2)}, u32[]{:S(2)}) collective-permute-start(bf16[512,256]{1,0:T(8,128)(2,1)S(1)} %slice.357), channel_id=1, source_target_pairs={{0,2},{1,3},{2,0},{3,1},{4,6},{5,7},{6,4},{7,5},{8,10},{9,11},{10,... | collective-permute-start | bytes 786440 | tf_op jit(solution)/shard_map/ppermute | solution.py:27
  166.0 3.9 %copy-start.8 = (bf16[512,1024]{1,0:T(8,128)(2,1)}, bf16[512,1024]{1,0:T(8,128)(2,1)S(1)}, u32[]{:S(2)}) copy-start(bf16[512,1024]{1,0:T(8,128)(2,1)S(1)} %fusion.21) | copy-start | bytes 3145732

commit v3 on v0

--- a/solution.py
+++ b/solution.py
@@ -1,12 +1,587 @@
+import functools
+
 import jax
 import jax.numpy as jnp
 from jax import lax
+from jax.experimental import pallas as pl
+from jax.experimental.pallas import tpu as pltpu
 from jax.sharding import PartitionSpec as P
 
+BF = jnp.bfloat16
+F32 = jnp.float32
+MIB = 1024 * 1024
+TOKEN_CHUNKS = ((256, 256), (512,))
+OUT_CHUNKS = (256, 256, 256, 256)
+
+
+def params(mib):
+    return pltpu.CompilerParams(vmem_limit_bytes=mib * MIB)
+
+
+def cost(flops, moved):
+    return pl.CostEstimate(flops=int(flops), bytes_accessed=int(moved), transcendentals=0)
+
+
+def swapped(x, axis, mask):
+    size = lax.axis_size(axis)
+    return lax.ppermute(x, axis, [(i, i ^ mask) for i in range(size)])
+
+
+def shifted(x, axis, by):
+    size = lax.axis_size(axis)
+    return lax.ppermute(x, axis, [(i, (i + by) % size) for i in range(size)])
+
+
+def after(first, *others):
+    out = lax.optimization_barrier((first,) + others)[1:]
+    return out[0] if len(out) == 1 else out
+
+
+SMEM_SPEC = pl.BlockSpec(memory_space=pltpu.SMEM)
+VMEM_SPEC = pl.BlockSpec(memory_space=pltpu.VMEM)
+HBM_SPEC = pl.BlockSpec(memory_space=pltpu.HBM)
+
+
+def in_hbm(x):
+    return pltpu.with_memory_space_constraint(x, pltpu.HBM)
+
+
+def across_tokens(w, x):
+    return lax.dot_general(w, x, (((1,), (1,)), ((), ())), preferred_element_type=F32)
+
+
+def row_start(place, share, owner, first):
+    return pl.multiple_of((place ^ owner) * share + first, 128)
+
+
+def stage_kernel(xs_at, ahead_at, share, with_sum, info, *refs):
+    refs = list(refs)
+    take = lambda n: [refs.pop(0) for _ in range(n)]
+    pieces = len(xs_at)
+    xs, ws, (gate_w,) = take(pieces), take(4), take(1)
+    sums = take(5) if with_sum else None
+    outs = take(5)
+    ahead = take(4) if ahead_at else []
+    held = take(4)
+    sems, ahead_sems = take(2) if ahead_at else (take(1)[0], None)
+    place = info[0]
+
+    def copies(at, targets, semaphores):
+        result = []
+        for i, (w, target) in enumerate(zip(ws, targets)):
+            low, group = 0, []
+            for p, (owner, first, count) in enumerate(at):
+                group.append(
+                    pltpu.make_async_copy(
+                        w.at[pl.ds(row_start(place, share, owner, first), count)],
+                        target.at[pl.ds(low, count)],
+                        semaphores.at[i, p],
+                    )
+                )
+                low += count
+            result.append(group)
+        return result
+
+    now = copies(xs_at, held, sems)
+    for group in now:
+        for copy in group:
+            copy.start()
+    later = copies(ahead_at, ahead, ahead_sems) if ahead_at else []
+    for group in later:
+        for copy in group:
+            copy.start()
+    gates = sums[4][...] if with_sum else 0.0
+    for (owner, first, count), x in zip(xs_at, xs):
+        gates = gates + across_tokens(
+            gate_w[:, pl.ds(row_start(place, share, owner, first), count)], x[...]
+        )
+    outs[4][...] = gates
+    for i in range(4):
+        for copy in now[i]:
+            copy.wait()
+
+        def body(j, _, i=i):
+            columns = pl.ds(pl.multiple_of(j * 256, 256), 256)
+            total = sums[i][:, columns] if with_sum else None
+            low = 0
+            for (_, _, count), x in zip(xs_at, xs):
+                part = jnp.dot(
+                    x[...], held[i][low : low + count, columns], preferred_element_type=F32
+                )
+                total = part if total is None else total + part
+                low += count
+            outs[i][:, columns] = total
+            return 0
+
+        lax.fori_loop(0, outs[i].shape[1] // 256, body, 0)
+    for group in later:
+        for copy in group:
+            copy.wait()
+
+
+def stage(info, xs, xs_at, weights, gate_w, share, sums=None, ahead_at=None):
+    length = xs[0].shape[0]
+    count = sum(c for _, _, c in xs_at)
+    shapes = [pltpu.VMEM((length, w.shape[1]), F32) for w in weights]
+    shapes.append(pltpu.VMEM((gate_w.shape[0], length), F32))
+    scratch = [pltpu.VMEM((count, w.shape[1]), BF) for w in weights]
+    scratch.append(pltpu.SemaphoreType.DMA((4, len(xs_at))))
+    if ahead_at:
+        rows = sum(c for _, _, c in ahead_at)
+        shapes += [pltpu.VMEM((rows, w.shape[1]), BF) for w in weights]
+        scratch.append(pltpu.SemaphoreType.DMA((4, len(ahead_at))))
+    operands = [info, *xs, *[in_hbm(w) for w in weights], gate_w]
+    specs = [SMEM_SPEC] + [VMEM_SPEC] * len(xs) + [HBM_SPEC] * 4 + [VMEM_SPEC]
+    aliases = {}
+    if sums is not None:
+        aliases = {len(operands) + i: i for i in range(5)}
+        operands += sums
+        specs += [VMEM_SPEC] * 5
+    return pl.pallas_call(
+        functools.partial(stage_kernel, xs_at, ahead_at, share, sums is not None),
+        out_shape=tuple(shapes),
+        in_specs=specs,
+        out_specs=(VMEM_SPEC,) * len(shapes),
+        scratch_shapes=scratch,
+        input_output_aliases=aliases,
+        compiler_params=params(24),
+        cost_estimate=cost(1e6, 1e5),
+    )(*operands)
+
+
+def last_kernel(xs_count, *refs):
+    xs = refs[:xs_count]
+    query_w, gate_w, query_sum, gate_sum, query_out, gate_out = refs[xs_count:]
+    for w, total, out, finish in (
+        (query_w, query_sum, query_out, lambda x: x),
+        (gate_w, gate_sum, gate_out, jax.nn.sigmoid),
+    ):
+
+        def body(j, _, w=w, total=total, out=out, finish=finish):
+            columns = pl.ds(pl.multiple_of(j * 256, 256), 256)
+            low, value = 0, total[:, columns]
+            for x in xs:
+                count = x.shape[1]
+                value = value + jnp.dot(
+                    x[...], w[low : low + count, columns], preferred_element_type=F32
+                )
+                low += count
+            out[:, columns] = finish(value).astype(out.dtype)
+            return 0
+
+        lax.fori_loop(0, out.shape[1] // 256, body, 0)
+
+
+def last_stage(xs, query_w, gate_w, query_sum, gate_sum):
+    return pl.pallas_call(
+        functools.partial(last_kernel, len(xs)),
+        out_shape=(
+            pltpu.VMEM(query_sum.shape, BF),
+            pltpu.VMEM(gate_sum.shape, F32),
+        ),
+        in_specs=[VMEM_SPEC] * (len(xs) + 4),
+        out_specs=(VMEM_SPEC,) * 2,
+        compiler_params=params(12),
+        cost_estimate=cost(1e6, 1e5),
+    )(*xs, query_w, gate_w, query_sum, gate_sum)
+
+
+def segments(docs, positions):
+    total = jnp.zeros_like(positions)
+    bound = jnp.int32(0)
+    for j in range(docs.shape[0] - 1):
+        bound = bound + docs[j]
+        total = total + (positions >= bound).astype(jnp.int32)
+    return total
+
+
+def gate_rows(both, offset, docs, bias):
+    heads, length = both.shape[0] // 2, both.shape[1]
+    row = lax.broadcasted_iota(jnp.int32, (heads, length), 0)
+    lane = lax.broadcasted_iota(jnp.int32, (heads, length), 1)
+    input_bias = jnp.zeros((heads, length), F32)
+    forget_bias = jnp.zeros((heads, length), F32)
+    for h in range(heads):
+        input_bias = jnp.where(row == h, bias[0, h], input_bias)
+        forget_bias = jnp.where(row == h, bias[1, h], forget_bias)
+    input_pre = both[:heads] + input_bias
+    forget = both[heads:] + forget_bias
+    decay = jnp.minimum(forget, 0.0) - jnp.log1p(jnp.exp(-jnp.abs(forget)))
+    step = 1
+    while step < length:
+        decay = decay + jnp.where(lane >= step, pltpu.roll(decay, step, 1), 0.0)
+        step *= 2
+    u = input_pre - decay
+    segment = segments(docs, lane + offset)
+    last = segments(docs, lane * 0 + (offset + length - 1))
+    open_rows = segment == last
+    top = jnp.max(jnp.where(open_rows, u, -jnp.inf), axis=1, keepdims=True)
+    weight = jnp.where(open_rows, jnp.exp(u - top), 0.0)
+    total = decay[:, length - 1 : length]
+    narrow = lax.broadcasted_iota(jnp.int32, (heads, 128), 1)
+    stats = jnp.where(narrow == 0, total + top, jnp.where(narrow == 1, total, 0.0))
+    return u, weight, stats
+
+
+def summary_kernel(xs_at, share, heads, info, docs, bias, *refs):
+    xs = refs[: len(xs_at)]
+    key_w, value_w, gate_w, key_sum, value_sum, gate_sum = refs[len(xs_at) : len(xs_at) + 6]
+    key_out, value_out, keep_out, send_out, small_out, u_out, state = refs[len(xs_at) + 6 :]
+    place, side, offset = info[0], info[1], info[2]
+    size, wide = state.shape
+    gates = gate_sum[...]
+    for (owner, first, count), x in zip(xs_at, xs):
+        gates = gates + across_tokens(
+            gate_w[:, pl.ds(row_start(place, share, owner, first), count)], x[...]
+        )
+    u, weight, stats = gate_rows(gates, offset, docs, bias)
+    u_out[...] = u
+    small_out[:, size:] = stats
+    spare = jnp.zeros((128 - weight.shape[0], weight.shape[1]), F32)
+    columns = jnp.concatenate([weight, spare], axis=0).T
+    half = size // 2
+    for h in range(heads):
+        key_at, value_at = slice(h * size, (h + 1) * size), slice(h * wide, (h + 1) * wide)
+        key, value, low = key_sum[:, key_at], value_sum[:, value_at], 0
+        for x in xs:
+            count = x.shape[1]
+            rows = slice(low, low + count)
+            key = key + jnp.dot(x[...], key_w[rows, key_at], preferred_element_type=F32)
+            value = value + jnp.dot(x[...], value_w[rows, value_at], preferred_element_type=F32)
+            low += count
+        key = (key * size ** (-0.5)).astype(BF)
+        value = value.astype(BF)
+        key_out[:, key_at] = key
+        value_out[:, value_at] = value
+        scaled = (columns[:, h : h + 1] * key.astype(F32)).astype(BF)
+        small_out[h : h + 1, :size] = jnp.sum(scaled.astype(F32), axis=0, keepdims=True)
+        state[...] = lax.dot_general(
+            scaled, value, (((0,), (0,)), ((), ())), preferred_element_type=F32
+        )
+        keep_out[h] = state[pl.ds(pl.multiple_of(side * half, half), half)].astype(BF)
+        send_out[h] = state[pl.ds(pl.multiple_of((1 - side) * half, half), half)].astype(BF)
+
+
+def block_summary(
+    info, docs, bias, xs, xs_at, key_w, value_w, gate_w, key_sum, value_sum, gates, share, heads
+):
+    length = xs[0].shape[0]
+    size, wide = key_w.shape[1] // heads, value_w.shape[1] // heads
+    return pl.pallas_call(
+        functools.partial(summary_kernel, xs_at, share, heads),
+        out_shape=(
+            pltpu.VMEM((length, heads * size), BF),
+            pltpu.VMEM((length, heads * wide), BF),
+            pltpu.VMEM((heads, size // 2, wide), BF),
+            pltpu.VMEM((heads, size // 2, wide), BF),
+            pltpu.VMEM((heads, size + 128), F32),
+            pltpu.VMEM((heads, length), F32),
+        ),
+        in_specs=[SMEM_SPEC] * 3 + [VMEM_SPEC] * (len(xs) + 6),
+        out_specs=(VMEM_SPEC,) * 6,
+        scratch_shapes=[pltpu.VMEM((size, wide), F32)],
+        compiler_params=params(16),
+        cost_estimate=cost(4e9, 4e6),
+    )(info, docs, bias, *xs, key_w, value_w, gate_w, key_sum, value_sum, gates)
+
+
+def inner_kernel(
+    heads, info, docs, top_in, query, key, value, u, norm, gate, w_out,
+    base_out, slope_out, w_here, sem,
+):
+    fetch = pltpu.make_async_copy(w_out, w_here, sem)
+    fetch.start()
+    length = query.shape[0]
+    size, wide = query.shape[1] // heads, value.shape[1] // heads
+    offset = info[2]
+    chunk = 128
+    one = jnp.zeros((chunk, 1), jnp.int32)
+    before = segments(docs, one + jnp.maximum(offset - 1, 0))
+    for head in range(heads):
+        keys_at = slice(head * size, (head + 1) * size)
+        values_at = slice(head * wide, (head + 1) * wide)
+        u_row = u[head : head + 1, :]
+        norm_row = norm[head : head + 1, :]
+        top = top_in[head]
+        for low in range(0, length, chunk):
+            high = low + chunk
+            position_t = lax.broadcasted_iota(jnp.int32, (chunk, 1), 0) + low
+            position_s = lax.broadcasted_iota(jnp.int32, (1, high), 1)
+            segment_t = segments(docs, position_t + offset)
+            segment_s = segments(docs, position_s + offset)
+            allowed = (position_s <= position_t) & (segment_s == segment_t)
+            expo = jnp.where(allowed, u_row[:, :high], -jnp.inf)
+            peak = jnp.max(expo, axis=1, keepdims=True)
+            q = query[low:high, keys_at]
+            scores = lax.dot_general(
+                q, key[:high, keys_at], (((1,), (1,)), ((), ())), preferred_element_type=F32
+            )
+            weighted = jnp.exp(expo - peak) * scores
+            num = jnp.dot(
+                weighted.astype(BF), value[:high, values_at], preferred_element_type=F32
+            )
+            den = jnp.sum(weighted, axis=1, keepdims=True)
+            carried = segment_t == before
+            ceiling = jnp.where(carried, jnp.maximum(peak, top), peak)
+            inner_weight = jnp.exp(peak - ceiling)
+            outer_weight = jnp.where(carried, jnp.exp(jnp.minimum(top - ceiling, 0.0)), 0.0)
+            outer_den = jnp.sum(q.astype(F32) * norm_row, axis=1, keepdims=True)
+            full = inner_weight * den + outer_weight * outer_den
+            inverse = 1.0 / jnp.maximum(jnp.abs(full), 1.0)
+            g = gate[low:high, values_at]
+            base_out[low:high, values_at] = g * (num * (inner_weight * inverse))
+            slope_out[low:high, values_at] = g * (outer_weight * inverse)
+    fetch.wait()
+
+
+def inner(info, docs, top, query, key, value, u, norm, gate, w_out, heads):
+    length, depth = value.shape
+    return pl.pallas_call(
+        functools.partial(inner_kernel, heads),
+        out_shape=(
+            pltpu.VMEM((length, depth), F32),
+            pltpu.VMEM((length, depth), F32),
+            pltpu.VMEM(w_out.shape, BF),
+        ),
+        in_specs=[SMEM_SPEC] * 3 + [VMEM_SPEC] * 6 + [HBM_SPEC],
+        out_specs=(VMEM_SPEC,) * 3,
+        scratch_shapes=[pltpu.SemaphoreType.DMA],
+        compiler_params=params(12),
+        cost_estimate=cost(1e6, 1e5),
+    )(info, docs, top, query, key, value, u, norm, gate, in_hbm(w_out))
+
+
+def some_columns(info, hidden, w, send, keep, start):
+    place = info[0]
+    wide = send.shape[1] // 2
+    share = w.shape[1] // 4
+    for step, owner in enumerate((1, 3, 0, 2)):
+        columns = pl.ds(pl.multiple_of((place ^ owner) * share + start, 128), wide)
+        part = jnp.dot(hidden[...], w[:, columns], preferred_element_type=F32).astype(BF)
+        out = (send, keep)[step // 2]
+        low = (step % 2) * wide
+        out[:, low : low + wide] = part
+
+
+def hidden_kernel(heads, info, query, own, other, base, slope, w, hidden, send, keep, state):
+    half = own.shape[1]
+    side = info[1]
+    size, wide = 2 * half, own.shape[2]
+    for h in range(heads):
+        state[pl.ds(pl.multiple_of(side * half, half), half)] = own[h]
+        state[pl.ds(pl.multiple_of((1 - side) * half, half), half)] = other[h]
+        outer = jnp.dot(
+            query[:, h * size : (h + 1) * size], state[...], preferred_element_type=F32
+        )
+        columns = slice(h * wide, (h + 1) * wide)
+        hidden[:, columns] = (base[:, columns] + slope[:, columns] * outer).astype(BF)
+    some_columns(info, hidden, w, send, keep, 0)
+
+
+def hidden_and_first(info, query, own, other, base, slope, w_here, wide, heads):
+    length, depth = base.shape
+    return pl.pallas_call(
+        functools.partial(hidden_kernel, heads),
+        out_shape=(
+            pltpu.VMEM((length, depth), BF),
+            pltpu.VMEM((length, 2 * wide), BF),
+            pltpu.VMEM((length, 2 * wide), BF),
+        ),
+        in_specs=[SMEM_SPEC] + [VMEM_SPEC] * 6,
+        out_specs=(VMEM_SPEC,) * 3,
+        scratch_shapes=[pltpu.VMEM((2 * own.shape[1], own.shape[2]), BF)],
+        compiler_params=params(12),
+        cost_estimate=cost(3e9, 8e6),
+    )(info, query, own, other, base, slope, w_here)
+
+
+def columns_kernel(start, info, hidden, w, send, keep):
+    some_columns(info, hidden, w, send, keep, start)
+
+
+def next_columns(info, hidden, w_here, wide, start):
+    length = hidden.shape[0]
+    return pl.pallas_call(
+        functools.partial(columns_kernel, start),
+        out_shape=(pltpu.VMEM((length, 2 * wide), BF),) * 2,
+        in_specs=[SMEM_SPEC, VMEM_SPEC, VMEM_SPEC],
+        out_specs=(VMEM_SPEC,) * 2,
+        compiler_params=params(12),
+        cost_estimate=cost(1e6, 1e5),
+    )(info, hidden, w_here)
+
+
+def pick(flag, a, b):
+    return jnp.where(flag, a, b)
+
+
+def local(
+    tokens,
+    w_query,
+    w_key,
+    w_value,
+    w_outgate,
+    w_gates,
+    gate_bias,
+    w_out,
+    carry_matrix,
+    carry_norm,
+    carry_max,
+    doc_lengths,
+):
+    length, share = tokens.shape
+    heads = gate_bias.shape[1]
+    size = w_query.shape[1] // heads
+    place = lax.axis_index("tensor")
+    block = lax.axis_index("seq")
+    blocks = lax.axis_size("seq")
+    offset = (block * length).astype(jnp.int32)
+    tensor = lambda x, mask: swapped(x, "tensor", mask)
+    pair = lambda x: swapped(x, "seq", 1)
+    down = lambda x: shifted(x, "seq", 2)
+
+    groups, source, start = [], tokens, 0
+    for chunks in TOKEN_CHUNKS:
+        group = []
+        for c in chunks:
+            piece = source[:, start : start + c]
+            group.append((start, c, tensor(piece, 2)))
+            source = after(piece, source)
+            start += c
+        groups.append(group)
+    beside = tensor(tokens, 1)
+    gate_w = w_gates.transpose(0, 2, 1).reshape(2 * heads, 4 * share)
+
+    side = (block % 2).astype(jnp.int32)
+    info = jnp.stack([place, side, offset]).astype(jnp.int32)
+    weights = (w_key, w_value, w_query, w_outgate)
+    at = [[(o, s, c) for s, c, _ in group for o in (2, 3)] for group in groups]
+    near_at = [(0, 0, share), (1, 0, share)]
+    sums = stage(info, [source, beside], near_at, weights, gate_w, share)
+    for i, group in enumerate(groups):
+        xs = lax.optimization_barrier((*[x for _, _, x in group], *sums))
+        xs, sums = xs[: len(group)], xs[len(group) :]
+        xs = [y for x in xs for y in (x, tensor(x, 1))]
+        if i < len(groups) - 1:
+            *sums, w_key_last, w_value_last, w_query_last, w_gate_last = stage(
+                info, xs, at[i], weights, gate_w, share, sums, at[-1]
+            )
+    keys, values, kept, sent, small, u = block_summary(
+        info, doc_lengths, gate_bias, xs, at[-1], w_key_last, w_value_last, gate_w,
+        sums[0], sums[1], sums[4], share, heads,
+    )
+
+    even = side == 0
+    z = block // 2
+    reach = blocks // 4
+    small_other = pair(small)
+    got = pair(sent)
+    small_other, got = lax.optimization_barrier((small_other, got))
+    last_xs = after(keys, *xs)
+    queries, gate = last_stage(last_xs, w_query_last, w_gate_last, sums[2], sums[3])
+
+    def segment_at(position):
+        return segments(doc_lengths, position)
+
+    def reset(index):
+        first = jnp.maximum(index * length - 1, 0)
+        return segment_at((index + 1) * length - 1) != segment_at(first)
+
+    def packed(norm, m, g):
+        return jnp.concatenate(
+            [norm, m[:, None], g[:, None], jnp.zeros((heads, 126), F32)], axis=1
+        )
+
+    def unpacked(x):
+        return x[:, :size], x[:, size], x[:, size + 1]
+
+    norm_own, m_own, g_own = unpacked(small)
+    norm_other, m_other, g_other = unpacked(small_other)
+    m_even, g_even = pick(even, m_own, m_other), pick(even, g_own, g_other)
+    m_odd, g_odd = pick(even, m_other, m_own), pick(even, g_other, g_own)
+    reset_even, reset_odd = reset(2 * z), reset(2 * z + 1)
+    m_pair = jnp.maximum(pick(reset_odd, -jnp.inf, m_even + g_odd), m_odd)
+    pair_even = pick(reset_odd, 0.0, jnp.exp(jnp.minimum(m_even + g_odd - m_pair, 0.0)))
+    pair_odd = jnp.exp(m_odd - m_pair)
+    pair_own = pick(even, pair_even, pair_odd)
+    pair_other = pick(even, pair_odd, pair_even)
+
+    spread = lambda w: w[:, None, None]
+    norm_pair = pair_own[:, None] * norm_own + pair_other[:, None] * norm_other
+    norm_even = pick(even, norm_own, norm_other)
+    kept, got = kept.astype(F32), got.astype(F32)
+    state_even = pick(even, kept, got)
+    state_pair = (spread(pair_own) * kept + spread(pair_other) * got).astype(BF)
+
+    travel = packed(norm_pair, m_pair, g_even + g_odd)
+    smalls, states = [], []
+    for k in range(reach):
+        travel, state_pair = lax.optimization_barrier((down(travel), down(state_pair)))
+        smalls.append(unpacked(travel))
+        states.append(state_pair)
+    expos = []
+    passed = jnp.zeros_like(m_pair)
+    unbroken = jnp.bool_(True)
+    for k in range(1, reach + 1):
+        there = z >= k
+        expos.append(pick(there & unbroken, smalls[k - 1][1] + passed, -jnp.inf))
+        passed = passed + pick(there, smalls[k - 1][2], 0.0)
+        broken = there & (reset(2 * (z - k)) | reset(2 * (z - k) + 1))
+        unbroken = unbroken & ~broken
+    expos.append(pick((z <= reach) & unbroken, carry_max + passed, -jnp.inf))
+    expos = jnp.stack(expos)
+    top_even = jnp.max(expos, axis=0)
+    expos_odd = pick(reset_even, -jnp.inf, expos + g_even)
+    top_odd = jnp.maximum(jnp.max(expos_odd, axis=0), m_even)
+    weights_even = jnp.exp(expos - top_even)
+    weights_odd = jnp.exp(expos_odd - top_odd)
+    direct = jnp.exp(m_even - top_odd)
+    weights_own = pick(even, weights_even, weights_odd)
+    weights_other = pick(even, weights_odd, weights_even)
+    direct_own = pick(even, 0.0, direct)
+    direct_other = pick(even, direct, 0.0)
+    top_own = pick(even, top_even, top_odd)
+
+    norm_in = direct_own[:, None] * norm_even + weights_own[reach][:, None] * carry_norm
+    carried = lax.dynamic_slice(
+        carry_matrix, (0, side * (size // 2), 0), (heads, size // 2, carry_matrix.shape[2])
+    )
+    state_own = spread(weights_own[reach]) * carried + spread(direct_own) * state_even
+    state_other = spread(weights_other[reach]) * carried + spread(direct_other) * state_even
+    for k in range(reach):
+        norm_in = norm_in + weights_own[k][:, None] * smalls[k][0]
+        state_own = state_own + spread(weights_own[k]) * states[k].astype(F32)
+        state_other = state_other + spread(weights_other[k]) * states[k].astype(F32)
+    state_got = pair(state_other.astype(BF))
+    base, slope, w_here = inner(
+        info, doc_lengths, top_own, queries, keys, values, u, norm_in, gate, w_out, heads
+    )
+
+    out = tokens
+    start = 0
+    leaving = []
+    for wide in OUT_CHUNKS:
+        if start == 0:
+            hidden, send, keep = hidden_and_first(
+                info, queries, state_own.astype(BF), state_got, base, slope, w_here, wide, heads
+            )
+        else:
+            now = after(leaving[-2], hidden) if len(leaving) > 1 else hidden
+            send, keep = next_columns(info, now, w_here, wide, start)
+        both = keep.astype(F32) + tensor(send, 1).astype(F32)
+        leaving.append(both[:, wide:].astype(BF))
+        came = tensor(leaving[-1], 2)
+        summed = both[:, :wide] + came.astype(F32)
+        columns = slice(start, start + wide)
+        out = out.at[:, columns].set((tokens[:, columns].astype(F32) + summed).astype(BF))
+        start += wide
+    return out
+
+
 FULL_ACCURACY = lax.Precision.HIGHEST
 
 
-def shifted(x, axis, by):
+def plain_shifted(x, axis, by):
     devices = lax.axis_size(axis)
     pairs = [(i, i + by) for i in range(devices) if 0 <= i + by < devices]
     return lax.ppermute(x, axis, pairs)
@@ -87,7 +662,7 @@
     return numerator / jnp.maximum(jnp.abs(denominator), 1.0)[:, :, None]
 
 
-def local(
+def plain_local(
     tokens,
     w_query,
     w_key,
@@ -141,7 +716,7 @@
 
     def relay(iteration, current):
         leaving = combine(current + (zero_heads, zero_heads), summary)[:3]
-        arrived = shifted(leaving, "seq", 1)
+        arrived = plain_shifted(leaving, "seq", 1)
         return tuple(
             (
                 jnp.where(is_leader, initial, received)
@@ -162,8 +737,9 @@
 
 
 def solution(mesh):
+    fast = mesh.shape["tensor"] == 4 and mesh.shape["seq"] % 4 == 0
     return jax.shard_map(
-        local,
+        local if fast else plain_local,
         mesh=mesh,
         in_specs=(
             P("seq", "tensor"),

time: 364 us -> 128 us (0.35)
  waiting for transfers between devices: 173 us -> 27.4 us
  starting transfers between devices: 89.5 us -> 18.9 us
  matrix products: 53.4 us -> 0 us
  Pallas kernels: 0 us -> 39.6 us
  other arithmetic: 18.1 us -> 9.98 us
  local copies, waits for them, and re-layouts: 13.2 us -> 20.8 us
  between operations: 14.9 us -> 10 us
    ppermute x21 -> x22, starting transfers between devices: 89.4 us -> 18.9 us  [the longest x18 14.2 us: swapped(): return lax.ppermute(x, axis, [(i, i ^ mask) for i in range(size)])]
    ppermute x21 -> x22, waiting for transfers between devices: 92.6 us -> 27.4 us  [the longest x18 21.2 us: swapped(): return lax.ppermute(x, axis, [(i, i ^ mask) for i in range(size)])]
    dot_general x11 -> x0, matrix products: 53.4 us -> none  [the longest x3 20.4 us: local(): jnp.dot(column_block, matrix, preferred_element_type=jnp.float32)]
    reduce_scatter x1 -> x0, waiting for transfers between devices: 48.6 us -> none  [local(): lax.psum_scatter(partial_value.astype(jnp.bfloat16), 'tensor', scatter_di...]
    pallas_call x0 -> x9, Pallas kernels: none -> 39.6 us  [the longest x2 19.2 us: stage(): pl.pallas_call(functools.partial(stage_kernel, xs_at, ahead_at, share, su...]
    all_gather x1 -> x0, waiting for transfers between devices: 31.3 us -> none  [local(): column_block = lax.all_gather(tokens, 'tensor', axis=1, tiled=True)]
    unnamed x26 -> x51, local copies, waits for them, and re-layouts: 3.01 us -> 14.6 us
    select_n x42 -> x8, other arithmetic: 11 us -> 0.54 us  [pick(): return jnp.where(flag, a, b)]
  transfers between devices with their start and end apart: 23 -> 22, of which waited for: 9 -> 10; matrix products, arithmetic and copies ran while one was open for 2% -> 9% of each run, Pallas kernels for 0% -> 26%
where the time goes in v3:
time: 128 us; the launch traced here: 127 us
  Pallas kernels  39.6 us (31%)
  waiting for transfers between devices  27.4 us (21%)
  local copies, waits for them, and re-layouts  20.8 us (16%)
  starting transfers between devices  18.9 us (15%)
  between operations  10 us (8%)
  other arithmetic  9.98 us (8%)
    ppermute x18, waiting for transfers between devices, swapped(): return lax.ppermute(x, axis, [(i, i ^ mask) for i in range(size)])  21.2 us
    pallas_call x2, Pallas kernels, stage(): pl.pallas_call(functools.partial(stage_kernel, xs_at, ahead_at, share, su...  19.2 us
    unnamed x51, local copies, waits for them, and re-layouts  14.6 us
    ppermute x18, starting transfers between devices, swapped(): return lax.ppermute(x, axis, [(i, i ^ mask) for i in range(size)])  14.2 us
    ppermute x4, waiting for transfers between devices, shifted(): return lax.ppermute(x, axis, [(i, (i + by) % size) for i in range(size)])  6.25 us
    pallas_call x3, Pallas kernels, next_columns(): pl.pallas_call(functools.partial(columns_kernel, start), out_shape=(pltpu...  5.46 us
    pallas_call x1, Pallas kernels, block_summary(): pl.pallas_call(functools.partial(summary_kernel, xs_at, share, heads), ou...  5.07 us
    ppermute x4, starting transfers between devices, shifted(): return lax.ppermute(x, axis, [(i, (i + by) % size) for i in range(size)])  4.73 us
  transfers between devices with their start and end apart: 22, of which 10 were waited for; matrix products, arithmetic and copies ran while one was open for 9% of the time, Pallas kernels for 26%

profile of v3, /device:TPU:0, one launch (start us, length us, event | category | flops | bytes accessed | tf_op | source)
XLA Modules:
  0.0 126.7 jit_solution(3778756831602052753)
XLA Ops:
  0.0 0.5 collective-permute-start.3
  0.5 1.7 %slice.218 = bf16[512,256]{1,0:T(8,128)(2,1)} slice(bf16[512,1024]{1,0:T(8,128)(2,1)} %refs_0_), slice={[0:512], [0:256]} | slice | bytes 524288 | tf_op jit(solution)/shard_map/slice | solution.py:576
  2.1 1.7 %slice.219 = bf16[512,256]{1,0:T(8,128)(2,1)} slice(bf16[512,1024]{1,0:T(8,128)(2,1)} %refs_0_), slice={[0:512], [256:512]} | slice | bytes 524288 | tf_op jit(solution)/shard_map/slice | solution.py:447
  3.8 2.6 %collective-permute-start.2 = (bf16[512,256]{1,0:T(8,128)(2,1)}, bf16[512,256]{1,0:T(8,128)(2,1)S(1)}, u32[]{:S(2)}, u32[]{:S(2)}) collective-permute-start(bf16[512,256]{1,0:T(8,128)(2,1)} %slice.219), channel_id=1, source_target_pairs={{0,2},{1,3},{2,0},{3,1},{4,6},{5,7},{6,4},{7,5},{8,10},{9,11},{10,... | collective-permute-start | bytes 786440 | tf_op jit(solution)/shard_map/ppermute | solution.py:27
  6.4 1.9 %slice.220 = bf16[512,512]{1,0:T(8,128)(2,1)} slice(bf16[512,1024]{1,0:T(8,128)(2,1)} %refs_0_), slice={[0:512], [512:1024]} | slice | bytes 1048576 | tf_op jit(solution)/shard_map/slice | solution.py:447
  8.3 2.0 %collective-permute-start = (bf16[512,512]{1,0:T(8,128)(2,1)}, bf16[512,512]{1,0:T(8,128)(2,1)}, u32[]{:S(2)}, u32[]{:S(2)}) collective-permute-start(bf16[512,512]{1,0:T(8,128)(2,1)} %slice.220), channel_id=1, source_target_pairs={{0,2},{1,3},{2,0},{3,1},{4,6},{5,7},{6,4},{7,5},{8,10},{9,11},{10,... | collective-permute-start | bytes 1572872 | tf_op jit(solution)/shard_map/ppermute | solution.py:27
  10.4 1.0 copy-done.11
  11.4 1.2 copy-done.12
  12.6 11.0 %shard_map.118 = (f32[512,512]{1,0:T(8,128)S(1)}, f32[512,1024]{1,0:T(8,128)S(1)}, f32[512,512]{1,0:T(8,128)S(1)}, f32[512,1024]{1,0:T(8,128)S(1)}, f32[4,512]{1,0:T(4,128)S(1)}) custom-call(s32[3]{0:T(128)S(1)} %pad_add_fusion.info, bf16[512,1024]{1,0:T(8,128)(2,1)S(1)} %copy-done, bf16[512,1024]{1,0:T(8,128)(2,1)S(1)} %copy-done.12, ...), custom_call_target="tpu_custom_call" | custom-call | flops 1000000 | bytes 100000 | tf_op jit(solution)/shard_map/pallas_call | solution.py:140
  23.8 0.5 collective-permute-start.5
  24.3 1.2 collective-permute-done.4.refs_1_
  25.7 8.1 %shard_map.119 = (f32[512,512]{1,0:T(8,128)S(1)}, f32[512,1024]{1,0:T(8,128)S(1)}, f32[512,512]{1,0:T(8,128)S(1)}, f32[512,1024]{1,0:T(8,128)S(1)}, f32[4,512]{1...) custom-call(s32[3]{0:T(128)S(1)} %pad_add_fusion.info, ...), custom_call_target="tpu_custom_call", output_to_operand_aliasing={{0}: (10, {}), {1}: (11, {}), {2}: (12, {}), {3}: (13, {}),... | custom-call | flops 1000000 | bytes 100000 | tf_op jit(solution)/shard_map/pallas_call | solution.py:140
  33.8 0.2 collective-permute-start.6
  34.0 2.0 %collective-permute-done.6.refs_1_ = bf16[512,512]{1,0:T(8,128)(2,1)S(1)} collective-permute-done((bf16[512,512]{1,0:T(8,128)(2,1)}, bf16[512,512]{1,0:T(8,128)(2,1)S(1)}, u32[]{:S(2)}, u32[]{:S(2)}) %collective-permute-start.6) | collective-permute-done | bytes 524320 | tf_op jit(solution)/shard_map/ppermute | solution.py:27
  36.0 5.1 %shard_map.120 = (bf16[512,512]{1,0:T(8,128)(2,1)S(1)}, bf16[512,1024]{1,0:T(8,128)(2,1)S(1)}, bf16[2,128,512]{2,1,0:T(8,128)(2,1)S(1)}, bf16[2,128,512]{2,1,0:T...) custom-call(s32[3]{0:T(128)S(1)} %pad_add_fusion.info, s32[4]{0:T(128)S(1)} %copy-done.19, ...), custom_call_target="tpu_custom_call" | custom-call | flops 4000000000 | bytes 4000000 | tf_op jit(solution)/shard_map/pallas_call | solution.py:270
  41.1 1.0 copy-done.13
  42.1 0.8 copy-done.17
  42.9 1.5 %collective-permute-start.8 = (bf16[2,128,512]{2,1,0:T(8,128)(2,1)}, bf16[2,128,512]{2,1,0:T(8,128)(2,1)}, u32[]{:S(2)}, u32[]{:S(2)}) collective-permute-start(bf16[2,128,512]{2,1,0:T(8,128)(2,1)} %get-tuple-element.148), channel_id=1, source_target_pairs={{0,4},{4,0},{8,12},{12,8},{16,20},{20,16},{24,28},{28,24},{1,5},{5... | collective-permute-start | bytes 786440 | tf_op jit(solution)/shard_map/ppermute | solution.py:27
  44.4 0.5 collective-permute-start.7
  44.9 0.7 fusion.39
  48.8 2.8 %collective-permute-done.7 = f32[2,384]{1,0:T(2,128)S(1)} collective-permute-done((f32[2,384]{1,0:T(2,128)S(1)}, f32[2,384]{1,0:T(2,128)S(1)}, u32[]{:S(2)}, u32[]{:S(2)}) %collective-permute-start.7) | collective-permute-done | bytes 3104 | tf_op jit(solution)/shard_map/ppermute | solution.py:27
  51.6 0.2 fusion.38
  51.8 0.2 select_reduce_fusion.1
  52.0 1.1 fusion.1
  53.1 1.6 %collective-permute-start.10 = (bf16[2,128,512]{2,1,0:T(8,128)(2,1)S(1)}, bf16[2,128,512]{2,1,0:T(8,128)(2,1)}, u32[]{:S(2)}, u32[]{:S(2)}) collective-permute-start(bf16[2,128,512]{2,1,0:T(8,128)(2,1)S(1)} %fusion.1), channel_id=1, source_target_pairs={{0,8},{4,12},{8,16},{12,20},{16,24},{20,28},{24,0},{28,4},{1,9},{5... | collective-permute-start | bytes 786440 | tf_op jit(solution)/shard_map/ppermute | solution.py:32
  54.9 1.6 %collective-permute-start.9 = (f32[2,384]{1,0:T(2,128)S(1)}, f32[2,384]{1,0:T(2,128)S(1)}, u32[]{:S(2)}, u32[]{:S(2)}) collective-permute-start(f32[2,384]{1,0:T(2,128)S(1)} %maximum_maximum_fusion), channel_id=1, source_target_pairs={{0,8},{4,12},{8,16},{12,20},{16,24},{20,28},{24,0},{28,4},{1,9},{5... | collective-permute-start | bytes 9224 | tf_op jit(solution)/shard_map/ppermute | solution.py:32
  56.5 6.2 %collective-permute-done.9 = f32[2,384]{1,0:T(2,128)S(1)} collective-permute-done((f32[2,384]{1,0:T(2,128)S(1)}, f32[2,384]{1,0:T(2,128)S(1)}, u32[]{:S(2)}, u32[]{:S(2)}) %collective-permute-start.9) | collective-permute-done | bytes 3104 | tf_op jit(solution)/shard_map/ppermute | solution.py:32
  69.2 1.5 %collective-permute-start.11 = (f32[2,384]{1,0:T(2,128)S(1)}, f32[2,384]{1,0:T(2,128)S(1)}, u32[]{:S(2)}, u32[]{:S(2)}) collective-permute-start(f32[2,384]{1,0:T(2,128)S(1)} %collective-permute-done.9), channel_id=1, source_target_pairs={{0,8},{4,12},{8,16},{12,20},{16,24},{20,28},{24,0},{28,4},{1,9},{5... | collective-permute-start | bytes 9224 | tf_op jit(solution)/shard_map/ppermute | solution.py:32
  70.7 1.2 copy-done.2
  71.9 1.6 %copy-done.4 = bf16[1024,1024]{1,0:T(8,128)(2,1)S(1)} copy-done((bf16[1024,1024]{1,0:T(8,128)(2,1)S(1)}, bf16[1024,1024]{1,0:T(8,128)(2,1)}, u32[]{:S(2)}) %copy-start.4) | copy-done | bytes 2097176
  73.5 1.2 copy-done.10
  74.7 1.0 copy-done.16
  75.8 3.8 %shard_map.121 = (bf16[512,512]{1,0:T(8,128)(2,1)S(1)}, f32[512,1024]{1,0:T(8,128)S(1)}) custom-call(bf16[512,512]{1,0:T(8,128)(2,1)} %collective-permute-done.refs_0_, bf16[512,512]{1,0:T(8,128)(2,1)S(1)} %copy-done.16, bf16[1024,512]{1,0:T(8,128)(2,1)S(1)} %copy-done.10, bf16[1024,1024]{1,0:T(8,128)(2,1)S(1)} %copy-done.4, f32[512,512]{1,0:T(8,128)S(1)} %copy-done.2, ...), custom_call_target="tpu_custom_call" | custom-call | flops 1000000 | bytes 100000 | tf_op jit(solution)/shard_map/pallas_call | solution.py:176
  79.6 1.3 %copy-done.5 = f32[512,1024]{1,0:T(8,128)} copy-done((f32[512,1024]{1,0:T(8,128)}, f32[512,1024]{1,0:T(8,128)S(1)}, u32[]{:S(2)}) %copy-start.5) | copy-done | bytes 2097176
  80.9 0.8 copy-done.7
  81.7 0.2 maximum_reduce_fusion
  82.1 1.9 %fusion.7 = (bf16[2,128,512]{2,1,0:T(8,128)(2,1)S(1)}, bf16[2,128,512]{2,1,0:T(8,128)(2,1)S(1)}) fusion(bf16[2,128,512]{2,1,0:T(8,128)(2,1)} %collective-permute-done.10, bf16[2,128,512]{2,1,0:T(8,128)(2,1)} %collective-permute-done.12, bf16[2,128,512]{2,1,0:T(8,128)(2,1)} %collective-permute-done.8, bf16[2,128,512]{2,1,0:T(8,128)(2,1)S(1)} %get-tuple-element.150, ...), kind=kLoop, calls=%fused_computation.18 | loop fusion | flops 2752512 | bytes 2097221 | tf_op jit(solution)/shard_map/convert_element_type | solution.py:555
  84.0 1.5 %collective-permute-start.13 = (bf16[2,128,512]{2,1,0:T(8,128)(2,1)S(1)}, bf16[2,128,512]{2,1,0:T(8,128)(2,1)S(1)}, u32[]{:S(2)}, u32[]{:S(2)}) collective-permute-start(bf16[2,128,512]{2,1,0:T(8,128)(2,1)S(1)} %get-tuple-element.192), channel_id=1, source_target_pairs={{0,4},{4,0},{8,12},{12,8},{16,20},{20,16},{24,28},{28,24},{1,5},{5... | collective-permute-start | bytes 786440 | tf_op jit(solution)/shard_map/ppermute | solution.py:27
  85.7 1.0 copy-done.8
  86.8 1.2 copy-done.14
  88.0 1.0 copy-done.18
  89.1 3.9 %shard_map.122 = (f32[512,1024]{1,0:T(8,128)S(1)}, f32[512,1024]{1,0:T(8,128)S(1)}, bf16[1024,4096]{1,0:T(8,128)(2,1)S(1)}) custom-call(s32[3]{0:T(128)S(1)} %pad_add_fusion.info, s32[4]{0:T(128)S(1)} %copy-done.19, f32[2]{0:T(128)S(1)} %get-tuple-element.180.top_in, bf16[512,512]{1,0:T(8,128)(2,1)S(1)} %copy-done.8, bf16[512,512]{1,0:T(8,128)(2,1)S(1)} %copy-done.18, ...), custom_call_target="tpu_custom_call" | custom-call | flops 1000000 | bytes 100000 | tf_op jit(solution)/shard_map/pallas_call | solution.py:339
  93.0 2.2 %shard_map.123 = (bf16[512,1024]{1,0:T(8,128)(2,1)S(1)}, bf16[512,512]{1,0:T(8,128)(2,1)S(1)}, bf16[512,512]{1,0:T(8,128)(2,1)S(1)}) custom-call(s32[3]{0:T(128)S(1)} %pad_add_fusion.info, bf16[512,512]{1,0:T(8,128)(2,1)S(1)} %copy-done.8, bf16[2,128,512]{2,1,0:T(8,128)(2,1)S(1)} %get-tuple-element.193.own, ...), custom_call_target="tpu_custom_call" | custom-call | flops 3000000000 | bytes 8000000 | tf_op jit(solution)/shard_map/pallas_call | solution.py:383
  95.3 1.8 %shard_map.124 = (bf16[512,512]{1,0:T(8,128)(2,1)S(1)}, bf16[512,512]{1,0:T(8,128)(2,1)S(1)}) custom-call(s32[3]{0:T(128)S(1)} %pad_add_fusion.info, bf16[512,1024]{1,0:T(8,128)(2,1)S(1)} %get-tuple-element.170.hidden, bf16[1024,4096]{1,0:T(8,128)(2,1)S(1)} %get-tuple-element.161.w), custom_call_target="tpu_custom_call" | custom-call | flops 1000000 | bytes 100000 | tf_op jit(solution)/shard_map/pallas_call | solution.py:404
  97.1 0.6 collective-permute-start.16
  97.9 0.6 collective-permute-start.15
  98.5 0.8 collective-permute-done.16
  99.4 0.8 collective-permute-start.17
  100.3 1.8 %shard_map.125 = (bf16[512,512]{1,0:T(8,128)(2,1)S(1)}, bf16[512,512]{1,0:T(8,128)(2,1)S(1)}) custom-call(s32[3]{0:T(128)S(1)} %pad_add_fusion.info, bf16[512,1024]{1,0:T(8,128)(2,1)S(1)} %get-tuple-element.170.hidden, bf16[1024,4096]{1,0:T(8,128)(2,1)S(1)} %get-tuple-element.161.w), custom_call_target="tpu_custom_call" | custom-call | flops 1000000 | bytes 100000 | tf_op jit(solution)/shard_map/pallas_call | solution.py:404
  102.3 0.6 compare_reduce_fusion.2
  102.9 0.7 compare_reduce_fusion.1
  103.6 0.7 compare_reduce_fusion
  104.2 1.8 %shard_map.126 = (bf16[512,512]{1,0:T(8,128)(2,1)S(1)}, bf16[512,512]{1,0:T(8,128)(2,1)S(1)}) custom-call(s32[3]{0:T(128)S(1)} %pad_add_fusion.info, bf16[512,1024]{1,0:T(8,128)(2,1)S(1)} %get-tuple-element.170.hidden, bf16[1024,4096]{1,0:T(8,128)(2,1)S(1)} %get-tuple-element.161.w), custom_call_target="tpu_custom_call" | custom-call | flops 1000000 | bytes 100000 | tf_op jit(solution)/shard_map/pallas_call | solution.py:404
  106.1 0.6 collective-permute-start.20
  106.6 0.5 collective-permute-done.15
  107.1 0.8 fusion.17
  108.0 3.8 %collective-permute-done.17 = bf16[512,256]{1,0:T(8,128)(2,1)S(1)} collective-permute-done((bf16[512,256]{1,0:T(8,128)(2,1)S(1)}, bf16[512,256]{1,0:T(8,128)(2,1)S(1)}, u32[]{:S(2)}, u32[]{:S(2)}) %collective-permute-start.17) | collective-permute-done | bytes 262176 | tf_op jit(solution)/shard_map/ppermute | solution.py:27
  111.8 0.8 fusion.19
  112.9 0.6 collective-permute-start.19
  113.7 1.6 %collective-permute-start.21 = (bf16[512,256]{1,0:T(8,128)(2,1)S(1)}, bf16[512,256]{1,0:T(8,128)(2,1)S(1)}, u32[]{:S(2)}, u32[]{:S(2)}) collective-permute-start(bf16[512,256]{1,0:T(8,128)(2,1)S(1)} %slice.357), channel_id=1, source_target_pairs={{0,2},{1,3},{2,0},{3,1},{4,6},{5,7},{6,4},{7,5},{8,10},{9,11},{10,... | collective-permute-start | bytes 786440 | tf_op jit(solution)/shard_map/ppermute | solution.py:27
  115.2 6.9 %collective-permute-done.19 = bf16[512,256]{1,0:T(8,128)(2,1)S(1)} collective-permute-done((bf16[512,256]{1,0:T(8,128)(2,1)S(1)}, bf16[512,256]{1,0:T(8,128)(2,1)S(1)}, u32[]{:S(2)}, u32[]{:S(2)}) %collective-permute-start.19) | collective-permute-done | bytes 262176 | tf_op jit(solution)/shard_map/ppermute | solution.py:27
  122.2 0.8 fusion.21
  123.0 2.9 %collective-permute-done.21 = bf16[512,256]{1,0:T(8,128)(2,1)S(1)} collective-permute-done((bf16[512,256]{1,0:T(8,128)(2,1)S(1)}, bf16[512,256]{1,0:T(8,128)(2,1)S(1)}, u32[]{:S(2)}, u32[]{:S(2)}) %collective-permute-start.21) | collective-permute-done | bytes 262176 | tf_op jit(solution)/shard_map/ppermute | solution.py:27
  125.9 0.8 fusion.22
  (82 shorter events, 2.0 us)
Async XLA Ops:
  0.0 11.4 %copy-start = (bf16[512,1024]{1,0:T(8,128)(2,1)S(1)}, bf16[512,1024]{1,0:T(8,128)(2,1)}, u32[]{:S(2)}) copy-start(bf16[512,1024]{1,0:T(8,128)(2,1)} %refs_0_) | copy-start | bytes 3145732
  0.0 10.3 %copy-start.22 = (bf16[2,4096,2]{1,2,0:T(2,128)(2,1)S(1)}, bf16[2,4096,2]{1,2,0:T(2,128)(2,1)}, u32[]{:S(2)}) copy-start(bf16[2,4096,2]{1,2,0:T(2,128)(2,1)} %param.25) | copy-start | bytes 98308
  0.0 10.4 %collective-permute-start.3 = (bf16[512,1024]{1,0:T(8,128)(2,1)}, bf16[512,1024]{1,0:T(8,128)(2,1)S(1)}, u32[]{:S(2)}, u32[]{:S(2)}) collective-permute-start(bf16[512,1024]{1,0:T(8,128)(2,1)} %refs_0_), channel_id=1, source_target_pairs={{0,1},{1,0},{2,3},{3,2},{4,5},{5,4},{6,7},{7,6},{8,9},{9,8},{10,11... | collective-permute-start | bytes 3145736 | tf_op jit(solution)/shard_map/ppermute | solution.py:27
  3.8 19.9 %collective-permute-start.2 = (bf16[512,256]{1,0:T(8,128)(2,1)}, bf16[512,256]{1,0:T(8,128)(2,1)S(1)}, u32[]{:S(2)}, u32[]{:S(2)}) collective-permute-start(bf16[512,256]{1,0:T(8,128)(2,1)} %slice.219), channel_id=1, source_target_pairs={{0,2},{1,3},{2,0},{3,1},{4,6},{5,7},{6,4},{7,5},{8,10},{9,11},{10,... | collective-permute-start | bytes 786440 | tf_op jit(solution)/shard_map/ppermute | solution.py:27
  6.4 17.3 %collective-permute-start.1 = (bf16[512,256]{1,0:T(8,128)(2,1)}, bf16[512,256]{1,0:T(8,128)(2,1)}, u32[]{:S(2)}, u32[]{:S(2)}) collective-permute-start(bf16[512,256]{1,0:T(8,128)(2,1)} %slice.218), channel_id=1, source_target_pairs={{0,2},{1,3},{2,0},{3,1},{4,6},{5,7},{6,4},{7,5},{8,10},{9,11},{10,... | collective-permute-start | bytes 786440 | tf_op jit(solution)/shard_map/ppermute | solution.py:27
  8.3 25.5 %collective-permute-start = (bf16[512,512]{1,0:T(8,128)(2,1)}, bf16[512,512]{1,0:T(8,128)(2,1)}, u32[]{:S(2)}, u32[]{:S(2)}) collective-permute-start(bf16[512,512]{1,0:T(8,128)(2,1)} %slice.220), channel_id=1, source_target_pairs={{0,2},{1,3},{2,0},{3,1},{4,6},{5,7},{6,4},{7,5},{8,10},{9,11},{10,... | collective-permute-start | bytes 1572872 | tf_op jit(solution)/shard_map/ppermute | solution.py:27
  10.4 1.0 copy-start.11
  11.4 1.2 copy-start.12
  23.7 12.4 %copy-start.19 = (s32[4]{0:T(128)S(1)}, s32[4]{0:T(128)}, u32[]{:S(2)}) copy-start(s32[4]{0:T(128)} %docs.3) | copy-start | bytes 52
  23.7 12.4 %copy-start.20 = (f32[2,2]{1,0:T(2,128)S(1)}, f32[2,2]{1,0:T(2,128)}, u32[]{:S(2)}) copy-start(f32[2,2]{1,0:T(2,128)} %bias.1) | copy-start | bytes 52
  23.7 1.8 %collective-permute-start.4 = (bf16[512,256]{1,0:T(8,128)(2,1)}, bf16[512,256]{1,0:T(8,128)(2,1)S(1)}, u32[]{:S(2)}, u32[]{:S(2)}) collective-permute-start(bf16[512,256]{1,0:T(8,128)(2,1)} %collective-permute-done.1.refs_0_), channel_id=1, source_target_pairs={{0,1},{1,0},{2,3},{3,2},{4,5},{5,4},{6,7},{7,6},{8,9},{9,8},{10,11... | collective-permute-start | bytes 786440 | tf_op jit(solution)/shard_map/ppermute | solution.py:27
  23.8 1.9 %collective-permute-start.5 = (bf16[512,256]{1,0:T(8,128)(2,1)S(1)}, bf16[512,256]{1,0:T(8,128)(2,1)S(1)}, u32[]{:S(2)}, u32[]{:S(2)}) collective-permute-start(bf16[512,256]{1,0:T(8,128)(2,1)S(1)} %collective-permute-done.2.refs_2_), channel_id=1, source_target_pairs={{0,1},{1,0},{2,3},{3,2},{4,5},{5,4},{6,7},{7,6},{8,9},{9,8},{10,11... | collective-permute-start | bytes 786440 | tf_op jit(solution)/shard_map/ppermute | solution.py:27
  33.8 7.3 %copy-start.1 = (f32[512,512]{1,0:T(8,128)}, f32[512,512]{1,0:T(8,128)S(1)}, u32[]{:S(2)}) copy-start(f32[512,512]{1,0:T(8,128)S(1)} %get-tuple-element.144.refs_4_) | copy-start | bytes 3145732
  33.8 7.3 %copy-start.3 = (bf16[1024,1024]{1,0:T(8,128)(2,1)}, bf16[1024,1024]{1,0:T(8,128)(2,1)S(1)}, u32[]{:S(2)}) copy-start(bf16[1024,1024]{1,0:T(8,128)(2,1)S(1)} %get-tuple-element.143.refs_3_) | copy-start | bytes 6291460
  33.8 7.3 %copy-start.9 = (bf16[1024,512]{1,0:T(8,128)(2,1)}, bf16[1024,512]{1,0:T(8,128)(2,1)S(1)}, u32[]{:S(2)}) copy-start(bf16[1024,512]{1,0:T(8,128)(2,1)S(1)} %get-tuple-element.142.refs_2_) | copy-start | bytes 3145732
  33.8 2.2 %collective-permute-start.6 = (bf16[512,512]{1,0:T(8,128)(2,1)}, bf16[512,512]{1,0:T(8,128)(2,1)S(1)}, u32[]{:S(2)}, u32[]{:S(2)}) collective-permute-start(bf16[512,512]{1,0:T(8,128)(2,1)} %collective-permute-done.refs_0_), channel_id=1, source_target_pairs={{0,1},{1,0},{2,3},{3,2},{4,5},{5,4},{6,7},{7,6},{8,9},{9,8},{10,11... | collective-permute-start | bytes 1572872 | tf_op jit(solution)/shard_map/ppermute | solution.py:27
  36.0 5.1 %copy-start.15 = (bf16[512,512]{1,0:T(8,128)(2,1)}, bf16[512,512]{1,0:T(8,128)(2,1)S(1)}, u32[]{:S(2)}) copy-start(bf16[512,512]{1,0:T(8,128)(2,1)S(1)} %collective-permute-done.6.refs_1_) | copy-start | bytes 1572868
  41.1 1.0 copy-start.13
  42.1 0.8 copy-start.17
  42.9 8.7 %collective-permute-start.8 = (bf16[2,128,512]{2,1,0:T(8,128)(2,1)}, bf16[2,128,512]{2,1,0:T(8,128)(2,1)}, u32[]{:S(2)}, u32[]{:S(2)}) collective-permute-start(bf16[2,128,512]{2,1,0:T(8,128)(2,1)} %get-tuple-element.148), channel_id=1, source_target_pairs={{0,4},{4,0},{8,12},{12,8},{16,20},{20,16},{24,28},{28,24},{1,5},{5... | collective-permute-start | bytes 786440 | tf_op jit(solution)/shard_map/ppermute | solution.py:27
  44.4 7.2 %collective-permute-start.7 = (f32[2,384]{1,0:T(2,128)S(1)}, f32[2,384]{1,0:T(2,128)S(1)}, u32[]{:S(2)}, u32[]{:S(2)}) collective-permute-start(f32[2,384]{1,0:T(2,128)S(1)} %get-tuple-element.147), channel_id=1, source_target_pairs={{0,4},{4,0},{8,12},{12,8},{16,20},{20,16},{24,28},{28,24},{1,5},{5... | collective-permute-start | bytes 9224 | tf_op jit(solution)/shard_map/ppermute | solution.py:27
  53.1 9.6 %collective-permute-start.10 = (bf16[2,128,512]{2,1,0:T(8,128)(2,1)S(1)}, bf16[2,128,512]{2,1,0:T(8,128)(2,1)}, u32[]{:S(2)}, u32[]{:S(2)}) collective-permute-start(bf16[2,128,512]{2,1,0:T(8,128)(2,1)S(1)} %fusion.1), channel_id=1, source_target_pairs={{0,8},{4,12},{8,16},{12,20},{16,24},{20,28},{24,0},{28,4},{1,9},{5... | collective-permute-start | bytes 786440 | tf_op jit(solution)/shard_map/ppermute | solution.py:32
  54.9 7.8 %collective-permute-start.9 = (f32[2,384]{1,0:T(2,128)S(1)}, f32[2,384]{1,0:T(2,128)S(1)}, u32[]{:S(2)}, u32[]{:S(2)}) collective-permute-start(f32[2,384]{1,0:T(2,128)S(1)} %maximum_maximum_fusion), channel_id=1, source_target_pairs={{0,8},{4,12},{8,16},{12,20},{16,24},{20,28},{24,0},{28,4},{1,9},{5... | collective-permute-start | bytes 9224 | tf_op jit(solution)/shard_map/ppermute | solution.py:32
  62.7 19.0 %collective-permute-start.12 = (bf16[2,128,512]{2,1,0:T(8,128)(2,1)}, bf16[2,128,512]{2,1,0:T(8,128)(2,1)}, u32[]{:S(2)}, u32[]{:S(2)}) collective-permute-start(bf16[2,128,512]{2,1,0:T(8,128)(2,1)} %collective-permute-done.10), channel_id=1, source_target_pairs={{0,8},{4,12},{8,16},{12,20},{16,24},{20,28},{24,0},{28,4},{1,9},{5... | collective-permute-start | bytes 786440 | tf_op jit(solution)/shard_map/ppermute | solution.py:32
  69.2 12.5 %collective-permute-start.11 = (f32[2,384]{1,0:T(2,128)S(1)}, f32[2,384]{1,0:T(2,128)S(1)}, u32[]{:S(2)}, u32[]{:S(2)}) collective-permute-start(f32[2,384]{1,0:T(2,128)S(1)} %collective-permute-done.9), channel_id=1, source_target_pairs={{0,8},{4,12},{8,16},{12,20},{16,24},{20,28},{24,0},{28,4},{1,9},{5... | collective-permute-start | bytes 9224 | tf_op jit(solution)/shard_map/ppermute | solution.py:32
  70.7 1.2 copy-start.2
  71.9 1.6 %copy-start.4 = (bf16[1024,1024]{1,0:T(8,128)(2,1)S(1)}, bf16[1024,1024]{1,0:T(8,128)(2,1)}, u32[]{:S(2)}) copy-start(bf16[1024,1024]{1,0:T(8,128)(2,1)} %copy-done.3) | copy-start | bytes 6291460
  73.5 1.2 copy-start.10
  74.7 1.0 copy-start.16
  75.8 6.2 %copy-start.23 = (f32[2]{0:T(128)S(1)}, f32[2]{0:T(128)}, u32[]{:S(2)}) copy-start(f32[2]{0:T(128)} %param.30) | copy-start | bytes 28
  79.6 1.3 %copy-start.5 = (f32[512,1024]{1,0:T(8,128)}, f32[512,1024]{1,0:T(8,128)S(1)}, u32[]{:S(2)}) copy-start(f32[512,1024]{1,0:T(8,128)S(1)} %get-tuple-element.158.gate) | copy-start | bytes 6291460
  80.9 0.8 copy-start.7
  81.7 4.0 %copy-start.24 = (f32[2,256]{1,0:T(2,128)S(1)}, f32[2,256]{1,0:T(2,128)}, u32[]{:S(2)}) copy-start(f32[2,256]{1,0:T(2,128)} %param.29) | copy-start | bytes 6148
  81.7 4.1 %copy-start.6 = (f32[512,1024]{1,0:T(8,128)S(1)}, f32[512,1024]{1,0:T(8,128)}, u32[]{:S(2)}) copy-start(f32[512,1024]{1,0:T(8,128)} %copy-done.5) | copy-start | bytes 6291460
  84.0 9.0 %collective-permute-start.13 = (bf16[2,128,512]{2,1,0:T(8,128)(2,1)S(1)}, bf16[2,128,512]{2,1,0:T(8,128)(2,1)S(1)}, u32[]{:S(2)}, u32[]{:S(2)}) collective-permute-start(bf16[2,128,512]{2,1,0:T(8,128)(2,1)S(1)} %get-tuple-element.192), channel_id=1, source_target_pairs={{0,4},{4,0},{8,12},{12,8},{16,20},{20,16},{24,28},{28,24},{1,5},{5... | collective-permute-start | bytes 786440 | tf_op jit(solution)/shard_map/ppermute | solution.py:27
  85.7 1.0 copy-start.8
  86.8 1.2 copy-start.14
  88.0 1.0 copy-start.18
  95.3 2.5 %collective-permute-start.14 = (bf16[512,512]{1,0:T(8,128)(2,1)S(1)}, bf16[512,512]{1,0:T(8,128)(2,1)S(1)}, u32[]{:S(2)}, u32[]{:S(2)}) collective-permute-start(bf16[512,512]{1,0:T(8,128)(2,1)S(1)} %get-tuple-element.163), channel_id=1, source_target_pairs={{0,1},{1,0},{2,3},{3,2},{4,5},{5,4},{6,7},{7,6},{8,9},{9,8},{10,11... | collective-permute-start | bytes 1572872 | tf_op jit(solution)/shard_map/ppermute | solution.py:27
  97.1 2.1 %collective-permute-start.16 = (bf16[512,512]{1,0:T(8,128)(2,1)S(1)}, bf16[512,512]{1,0:T(8,128)(2,1)S(1)}, u32[]{:S(2)}, u32[]{:S(2)}) collective-permute-start(bf16[512,512]{1,0:T(8,128)(2,1)S(1)} %get-tuple-element.166), channel_id=1, source_target_pairs={{0,1},{1,0},{2,3},{3,2},{4,5},{5,4},{6,7},{7,6},{8,9},{9,8},{10,11... | collective-permute-start | bytes 1572872 | tf_op jit(solution)/shard_map/ppermute | solution.py:27
  97.9 9.2 %collective-permute-start.15 = (bf16[512,256]{1,0:T(8,128)(2,1)S(1)}, bf16[512,256]{1,0:T(8,128)(2,1)S(1)}, u32[]{:S(2)}, u32[]{:S(2)}) collective-permute-start(bf16[512,256]{1,0:T(8,128)(2,1)S(1)} %slice.360), channel_id=1, source_target_pairs={{0,2},{1,3},{2,0},{3,1},{4,6},{5,7},{6,4},{7,5},{8,10},{9,11},{10,... | collective-permute-start | bytes 786440 | tf_op jit(solution)/shard_map/ppermute | solution.py:27
  99.4 12.4 %collective-permute-start.17 = (bf16[512,256]{1,0:T(8,128)(2,1)S(1)}, bf16[512,256]{1,0:T(8,128)(2,1)S(1)}, u32[]{:S(2)}, u32[]{:S(2)}) collective-permute-start(bf16[512,256]{1,0:T(8,128)(2,1)S(1)} %slice.359), channel_id=1, source_target_pairs={{0,2},{1,3},{2,0},{3,1},{4,6},{5,7},{6,4},{7,5},{8,10},{9,11},{10,... | collective-permute-start | bytes 786440 | tf_op jit(solution)/shard_map/ppermute | solution.py:27
  102.1 10.6 %collective-permute-start.18 = (bf16[512,512]{1,0:T(8,128)(2,1)S(1)}, bf16[512,512]{1,0:T(8,128)(2,1)S(1)}, u32[]{:S(2)}, u32[]{:S(2)}) collective-permute-start(bf16[512,512]{1,0:T(8,128)(2,1)S(1)} %get-tuple-element.169), channel_id=1, source_target_pairs={{0,1},{1,0},{2,3},{3,2},{4,5},{5,4},{6,7},{7,6},{8,9},{9,8},{10,11... | collective-permute-start | bytes 1572872 | tf_op jit(solution)/shard_map/ppermute | solution.py:27
  106.1 7.4 %collective-permute-start.20 = (bf16[512,512]{1,0:T(8,128)(2,1)S(1)}, bf16[512,512]{1,0:T(8,128)(2,1)S(1)}, u32[]{:S(2)}, u32[]{:S(2)}) collective-permute-start(bf16[512,512]{1,0:T(8,128)(2,1)S(1)} %get-tuple-element.172), channel_id=1, source_target_pairs={{0,1},{1,0},{2,3},{3,2},{4,5},{5,4},{6,7},{7,6},{8,9},{9,8},{10,11... | collective-permute-start | bytes 1572872 | tf_op jit(solution)/shard_map/ppermute | solution.py:27
  112.9 9.3 %collective-permute-start.19 = (bf16[512,256]{1,0:T(8,128)(2,1)S(1)}, bf16[512,256]{1,0:T(8,128)(2,1)S(1)}, u32[]{:S(2)}, u32[]{:S(2)}) collective-permute-start(bf16[512,256]{1,0:T(8,128)(2,1)S(1)} %slice.358), channel_id=1, source_target_pairs={{0,2},{1,3},{2,0},{3,1},{4,6},{5,7},{6,4},{7,5},{8,10},{9,11},{10,... | collective-permute-start | bytes 786440 | tf_op jit(solution)/shard_map/ppermute | solution.py:27
  113.7 12.3 %collective-permute-start.21 = (bf16[512,256]{1,0:T(8,128)(2,1)S(1)}, bf16[512,256]{1,0:T(8,128)(2,1)S(1)}, u32[]{:S(2)}, u32[]{:S(2)}) collective-permute-start(bf16[512,256]{1,0:T(8,128)(2,1)S(1)} %slice.357), channel_id=1, source_target_pairs={{0,2},{1,3},{2,0},{3,1},{4,6},{5,7},{6,4},{7,5},{8,10},{9,11},{10,... | collective-permute-start | bytes 786440 | tf_op jit(solution)/shard_map/ppermute | solution.py:27
  123.0 2.9 %copy-start.21 = (bf16[512,1024]{1,0:T(8,128)(2,1)}, bf16[512,1024]{1,0:T(8,128)(2,1)S(1)}, u32[]{:S(2)}) copy-start(bf16[512,1024]{1,0:T(8,128)(2,1)S(1)} %fusion.21) | copy-start | bytes 3145732

commit v4 on v3

--- a/solution.py
+++ b/solution.py
@@ -44,6 +44,30 @@
 
 def in_hbm(x):
     return pltpu.with_memory_space_constraint(x, pltpu.HBM)
+
+
+def split_kernel(starts, tokens, *refs):
+    outs, sem = refs[:-1], refs[-1]
+    copies = []
+    for i, (low, out) in enumerate(zip(starts, outs)):
+        source = tokens.at[:, low : low + out.shape[1]]
+        copies.append(pltpu.make_async_copy(source, out, sem.at[i]))
+        copies[-1].start()
+    for copy in copies:
+        copy.wait()
+
+
+def split_tokens(tokens, starts, sizes):
+    length = tokens.shape[0]
+    return pl.pallas_call(
+        functools.partial(split_kernel, starts),
+        out_shape=tuple(pltpu.VMEM((length, c), BF) for c in sizes),
+        in_specs=[HBM_SPEC],
+        out_specs=(VMEM_SPEC,) * len(sizes),
+        scratch_shapes=[pltpu.SemaphoreType.DMA((len(sizes),))],
+        compiler_params=params(4),
+        cost_estimate=cost(1e6, 1e5),
+    )(in_hbm(tokens))
 
 
 def across_tokens(w, x):
@@ -285,6 +309,132 @@
     )(info, docs, bias, *xs, key_w, value_w, gate_w, key_sum, value_sum, gates)
 
 
+def reset_of(docs, index, length):
+    first = jnp.maximum(index * length - 1, 0)
+    return segments(docs, (index + 1) * length - 1) != segments(docs, first)
+
+
+def pair_scales(info, docs, length, size, own, other):
+    even = info[1] == 0
+    first = info[2] // length - info[1]
+    m_own, g_own = own[:, size : size + 1], own[:, size + 1 : size + 2]
+    m_other, g_other = other[:, size : size + 1], other[:, size + 1 : size + 2]
+    m_even, g_even = jnp.where(even, m_own, m_other), jnp.where(even, g_own, g_other)
+    m_odd, g_odd = jnp.where(even, m_other, m_own), jnp.where(even, g_other, g_own)
+    reset_odd = reset_of(docs, first + 1, length)
+    m_pair = jnp.maximum(jnp.where(reset_odd, -jnp.inf, m_even + g_odd), m_odd)
+    pair_even = jnp.where(reset_odd, 0.0, jnp.exp(jnp.minimum(m_even + g_odd - m_pair, 0.0)))
+    pair_odd = jnp.exp(m_odd - m_pair)
+    weights = jnp.where(even, pair_even, pair_odd), jnp.where(even, pair_odd, pair_even)
+    return m_even, g_even, g_odd, m_pair, weights
+
+
+def pair_kernel(length, info, docs, own, other, kept, got, state_out, small_out):
+    heads = own.shape[0]
+    size = own.shape[1] - 128
+    _, g_even, g_odd, m_pair, (w_own, w_other) = pair_scales(
+        info, docs, length, size, own[...], other[...]
+    )
+    small_out[:, :size] = w_own * own[:, :size] + w_other * other[:, :size]
+    lane = lax.broadcasted_iota(jnp.int32, (heads, 128), 1)
+    small_out[:, size:] = jnp.where(
+        lane == 0, m_pair, jnp.where(lane == 1, g_even + g_odd, 0.0)
+    )
+    for h in range(heads):
+        at = slice(h, h + 1)
+        state = w_own[at] * kept[h].astype(F32) + w_other[at] * got[h].astype(F32)
+        state_out[h] = state.astype(BF)
+
+
+def pair_summary(info, docs, small, small_other, kept, got, length):
+    return pl.pallas_call(
+        functools.partial(pair_kernel, length),
+        out_shape=(pltpu.VMEM(kept.shape, BF), pltpu.VMEM(small.shape, F32)),
+        in_specs=[SMEM_SPEC] * 2 + [VMEM_SPEC] * 4,
+        out_specs=(VMEM_SPEC,) * 2,
+        compiler_params=params(4),
+        cost_estimate=cost(1e6, 1e5),
+    )(info, docs, small, small_other, kept, got)
+
+
+def incoming_kernel(length, reach, info, docs, own, other, kept, got, *refs):
+    smalls, states = refs[:reach], refs[reach : 2 * reach]
+    carry, carry_norm, carry_max = refs[2 * reach : 2 * reach + 3]
+    own_out, other_out, norm_out, top_out = refs[2 * reach + 3 :]
+    heads = own.shape[0]
+    size = own.shape[1] - 128
+    half = size // 2
+    side = info[1]
+    even = side == 0
+    first = info[2] // length - side
+    m_even, g_even, _, _, _ = pair_scales(info, docs, length, size, own[...], other[...])
+    reset_even = reset_of(docs, first, length)
+    expos = []
+    passed = jnp.zeros((heads, 1), F32)
+    unbroken = jnp.bool_(True)
+    for k in range(1, reach + 1):
+        there = first >= 2 * k
+        index = jnp.maximum(first - 2 * k, 0)
+        m_k, g_k = smalls[k - 1][:, size : size + 1], smalls[k - 1][:, size + 1 : size + 2]
+        expos.append(jnp.where(there & unbroken, m_k + passed, -jnp.inf))
+        passed = passed + jnp.where(there, g_k, 0.0)
+        broken = reset_of(docs, index, length) | reset_of(docs, index + 1, length)
+        unbroken = unbroken & ~(there & broken)
+    in_reach = (first <= 2 * reach) & unbroken
+    expos.append(jnp.where(in_reach, carry_max[...] + passed, -jnp.inf))
+    top_even = functools.reduce(jnp.maximum, expos)
+    expos_odd = [jnp.where(reset_even, -jnp.inf, e + g_even) for e in expos]
+    top_odd = functools.reduce(jnp.maximum, expos_odd, m_even)
+    w_even = [jnp.exp(e - top_even) for e in expos]
+    w_odd = [jnp.exp(e - top_odd) for e in expos_odd]
+    direct = jnp.exp(m_even - top_odd)
+    w_own = [jnp.where(even, a, b) for a, b in zip(w_even, w_odd)]
+    w_other = [jnp.where(even, b, a) for a, b in zip(w_even, w_odd)]
+    direct_own = jnp.where(even, 0.0, direct)
+    direct_other = jnp.where(even, direct, 0.0)
+    top_out[...] = jnp.where(even, top_even, top_odd) + jnp.zeros((heads, 128), F32)
+    norm = direct_own * jnp.where(even, own[:, :size], other[:, :size])
+    norm = norm + w_own[reach] * carry_norm[...]
+    for k in range(reach):
+        norm = norm + w_own[k] * smalls[k][:, :size]
+    norm_out[...] = norm
+    rows = pl.ds(pl.multiple_of(side * half, half), half)
+    for h in range(heads):
+        at = slice(h, h + 1)
+        here = jnp.where(even, kept[h].astype(F32), got[h].astype(F32))
+        base = carry[h, rows, :]
+        mine = w_own[reach][at] * base + direct_own[at] * here
+        theirs = w_other[reach][at] * base + direct_other[at] * here
+        for k in range(reach):
+            state = states[k][h].astype(F32)
+            mine = mine + w_own[k][at] * state
+            theirs = theirs + w_other[k][at] * state
+        own_out[h] = mine.astype(BF)
+        other_out[h] = theirs.astype(BF)
+
+
+def incoming_state(
+    info, docs, small, small_other, kept, got, smalls, states, carry, carry_norm, carry_max, length
+):
+    heads = small.shape[0]
+    return pl.pallas_call(
+        functools.partial(incoming_kernel, length, len(smalls)),
+        out_shape=(
+            pltpu.VMEM(kept.shape, BF),
+            pltpu.VMEM(kept.shape, BF),
+            pltpu.VMEM(carry_norm.shape, F32),
+            pltpu.VMEM((heads, 128), F32),
+        ),
+        in_specs=[SMEM_SPEC] * 2 + [VMEM_SPEC] * (7 + 2 * len(smalls)),
+        out_specs=(VMEM_SPEC,) * 4,
+        compiler_params=params(6),
+        cost_estimate=cost(1e6, 1e5),
+    )(
+        info, docs, small, small_other, kept, got, *smalls, *states,
+        carry, carry_norm, carry_max[:, None],
+    )
+
+
 def inner_kernel(
     heads, info, docs, top_in, query, key, value, u, norm, gate, w_out,
     base_out, slope_out, w_here, sem,
@@ -302,7 +452,7 @@
         values_at = slice(head * wide, (head + 1) * wide)
         u_row = u[head : head + 1, :]
         norm_row = norm[head : head + 1, :]
-        top = top_in[head]
+        top = top_in[head : head + 1, 0:1]
         for low in range(0, length, chunk):
             high = low + chunk
             position_t = lax.broadcasted_iota(jnp.int32, (chunk, 1), 0) + low
@@ -343,7 +493,7 @@
             pltpu.VMEM((length, depth), F32),
             pltpu.VMEM(w_out.shape, BF),
         ),
-        in_specs=[SMEM_SPEC] * 3 + [VMEM_SPEC] * 6 + [HBM_SPEC],
+        in_specs=[SMEM_SPEC] * 2 + [VMEM_SPEC] * 7 + [HBM_SPEC],
         out_specs=(VMEM_SPEC,) * 3,
         scratch_shapes=[pltpu.SemaphoreType.DMA],
         compiler_params=params(12),
@@ -409,10 +559,6 @@
         compiler_params=params(12),
         cost_estimate=cost(1e6, 1e5),
     )(info, hidden, w_here)
-
-
-def pick(flag, a, b):
-    return jnp.where(flag, a, b)
 
 
 def local(
@@ -440,16 +586,15 @@
     pair = lambda x: swapped(x, "seq", 1)
     down = lambda x: shifted(x, "seq", 2)
 
-    groups, source, start = [], tokens, 0
+    beside = tensor(tokens, 1)
+    sizes = [c for chunks in TOKEN_CHUNKS for c in chunks]
+    starts = [sum(sizes[:i]) for i in range(len(sizes))]
+    *pieces, source = split_tokens(tokens, starts + [0], sizes + [share])
+    pieces = [(s, c, tensor(x, 2)) for s, c, x in zip(starts, sizes, pieces)]
+    groups = []
     for chunks in TOKEN_CHUNKS:
-        group = []
-        for c in chunks:
-            piece = source[:, start : start + c]
-            group.append((start, c, tensor(piece, 2)))
-            source = after(piece, source)
-            start += c
-        groups.append(group)
-    beside = tensor(tokens, 1)
+        groups.append(pieces[: len(chunks)])
+        pieces = pieces[len(chunks) :]
     gate_w = w_gates.transpose(0, 2, 1).reshape(2 * heads, 4 * share)
 
     side = (block % 2).astype(jnp.int32)
@@ -471,111 +616,49 @@
         sums[0], sums[1], sums[4], share, heads,
     )
 
-    even = side == 0
-    z = block // 2
-    reach = blocks // 4
     small_other = pair(small)
     got = pair(sent)
-    small_other, got = lax.optimization_barrier((small_other, got))
     last_xs = after(keys, *xs)
     queries, gate = last_stage(last_xs, w_query_last, w_gate_last, sums[2], sums[3])
-
-    def segment_at(position):
-        return segments(doc_lengths, position)
-
-    def reset(index):
-        first = jnp.maximum(index * length - 1, 0)
-        return segment_at((index + 1) * length - 1) != segment_at(first)
-
-    def packed(norm, m, g):
-        return jnp.concatenate(
-            [norm, m[:, None], g[:, None], jnp.zeros((heads, 126), F32)], axis=1
-        )
-
-    def unpacked(x):
-        return x[:, :size], x[:, size], x[:, size + 1]
-
-    norm_own, m_own, g_own = unpacked(small)
-    norm_other, m_other, g_other = unpacked(small_other)
-    m_even, g_even = pick(even, m_own, m_other), pick(even, g_own, g_other)
-    m_odd, g_odd = pick(even, m_other, m_own), pick(even, g_other, g_own)
-    reset_even, reset_odd = reset(2 * z), reset(2 * z + 1)
-    m_pair = jnp.maximum(pick(reset_odd, -jnp.inf, m_even + g_odd), m_odd)
-    pair_even = pick(reset_odd, 0.0, jnp.exp(jnp.minimum(m_even + g_odd - m_pair, 0.0)))
-    pair_odd = jnp.exp(m_odd - m_pair)
-    pair_own = pick(even, pair_even, pair_odd)
-    pair_other = pick(even, pair_odd, pair_even)
-
-    spread = lambda w: w[:, None, None]
-    norm_pair = pair_own[:, None] * norm_own + pair_other[:, None] * norm_other
-    norm_even = pick(even, norm_own, norm_other)
-    kept, got = kept.astype(F32), got.astype(F32)
-    state_even = pick(even, kept, got)
-    state_pair = (spread(pair_own) * kept + spread(pair_other) * got).astype(BF)
-
-    travel = packed(norm_pair, m_pair, g_even + g_odd)
+    small_other, got, queries = lax.optimization_barrier((small_other, got, queries))
+    state_pair, travel = pair_summary(
+        info, doc_lengths, small, small_other, kept, got, length
+    )
     smalls, states = [], []
-    for k in range(reach):
+    for _ in range(blocks // 4):
         travel, state_pair = lax.optimization_barrier((down(travel), down(state_pair)))
-        smalls.append(unpacked(travel))
+        smalls.append(travel)
         states.append(state_pair)
-    expos = []
-    passed = jnp.zeros_like(m_pair)
-    unbroken = jnp.bool_(True)
-    for k in range(1, reach + 1):
-        there = z >= k
-        expos.append(pick(there & unbroken, smalls[k - 1][1] + passed, -jnp.inf))
-        passed = passed + pick(there, smalls[k - 1][2], 0.0)
-        broken = there & (reset(2 * (z - k)) | reset(2 * (z - k) + 1))
-        unbroken = unbroken & ~broken
-    expos.append(pick((z <= reach) & unbroken, carry_max + passed, -jnp.inf))
-    expos = jnp.stack(expos)
-    top_even = jnp.max(expos, axis=0)
-    expos_odd = pick(reset_even, -jnp.inf, expos + g_even)
-    top_odd = jnp.maximum(jnp.max(expos_odd, axis=0), m_even)
-    weights_even = jnp.exp(expos - top_even)
-    weights_odd = jnp.exp(expos_odd - top_odd)
-    direct = jnp.exp(m_even - top_odd)
-    weights_own = pick(even, weights_even, weights_odd)
-    weights_other = pick(even, weights_odd, weights_even)
-    direct_own = pick(even, 0.0, direct)
-    direct_other = pick(even, direct, 0.0)
-    top_own = pick(even, top_even, top_odd)
-
-    norm_in = direct_own[:, None] * norm_even + weights_own[reach][:, None] * carry_norm
-    carried = lax.dynamic_slice(
-        carry_matrix, (0, side * (size // 2), 0), (heads, size // 2, carry_matrix.shape[2])
-    )
-    state_own = spread(weights_own[reach]) * carried + spread(direct_own) * state_even
-    state_other = spread(weights_other[reach]) * carried + spread(direct_other) * state_even
-    for k in range(reach):
-        norm_in = norm_in + weights_own[k][:, None] * smalls[k][0]
-        state_own = state_own + spread(weights_own[k]) * states[k].astype(F32)
-        state_other = state_other + spread(weights_other[k]) * states[k].astype(F32)
-    state_got = pair(state_other.astype(BF))
+    state_own, state_other, norm_in, top_own = incoming_state(
+        info, doc_lengths, small, small_other, kept, got, smalls, states,
+        carry_matrix, carry_norm, carry_max, length,
+    )
+    state_got = pair(state_other)
     base, slope, w_here = inner(
         info, doc_lengths, top_own, queries, keys, values, u, norm_in, gate, w_out, heads
     )
 
-    out = tokens
     start = 0
-    leaving = []
+    leaving, arriving = [], []
     for wide in OUT_CHUNKS:
         if start == 0:
             hidden, send, keep = hidden_and_first(
-                info, queries, state_own.astype(BF), state_got, base, slope, w_here, wide, heads
+                info, queries, state_own, state_got, base, slope, w_here, wide, heads
             )
         else:
             now = after(leaving[-2], hidden) if len(leaving) > 1 else hidden
             send, keep = next_columns(info, now, w_here, wide, start)
         both = keep.astype(F32) + tensor(send, 1).astype(F32)
         leaving.append(both[:, wide:].astype(BF))
-        came = tensor(leaving[-1], 2)
-        summed = both[:, :wide] + came.astype(F32)
-        columns = slice(start, start + wide)
-        out = out.at[:, columns].set((tokens[:, columns].astype(F32) + summed).astype(BF))
+        arriving.append((start, wide, both[:, :wide], tensor(leaving[-1], 2)))
         start += wide
-    return out
+    out = source
+    for start, wide, both, came in arriving[:-1]:
+        columns = source[:, start : start + wide].astype(F32) + (both + came.astype(F32))
+        out = lax.dynamic_update_slice(out, columns.astype(BF), (0, start))
+    start, wide, both, came = arriving[-1]
+    columns = source[:, start : start + wide].astype(F32) + (both + came.astype(F32))
+    return lax.dynamic_update_slice(out, columns.astype(BF), (0, start))
 
 
 FULL_ACCURACY = lax.Precision.HIGHEST

time: 128 us -> 106 us (0.83)
  local copies, waits for them, and re-layouts: 20.8 us -> 6.83 us
  between operations: 10 us -> 0.34 us
  waiting for transfers between devices: 27.4 us -> 36.3 us
  other arithmetic: 9.98 us -> 1.22 us
  Pallas kernels: 39.6 us -> 42.1 us
    unnamed x51 -> x32, local copies, waits for them, and re-layouts: 14.6 us -> 5.82 us
    ppermute x4, waiting for transfers between devices: 6.25 us -> 14.1 us  [shifted(): return lax.ppermute(x, axis, [(i, (i + by) % size) for i in range(size)])]
    slice x4 -> x0, local copies, waits for them, and re-layouts: 5.85 us -> none  [the longest x2 3.52 us: local(): piece = source[:, start:start + c]]
    pallas_call x0 -> x3, Pallas kernels: none -> 5.19 us  [the longest x1 2.57 us: split_tokens(): pl.pallas_call(functools.partial(split_kernel, starts), out_shape=tuple((...]
    scatter x4 -> x0, other arithmetic: 3.3 us -> none  [local(): out.at[:, columns].set((tokens[:, columns].astype(F32) + summed).astype(BF))]
    convert_element_type x2 -> x0, other arithmetic: 3.01 us -> none  [the longest x1 1.89 us: local(): state_got = pair(state_other.astype(BF))]
    another operation x4 -> x0, other arithmetic: 1.97 us -> none
    pallas_call x1, Pallas kernels: 5.07 us -> 3.69 us  [block_summary(): pl.pallas_call(functools.partial(summary_kernel, xs_at, share, heads), ou...]
  transfers between devices with their start and end apart: 22 -> 22, of which waited for: 10 -> 12; matrix products, arithmetic and copies ran while one was open for 9% -> 2% of each run, Pallas kernels for 26% -> 32%
where the time goes in v4:
time: 106 us
  Pallas kernels  42.1 us (40%)
  waiting for transfers between devices  36.3 us (34%)
  starting transfers between devices  18.9 us (18%)
  local copies, waits for them, and re-layouts  6.83 us (6%)
  other arithmetic  1.22 us (1%)
    ppermute x18, waiting for transfers between devices, swapped(): return lax.ppermute(x, axis, [(i, i ^ mask) for i in range(size)])  22.2 us
    pallas_call x2, Pallas kernels, stage(): pl.pallas_call(functools.partial(stage_kernel, xs_at, ahead_at, share, su...  18.8 us
    ppermute x18, starting transfers between devices, swapped(): return lax.ppermute(x, axis, [(i, i ^ mask) for i in range(size)])  14.2 us
    ppermute x4, waiting for transfers between devices, shifted(): return lax.ppermute(x, axis, [(i, (i + by) % size) for i in range(size)])  14.1 us
    unnamed x32, local copies, waits for them, and re-layouts  5.82 us
    pallas_call x3, Pallas kernels, next_columns(): pl.pallas_call(functools.partial(columns_kernel, start), out_shape=(pltpu...  5.47 us
    ppermute x4, starting transfers between devices, shifted(): return lax.ppermute(x, axis, [(i, (i + by) % size) for i in range(size)])  4.67 us
    pallas_call x1, Pallas kernels, inner(): pl.pallas_call(functools.partial(inner_kernel, heads), out_shape=(pltpu.V...  4.19 us
  transfers between devices with their start and end apart: 22, of which 12 were waited for; matrix products, arithmetic and copies ran while one was open for 2% of the time, Pallas kernels for 32%

profile of v4, /device:TPU:0, one launch (start us, length us, event | category | flops | bytes accessed | tf_op | source)
XLA Modules:
  0.0 105.7 jit_solution(14181288737661681314)
XLA Ops:
  0.0 0.5 collective-permute-start.3
  0.5 2.6 %shard_map.118 = (bf16[512,256]{1,0:T(8,128)(2,1)}, bf16[512,256]{1,0:T(8,128)(2,1)}, bf16[512,512]{1,0:T(8,128)(2,1)}, bf16[512,1024]{1,0:T(8,128)(2,1)S(1)}) custom-call(bf16[512,1024]{1,0:T(8,128)(2,1)} %tokens.1), custom_call_target="tpu_custom_call" | custom-call | flops 1000000 | bytes 100000 | tf_op jit(solution)/shard_map/pallas_call | solution.py:62
  3.0 2.6 %collective-permute-start.1 = (bf16[512,256]{1,0:T(8,128)(2,1)}, bf16[512,256]{1,0:T(8,128)(2,1)S(1)}, u32[]{:S(2)}, u32[]{:S(2)}) collective-permute-start(bf16[512,256]{1,0:T(8,128)(2,1)} %get-tuple-element.75), channel_id=1, source_target_pairs={{0,2},{1,3},{2,0},{3,1},{4,6},{5,7},{6,4},{7,5},{8,10},{9,11},{10,... | collective-permute-start | bytes 786440 | tf_op jit(solution)/shard_map/ppermute | solution.py:27
  5.6 0.1 collective-permute-start.2
  5.7 1.9 %collective-permute-start = (bf16[512,512]{1,0:T(8,128)(2,1)}, bf16[512,512]{1,0:T(8,128)(2,1)S(1)}, u32[]{:S(2)}, u32[]{:S(2)}) collective-permute-start(bf16[512,512]{1,0:T(8,128)(2,1)} %get-tuple-element.74), channel_id=1, source_target_pairs={{0,2},{1,3},{2,0},{3,1},{4,6},{5,7},{6,4},{7,5},{8,10},{9,11},{10,... | collective-permute-start | bytes 1572872 | tf_op jit(solution)/shard_map/ppermute | solution.py:27
  7.6 0.8 reshape.3.refs_6_.refs_8_.refs_4_
  8.4 0.1 pad_add_fusion.info
  8.5 11.0 %shard_map.119 = (f32[512,512]{1,0:T(8,128)S(1)}, f32[512,1024]{1,0:T(8,128)S(1)}, f32[512,512]{1,0:T(8,128)S(1)}, f32[512,1024]{1,0:T(8,128)S(1)}, f32[4,512]{1,0:T(4,128)S(1)}) custom-call(s32[3]{0:T(128)S(1)} %pad_add_fusion.info, bf16[512,1024]{1,0:T(8,128)(2,1)S(1)} %get-tuple-element.73.refs_0_, bf16[512,1024]{1,0:T(8,128)(2,1)S(1)} %collective-permute-done.3.refs_1_, ...), custom_call_target="tpu_custom_call" | custom-call | flops 1000000 | bytes 100000 | tf_op jit(solution)/shard_map/pallas_call | solution.py:164
  19.6 0.0 copy-start.11
  19.6 0.0 copy-start.13
  19.6 0.1 collective-permute-start.4
  19.7 0.5 collective-permute-start.5
  20.2 1.0 collective-permute-done.4.refs_1_
  21.2 0.4 collective-permute-done.5.refs_3_
  21.6 7.7 %shard_map.120 = (f32[512,512]{1,0:T(8,128)S(1)}, f32[512,1024]{1,0:T(8,128)S(1)}, f32[512,512]{1,0:T(8,128)S(1)}, f32[512,1024]{1,0:T(8,128)S(1)}, f32[4,512]{1...) custom-call(s32[3]{0:T(128)S(1)} %pad_add_fusion.info, ...), custom_call_target="tpu_custom_call", output_to_operand_aliasing={{0}: (10, {}), {1}: (11, {}), {2}: (12, {}), {3}: (13, {}),... | custom-call | flops 1000000 | bytes 100000 | tf_op jit(solution)/shard_map/pallas_call | solution.py:164
  29.3 0.4 collective-permute-done.refs_0_
  29.7 1.9 %collective-permute-done.6.refs_1_ = bf16[512,512]{1,0:T(8,128)(2,1)S(1)} collective-permute-done((bf16[512,512]{1,0:T(8,128)(2,1)S(1)}, bf16[512,512]{1,0:T(8,128)(2,1)S(1)}, u32[]{:S(2)}, u32[]{:S(2)}) %collective-permute-start.6) | collective-permute-done | bytes 524320 | tf_op jit(solution)/shard_map/ppermute | solution.py:27
  31.6 3.7 %shard_map.121 = (bf16[512,512]{1,0:T(8,128)(2,1)S(1)}, bf16[512,1024]{1,0:T(8,128)(2,1)S(1)}, bf16[2,128,512]{2,1,0:T(8,128)(2,1)S(1)}, bf16[2,128,512]{2,1,0:T...) custom-call(s32[3]{0:T(128)S(1)} %pad_add_fusion.info, s32[4]{0:T(128)S(1)} %copy-done.11, ...), custom_call_target="tpu_custom_call" | custom-call | flops 4000000000 | bytes 4000000 | tf_op jit(solution)/shard_map/pallas_call | solution.py:294
  35.3 1.8 %collective-permute-start.8 = (bf16[2,128,512]{2,1,0:T(8,128)(2,1)S(1)}, bf16[2,128,512]{2,1,0:T(8,128)(2,1)S(1)}, u32[]{:S(2)}, u32[]{:S(2)}) collective-permute-start(bf16[2,128,512]{2,1,0:T(8,128)(2,1)S(1)} %get-tuple-element.101), channel_id=1, source_target_pairs={{0,4},{4,0},{8,12},{12,8},{16,20},{20,16},{24,28},{28,24},{1,5},{5... | collective-permute-start | bytes 786440 | tf_op jit(solution)/shard_map/ppermute | solution.py:27
  37.1 0.3 collective-permute-start.7
  37.4 1.0 copy-done.8
  38.4 2.7 %shard_map.122 = (bf16[512,512]{1,0:T(8,128)(2,1)S(1)}, f32[512,1024]{1,0:T(8,128)S(1)}) custom-call(bf16[512,512]{1,0:T(8,128)(2,1)S(1)} %copy-done.8, bf16[512,512]{1,0:T(8,128)(2,1)S(1)} %collective-permute-done.6.refs_1_, bf16[1024,512]{1,0:T(8,128)(2,1)S(1)} %get-tuple-element.105.refs_2_, bf16[1024,1024]{1,0:T(8,128)(2,1)S(1)} %get-tuple-element.106.refs_3_, ...), custom_call_target="tpu_custom_call" | custom-call | flops 1000000 | bytes 100000 | tf_op jit(solution)/shard_map/pallas_call | solution.py:200
  41.2 0.8 copy-done
  42.0 1.8 %collective-permute-done.7.other = f32[2,384]{1,0:T(2,128)S(1)} collective-permute-done((f32[2,384]{1,0:T(2,128)S(1)}, f32[2,384]{1,0:T(2,128)S(1)}, u32[]{:S(2)}, u32[]{:S(2)}) %collective-permute-start.7) | collective-permute-done | bytes 3104 | tf_op jit(solution)/shard_map/ppermute | solution.py:27
  43.8 0.8 shard_map.123
  44.6 0.7 copy-done.3
  45.3 1.8 %collective-permute-start.10 = (bf16[2,128,512]{2,1,0:T(8,128)(2,1)S(1)}, bf16[2,128,512]{2,1,0:T(8,128)(2,1)}, u32[]{:S(2)}, u32[]{:S(2)}) collective-permute-start(bf16[2,128,512]{2,1,0:T(8,128)(2,1)S(1)} %get-tuple-element.115), channel_id=1, source_target_pairs={{0,8},{4,12},{8,16},{12,20},{16,24},{20,28},{24,0},{28,4},{1,9},{5... | collective-permute-start | bytes 786440 | tf_op jit(solution)/shard_map/ppermute | solution.py:32
  47.1 1.6 %collective-permute-start.9 = (f32[2,384]{1,0:T(2,128)S(1)}, f32[2,384]{1,0:T(2,128)S(1)}, u32[]{:S(2)}, u32[]{:S(2)}) collective-permute-start(f32[2,384]{1,0:T(2,128)S(1)} %get-tuple-element.114), channel_id=1, source_target_pairs={{0,8},{4,12},{8,16},{12,20},{16,24},{20,28},{24,0},{28,4},{1,9},{5... | collective-permute-start | bytes 9224 | tf_op jit(solution)/shard_map/ppermute | solution.py:32
  48.6 6.4 %collective-permute-done.9.refs_0_ = f32[2,384]{1,0:T(2,128)S(1)} collective-permute-done((f32[2,384]{1,0:T(2,128)S(1)}, f32[2,384]{1,0:T(2,128)S(1)}, u32[]{:S(2)}, u32[]{:S(2)}) %collective-permute-start.9) | collective-permute-done | bytes 3104 | tf_op jit(solution)/shard_map/ppermute | solution.py:32
  55.0 1.3 %collective-permute-start.11 = (f32[2,384]{1,0:T(2,128)S(1)}, f32[2,384]{1,0:T(2,128)S(1)}, u32[]{:S(2)}, u32[]{:S(2)}) collective-permute-start(f32[2,384]{1,0:T(2,128)S(1)} %collective-permute-done.9.refs_0_), channel_id=1, source_target_pairs={{0,8},{4,12},{8,16},{12,20},{16,24},{20,28},{24,0},{28,4},{1,9},{5... | collective-permute-start | bytes 9224 | tf_op jit(solution)/shard_map/ppermute | solution.py:32
  56.3 0.1 copy.18.refs_6_
  56.4 7.7 %collective-permute-done.11.refs_1_ = f32[2,384]{1,0:T(2,128)S(1)} collective-permute-done((f32[2,384]{1,0:T(2,128)S(1)}, f32[2,384]{1,0:T(2,128)S(1)}, u32[]{:S(2)}, u32[]{:S(2)}) %collective-permute-start.11) | collective-permute-done | bytes 3104 | tf_op jit(solution)/shard_map/ppermute | solution.py:32
  64.1 1.2 %copy-done.2 = f32[2,256,512]{2,1,0:T(8,128)S(1)} copy-done((f32[2,256,512]{2,1,0:T(8,128)S(1)}, f32[2,256,512]{2,1,0:T(8,128)}, u32[]{:S(2)}) %copy-start.2) | copy-done | bytes 1048600
  65.3 0.9 copy-done.4
  66.3 1.8 %shard_map.124 = (bf16[2,128,512]{2,1,0:T(8,128)(2,1)S(1)}, bf16[2,128,512]{2,1,0:T(8,128)(2,1)S(1)}, f32[2,256]{1,0:T(2,128)S(1)}, f32[2,128]{1,0:T(2,128)S(1)}) custom-call(s32[3]{0:T(128)S(1)} %pad_add_fusion.info, s32[4]{0:T(128)S(1)} %copy-done.11, f32[2,384]{1,0:T(2,128)S(1)} %get-tuple-element.100.own, f32[2,384]{1,0:T(2,128)S(1)} %collective-permute-done.7.other, ...), custom_call_target="tpu_custom_call" | custom-call | flops 1000000 | bytes 100000 | tf_op jit(solution)/shard_map/pallas_call | solution.py:420
  68.1 1.2 %collective-permute-start.13 = (bf16[2,128,512]{2,1,0:T(8,128)(2,1)S(1)}, bf16[2,128,512]{2,1,0:T(8,128)(2,1)S(1)}, u32[]{:S(2)}, u32[]{:S(2)}) collective-permute-start(bf16[2,128,512]{2,1,0:T(8,128)(2,1)S(1)} %get-tuple-element.121), channel_id=1, source_target_pairs={{0,4},{4,0},{8,12},{12,8},{16,20},{20,16},{24,28},{28,24},{1,5},{5... | collective-permute-start | bytes 786440 | tf_op jit(solution)/shard_map/ppermute | solution.py:27
  69.4 4.2 %shard_map.125 = (f32[512,1024]{1,0:T(8,128)S(1)}, f32[512,1024]{1,0:T(8,128)S(1)}, bf16[1024,4096]{1,0:T(8,128)(2,1)S(1)}) custom-call(s32[3]{0:T(128)S(1)} %pad_add_fusion.info, s32[4]{0:T(128)S(1)} %copy-done.11, f32[2,128]{1,0:T(2,128)S(1)} %get-tuple-element.122.top_in, bf16[512,512]{1,0:T(8,128)(2,1)S(1)} %copy-done.1, ...), custom_call_target="tpu_custom_call" | custom-call | flops 1000000 | bytes 100000 | tf_op jit(solution)/shard_map/pallas_call | solution.py:489
  73.6 1.0 collective-permute-done.13.other
  74.6 2.1 %shard_map.126 = (bf16[512,1024]{1,0:T(8,128)(2,1)S(1)}, bf16[512,512]{1,0:T(8,128)(2,1)S(1)}, bf16[512,512]{1,0:T(8,128)(2,1)S(1)}) custom-call(s32[3]{0:T(128)S(1)} %pad_add_fusion.info, bf16[512,512]{1,0:T(8,128)(2,1)S(1)} %copy-done.1, bf16[2,128,512]{2,1,0:T(8,128)(2,1)S(1)} %get-tuple-element.120.own, ...), custom_call_target="tpu_custom_call" | custom-call | flops 3000000000 | bytes 8000000 | tf_op jit(solution)/shard_map/pallas_call | solution.py:533
  76.7 0.1 collective-permute-start.14
  76.7 1.8 %shard_map.127 = (bf16[512,512]{1,0:T(8,128)(2,1)S(1)}, bf16[512,512]{1,0:T(8,128)(2,1)S(1)}) custom-call(s32[3]{0:T(128)S(1)} %pad_add_fusion.info, bf16[512,1024]{1,0:T(8,128)(2,1)S(1)} %get-tuple-element.138.hidden, bf16[1024,4096]{1,0:T(8,128)(2,1)S(1)} %get-tuple-element.129.w), custom_call_target="tpu_custom_call" | custom-call | flops 1000000 | bytes 100000 | tf_op jit(solution)/shard_map/pallas_call | solution.py:554
  78.6 0.6 collective-permute-start.16
  79.1 0.1 copy.24
  79.2 0.1 convert_add_fusion.3
  79.4 1.3 %collective-permute-start.15 = (bf16[512,256]{1,0:T(8,128)(2,1)S(1)}, bf16[512,256]{1,0:T(8,128)(2,1)S(1)}, u32[]{:S(2)}, u32[]{:S(2)}) collective-permute-start(bf16[512,256]{1,0:T(8,128)(2,1)S(1)} %slice.99), channel_id=1, source_target_pairs={{0,2},{1,3},{2,0},{3,1},{4,6},{5,7},{6,4},{7,5},{8,10},{9,11},{10,... | collective-permute-start | bytes 786440 | tf_op jit(solution)/shard_map/ppermute | solution.py:27
  80.7 1.8 %shard_map.128 = (bf16[512,512]{1,0:T(8,128)(2,1)S(1)}, bf16[512,512]{1,0:T(8,128)(2,1)S(1)}) custom-call(s32[3]{0:T(128)S(1)} %pad_add_fusion.info, bf16[512,1024]{1,0:T(8,128)(2,1)S(1)} %get-tuple-element.138.hidden, bf16[1024,4096]{1,0:T(8,128)(2,1)S(1)} %get-tuple-element.129.w), custom_call_target="tpu_custom_call" | custom-call | flops 1000000 | bytes 100000 | tf_op jit(solution)/shard_map/pallas_call | solution.py:554
  82.6 0.1 collective-permute-start.18
  82.7 0.1 convert_add_fusion.2
  82.9 0.8 collective-permute-start.17
  83.7 1.8 %shard_map.129 = (bf16[512,512]{1,0:T(8,128)(2,1)S(1)}, bf16[512,512]{1,0:T(8,128)(2,1)S(1)}) custom-call(s32[3]{0:T(128)S(1)} %pad_add_fusion.info, bf16[512,1024]{1,0:T(8,128)(2,1)S(1)} %get-tuple-element.138.hidden, bf16[1024,4096]{1,0:T(8,128)(2,1)S(1)} %get-tuple-element.129.w), custom_call_target="tpu_custom_call" | custom-call | flops 1000000 | bytes 100000 | tf_op jit(solution)/shard_map/pallas_call | solution.py:554
  85.5 0.3 collective-permute-start.20
  85.8 2.9 %collective-permute-done.15 = bf16[512,256]{1,0:T(8,128)(2,1)S(1)} collective-permute-done((bf16[512,256]{1,0:T(8,128)(2,1)S(1)}, bf16[512,256]{1,0:T(8,128)(2,1)S(1)}, u32[]{:S(2)}, u32[]{:S(2)}) %collective-permute-start.15) | collective-permute-done | bytes 262176 | tf_op jit(solution)/shard_map/ppermute | solution.py:27
  88.7 0.2 fusion.8
  88.9 0.1 convert_add_fusion.1
  89.1 1.3 %collective-permute-start.19 = (bf16[512,256]{1,0:T(8,128)(2,1)S(1)}, bf16[512,256]{1,0:T(8,128)(2,1)S(1)}, u32[]{:S(2)}, u32[]{:S(2)}) collective-permute-start(bf16[512,256]{1,0:T(8,128)(2,1)S(1)} %slice.97), channel_id=1, source_target_pairs={{0,2},{1,3},{2,0},{3,1},{4,6},{5,7},{6,4},{7,5},{8,10},{9,11},{10,... | collective-permute-start | bytes 786440 | tf_op jit(solution)/shard_map/ppermute | solution.py:27
  90.4 0.1 convert_add_fusion
  90.6 0.8 collective-permute-start.21
  91.4 2.9 %collective-permute-done.17 = bf16[512,256]{1,0:T(8,128)(2,1)S(1)} collective-permute-done((bf16[512,256]{1,0:T(8,128)(2,1)S(1)}, bf16[512,256]{1,0:T(8,128)(2,1)S(1)}, u32[]{:S(2)}, u32[]{:S(2)}) %collective-permute-start.17) | collective-permute-done | bytes 262176 | tf_op jit(solution)/shard_map/ppermute | solution.py:27
  94.3 0.1 fusion.9
  94.4 5.5 %collective-permute-done.19 = bf16[512,256]{1,0:T(8,128)(2,1)S(1)} collective-permute-done((bf16[512,256]{1,0:T(8,128)(2,1)S(1)}, bf16[512,256]{1,0:T(8,128)(2,1)S(1)}, u32[]{:S(2)}, u32[]{:S(2)}) %collective-permute-start.19) | collective-permute-done | bytes 262176 | tf_op jit(solution)/shard_map/ppermute | solution.py:27
  99.9 0.1 fusion.10
  100.0 4.6 %collective-permute-done.21 = bf16[512,256]{1,0:T(8,128)(2,1)S(1)} collective-permute-done((bf16[512,256]{1,0:T(8,128)(2,1)S(1)}, bf16[512,256]{1,0:T(8,128)(2,1)S(1)}, u32[]{:S(2)}, u32[]{:S(2)}) %collective-permute-start.21) | collective-permute-done | bytes 262176 | tf_op jit(solution)/shard_map/ppermute | solution.py:27
  104.6 0.1 fusion.11
  104.7 1.0 copy.28
  (39 shorter events, 0.2 us)
Async XLA Ops:
  0.0 8.5 %collective-permute-start.3 = (bf16[512,1024]{1,0:T(8,128)(2,1)}, bf16[512,1024]{1,0:T(8,128)(2,1)S(1)}, u32[]{:S(2)}, u32[]{:S(2)}) collective-permute-start(bf16[512,1024]{1,0:T(8,128)(2,1)} %tokens.1), channel_id=1, source_target_pairs={{0,1},{1,0},{2,3},{3,2},{4,5},{5,4},{6,7},{7,6},{8,9},{9,8},{10,11... | collective-permute-start | bytes 3145736 | tf_op jit(solution)/shard_map/ppermute | solution.py:27
  3.0 16.5 %collective-permute-start.1 = (bf16[512,256]{1,0:T(8,128)(2,1)}, bf16[512,256]{1,0:T(8,128)(2,1)S(1)}, u32[]{:S(2)}, u32[]{:S(2)}) collective-permute-start(bf16[512,256]{1,0:T(8,128)(2,1)} %get-tuple-element.75), channel_id=1, source_target_pairs={{0,2},{1,3},{2,0},{3,1},{4,6},{5,7},{6,4},{7,5},{8,10},{9,11},{10,... | collective-permute-start | bytes 786440 | tf_op jit(solution)/shard_map/ppermute | solution.py:27
  5.6 14.0 %collective-permute-start.2 = (bf16[512,256]{1,0:T(8,128)(2,1)}, bf16[512,256]{1,0:T(8,128)(2,1)S(1)}, u32[]{:S(2)}, u32[]{:S(2)}) collective-permute-start(bf16[512,256]{1,0:T(8,128)(2,1)} %get-tuple-element.76), channel_id=1, source_target_pairs={{0,2},{1,3},{2,0},{3,1},{4,6},{5,7},{6,4},{7,5},{8,10},{9,11},{10,... | collective-permute-start | bytes 786440 | tf_op jit(solution)/shard_map/ppermute | solution.py:27
  5.7 24.0 %collective-permute-start = (bf16[512,512]{1,0:T(8,128)(2,1)}, bf16[512,512]{1,0:T(8,128)(2,1)S(1)}, u32[]{:S(2)}, u32[]{:S(2)}) collective-permute-start(bf16[512,512]{1,0:T(8,128)(2,1)} %get-tuple-element.74), channel_id=1, source_target_pairs={{0,2},{1,3},{2,0},{3,1},{4,6},{5,7},{6,4},{7,5},{8,10},{9,11},{10,... | collective-permute-start | bytes 1572872 | tf_op jit(solution)/shard_map/ppermute | solution.py:27
  19.6 12.0 %copy-start.11 = (s32[4]{0:T(128)S(1)}, s32[4]{0:T(128)}, u32[]{:S(2)}) copy-start(s32[4]{0:T(128)} %docs.7) | copy-start | bytes 52
  19.6 12.0 %copy-start.13 = (f32[2,2]{1,0:T(2,128)S(1)}, f32[2,2]{1,0:T(2,128)}, u32[]{:S(2)}) copy-start(f32[2,2]{1,0:T(2,128)} %bias.1) | copy-start | bytes 52
  19.6 1.6 %collective-permute-start.4 = (bf16[512,256]{1,0:T(8,128)(2,1)S(1)}, bf16[512,256]{1,0:T(8,128)(2,1)S(1)}, u32[]{:S(2)}, u32[]{:S(2)}) collective-permute-start(bf16[512,256]{1,0:T(8,128)(2,1)S(1)} %collective-permute-done.1.refs_0_), channel_id=1, source_target_pairs={{0,1},{1,0},{2,3},{3,2},{4,5},{5,4},{6,7},{7,6},{8,9},{9,8},{10,11... | collective-permute-start | bytes 786440 | tf_op jit(solution)/shard_map/ppermute | solution.py:27
  19.7 1.9 %collective-permute-start.5 = (bf16[512,256]{1,0:T(8,128)(2,1)S(1)}, bf16[512,256]{1,0:T(8,128)(2,1)S(1)}, u32[]{:S(2)}, u32[]{:S(2)}) collective-permute-start(bf16[512,256]{1,0:T(8,128)(2,1)S(1)} %collective-permute-done.2.refs_2_), channel_id=1, source_target_pairs={{0,1},{1,0},{2,3},{3,2},{4,5},{5,4},{6,7},{7,6},{8,9},{9,8},{10,11... | collective-permute-start | bytes 786440 | tf_op jit(solution)/shard_map/ppermute | solution.py:27
  29.7 5.6 %copy-start.7 = (bf16[512,512]{1,0:T(8,128)(2,1)}, bf16[512,512]{1,0:T(8,128)(2,1)S(1)}, u32[]{:S(2)}) copy-start(bf16[512,512]{1,0:T(8,128)(2,1)S(1)} %collective-permute-done.refs_0_) | copy-start | bytes 1572868
  29.7 1.9 %collective-permute-start.6 = (bf16[512,512]{1,0:T(8,128)(2,1)S(1)}, bf16[512,512]{1,0:T(8,128)(2,1)S(1)}, u32[]{:S(2)}, u32[]{:S(2)}) collective-permute-start(bf16[512,512]{1,0:T(8,128)(2,1)S(1)} %collective-permute-done.refs_0_), channel_id=1, source_target_pairs={{0,1},{1,0},{2,3},{3,2},{4,5},{5,4},{6,7},{7,6},{8,9},{9,8},{10,11... | collective-permute-start | bytes 1572872 | tf_op jit(solution)/shard_map/ppermute | solution.py:27
  35.3 5.9 %copy-start.5 = (bf16[512,1024]{1,0:T(8,128)(2,1)}, bf16[512,1024]{1,0:T(8,128)(2,1)S(1)}, u32[]{:S(2)}) copy-start(bf16[512,1024]{1,0:T(8,128)(2,1)S(1)} %get-tuple-element.123.value) | copy-start | bytes 3145732
  35.3 5.9 %copy-start.9 = (bf16[512,512]{1,0:T(8,128)(2,1)}, bf16[512,512]{1,0:T(8,128)(2,1)S(1)}, u32[]{:S(2)}) copy-start(bf16[512,512]{1,0:T(8,128)(2,1)S(1)} %get-tuple-element.102.key) | copy-start | bytes 1572868
  35.3 8.5 %collective-permute-start.8 = (bf16[2,128,512]{2,1,0:T(8,128)(2,1)S(1)}, bf16[2,128,512]{2,1,0:T(8,128)(2,1)S(1)}, u32[]{:S(2)}, u32[]{:S(2)}) collective-permute-start(bf16[2,128,512]{2,1,0:T(8,128)(2,1)S(1)} %get-tuple-element.101), channel_id=1, source_target_pairs={{0,4},{4,0},{8,12},{12,8},{16,20},{20,16},{24,28},{28,24},{1,5},{5... | collective-permute-start | bytes 786440 | tf_op jit(solution)/shard_map/ppermute | solution.py:27
  37.1 6.7 %collective-permute-start.7 = (f32[2,384]{1,0:T(2,128)S(1)}, f32[2,384]{1,0:T(2,128)S(1)}, u32[]{:S(2)}, u32[]{:S(2)}) collective-permute-start(f32[2,384]{1,0:T(2,128)S(1)} %get-tuple-element.100.own), channel_id=1, source_target_pairs={{0,4},{4,0},{8,12},{12,8},{16,20},{20,16},{24,28},{28,24},{1,5},{5... | collective-permute-start | bytes 9224 | tf_op jit(solution)/shard_map/ppermute | solution.py:27
  37.4 1.0 copy-start.8
  38.4 17.9 %copy-start.14 = (f32[2]{0:T(128)S(1)}, f32[2]{0:T(128)}, u32[]{:S(2)}) copy-start(f32[2]{0:T(128)} %param.22) | copy-start | bytes 28
  38.4 25.7 %copy-start.12 = (f32[2,256]{1,0:T(2,128)S(1)}, f32[2,256]{1,0:T(2,128)}, u32[]{:S(2)}) copy-start(f32[2,256]{1,0:T(2,128)} %refs_5_.5) | copy-start | bytes 6148
  41.2 0.8 copy-start
  44.6 0.7 copy-start.3
  45.3 9.7 %collective-permute-start.10 = (bf16[2,128,512]{2,1,0:T(8,128)(2,1)S(1)}, bf16[2,128,512]{2,1,0:T(8,128)(2,1)}, u32[]{:S(2)}, u32[]{:S(2)}) collective-permute-start(bf16[2,128,512]{2,1,0:T(8,128)(2,1)S(1)} %get-tuple-element.115), channel_id=1, source_target_pairs={{0,8},{4,12},{8,16},{12,20},{16,24},{20,28},{24,0},{28,4},{1,9},{5... | collective-permute-start | bytes 786440 | tf_op jit(solution)/shard_map/ppermute | solution.py:32
  47.1 7.9 %collective-permute-start.9 = (f32[2,384]{1,0:T(2,128)S(1)}, f32[2,384]{1,0:T(2,128)S(1)}, u32[]{:S(2)}, u32[]{:S(2)}) collective-permute-start(f32[2,384]{1,0:T(2,128)S(1)} %get-tuple-element.114), channel_id=1, source_target_pairs={{0,8},{4,12},{8,16},{12,20},{16,24},{20,28},{24,0},{28,4},{1,9},{5... | collective-permute-start | bytes 9224 | tf_op jit(solution)/shard_map/ppermute | solution.py:32
  55.0 9.1 %collective-permute-start.12 = (bf16[2,128,512]{2,1,0:T(8,128)(2,1)}, bf16[2,128,512]{2,1,0:T(8,128)(2,1)}, u32[]{:S(2)}, u32[]{:S(2)}) collective-permute-start(bf16[2,128,512]{2,1,0:T(8,128)(2,1)} %collective-permute-done.10.refs_2_), channel_id=1, source_target_pairs={{0,8},{4,12},{8,16},{12,20},{16,24},{20,28},{24,0},{28,4},{1,9},{5... | collective-permute-start | bytes 786440 | tf_op jit(solution)/shard_map/ppermute | solution.py:32
  55.0 9.1 %collective-permute-start.11 = (f32[2,384]{1,0:T(2,128)S(1)}, f32[2,384]{1,0:T(2,128)S(1)}, u32[]{:S(2)}, u32[]{:S(2)}) collective-permute-start(f32[2,384]{1,0:T(2,128)S(1)} %collective-permute-done.9.refs_0_), channel_id=1, source_target_pairs={{0,8},{4,12},{8,16},{12,20},{16,24},{20,28},{24,0},{28,4},{1,9},{5... | collective-permute-start | bytes 9224 | tf_op jit(solution)/shard_map/ppermute | solution.py:32
  56.4 13.0 %copy-start.1 = (bf16[512,512]{1,0:T(8,128)(2,1)S(1)}, bf16[512,512]{1,0:T(8,128)(2,1)}, u32[]{:S(2)}) copy-start(bf16[512,512]{1,0:T(8,128)(2,1)} %copy-done) | copy-start | bytes 1572868
  64.1 1.2 %copy-start.2 = (f32[2,256,512]{2,1,0:T(8,128)S(1)}, f32[2,256,512]{2,1,0:T(8,128)}, u32[]{:S(2)}) copy-start(f32[2,256,512]{2,1,0:T(8,128)} %refs_4_.5) | copy-start | bytes 3145732
  65.3 0.9 copy-start.4
  66.3 3.1 %copy-start.6 = (bf16[512,1024]{1,0:T(8,128)(2,1)S(1)}, bf16[512,1024]{1,0:T(8,128)(2,1)}, u32[]{:S(2)}) copy-start(bf16[512,1024]{1,0:T(8,128)(2,1)} %copy-done.5) | copy-start | bytes 3145732
  66.3 3.1 %copy-start.10 = (bf16[512,512]{1,0:T(8,128)(2,1)S(1)}, bf16[512,512]{1,0:T(8,128)(2,1)}, u32[]{:S(2)}) copy-start(bf16[512,512]{1,0:T(8,128)(2,1)} %copy-done.9) | copy-start | bytes 1572868
  68.1 6.4 %collective-permute-start.13 = (bf16[2,128,512]{2,1,0:T(8,128)(2,1)S(1)}, bf16[2,128,512]{2,1,0:T(8,128)(2,1)S(1)}, u32[]{:S(2)}, u32[]{:S(2)}) collective-permute-start(bf16[2,128,512]{2,1,0:T(8,128)(2,1)S(1)} %get-tuple-element.121), channel_id=1, source_target_pairs={{0,4},{4,0},{8,12},{12,8},{16,20},{20,16},{24,28},{28,24},{1,5},{5... | collective-permute-start | bytes 786440 | tf_op jit(solution)/shard_map/ppermute | solution.py:27
  76.7 2.6 %collective-permute-start.14 = (bf16[512,512]{1,0:T(8,128)(2,1)S(1)}, bf16[512,512]{1,0:T(8,128)(2,1)S(1)}, u32[]{:S(2)}, u32[]{:S(2)}) collective-permute-start(bf16[512,512]{1,0:T(8,128)(2,1)S(1)} %get-tuple-element.131), channel_id=1, source_target_pairs={{0,1},{1,0},{2,3},{3,2},{4,5},{5,4},{6,7},{7,6},{8,9},{9,8},{10,11... | collective-permute-start | bytes 1572872 | tf_op jit(solution)/shard_map/ppermute | solution.py:27
  78.6 4.1 %collective-permute-start.16 = (bf16[512,512]{1,0:T(8,128)(2,1)S(1)}, bf16[512,512]{1,0:T(8,128)(2,1)S(1)}, u32[]{:S(2)}, u32[]{:S(2)}) collective-permute-start(bf16[512,512]{1,0:T(8,128)(2,1)S(1)} %get-tuple-element.134), channel_id=1, source_target_pairs={{0,1},{1,0},{2,3},{3,2},{4,5},{5,4},{6,7},{7,6},{8,9},{9,8},{10,11... | collective-permute-start | bytes 1572872 | tf_op jit(solution)/shard_map/ppermute | solution.py:27
  79.4 9.2 %collective-permute-start.15 = (bf16[512,256]{1,0:T(8,128)(2,1)S(1)}, bf16[512,256]{1,0:T(8,128)(2,1)S(1)}, u32[]{:S(2)}, u32[]{:S(2)}) collective-permute-start(bf16[512,256]{1,0:T(8,128)(2,1)S(1)} %slice.99), channel_id=1, source_target_pairs={{0,2},{1,3},{2,0},{3,1},{4,6},{5,7},{6,4},{7,5},{8,10},{9,11},{10,... | collective-permute-start | bytes 786440 | tf_op jit(solution)/shard_map/ppermute | solution.py:27
  82.6 6.3 %collective-permute-start.18 = (bf16[512,512]{1,0:T(8,128)(2,1)S(1)}, bf16[512,512]{1,0:T(8,128)(2,1)S(1)}, u32[]{:S(2)}, u32[]{:S(2)}) collective-permute-start(bf16[512,512]{1,0:T(8,128)(2,1)S(1)} %get-tuple-element.137), channel_id=1, source_target_pairs={{0,1},{1,0},{2,3},{3,2},{4,5},{5,4},{6,7},{7,6},{8,9},{9,8},{10,11... | collective-permute-start | bytes 1572872 | tf_op jit(solution)/shard_map/ppermute | solution.py:27
  82.9 11.4 %collective-permute-start.17 = (bf16[512,256]{1,0:T(8,128)(2,1)S(1)}, bf16[512,256]{1,0:T(8,128)(2,1)S(1)}, u32[]{:S(2)}, u32[]{:S(2)}) collective-permute-start(bf16[512,256]{1,0:T(8,128)(2,1)S(1)} %slice.98), channel_id=1, source_target_pairs={{0,2},{1,3},{2,0},{3,1},{4,6},{5,7},{6,4},{7,5},{8,10},{9,11},{10,... | collective-permute-start | bytes 786440 | tf_op jit(solution)/shard_map/ppermute | solution.py:27
  85.5 4.9 %collective-permute-start.20 = (bf16[512,512]{1,0:T(8,128)(2,1)S(1)}, bf16[512,512]{1,0:T(8,128)(2,1)S(1)}, u32[]{:S(2)}, u32[]{:S(2)}) collective-permute-start(bf16[512,512]{1,0:T(8,128)(2,1)S(1)} %get-tuple-element.140), channel_id=1, source_target_pairs={{0,1},{1,0},{2,3},{3,2},{4,5},{5,4},{6,7},{7,6},{8,9},{9,8},{10,11... | collective-permute-start | bytes 1572872 | tf_op jit(solution)/shard_map/ppermute | solution.py:27
  89.1 10.8 %collective-permute-start.19 = (bf16[512,256]{1,0:T(8,128)(2,1)S(1)}, bf16[512,256]{1,0:T(8,128)(2,1)S(1)}, u32[]{:S(2)}, u32[]{:S(2)}) collective-permute-start(bf16[512,256]{1,0:T(8,128)(2,1)S(1)} %slice.97), channel_id=1, source_target_pairs={{0,2},{1,3},{2,0},{3,1},{4,6},{5,7},{6,4},{7,5},{8,10},{9,11},{10,... | collective-permute-start | bytes 786440 | tf_op jit(solution)/shard_map/ppermute | solution.py:27
  90.6 14.0 %collective-permute-start.21 = (bf16[512,256]{1,0:T(8,128)(2,1)S(1)}, bf16[512,256]{1,0:T(8,128)(2,1)S(1)}, u32[]{:S(2)}, u32[]{:S(2)}) collective-permute-start(bf16[512,256]{1,0:T(8,128)(2,1)S(1)} %slice.96), channel_id=1, source_target_pairs={{0,2},{1,3},{2,0},{3,1},{4,6},{5,7},{6,4},{7,5},{8,10},{9,11},{10,... | collective-permute-start | bytes 786440 | tf_op jit(solution)/shard_map/ppermute | solution.py:27

commit v5 on v4

--- a/solution.py
+++ b/solution.py
@@ -44,6 +44,14 @@
 
 def in_hbm(x):
     return pltpu.with_memory_space_constraint(x, pltpu.HBM)
+
+
+def in_vmem(*xs):
+    return [pltpu.with_memory_space_constraint(x, pltpu.VMEM) for x in xs]
+
+
+def holding(kernel, held):
+    return (lambda *refs: kernel(*refs[len(held) :])) if held else kernel
 
 
 def split_kernel(starts, tokens, *refs):
@@ -78,49 +86,48 @@
     return pl.multiple_of((place ^ owner) * share + first, 128)
 
 
-def stage_kernel(xs_at, ahead_at, share, with_sum, info, *refs):
+def copies_of(weights, targets, semaphores, at, place, share):
+    result = []
+    for i, (w, target) in enumerate(zip(weights, targets)):
+        low, group = 0, []
+        for p, (owner, first, count) in enumerate(at):
+            group.append(
+                pltpu.make_async_copy(
+                    w.at[pl.ds(row_start(place, share, owner, first), count)],
+                    target.at[pl.ds(low, count)],
+                    semaphores.at[i, p],
+                )
+            )
+            low += count
+        result.append(group)
+    return result
+
+
+def stage_kernel(xs_at, ahead_at, share, names, with_sum, finishes, gated, info, *refs):
     refs = list(refs)
     take = lambda n: [refs.pop(0) for _ in range(n)]
-    pieces = len(xs_at)
-    xs, ws, (gate_w,) = take(pieces), take(4), take(1)
-    sums = take(5) if with_sum else None
-    outs = take(5)
-    ahead = take(4) if ahead_at else []
-    held = take(4)
-    sems, ahead_sems = take(2) if ahead_at else (take(1)[0], None)
+    count_w = names
+    xs, ws = take(len(xs_at)), take(count_w)
+    gate_w = take(1)[0] if gated else None
+    sums = take(count_w + gated) if with_sum else None
+    outs = take(count_w + gated)
+    ahead = take(count_w) if ahead_at else []
+    held = take(count_w)
+    sems = take(1)[0]
     place = info[0]
-
-    def copies(at, targets, semaphores):
-        result = []
-        for i, (w, target) in enumerate(zip(ws, targets)):
-            low, group = 0, []
-            for p, (owner, first, count) in enumerate(at):
-                group.append(
-                    pltpu.make_async_copy(
-                        w.at[pl.ds(row_start(place, share, owner, first), count)],
-                        target.at[pl.ds(low, count)],
-                        semaphores.at[i, p],
-                    )
-                )
-                low += count
-            result.append(group)
-        return result
-
-    now = copies(xs_at, held, sems)
-    for group in now:
+    now = copies_of(ws, held, sems, xs_at, place, share)
+    later = copies_of(ws, ahead, take(1)[0], ahead_at, place, share) if ahead_at else []
+    for group in now + later:
         for copy in group:
             copy.start()
-    later = copies(ahead_at, ahead, ahead_sems) if ahead_at else []
-    for group in later:
-        for copy in group:
-            copy.start()
-    gates = sums[4][...] if with_sum else 0.0
-    for (owner, first, count), x in zip(xs_at, xs):
-        gates = gates + across_tokens(
-            gate_w[:, pl.ds(row_start(place, share, owner, first), count)], x[...]
-        )
-    outs[4][...] = gates
-    for i in range(4):
+    if gated:
+        gates = sums[count_w][...] if with_sum else 0.0
+        for (owner, first, count), x in zip(xs_at, xs):
+            gates = gates + across_tokens(
+                gate_w[:, pl.ds(row_start(place, share, owner, first), count)], x[...]
+            )
+        outs[count_w][...] = gates
+    for i in range(count_w):
         for copy in now[i]:
             copy.wait()
 
@@ -134,7 +141,7 @@
                 )
                 total = part if total is None else total + part
                 low += count
-            outs[i][:, columns] = total
+            outs[i][:, columns] = finishes[i](total).astype(outs[i].dtype)
             return 0
 
         lax.fori_loop(0, outs[i].shape[1] // 256, body, 0)
@@ -143,26 +150,43 @@
             copy.wait()
 
 
-def stage(info, xs, xs_at, weights, gate_w, share, sums=None, ahead_at=None):
+def unchanged(x):
+    return x
+
+
+def stage(info, xs, xs_at, weights, share, gate_w=None, sums=None, ahead_at=None, finishes=None, held=()):
     length = xs[0].shape[0]
     count = sum(c for _, _, c in xs_at)
-    shapes = [pltpu.VMEM((length, w.shape[1]), F32) for w in weights]
-    shapes.append(pltpu.VMEM((gate_w.shape[0], length), F32))
+    gated = int(gate_w is not None)
+    kinds = [F32] * len(weights) if finishes is None else [k for _, k in finishes]
+    calls = [unchanged] * len(weights) if finishes is None else [f for f, _ in finishes]
+    shapes = [pltpu.VMEM((length, w.shape[1]), k) for w, k in zip(weights, kinds)]
+    if gated:
+        shapes.append(pltpu.VMEM((gate_w.shape[0], length), F32))
     scratch = [pltpu.VMEM((count, w.shape[1]), BF) for w in weights]
-    scratch.append(pltpu.SemaphoreType.DMA((4, len(xs_at))))
+    scratch.append(pltpu.SemaphoreType.DMA((len(weights), len(xs_at))))
     if ahead_at:
         rows = sum(c for _, _, c in ahead_at)
         shapes += [pltpu.VMEM((rows, w.shape[1]), BF) for w in weights]
-        scratch.append(pltpu.SemaphoreType.DMA((4, len(ahead_at))))
-    operands = [info, *xs, *[in_hbm(w) for w in weights], gate_w]
-    specs = [SMEM_SPEC] + [VMEM_SPEC] * len(xs) + [HBM_SPEC] * 4 + [VMEM_SPEC]
+        scratch.append(pltpu.SemaphoreType.DMA((len(weights), len(ahead_at))))
+    operands = [*in_vmem(*held), info, *in_vmem(*xs), *[in_hbm(w) for w in weights]]
+    specs = [VMEM_SPEC] * len(held) + [SMEM_SPEC] + [VMEM_SPEC] * len(xs) + [HBM_SPEC] * len(weights)
+    if gated:
+        operands.append(gate_w)
+        specs.append(VMEM_SPEC)
     aliases = {}
     if sums is not None:
-        aliases = {len(operands) + i: i for i in range(5)}
-        operands += sums
-        specs += [VMEM_SPEC] * 5
+        if finishes is None:
+            aliases = {len(operands) + i: i for i in range(len(sums))}
+        operands += in_vmem(*sums)
+        specs += [VMEM_SPEC] * len(sums)
     return pl.pallas_call(
-        functools.partial(stage_kernel, xs_at, ahead_at, share, sums is not None),
+        holding(
+            functools.partial(
+                stage_kernel, xs_at, ahead_at, share, len(weights), sums is not None, calls, gated
+            ),
+            held,
+        ),
         out_shape=tuple(shapes),
         in_specs=specs,
         out_specs=(VMEM_SPEC,) * len(shapes),
@@ -171,43 +195,6 @@
         compiler_params=params(24),
         cost_estimate=cost(1e6, 1e5),
     )(*operands)
-
-
-def last_kernel(xs_count, *refs):
-    xs = refs[:xs_count]
-    query_w, gate_w, query_sum, gate_sum, query_out, gate_out = refs[xs_count:]
-    for w, total, out, finish in (
-        (query_w, query_sum, query_out, lambda x: x),
-        (gate_w, gate_sum, gate_out, jax.nn.sigmoid),
-    ):
-
-        def body(j, _, w=w, total=total, out=out, finish=finish):
-            columns = pl.ds(pl.multiple_of(j * 256, 256), 256)
-            low, value = 0, total[:, columns]
-            for x in xs:
-                count = x.shape[1]
-                value = value + jnp.dot(
-                    x[...], w[low : low + count, columns], preferred_element_type=F32
-                )
-                low += count
-            out[:, columns] = finish(value).astype(out.dtype)
-            return 0
-
-        lax.fori_loop(0, out.shape[1] // 256, body, 0)
-
-
-def last_stage(xs, query_w, gate_w, query_sum, gate_sum):
-    return pl.pallas_call(
-        functools.partial(last_kernel, len(xs)),
-        out_shape=(
-            pltpu.VMEM(query_sum.shape, BF),
-            pltpu.VMEM(gate_sum.shape, F32),
-        ),
-        in_specs=[VMEM_SPEC] * (len(xs) + 4),
-        out_specs=(VMEM_SPEC,) * 2,
-        compiler_params=params(12),
-        cost_estimate=cost(1e6, 1e5),
-    )(*xs, query_w, gate_w, query_sum, gate_sum)
 
 
 def segments(docs, positions):
@@ -306,7 +293,7 @@
         scratch_shapes=[pltpu.VMEM((size, wide), F32)],
         compiler_params=params(16),
         cost_estimate=cost(4e9, 4e6),
-    )(info, docs, bias, *xs, key_w, value_w, gate_w, key_sum, value_sum, gates)
+    )(info, docs, bias, *in_vmem(*xs, key_w, value_w), gate_w, *in_vmem(key_sum, value_sum, gates))
 
 
 def reset_of(docs, index, length):
@@ -346,15 +333,15 @@
         state_out[h] = state.astype(BF)
 
 
-def pair_summary(info, docs, small, small_other, kept, got, length):
+def pair_summary(info, docs, small, small_other, kept, got, length, held):
     return pl.pallas_call(
-        functools.partial(pair_kernel, length),
+        holding(functools.partial(pair_kernel, length), held),
         out_shape=(pltpu.VMEM(kept.shape, BF), pltpu.VMEM(small.shape, F32)),
-        in_specs=[SMEM_SPEC] * 2 + [VMEM_SPEC] * 4,
+        in_specs=[VMEM_SPEC] * len(held) + [SMEM_SPEC] * 2 + [VMEM_SPEC] * 4,
         out_specs=(VMEM_SPEC,) * 2,
         compiler_params=params(4),
         cost_estimate=cost(1e6, 1e5),
-    )(info, docs, small, small_other, kept, got)
+    )(*in_vmem(*held), info, docs, *in_vmem(small, small_other, kept, got))
 
 
 def incoming_kernel(length, reach, info, docs, own, other, kept, got, *refs):
@@ -363,7 +350,6 @@
     own_out, other_out, norm_out, top_out = refs[2 * reach + 3 :]
     heads = own.shape[0]
     size = own.shape[1] - 128
-    half = size // 2
     side = info[1]
     even = side == 0
     first = info[2] // length - side
@@ -398,11 +384,10 @@
     for k in range(reach):
         norm = norm + w_own[k] * smalls[k][:, :size]
     norm_out[...] = norm
-    rows = pl.ds(pl.multiple_of(side * half, half), half)
     for h in range(heads):
         at = slice(h, h + 1)
         here = jnp.where(even, kept[h].astype(F32), got[h].astype(F32))
-        base = carry[h, rows, :]
+        base = carry[h]
         mine = w_own[reach][at] * base + direct_own[at] * here
         theirs = w_other[reach][at] * base + direct_other[at] * here
         for k in range(reach):
@@ -413,25 +398,50 @@
         other_out[h] = theirs.astype(BF)
 
 
+def carry_kernel(info, carry, out, sem):
+    half = out.shape[1]
+    rows = pl.ds(pl.multiple_of(info[1] * half, half), half)
+    copy = pltpu.make_async_copy(carry.at[:, rows], out, sem)
+    copy.start()
+    copy.wait()
+
+
+def carry_half(info, carry, held):
+    heads, size, wide = carry.shape
+    return pl.pallas_call(
+        holding(carry_kernel, held),
+        out_shape=pltpu.VMEM((heads, size // 2, wide), F32),
+        in_specs=[VMEM_SPEC] * len(held) + [SMEM_SPEC, HBM_SPEC],
+        out_specs=VMEM_SPEC,
+        scratch_shapes=[pltpu.SemaphoreType.DMA],
+        compiler_params=params(4),
+        cost_estimate=cost(1e6, 1e5),
+    )(*in_vmem(*held), info, in_hbm(carry))
+
+
 def incoming_state(
-    info, docs, small, small_other, kept, got, smalls, states, carry, carry_norm, carry_max, length
+    info, docs, small, small_other, kept, got, smalls, states, carry, carry_norm, carry_max, length,
+    held,
 ):
     heads = small.shape[0]
     return pl.pallas_call(
-        functools.partial(incoming_kernel, length, len(smalls)),
+        holding(functools.partial(incoming_kernel, length, len(smalls)), held),
         out_shape=(
             pltpu.VMEM(kept.shape, BF),
             pltpu.VMEM(kept.shape, BF),
             pltpu.VMEM(carry_norm.shape, F32),
             pltpu.VMEM((heads, 128), F32),
         ),
-        in_specs=[SMEM_SPEC] * 2 + [VMEM_SPEC] * (7 + 2 * len(smalls)),
+        in_specs=[VMEM_SPEC] * len(held)
+        + [SMEM_SPEC] * 2
+        + [VMEM_SPEC] * (7 + 2 * len(smalls)),
         out_specs=(VMEM_SPEC,) * 4,
         compiler_params=params(6),
         cost_estimate=cost(1e6, 1e5),
     )(
-        info, docs, small, small_other, kept, got, *smalls, *states,
-        carry, carry_norm, carry_max[:, None],
+        *in_vmem(*held), info, docs,
+        *in_vmem(small, small_other, kept, got, *smalls, *states, carry),
+        carry_norm, carry_max[:, None],
     )
 
 
@@ -498,7 +508,7 @@
         scratch_shapes=[pltpu.SemaphoreType.DMA],
         compiler_params=params(12),
         cost_estimate=cost(1e6, 1e5),
-    )(info, docs, top, query, key, value, u, norm, gate, in_hbm(w_out))
+    )(info, docs, *in_vmem(top, query, key, value, u, norm, gate), in_hbm(w_out))
 
 
 def some_columns(info, hidden, w, send, keep, start):
@@ -542,7 +552,7 @@
         scratch_shapes=[pltpu.VMEM((2 * own.shape[1], own.shape[2]), BF)],
         compiler_params=params(12),
         cost_estimate=cost(3e9, 8e6),
-    )(info, query, own, other, base, slope, w_here)
+    )(info, *in_vmem(query, own, other, base, slope, w_here))
 
 
 def columns_kernel(start, info, hidden, w, send, keep):
@@ -558,7 +568,7 @@
         out_specs=(VMEM_SPEC,) * 2,
         compiler_params=params(12),
         cost_estimate=cost(1e6, 1e5),
-    )(info, hidden, w_here)
+    )(info, *in_vmem(hidden, w_here))
 
 
 def local(
@@ -599,39 +609,52 @@
 
     side = (block % 2).astype(jnp.int32)
     info = jnp.stack([place, side, offset]).astype(jnp.int32)
-    weights = (w_key, w_value, w_query, w_outgate)
     at = [[(o, s, c) for s, c, _ in group for o in (2, 3)] for group in groups]
     near_at = [(0, 0, share), (1, 0, share)]
-    sums = stage(info, [source, beside], near_at, weights, gate_w, share)
+    key_value, query_gate = (w_key, w_value), (w_query, w_outgate)
+    sums = stage(info, [source, beside], near_at, key_value, share, gate_w)
+    later = stage(info, [after(sums[0], source), beside], near_at, query_gate, share)
+    all_xs, all_at = [], []
     for i, group in enumerate(groups):
-        xs = lax.optimization_barrier((*[x for _, _, x in group], *sums))
-        xs, sums = xs[: len(group)], xs[len(group) :]
+        xs = lax.optimization_barrier((*[x for _, _, x in group], *sums, *later))
+        xs, sums, later = xs[: len(group)], xs[len(group) : -2], xs[-2:]
         xs = [y for x in xs for y in (x, tensor(x, 1))]
+        all_xs += xs
+        all_at += at[i]
         if i < len(groups) - 1:
-            *sums, w_key_last, w_value_last, w_query_last, w_gate_last = stage(
-                info, xs, at[i], weights, gate_w, share, sums, at[-1]
+            last = i == len(groups) - 2
+            out = stage(
+                info, xs, at[i], key_value, share, gate_w, sums, at[-1] if last else None
             )
+            sums = out[:3]
+            if last:
+                w_key_last, w_value_last = out[3:]
     keys, values, kept, sent, small, u = block_summary(
         info, doc_lengths, gate_bias, xs, at[-1], w_key_last, w_value_last, gate_w,
-        sums[0], sums[1], sums[4], share, heads,
+        sums[0], sums[1], sums[2], share, heads,
     )
 
     small_other = pair(small)
     got = pair(sent)
-    last_xs = after(keys, *xs)
-    queries, gate = last_stage(last_xs, w_query_last, w_gate_last, sums[2], sums[3])
+    queries, gate = stage(
+        info, after(keys, *all_xs), all_at, query_gate, share, None, later,
+        finishes=((unchanged, BF), (jax.nn.sigmoid, F32)), held=(keys, values, kept),
+    )
     small_other, got, queries = lax.optimization_barrier((small_other, got, queries))
     state_pair, travel = pair_summary(
-        info, doc_lengths, small, small_other, kept, got, length
+        info, doc_lengths, small, small_other, kept, got, length, (keys, values, queries, gate)
     )
     smalls, states = [], []
     for _ in range(blocks // 4):
         travel, state_pair = lax.optimization_barrier((down(travel), down(state_pair)))
         smalls.append(travel)
         states.append(state_pair)
+        if len(states) == 1:
+            held = (keys, values, queries, gate, kept, got)
+            carry = carry_half(after(travel, info), carry_matrix, held)
     state_own, state_other, norm_in, top_own = incoming_state(
         info, doc_lengths, small, small_other, kept, got, smalls, states,
-        carry_matrix, carry_norm, carry_max, length,
+        carry, carry_norm, carry_max, length, (keys, values, queries, gate),
     )
     state_got = pair(state_other)
     base, slope, w_here = inner(

time: 106 us -> 105 us (level)
  waiting for transfers between devices: 36.3 us -> 29.6 us
  Pallas kernels: 42.1 us -> 46.8 us
    ppermute x4, waiting for transfers between devices: 14.1 us -> 8.74 us  [shifted(): return lax.ppermute(x, axis, [(i, (i + by) % size) for i in range(size)])]
    pallas_call x5 -> x7, Pallas kernels: 24.1 us -> 28.9 us  [the longest x4 24.8 us: stage(): pl.pallas_call(holding(functools.partial(stage_kernel, xs_at, ahead_at, s...]
    ppermute x18, waiting for transfers between devices: 22.2 us -> 20.8 us  [swapped(): return lax.ppermute(x, axis, [(i, i ^ mask) for i in range(size)])]
    unnamed x32 -> x44, local copies, waits for them, and re-layouts: 5.82 us -> 6.44 us
  transfers between devices with their start and end apart: 22 -> 22, of which waited for: 12 -> 11; matrix products, arithmetic and copies ran while one was open for 2% -> 2% of each run, Pallas kernels for 32% -> 37%
where the time goes in v5:
time: 105 us
  Pallas kernels  46.8 us (45%)
  waiting for transfers between devices  29.6 us (28%)
  starting transfers between devices  19 us (18%)
  local copies, waits for them, and re-layouts  7.46 us (7%)
  other arithmetic  1.22 us (1%)
    pallas_call x4, Pallas kernels, stage(): pl.pallas_call(holding(functools.partial(stage_kernel, xs_at, ahead_at, s...  24.8 us
    ppermute x18, waiting for transfers between devices, swapped(): return lax.ppermute(x, axis, [(i, i ^ mask) for i in range(size)])  20.8 us
    ppermute x18, starting transfers between devices, swapped(): return lax.ppermute(x, axis, [(i, i ^ mask) for i in range(size)])  14.3 us
    ppermute x4, waiting for transfers between devices, shifted(): return lax.ppermute(x, axis, [(i, (i + by) % size) for i in range(size)])  8.74 us
    unnamed x44, local copies, waits for them, and re-layouts  6.44 us
    pallas_call x3, Pallas kernels, next_columns(): pl.pallas_call(functools.partial(columns_kernel, start), out_shape=(pltpu...  5.47 us
    ppermute x4, starting transfers between devices, shifted(): return lax.ppermute(x, axis, [(i, (i + by) % size) for i in range(size)])  4.7 us
    pallas_call x1, Pallas kernels, inner(): pl.pallas_call(functools.partial(inner_kernel, heads), out_shape=(pltpu.V...  4.19 us
  transfers between devices with their start and end apart: 22, of which 11 were waited for; matrix products, arithmetic and copies ran while one was open for 2% of the time, Pallas kernels for 37%

profile of v5, /device:TPU:0, one launch (start us, length us, event | category | flops | bytes accessed | tf_op | source)
XLA Modules:
  0.0 104.5 jit_solution(10040324383125441207)
XLA Ops:
  0.0 0.5 collective-permute-start.3
  0.5 2.5 %shard_map.118 = (bf16[512,256]{1,0:T(8,128)(2,1)}, bf16[512,256]{1,0:T(8,128)(2,1)S(1)}, bf16[512,512]{1,0:T(8,128)(2,1)}, bf16[512,1024]{1,0:T(8,128)(2,1)S(1)}) custom-call(bf16[512,1024]{1,0:T(8,128)(2,1)} %tokens.1), custom_call_target="tpu_custom_call" | custom-call | flops 1000000 | bytes 100000 | tf_op jit(solution)/shard_map/pallas_call | solution.py:70
  2.9 2.6 %collective-permute-start.1 = (bf16[512,256]{1,0:T(8,128)(2,1)}, bf16[512,256]{1,0:T(8,128)(2,1)S(1)}, u32[]{:S(2)}, u32[]{:S(2)}) collective-permute-start(bf16[512,256]{1,0:T(8,128)(2,1)} %get-tuple-element.77), channel_id=1, source_target_pairs={{0,2},{1,3},{2,0},{3,1},{4,6},{5,7},{6,4},{7,5},{8,10},{9,11},{10,... | collective-permute-start | bytes 786440 | tf_op jit(solution)/shard_map/ppermute | solution.py:27
  5.5 0.1 collective-permute-start.2
  5.6 1.9 %collective-permute-start = (bf16[512,512]{1,0:T(8,128)(2,1)}, bf16[512,512]{1,0:T(8,128)(2,1)S(1)}, u32[]{:S(2)}, u32[]{:S(2)}) collective-permute-start(bf16[512,512]{1,0:T(8,128)(2,1)} %get-tuple-element.76), channel_id=1, source_target_pairs={{0,2},{1,3},{2,0},{3,1},{4,6},{5,7},{6,4},{7,5},{8,10},{9,11},{10,... | collective-permute-start | bytes 1572872 | tf_op jit(solution)/shard_map/ppermute | solution.py:27
  7.6 0.8 reshape.3.refs_4_.refs_6_
  8.3 0.1 pad_add_fusion.info.refs_3_.refs_4_.refs_6_
  8.4 6.5 %shard_map.119 = (f32[512,512]{1,0:T(8,128)S(1)}, f32[512,1024]{1,0:T(8,128)S(1)}, f32[4,512]{1,0:T(4,128)S(1)}) custom-call(s32[3]{0:T(128)S(1)} %pad_add_fusion.info.refs_3_.refs_4_.refs_6_, bf16[512,1024]{1,0:T(8,128)(2,1)S(1)} %get-tuple-element.82.refs_0_, bf16[512,1024]{1,0:T(8,128)(2,1)S(1)} %collective-permute-done.3.refs_1_, ...), custom_call_target="tpu_custom_call" | custom-call | flops 1000000 | bytes 100000 | tf_op jit(solution)/shard_map/pallas_call | solution.py:183
  14.9 6.5 %shard_map.120 = (f32[512,512]{1,0:T(8,128)S(1)}, f32[512,1024]{1,0:T(8,128)S(1)}) custom-call(s32[3]{0:T(128)S(1)} %pad_add_fusion.info.refs_3_.refs_4_.refs_6_, bf16[512,1024]{1,0:T(8,128)(2,1)S(1)} %get-tuple-element.82.refs_0_, bf16[512,1024]{1,0:T(8,128)(2,1)S(1)} %collective-permute-done.3.refs_1_, bf16[4096,512]{1,0:T(8,128)(2,1)} %refs_10_.1, ...), custom_call_target="tpu_custom_call" | custom-call | flops 1000000 | bytes 100000 | tf_op jit(solution)/shard_map/pallas_call | solution.py:183
  21.5 0.1 collective-permute-start.4
  21.6 0.5 collective-permute-start.5
  22.1 1.0 collective-permute-done.4.refs_1_.refs_5_
  23.1 0.4 collective-permute-done.5.refs_3_.refs_7_
  23.5 5.2 %shard_map.121 = (f32[512,512]{1,0:T(8,128)S(1)}, f32[512,1024]{1,0:T(8,128)S(1)}, f32[4,512]{1,0:T(4,128)S(1)}, bf16[1024,512]{1,0:T(8,128)(2,1)S(1)}, bf16[1024,1024]{1,0:T(8,128)(2,1)S(1)}) custom-call(s32[3]{0:T(128)S(1)} %pad_add_fusion.info.refs_3_.refs_4_.refs_6_, ...), custom_call_target="tpu_custom_call", output_to_operand_aliasing={{0}: (8, {}), {1}: (9, {}), {2}: (10, {})} | custom-call | flops 1000000 | bytes 100000 | tf_op jit(solution)/shard_map/pallas_call | solution.py:183
  28.7 0.8 collective-permute-done.refs_0_.refs_8_
  29.6 1.9 %collective-permute-done.6.refs_1_.refs_9_ = bf16[512,512]{1,0:T(8,128)(2,1)S(1)} collective-permute-done((bf16[512,512]{1,0:T(8,128)(2,1)S(1)}, bf16[512,512]{1,0:T(8,128)(2,1)S(1)}, u32[]{:S(2)}, u32[]{:S(2)}) %collective-permute-start.6) | collective-permute-done | bytes 524320 | tf_op jit(solution)/shard_map/ppermute | solution.py:27
  31.5 3.7 %shard_map.122 = (bf16[512,512]{1,0:T(8,128)(2,1)S(1)}, bf16[512,1024]{1,0:T(8,128)(2,1)S(1)}, bf16[2,128,512]{2,1,0:T(8,128)(2,1)S(1)}, bf16[2,128,512]{2,1,0:T...) custom-call(s32[3]{0:T(128)S(1)} %pad_add_fusion.info.refs_3_.refs_4_.refs_6_, s32[4]{0:T(128)S(1)} %copy-done.17, ...), custom_call_target="tpu_custom_call" | custom-call | flops 4000000000 | bytes 4000000 | tf_op jit(solution)/shard_map/pallas_call | solution.py:281
  35.2 1.8 %collective-permute-start.8 = (bf16[2,128,512]{2,1,0:T(8,128)(2,1)S(1)}, bf16[2,128,512]{2,1,0:T(8,128)(2,1)S(1)}, u32[]{:S(2)}, u32[]{:S(2)}) collective-permute-start(bf16[2,128,512]{2,1,0:T(8,128)(2,1)S(1)} %get-tuple-element.102), channel_id=1, source_target_pairs={{0,4},{4,0},{8,12},{12,8},{16,20},{20,16},{24,28},{28,24},{1,5},{5... | collective-permute-start | bytes 786440 | tf_op jit(solution)/shard_map/ppermute | solution.py:27
  37.0 0.3 collective-permute-start.7
  37.3 1.0 copy-done.16
  38.4 6.6 %shard_map.123 = (bf16[512,512]{1,0:T(8,128)(2,1)S(1)}, f32[512,1024]{1,0:T(8,128)S(1)}) custom-call(bf16[512,512]{1,0:T(8,128)(2,1)S(1)} %get-tuple-element.103.refs_0_.key, bf16[512,1024]{1,0:T(8,128)(2,1)S(1)} %get-tuple-element.104.refs_1_.value, bf16[2,128,512]{2,1,0:T(8,128)(2,1)S(1)} %get-tuple-element.105.refs_2_.refs_8_.refs_4_, ...), custom_call_target="tpu_custom_call" | custom-call | flops 1000000 | bytes 100000 | tf_op jit(solution)/shard_map/pallas_call | solution.py:183
  45.0 0.8 shard_map.124
  45.8 0.0 copy-done.9
  45.8 1.8 %collective-permute-start.10 = (bf16[2,128,512]{2,1,0:T(8,128)(2,1)S(1)}, bf16[2,128,512]{2,1,0:T(8,128)(2,1)}, u32[]{:S(2)}, u32[]{:S(2)}) collective-permute-start(bf16[2,128,512]{2,1,0:T(8,128)(2,1)S(1)} %get-tuple-element.120), channel_id=1, source_target_pairs={{0,8},{4,12},{8,16},{12,20},{16,24},{20,28},{24,0},{28,4},{1,9},{5... | collective-permute-start | bytes 786440 | tf_op jit(solution)/shard_map/ppermute | solution.py:32
  47.7 1.6 %collective-permute-start.9 = (f32[2,384]{1,0:T(2,128)S(1)}, f32[2,384]{1,0:T(2,128)S(1)}, u32[]{:S(2)}, u32[]{:S(2)}) collective-permute-start(f32[2,384]{1,0:T(2,128)S(1)} %get-tuple-element.119), channel_id=1, source_target_pairs={{0,8},{4,12},{8,16},{12,20},{16,24},{20,28},{24,0},{28,4},{1,9},{5... | collective-permute-start | bytes 9224 | tf_op jit(solution)/shard_map/ppermute | solution.py:32
  49.2 6.6 %collective-permute-done.9.refs_10_ = f32[2,384]{1,0:T(2,128)S(1)} collective-permute-done((f32[2,384]{1,0:T(2,128)S(1)}, f32[2,384]{1,0:T(2,128)S(1)}, u32[]{:S(2)}, u32[]{:S(2)}) %collective-permute-start.9) | collective-permute-done | bytes 3104 | tf_op jit(solution)/shard_map/ppermute | solution.py:32
  55.9 1.3 %collective-permute-start.11 = (f32[2,384]{1,0:T(2,128)S(1)}, f32[2,384]{1,0:T(2,128)S(1)}, u32[]{:S(2)}, u32[]{:S(2)}) collective-permute-start(f32[2,384]{1,0:T(2,128)S(1)} %collective-permute-done.9.refs_10_), channel_id=1, source_target_pairs={{0,8},{4,12},{8,16},{12,20},{16,24},{20,28},{24,0},{28,4},{1,9},{5... | collective-permute-start | bytes 9224 | tf_op jit(solution)/shard_map/ppermute | solution.py:32
  57.2 0.1 copy.16.refs_16_
  57.3 1.2 %copy-done.1 = bf16[512,1024]{1,0:T(8,128)(2,1)S(1)} copy-done((bf16[512,1024]{1,0:T(8,128)(2,1)S(1)}, bf16[512,1024]{1,0:T(8,128)(2,1)}, u32[]{:S(2)}) %copy-start.1) | copy-done | bytes 1048600
  58.5 1.0 copy-done.4
  59.5 1.0 copy-done.7
  60.6 0.9 copy-done.10
  61.5 1.6 %shard_map.125.refs_14_ = f32[2,128,512]{2,1,0:T(8,128)S(1)} custom-call(bf16[512,512]{1,0:T(8,128)(2,1)S(1)} %copy-done.4, bf16[512,1024]{1,0:T(8,128)(2,1)S(1)} %copy-done.1, bf16[512,512]{1,0:T(8,128)(2,1)S(1)} %copy-done.7, f32[512,1024]{1,0:T(8,128)S(1)} %get-tuple-element.116.refs_3_.gate, ...), custom_call_target="tpu_custom_call" | custom-call | flops 1000000 | bytes 100000 | tf_op jit(solution)/shard_map/pallas_call | solution.py:411
  63.1 2.1 %collective-permute-done.11.refs_11_ = f32[2,384]{1,0:T(2,128)S(1)} collective-permute-done((f32[2,384]{1,0:T(2,128)S(1)}, f32[2,384]{1,0:T(2,128)S(1)}, u32[]{:S(2)}, u32[]{:S(2)}) %collective-permute-start.11) | collective-permute-done | bytes 3104 | tf_op jit(solution)/shard_map/ppermute | solution.py:32
  65.3 1.7 %shard_map.126 = (bf16[2,128,512]{2,1,0:T(8,128)(2,1)S(1)}, bf16[2,128,512]{2,1,0:T(8,128)(2,1)S(1)}, f32[2,256]{1,0:T(2,128)S(1)}, f32[2,128]{1,0:T(2,128)S(1)}) custom-call(bf16[512,512]{1,0:T(8,128)(2,1)S(1)} %copy-done.5, bf16[512,1024]{1,0:T(8,128)(2,1)S(1)} %copy-done.2, bf16[512,512]{1,0:T(8,128)(2,1)S(1)} %copy-done.7, ...), custom_call_target="tpu_custom_call" | custom-call | flops 1000000 | bytes 100000 | tf_op jit(solution)/shard_map/pallas_call | solution.py:427
  67.0 1.3 %collective-permute-start.13 = (bf16[2,128,512]{2,1,0:T(8,128)(2,1)S(1)}, bf16[2,128,512]{2,1,0:T(8,128)(2,1)S(1)}, u32[]{:S(2)}, u32[]{:S(2)}) collective-permute-start(bf16[2,128,512]{2,1,0:T(8,128)(2,1)S(1)} %get-tuple-element.127), channel_id=1, source_target_pairs={{0,4},{4,0},{8,12},{12,8},{16,20},{20,16},{24,28},{28,24},{1,5},{5... | collective-permute-start | bytes 786440 | tf_op jit(solution)/shard_map/ppermute | solution.py:27
  68.3 4.2 %shard_map.127 = (f32[512,1024]{1,0:T(8,128)S(1)}, f32[512,1024]{1,0:T(8,128)S(1)}, bf16[1024,4096]{1,0:T(8,128)(2,1)S(1)}) custom-call(s32[3]{0:T(128)S(1)} %pad_add_fusion.info.refs_3_.refs_4_.refs_6_, s32[4]{0:T(128)S(1)} %copy-done.17, f32[2,128]{1,0:T(2,128)S(1)} %get-tuple-element.128.top_in, bf16[512,512]{1,0:T(8,128)(2,1)S(1)} %copy-done.7, ...), custom_call_target="tpu_custom_call" | custom-call | flops 1000000 | bytes 100000 | tf_op jit(solution)/shard_map/pallas_call | solution.py:499
  72.5 0.9 collective-permute-done.13.other
  73.4 2.1 %shard_map.128 = (bf16[512,1024]{1,0:T(8,128)(2,1)S(1)}, bf16[512,512]{1,0:T(8,128)(2,1)S(1)}, bf16[512,512]{1,0:T(8,128)(2,1)S(1)}) custom-call(s32[3]{0:T(128)S(1)} %pad_add_fusion.info.refs_3_.refs_4_.refs_6_, bf16[512,512]{1,0:T(8,128)(2,1)S(1)} %copy-done.8, bf16[2,128,512]{2,1,0:T(8,128)(2,1)S(1)} %get-tuple-element.126.own, ...), custom_call_target="tpu_custom_call" | custom-call | flops 3000000000 | bytes 8000000 | tf_op jit(solution)/shard_map/pallas_call | solution.py:543
  75.5 0.1 collective-permute-start.14
  75.6 1.8 %shard_map.129 = (bf16[512,512]{1,0:T(8,128)(2,1)S(1)}, bf16[512,512]{1,0:T(8,128)(2,1)S(1)}) custom-call(s32[3]{0:T(128)S(1)} %pad_add_fusion.info.refs_3_.refs_4_.refs_6_, bf16[512,1024]{1,0:T(8,128)(2,1)S(1)} %get-tuple-element.142.hidden, bf16[1024,4096]{1,0:T(8,128)(2,1)S(1)} %get-tuple-element.133.w), custom_call_target="tpu_custom_call" | custom-call | flops 1000000 | bytes 100000 | tf_op jit(solution)/shard_map/pallas_call | solution.py:564
  77.5 0.6 collective-permute-start.16
  78.0 0.1 copy.20
  78.1 0.1 convert_add_fusion.3
  78.3 1.3 %collective-permute-start.15 = (bf16[512,256]{1,0:T(8,128)(2,1)S(1)}, bf16[512,256]{1,0:T(8,128)(2,1)S(1)}, u32[]{:S(2)}, u32[]{:S(2)}) collective-permute-start(bf16[512,256]{1,0:T(8,128)(2,1)S(1)} %slice.99), channel_id=1, source_target_pairs={{0,2},{1,3},{2,0},{3,1},{4,6},{5,7},{6,4},{7,5},{8,10},{9,11},{10,... | collective-permute-start | bytes 786440 | tf_op jit(solution)/shard_map/ppermute | solution.py:27
  79.6 1.8 %shard_map.130 = (bf16[512,512]{1,0:T(8,128)(2,1)S(1)}, bf16[512,512]{1,0:T(8,128)(2,1)S(1)}) custom-call(s32[3]{0:T(128)S(1)} %pad_add_fusion.info.refs_3_.refs_4_.refs_6_, bf16[512,1024]{1,0:T(8,128)(2,1)S(1)} %get-tuple-element.142.hidden, bf16[1024,4096]{1,0:T(8,128)(2,1)S(1)} %get-tuple-element.133.w), custom_call_target="tpu_custom_call" | custom-call | flops 1000000 | bytes 100000 | tf_op jit(solution)/shard_map/pallas_call | solution.py:564
  81.5 0.1 collective-permute-start.18
  81.6 0.1 convert_add_fusion.2
  81.8 0.8 collective-permute-start.17
  82.6 1.8 %shard_map.131 = (bf16[512,512]{1,0:T(8,128)(2,1)S(1)}, bf16[512,512]{1,0:T(8,128)(2,1)S(1)}) custom-call(s32[3]{0:T(128)S(1)} %pad_add_fusion.info.refs_3_.refs_4_.refs_6_, bf16[512,1024]{1,0:T(8,128)(2,1)S(1)} %get-tuple-element.142.hidden, bf16[1024,4096]{1,0:T(8,128)(2,1)S(1)} %get-tuple-element.133.w), custom_call_target="tpu_custom_call" | custom-call | flops 1000000 | bytes 100000 | tf_op jit(solution)/shard_map/pallas_call | solution.py:564
  84.4 0.3 collective-permute-start.20
  84.7 2.9 %collective-permute-done.15 = bf16[512,256]{1,0:T(8,128)(2,1)S(1)} collective-permute-done((bf16[512,256]{1,0:T(8,128)(2,1)S(1)}, bf16[512,256]{1,0:T(8,128)(2,1)S(1)}, u32[]{:S(2)}, u32[]{:S(2)}) %collective-permute-start.15) | collective-permute-done | bytes 262176 | tf_op jit(solution)/shard_map/ppermute | solution.py:27
  87.5 0.2 fusion.8
  87.7 0.1 convert_add_fusion.1
  87.9 1.3 %collective-permute-start.19 = (bf16[512,256]{1,0:T(8,128)(2,1)S(1)}, bf16[512,256]{1,0:T(8,128)(2,1)S(1)}, u32[]{:S(2)}, u32[]{:S(2)}) collective-permute-start(bf16[512,256]{1,0:T(8,128)(2,1)S(1)} %slice.97), channel_id=1, source_target_pairs={{0,2},{1,3},{2,0},{3,1},{4,6},{5,7},{6,4},{7,5},{8,10},{9,11},{10,... | collective-permute-start | bytes 786440 | tf_op jit(solution)/shard_map/ppermute | solution.py:27
  89.3 0.1 convert_add_fusion
  89.5 0.8 collective-permute-start.21
  90.3 2.9 %collective-permute-done.17 = bf16[512,256]{1,0:T(8,128)(2,1)S(1)} collective-permute-done((bf16[512,256]{1,0:T(8,128)(2,1)S(1)}, bf16[512,256]{1,0:T(8,128)(2,1)S(1)}, u32[]{:S(2)}, u32[]{:S(2)}) %collective-permute-start.17) | collective-permute-done | bytes 262176 | tf_op jit(solution)/shard_map/ppermute | solution.py:27
  93.2 0.1 fusion.9
  93.3 5.5 %collective-permute-done.19 = bf16[512,256]{1,0:T(8,128)(2,1)S(1)} collective-permute-done((bf16[512,256]{1,0:T(8,128)(2,1)S(1)}, bf16[512,256]{1,0:T(8,128)(2,1)S(1)}, u32[]{:S(2)}, u32[]{:S(2)}) %collective-permute-start.19) | collective-permute-done | bytes 262176 | tf_op jit(solution)/shard_map/ppermute | solution.py:27
  98.8 0.1 fusion.10
  98.9 4.6 %collective-permute-done.21 = bf16[512,256]{1,0:T(8,128)(2,1)S(1)} collective-permute-done((bf16[512,256]{1,0:T(8,128)(2,1)S(1)}, bf16[512,256]{1,0:T(8,128)(2,1)S(1)}, u32[]{:S(2)}, u32[]{:S(2)}) %collective-permute-start.21) | collective-permute-done | bytes 262176 | tf_op jit(solution)/shard_map/ppermute | solution.py:27
  103.4 0.1 fusion.11
  103.6 1.0 copy.24
  (53 shorter events, 0.3 us)
Async XLA Ops:
  0.0 8.4 %collective-permute-start.3 = (bf16[512,1024]{1,0:T(8,128)(2,1)}, bf16[512,1024]{1,0:T(8,128)(2,1)S(1)}, u32[]{:S(2)}, u32[]{:S(2)}) collective-permute-start(bf16[512,1024]{1,0:T(8,128)(2,1)} %tokens.1), channel_id=1, source_target_pairs={{0,1},{1,0},{2,3},{3,2},{4,5},{5,4},{6,7},{7,6},{8,9},{9,8},{10,11... | collective-permute-start | bytes 3145736 | tf_op jit(solution)/shard_map/ppermute | solution.py:27
  2.9 18.5 %collective-permute-start.1 = (bf16[512,256]{1,0:T(8,128)(2,1)}, bf16[512,256]{1,0:T(8,128)(2,1)S(1)}, u32[]{:S(2)}, u32[]{:S(2)}) collective-permute-start(bf16[512,256]{1,0:T(8,128)(2,1)} %get-tuple-element.77), channel_id=1, source_target_pairs={{0,2},{1,3},{2,0},{3,1},{4,6},{5,7},{6,4},{7,5},{8,10},{9,11},{10,... | collective-permute-start | bytes 786440 | tf_op jit(solution)/shard_map/ppermute | solution.py:27
  5.5 16.0 %collective-permute-start.2 = (bf16[512,256]{1,0:T(8,128)(2,1)S(1)}, bf16[512,256]{1,0:T(8,128)(2,1)S(1)}, u32[]{:S(2)}, u32[]{:S(2)}) collective-permute-start(bf16[512,256]{1,0:T(8,128)(2,1)S(1)} %get-tuple-element.78), channel_id=1, source_target_pairs={{0,2},{1,3},{2,0},{3,1},{4,6},{5,7},{6,4},{7,5},{8,10},{9,11},{10,... | collective-permute-start | bytes 786440 | tf_op jit(solution)/shard_map/ppermute | solution.py:27
  5.6 24.0 %collective-permute-start = (bf16[512,512]{1,0:T(8,128)(2,1)}, bf16[512,512]{1,0:T(8,128)(2,1)S(1)}, u32[]{:S(2)}, u32[]{:S(2)}) collective-permute-start(bf16[512,512]{1,0:T(8,128)(2,1)} %get-tuple-element.76), channel_id=1, source_target_pairs={{0,2},{1,3},{2,0},{3,1},{4,6},{5,7},{6,4},{7,5},{8,10},{9,11},{10,... | collective-permute-start | bytes 1572872 | tf_op jit(solution)/shard_map/ppermute | solution.py:27
  21.5 7.2 %copy-start.11 = (bf16[512,256]{1,0:T(8,128)(2,1)}, bf16[512,256]{1,0:T(8,128)(2,1)S(1)}, u32[]{:S(2)}) copy-start(bf16[512,256]{1,0:T(8,128)(2,1)S(1)} %collective-permute-done.1.refs_0_.refs_4_) | copy-start | bytes 786436
  21.5 7.2 %copy-start.13 = (bf16[512,256]{1,0:T(8,128)(2,1)}, bf16[512,256]{1,0:T(8,128)(2,1)S(1)}, u32[]{:S(2)}) copy-start(bf16[512,256]{1,0:T(8,128)(2,1)S(1)} %collective-permute-done.2.refs_2_.refs_6_) | copy-start | bytes 786436
  21.5 10.0 %copy-start.17 = (s32[4]{0:T(128)S(1)}, s32[4]{0:T(128)}, u32[]{:S(2)}) copy-start(s32[4]{0:T(128)} %docs.3) | copy-start | bytes 52
  21.5 10.0 %copy-start.19 = (f32[2,2]{1,0:T(2,128)S(1)}, f32[2,2]{1,0:T(2,128)}, u32[]{:S(2)}) copy-start(f32[2,2]{1,0:T(2,128)} %bias.1) | copy-start | bytes 52
  21.5 1.6 %collective-permute-start.4 = (bf16[512,256]{1,0:T(8,128)(2,1)S(1)}, bf16[512,256]{1,0:T(8,128)(2,1)S(1)}, u32[]{:S(2)}, u32[]{:S(2)}) collective-permute-start(bf16[512,256]{1,0:T(8,128)(2,1)S(1)} %collective-permute-done.1.refs_0_.refs_4_), channel_id=1, source_target_pairs={{0,1},{1,0},{2,3},{3,2},{4,5},{5,4},{6,7},{7,6},{8,9},{9,8},{10,11... | collective-permute-start | bytes 786440 | tf_op jit(solution)/shard_map/ppermute | solution.py:27
  21.6 1.9 %collective-permute-start.5 = (bf16[512,256]{1,0:T(8,128)(2,1)S(1)}, bf16[512,256]{1,0:T(8,128)(2,1)S(1)}, u32[]{:S(2)}, u32[]{:S(2)}) collective-permute-start(bf16[512,256]{1,0:T(8,128)(2,1)S(1)} %collective-permute-done.2.refs_2_.refs_6_), channel_id=1, source_target_pairs={{0,1},{1,0},{2,3},{3,2},{4,5},{5,4},{6,7},{7,6},{8,9},{9,8},{10,11... | collective-permute-start | bytes 786440 | tf_op jit(solution)/shard_map/ppermute | solution.py:27
  29.6 5.6 %copy-start.15 = (bf16[512,512]{1,0:T(8,128)(2,1)}, bf16[512,512]{1,0:T(8,128)(2,1)S(1)}, u32[]{:S(2)}) copy-start(bf16[512,512]{1,0:T(8,128)(2,1)S(1)} %collective-permute-done.refs_0_.refs_8_) | copy-start | bytes 1572868
  29.6 1.9 %collective-permute-start.6 = (bf16[512,512]{1,0:T(8,128)(2,1)S(1)}, bf16[512,512]{1,0:T(8,128)(2,1)S(1)}, u32[]{:S(2)}, u32[]{:S(2)}) collective-permute-start(bf16[512,512]{1,0:T(8,128)(2,1)S(1)} %collective-permute-done.refs_0_.refs_8_), channel_id=1, source_target_pairs={{0,1},{1,0},{2,3},{3,2},{4,5},{5,4},{6,7},{7,6},{8,9},{9,8},{10,11... | collective-permute-start | bytes 1572872 | tf_op jit(solution)/shard_map/ppermute | solution.py:27
  31.5 5.8 %copy-start.12 = (bf16[512,256]{1,0:T(8,128)(2,1)S(1)}, bf16[512,256]{1,0:T(8,128)(2,1)}, u32[]{:S(2)}) copy-start(bf16[512,256]{1,0:T(8,128)(2,1)} %copy-done.11) | copy-start | bytes 786436
  31.5 5.8 %copy-start.14 = (bf16[512,256]{1,0:T(8,128)(2,1)S(1)}, bf16[512,256]{1,0:T(8,128)(2,1)}, u32[]{:S(2)}) copy-start(bf16[512,256]{1,0:T(8,128)(2,1)} %copy-done.13) | copy-start | bytes 786436
  35.2 9.8 %copy-start = (bf16[512,1024]{1,0:T(8,128)(2,1)}, bf16[512,1024]{1,0:T(8,128)(2,1)S(1)}, u32[]{:S(2)}) copy-start(bf16[512,1024]{1,0:T(8,128)(2,1)S(1)} %get-tuple-element.104.refs_1_.value) | copy-start | bytes 3145732
  35.2 9.8 %copy-start.3 = (bf16[512,512]{1,0:T(8,128)(2,1)}, bf16[512,512]{1,0:T(8,128)(2,1)S(1)}, u32[]{:S(2)}) copy-start(bf16[512,512]{1,0:T(8,128)(2,1)S(1)} %get-tuple-element.103.refs_0_.key) | copy-start | bytes 1572868
  35.2 9.7 %collective-permute-start.8 = (bf16[2,128,512]{2,1,0:T(8,128)(2,1)S(1)}, bf16[2,128,512]{2,1,0:T(8,128)(2,1)S(1)}, u32[]{:S(2)}, u32[]{:S(2)}) collective-permute-start(bf16[2,128,512]{2,1,0:T(8,128)(2,1)S(1)} %get-tuple-element.102), channel_id=1, source_target_pairs={{0,4},{4,0},{8,12},{12,8},{16,20},{20,16},{24,28},{28,24},{1,5},{5... | collective-permute-start | bytes 786440 | tf_op jit(solution)/shard_map/ppermute | solution.py:27
  37.0 8.0 %collective-permute-start.7 = (f32[2,384]{1,0:T(2,128)S(1)}, f32[2,384]{1,0:T(2,128)S(1)}, u32[]{:S(2)}, u32[]{:S(2)}) collective-permute-start(f32[2,384]{1,0:T(2,128)S(1)} %get-tuple-element.101.refs_6_), channel_id=1, source_target_pairs={{0,4},{4,0},{8,12},{12,8},{16,20},{20,16},{24,28},{28,24},{1,5},{5... | collective-permute-start | bytes 9224 | tf_op jit(solution)/shard_map/ppermute | solution.py:27
  37.3 1.0 copy-start.16
  44.9 0.9 copy-start.6
  45.0 0.9 copy-start.9
  45.0 12.2 %copy-start.20 = (f32[2]{0:T(128)S(1)}, f32[2]{0:T(128)}, u32[]{:S(2)}) copy-start(f32[2]{0:T(128)} %param.22) | copy-start | bytes 28
  45.8 10.0 %collective-permute-start.10 = (bf16[2,128,512]{2,1,0:T(8,128)(2,1)S(1)}, bf16[2,128,512]{2,1,0:T(8,128)(2,1)}, u32[]{:S(2)}, u32[]{:S(2)}) collective-permute-start(bf16[2,128,512]{2,1,0:T(8,128)(2,1)S(1)} %get-tuple-element.120), channel_id=1, source_target_pairs={{0,8},{4,12},{8,16},{12,20},{16,24},{20,28},{24,0},{28,4},{1,9},{5... | collective-permute-start | bytes 786440 | tf_op jit(solution)/shard_map/ppermute | solution.py:32
  47.7 8.2 %collective-permute-start.9 = (f32[2,384]{1,0:T(2,128)S(1)}, f32[2,384]{1,0:T(2,128)S(1)}, u32[]{:S(2)}, u32[]{:S(2)}) collective-permute-start(f32[2,384]{1,0:T(2,128)S(1)} %get-tuple-element.119), channel_id=1, source_target_pairs={{0,8},{4,12},{8,16},{12,20},{16,24},{20,28},{24,0},{28,4},{1,9},{5... | collective-permute-start | bytes 9224 | tf_op jit(solution)/shard_map/ppermute | solution.py:32
  55.9 9.4 %collective-permute-start.12 = (bf16[2,128,512]{2,1,0:T(8,128)(2,1)}, bf16[2,128,512]{2,1,0:T(8,128)(2,1)}, u32[]{:S(2)}, u32[]{:S(2)}) collective-permute-start(bf16[2,128,512]{2,1,0:T(8,128)(2,1)} %collective-permute-done.10.refs_12_), channel_id=1, source_target_pairs={{0,8},{4,12},{8,16},{12,20},{16,24},{20,28},{24,0},{28,4},{1,9},{5... | collective-permute-start | bytes 786440 | tf_op jit(solution)/shard_map/ppermute | solution.py:32
  55.9 9.4 %collective-permute-start.11 = (f32[2,384]{1,0:T(2,128)S(1)}, f32[2,384]{1,0:T(2,128)S(1)}, u32[]{:S(2)}, u32[]{:S(2)}) collective-permute-start(f32[2,384]{1,0:T(2,128)S(1)} %collective-permute-done.9.refs_10_), channel_id=1, source_target_pairs={{0,8},{4,12},{8,16},{12,20},{16,24},{20,28},{24,0},{28,4},{1,9},{5... | collective-permute-start | bytes 9224 | tf_op jit(solution)/shard_map/ppermute | solution.py:32
  57.3 1.2 %copy-start.1 = (bf16[512,1024]{1,0:T(8,128)(2,1)S(1)}, bf16[512,1024]{1,0:T(8,128)(2,1)}, u32[]{:S(2)}) copy-start(bf16[512,1024]{1,0:T(8,128)(2,1)} %copy-done) | copy-start | bytes 3145732
  58.5 1.0 copy-start.4
  59.5 1.0 copy-start.7
  60.6 0.9 copy-start.10
  61.5 3.7 %copy-start.2 = (bf16[512,1024]{1,0:T(8,128)(2,1)S(1)}, bf16[512,1024]{1,0:T(8,128)(2,1)}, u32[]{:S(2)}) copy-start(bf16[512,1024]{1,0:T(8,128)(2,1)} %copy-done) | copy-start | bytes 3145732
  61.5 3.7 %copy-start.5 = (bf16[512,512]{1,0:T(8,128)(2,1)S(1)}, bf16[512,512]{1,0:T(8,128)(2,1)}, u32[]{:S(2)}) copy-start(bf16[512,512]{1,0:T(8,128)(2,1)} %copy-done.3) | copy-start | bytes 1572868
  61.5 3.7 %copy-start.18 = (f32[2,256]{1,0:T(2,128)S(1)}, f32[2,256]{1,0:T(2,128)}, u32[]{:S(2)}) copy-start(f32[2,256]{1,0:T(2,128)} %refs_15_.1) | copy-start | bytes 6148
  67.0 6.4 %collective-permute-start.13 = (bf16[2,128,512]{2,1,0:T(8,128)(2,1)S(1)}, bf16[2,128,512]{2,1,0:T(8,128)(2,1)S(1)}, u32[]{:S(2)}, u32[]{:S(2)}) collective-permute-start(bf16[2,128,512]{2,1,0:T(8,128)(2,1)S(1)} %get-tuple-element.127), channel_id=1, source_target_pairs={{0,4},{4,0},{8,12},{12,8},{16,20},{20,16},{24,28},{28,24},{1,5},{5... | collective-permute-start | bytes 786440 | tf_op jit(solution)/shard_map/ppermute | solution.py:27
  68.3 5.1 %copy-start.8 = (bf16[512,512]{1,0:T(8,128)(2,1)S(1)}, bf16[512,512]{1,0:T(8,128)(2,1)}, u32[]{:S(2)}) copy-start(bf16[512,512]{1,0:T(8,128)(2,1)} %copy-done.6) | copy-start | bytes 1572868
  75.5 2.6 %collective-permute-start.14 = (bf16[512,512]{1,0:T(8,128)(2,1)S(1)}, bf16[512,512]{1,0:T(8,128)(2,1)S(1)}, u32[]{:S(2)}, u32[]{:S(2)}) collective-permute-start(bf16[512,512]{1,0:T(8,128)(2,1)S(1)} %get-tuple-element.135), channel_id=1, source_target_pairs={{0,1},{1,0},{2,3},{3,2},{4,5},{5,4},{6,7},{7,6},{8,9},{9,8},{10,11... | collective-permute-start | bytes 1572872 | tf_op jit(solution)/shard_map/ppermute | solution.py:27
  77.5 4.1 %collective-permute-start.16 = (bf16[512,512]{1,0:T(8,128)(2,1)S(1)}, bf16[512,512]{1,0:T(8,128)(2,1)S(1)}, u32[]{:S(2)}, u32[]{:S(2)}) collective-permute-start(bf16[512,512]{1,0:T(8,128)(2,1)S(1)} %get-tuple-element.138), channel_id=1, source_target_pairs={{0,1},{1,0},{2,3},{3,2},{4,5},{5,4},{6,7},{7,6},{8,9},{9,8},{10,11... | collective-permute-start | bytes 1572872 | tf_op jit(solution)/shard_map/ppermute | solution.py:27
  78.3 9.2 %collective-permute-start.15 = (bf16[512,256]{1,0:T(8,128)(2,1)S(1)}, bf16[512,256]{1,0:T(8,128)(2,1)S(1)}, u32[]{:S(2)}, u32[]{:S(2)}) collective-permute-start(bf16[512,256]{1,0:T(8,128)(2,1)S(1)} %slice.99), channel_id=1, source_target_pairs={{0,2},{1,3},{2,0},{3,1},{4,6},{5,7},{6,4},{7,5},{8,10},{9,11},{10,... | collective-permute-start | bytes 786440 | tf_op jit(solution)/shard_map/ppermute | solution.py:27
  81.5 6.3 %collective-permute-start.18 = (bf16[512,512]{1,0:T(8,128)(2,1)S(1)}, bf16[512,512]{1,0:T(8,128)(2,1)S(1)}, u32[]{:S(2)}, u32[]{:S(2)}) collective-permute-start(bf16[512,512]{1,0:T(8,128)(2,1)S(1)} %get-tuple-element.141), channel_id=1, source_target_pairs={{0,1},{1,0},{2,3},{3,2},{4,5},{5,4},{6,7},{7,6},{8,9},{9,8},{10,11... | collective-permute-start | bytes 1572872 | tf_op jit(solution)/shard_map/ppermute | solution.py:27
  81.8 11.4 %collective-permute-start.17 = (bf16[512,256]{1,0:T(8,128)(2,1)S(1)}, bf16[512,256]{1,0:T(8,128)(2,1)S(1)}, u32[]{:S(2)}, u32[]{:S(2)}) collective-permute-start(bf16[512,256]{1,0:T(8,128)(2,1)S(1)} %slice.98), channel_id=1, source_target_pairs={{0,2},{1,3},{2,0},{3,1},{4,6},{5,7},{6,4},{7,5},{8,10},{9,11},{10,... | collective-permute-start | bytes 786440 | tf_op jit(solution)/shard_map/ppermute | solution.py:27
  84.4 4.9 %collective-permute-start.20 = (bf16[512,512]{1,0:T(8,128)(2,1)S(1)}, bf16[512,512]{1,0:T(8,128)(2,1)S(1)}, u32[]{:S(2)}, u32[]{:S(2)}) collective-permute-start(bf16[512,512]{1,0:T(8,128)(2,1)S(1)} %get-tuple-element.144), channel_id=1, source_target_pairs={{0,1},{1,0},{2,3},{3,2},{4,5},{5,4},{6,7},{7,6},{8,9},{9,8},{10,11... | collective-permute-start | bytes 1572872 | tf_op jit(solution)/shard_map/ppermute | solution.py:27
  87.9 10.8 %collective-permute-start.19 = (bf16[512,256]{1,0:T(8,128)(2,1)S(1)}, bf16[512,256]{1,0:T(8,128)(2,1)S(1)}, u32[]{:S(2)}, u32[]{:S(2)}) collective-permute-start(bf16[512,256]{1,0:T(8,128)(2,1)S(1)} %slice.97), channel_id=1, source_target_pairs={{0,2},{1,3},{2,0},{3,1},{4,6},{5,7},{6,4},{7,5},{8,10},{9,11},{10,... | collective-permute-start | bytes 786440 | tf_op jit(solution)/shard_map/ppermute | solution.py:27
  89.5 14.0 %collective-permute-start.21 = (bf16[512,256]{1,0:T(8,128)(2,1)S(1)}, bf16[512,256]{1,0:T(8,128)(2,1)S(1)}, u32[]{:S(2)}, u32[]{:S(2)}) collective-permute-start(bf16[512,256]{1,0:T(8,128)(2,1)S(1)} %slice.96), channel_id=1, source_target_pairs={{0,2},{1,3},{2,0},{3,1},{4,6},{5,7},{6,4},{7,5},{8,10},{9,11},{10,... | collective-permute-start | bytes 786440 | tf_op jit(solution)/shard_map/ppermute | solution.py:27

commit v6 on v5

--- a/solution.py
+++ b/solution.py
@@ -599,7 +599,8 @@
     beside = tensor(tokens, 1)
     sizes = [c for chunks in TOKEN_CHUNKS for c in chunks]
     starts = [sum(sizes[:i]) for i in range(len(sizes))]
-    *pieces, source = split_tokens(tokens, starts + [0], sizes + [share])
+    pieces = split_tokens(tokens, starts, sizes)
+    source = tokens
     pieces = [(s, c, tensor(x, 2)) for s, c, x in zip(starts, sizes, pieces)]
     groups = []
     for chunks in TOKEN_CHUNKS:
@@ -613,14 +614,12 @@
     near_at = [(0, 0, share), (1, 0, share)]
     key_value, query_gate = (w_key, w_value), (w_query, w_outgate)
     sums = stage(info, [source, beside], near_at, key_value, share, gate_w)
-    later = stage(info, [after(sums[0], source), beside], near_at, query_gate, share)
-    all_xs, all_at = [], []
+    far = []
     for i, group in enumerate(groups):
-        xs = lax.optimization_barrier((*[x for _, _, x in group], *sums, *later))
-        xs, sums, later = xs[: len(group)], xs[len(group) : -2], xs[-2:]
+        xs = lax.optimization_barrier((*[x for _, _, x in group], *sums))
+        xs, sums = xs[: len(group)], xs[len(group) :]
         xs = [y for x in xs for y in (x, tensor(x, 1))]
-        all_xs += xs
-        all_at += at[i]
+        far.append(xs)
         if i < len(groups) - 1:
             last = i == len(groups) - 2
             out = stage(
@@ -636,22 +635,31 @@
 
     small_other = pair(small)
     got = pair(sent)
-    queries, gate = stage(
-        info, after(keys, *all_xs), all_at, query_gate, share, None, later,
-        finishes=((unchanged, BF), (jax.nn.sigmoid, F32)), held=(keys, values, kept),
-    )
-    small_other, got, queries = lax.optimization_barrier((small_other, got, queries))
+    held = (keys, values, kept)
+    later_xs = after(keys, *[x for xs in far[1:] for x in xs])
+    later = stage(info, later_xs, sum(at[1:], []), query_gate, share, held=held)
+    small_other, got, *later = lax.optimization_barrier((small_other, got, *later))
     state_pair, travel = pair_summary(
-        info, doc_lengths, small, small_other, kept, got, length, (keys, values, queries, gate)
+        info, doc_lengths, small, small_other, kept, got, length, (keys, values)
     )
     smalls, states = [], []
-    for _ in range(blocks // 4):
-        travel, state_pair = lax.optimization_barrier((down(travel), down(state_pair)))
+    held = (keys, values, kept, got)
+    for step in range(blocks // 4):
+        before = state_pair
+        travel, state_pair = down(travel), down(state_pair)
+        if step == 0:
+            near_xs = after(before, source, beside)
+            later = stage(info, near_xs, near_at, query_gate, share, None, later, held=held)
+        elif step == 1:
+            last_xs = after(before, *far[0])
+            queries, gate = stage(
+                info, last_xs, at[0], query_gate, share, None, later,
+                finishes=((unchanged, BF), (jax.nn.sigmoid, F32)), held=held,
+            )
+            carry = carry_half(after(queries, info), carry_matrix, held)
+        travel, state_pair, *later = lax.optimization_barrier((travel, state_pair, *later))
         smalls.append(travel)
         states.append(state_pair)
-        if len(states) == 1:
-            held = (keys, values, queries, gate, kept, got)
-            carry = carry_half(after(travel, info), carry_matrix, held)
     state_own, state_other, norm_in, top_own = incoming_state(
         info, doc_lengths, small, small_other, kept, got, smalls, states,
         carry, carry_norm, carry_max, length, (keys, values, queries, gate),
@@ -843,7 +851,7 @@
 
 
 def solution(mesh):
-    fast = mesh.shape["tensor"] == 4 and mesh.shape["seq"] % 4 == 0
+    fast = mesh.shape["tensor"] == 4 and mesh.shape["seq"] == 8
     return jax.shard_map(
         local if fast else plain_local,
         mesh=mesh,

time: 105 us -> 109 us (1.038)
  local copies, waits for them, and re-layouts: 7.46 us -> 10.3 us
  waiting for transfers between devices: 29.6 us -> 28 us
  Pallas kernels: 46.8 us -> 48.2 us
    ppermute x4, waiting for transfers between devices: 8.74 us -> 0.01 us  [shifted(): return lax.ppermute(x, axis, [(i, (i + by) % size) for i in range(size)])]
    ppermute x18, waiting for transfers between devices: 20.8 us -> 28 us  [swapped(): return lax.ppermute(x, axis, [(i, i ^ mask) for i in range(size)])]
    unnamed x44 -> x39, local copies, waits for them, and re-layouts: 6.44 us -> 9.32 us
    pallas_call x4 -> x5, Pallas kernels: 24.8 us -> 27.3 us  [stage(): pl.pallas_call(holding(functools.partial(stage_kernel, xs_at, ahead_at, s...]
    pallas_call x1, Pallas kernels: 2.48 us -> 1.24 us  [split_tokens(): pl.pallas_call(functools.partial(split_kernel, starts), out_shape=tuple((...]
where the time goes in v6:
time: 109 us
  Pallas kernels  48.2 us (44%)
  waiting for transfers between devices  28 us (26%)
  starting transfers between devices  19.8 us (18%)
  local copies, waits for them, and re-layouts  10.3 us (9%)
  other arithmetic  1.86 us (2%)
    ppermute x18, waiting for transfers between devices, swapped(): return lax.ppermute(x, axis, [(i, i ^ mask) for i in range(size)])  28 us
    pallas_call x5, Pallas kernels, stage(): pl.pallas_call(holding(functools.partial(stage_kernel, xs_at, ahead_at, s...  27.3 us
    ppermute x18, starting transfers between devices, swapped(): return lax.ppermute(x, axis, [(i, i ^ mask) for i in range(size)])  14.5 us
    unnamed x39, local copies, waits for them, and re-layouts  9.32 us
    pallas_call x3, Pallas kernels, next_columns(): pl.pallas_call(functools.partial(columns_kernel, start), out_shape=(pltpu...  5.47 us
    ppermute x4, starting transfers between devices, shifted(): return lax.ppermute(x, axis, [(i, (i + by) % size) for i in range(size)])  5.24 us
    pallas_call x1, Pallas kernels, inner(): pl.pallas_call(functools.partial(inner_kernel, heads), out_shape=(pltpu.V...  4.19 us
    pallas_call x1, Pallas kernels, block_summary(): pl.pallas_call(functools.partial(summary_kernel, xs_at, share, heads), ou...  3.69 us
  transfers between devices with their start and end apart: 22, of which 11 were waited for; matrix products, arithmetic and copies ran while one was open for 2% of the time, Pallas kernels for 37%

profile of v6, /device:TPU:0, one launch (start us, length us, event | category | flops | bytes accessed | tf_op | source)
XLA Modules:
  0.0 108.5 jit_solution(7766621718597258854)
XLA Ops:
  0.0 0.5 collective-permute-start.3
  0.5 1.2 %shard_map.118 = (bf16[512,256]{1,0:T(8,128)(2,1)S(1)}, bf16[512,256]{1,0:T(8,128)(2,1)S(1)}, bf16[512,512]{1,0:T(8,128)(2,1)S(1)}) custom-call(bf16[512,1024]{1,0:T(8,128)(2,1)} %refs_5_.4), custom_call_target="tpu_custom_call" | custom-call | flops 1000000 | bytes 100000 | tf_op jit(solution)/shard_map/pallas_call | solution.py:70
  1.7 2.6 %collective-permute-start.1 = (bf16[512,256]{1,0:T(8,128)(2,1)S(1)}, bf16[512,256]{1,0:T(8,128)(2,1)S(1)}, u32[]{:S(2)}, u32[]{:S(2)}) collective-permute-start(bf16[512,256]{1,0:T(8,128)(2,1)S(1)} %get-tuple-element.77), channel_id=1, source_target_pairs={{0,2},{1,3},{2,0},{3,1},{4,6},{5,7},{6,4},{7,5},{8,10},{9,11},{10,... | collective-permute-start | bytes 786440 | tf_op jit(solution)/shard_map/ppermute | solution.py:27
  4.3 0.1 collective-permute-start.2
  4.4 1.9 %collective-permute-start = (bf16[512,512]{1,0:T(8,128)(2,1)S(1)}, bf16[512,512]{1,0:T(8,128)(2,1)S(1)}, u32[]{:S(2)}, u32[]{:S(2)}) collective-permute-start(bf16[512,512]{1,0:T(8,128)(2,1)S(1)} %get-tuple-element.76), channel_id=1, source_target_pairs={{0,2},{1,3},{2,0},{3,1},{4,6},{5,7},{6,4},{7,5},{8,10},{9,11},{10,... | collective-permute-start | bytes 1572872 | tf_op jit(solution)/shard_map/ppermute | solution.py:27
  6.3 0.8 reshape.3.refs_4_.refs_6_
  7.1 0.1 pad_add_fusion.info.refs_3_.refs_2_.refs_4_
  7.2 1.2 %copy-done = bf16[512,1024]{1,0:T(8,128)(2,1)S(1)} copy-done((bf16[512,1024]{1,0:T(8,128)(2,1)S(1)}, bf16[512,1024]{1,0:T(8,128)(2,1)}, u32[]{:S(2)}) %copy-start) | copy-done | bytes 1048600
  8.4 6.5 %shard_map.119 = (f32[512,512]{1,0:T(8,128)S(1)}, f32[512,1024]{1,0:T(8,128)S(1)}, f32[4,512]{1,0:T(4,128)S(1)}) custom-call(s32[3]{0:T(128)S(1)} %pad_add_fusion.info.refs_3_.refs_2_.refs_4_, bf16[512,1024]{1,0:T(8,128)(2,1)S(1)} %copy-done, bf16[512,1024]{1,0:T(8,128)(2,1)S(1)} %collective-permute-done.3.refs_1_.refs_6_, bf16[4096,512]{1,0:T(8,128)(2,1)} %refs_4_.1, ...), custom_call_target="tpu_custom_call" | custom-call | flops 1000000 | bytes 100000 | tf_op jit(solution)/shard_map/pallas_call | solution.py:183
  15.0 2.1 %collective-permute-done.2.refs_2_.refs_7_ = bf16[512,256]{1,0:T(8,128)(2,1)S(1)} collective-permute-done((bf16[512,256]{1,0:T(8,128)(2,1)S(1)}, bf16[512,256]{1,0:T(8,128)(2,1)S(1)}, u32[]{:S(2)}, u32[]{:S(2)}) %collective-permute-start.2) | collective-permute-done | bytes 262176 | tf_op jit(solution)/shard_map/ppermute | solution.py:27
  17.1 0.5 collective-permute-start.5
  17.6 1.0 collective-permute-done.4.refs_1_.refs_6_
  18.6 0.4 collective-permute-done.5.refs_3_.refs_8_
  19.0 5.2 %shard_map.120 = (f32[512,512]{1,0:T(8,128)S(1)}, f32[512,1024]{1,0:T(8,128)S(1)}, f32[4,512]{1,0:T(4,128)S(1)}, bf16[1024,512]{1,0:T(8,128)(2,1)S(1)}, bf16[1024,1024]{1,0:T(8,128)(2,1)S(1)}) custom-call(s32[3]{0:T(128)S(1)} %pad_add_fusion.info.refs_3_.refs_2_.refs_4_, ...), custom_call_target="tpu_custom_call", output_to_operand_aliasing={{0}: (8, {}), {1}: (9, {}), {2}: (10, {})} | custom-call | flops 1000000 | bytes 100000 | tf_op jit(solution)/shard_map/pallas_call | solution.py:183
  24.2 3.9 %collective-permute-done.refs_0_.refs_4_ = bf16[512,512]{1,0:T(8,128)(2,1)S(1)} collective-permute-done((bf16[512,512]{1,0:T(8,128)(2,1)S(1)}, bf16[512,512]{1,0:T(8,128)(2,1)S(1)}, u32[]{:S(2)}, u32[]{:S(2)}) %collective-permute-start) | collective-permute-done | bytes 524320 | tf_op jit(solution)/shard_map/ppermute | solution.py:27
  28.1 1.9 %collective-permute-done.6.refs_1_.refs_5_ = bf16[512,512]{1,0:T(8,128)(2,1)S(1)} collective-permute-done((bf16[512,512]{1,0:T(8,128)(2,1)S(1)}, bf16[512,512]{1,0:T(8,128)(2,1)S(1)}, u32[]{:S(2)}, u32[]{:S(2)}) %collective-permute-start.6) | collective-permute-done | bytes 524320 | tf_op jit(solution)/shard_map/ppermute | solution.py:27
  30.0 3.7 %shard_map.121 = (bf16[512,512]{1,0:T(8,128)(2,1)S(1)}, bf16[512,1024]{1,0:T(8,128)(2,1)S(1)}, bf16[2,128,512]{2,1,0:T(8,128)(2,1)S(1)}, bf16[2,128,512]{2,1,0:T...) custom-call(s32[3]{0:T(128)S(1)} %pad_add_fusion.info.refs_3_.refs_2_.refs_4_, s32[4]{0:T(128)S(1)} %copy-done.14, ...), custom_call_target="tpu_custom_call" | custom-call | flops 4000000000 | bytes 4000000 | tf_op jit(solution)/shard_map/pallas_call | solution.py:281
  33.7 1.8 %collective-permute-start.8 = (bf16[2,128,512]{2,1,0:T(8,128)(2,1)S(1)}, bf16[2,128,512]{2,1,0:T(8,128)(2,1)S(1)}, u32[]{:S(2)}, u32[]{:S(2)}) collective-permute-start(bf16[2,128,512]{2,1,0:T(8,128)(2,1)S(1)} %get-tuple-element.100), channel_id=1, source_target_pairs={{0,4},{4,0},{8,12},{12,8},{16,20},{20,16},{24,28},{28,24},{1,5},{5... | collective-permute-start | bytes 786440 | tf_op jit(solution)/shard_map/ppermute | solution.py:27
  35.5 0.3 collective-permute-start.7
  35.8 4.5 %shard_map.122 = (f32[512,512]{1,0:T(8,128)S(1)}, f32[512,1024]{1,0:T(8,128)S(1)}) custom-call(bf16[512,512]{1,0:T(8,128)(2,1)S(1)} %get-tuple-element.96.refs_0_.key, bf16[512,1024]{1,0:T(8,128)(2,1)S(1)} %get-tuple-element.97.refs_1_.value, bf16[2,128,512]{2,1,0:T(8,128)(2,1)S(1)} %get-tuple-element.98.refs_2_.refs_6_.refs_8_, ...), custom_call_target="tpu_custom_call" | custom-call | flops 1000000 | bytes 100000 | tf_op jit(solution)/shard_map/pallas_call | solution.py:183
  40.3 1.9 %collective-permute-done.7.refs_5_.refs_7_ = f32[2,384]{1,0:T(2,128)S(1)} collective-permute-done((f32[2,384]{1,0:T(2,128)S(1)}, f32[2,384]{1,0:T(2,128)S(1)}, u32[]{:S(2)}, u32[]{:S(2)}) %collective-permute-start.7) | collective-permute-done | bytes 3104 | tf_op jit(solution)/shard_map/ppermute | solution.py:27
  42.2 0.8 shard_map.123
  43.0 1.8 %collective-permute-start.10 = (bf16[2,128,512]{2,1,0:T(8,128)(2,1)S(1)}, bf16[2,128,512]{2,1,0:T(8,128)(2,1)}, u32[]{:S(2)}, u32[]{:S(2)}) collective-permute-start(bf16[2,128,512]{2,1,0:T(8,128)(2,1)S(1)} %get-tuple-element.108), channel_id=1, source_target_pairs={{0,8},{4,12},{8,16},{12,20},{16,24},{20,28},{24,0},{28,4},{1,9},{5... | collective-permute-start | bytes 786440 | tf_op jit(solution)/shard_map/ppermute | solution.py:32
  44.8 1.6 %collective-permute-start.9 = (f32[2,384]{1,0:T(2,128)S(1)}, f32[2,384]{1,0:T(2,128)S(1)}, u32[]{:S(2)}, u32[]{:S(2)}) collective-permute-start(f32[2,384]{1,0:T(2,128)S(1)} %get-tuple-element.107), channel_id=1, source_target_pairs={{0,8},{4,12},{8,16},{12,20},{16,24},{20,28},{24,0},{28,4},{1,9},{5... | collective-permute-start | bytes 9224 | tf_op jit(solution)/shard_map/ppermute | solution.py:32
  46.4 6.6 %shard_map.124 = (f32[512,512]{1,0:T(8,128)S(1)}, f32[512,1024]{1,0:T(8,128)S(1)}) custom-call(bf16[512,512]{1,0:T(8,128)(2,1)S(1)} %get-tuple-element.96.refs_0_.key, bf16[512,1024]{1,0:T(8,128)(2,1)S(1)} %get-tuple-element.97.refs_1_.value, ...), custom_call_target="tpu_custom_call", output_to_operand_aliasing={{0}: (9, {}), {1}: (10, {})} | custom-call | flops 1000000 | bytes 100000 | tf_op jit(solution)/shard_map/pallas_call | solution.py:183
  53.0 1.3 %copy-done.2 = f32[512,1024]{1,0:T(8,128)} copy-done((f32[512,1024]{1,0:T(8,128)}, f32[512,1024]{1,0:T(8,128)S(1)}, u32[]{:S(2)}) %copy-start.2) | copy-done | bytes 2097176
  54.4 1.0 copy-done.6
  55.4 1.6 %collective-permute-start.12 = (bf16[2,128,512]{2,1,0:T(8,128)(2,1)}, bf16[2,128,512]{2,1,0:T(8,128)(2,1)}, u32[]{:S(2)}, u32[]{:S(2)}) collective-permute-start(bf16[2,128,512]{2,1,0:T(8,128)(2,1)} %collective-permute-done.10.refs_12_), channel_id=1, source_target_pairs={{0,8},{4,12},{8,16},{12,20},{16,24},{20,28},{24,0},{28,4},{1,9},{5... | collective-permute-start | bytes 786440 | tf_op jit(solution)/shard_map/ppermute | solution.py:32
  56.9 0.2 collective-permute-start.11
  57.2 0.1 copy.18.refs_16_
  57.3 1.6 %copy-done.3 = f32[512,1024]{1,0:T(8,128)S(1)} copy-done((f32[512,1024]{1,0:T(8,128)S(1)}, f32[512,1024]{1,0:T(8,128)}, u32[]{:S(2)}) %copy-start.3) | copy-done | bytes 2097176
  58.9 1.2 %copy-done.7 = f32[512,512]{1,0:T(8,128)S(1)} copy-done((f32[512,512]{1,0:T(8,128)S(1)}, f32[512,512]{1,0:T(8,128)}, u32[]{:S(2)}) %copy-start.7) | copy-done | bytes 1048600
  60.1 0.9 copy-done.9
  61.0 0.9 copy-done.11
  62.0 0.9 copy-done.13
  62.9 4.5 %shard_map.125 = (bf16[512,512]{1,0:T(8,128)(2,1)S(1)}, f32[512,1024]{1,0:T(8,128)S(1)}) custom-call(bf16[512,512]{1,0:T(8,128)(2,1)S(1)} %get-tuple-element.96.refs_0_.key, bf16[512,1024]{1,0:T(8,128)(2,1)S(1)} %get-tuple-element.97.refs_1_.value, bf16[2,128,512]{2,1,0:T(8,128)(2,1)S(1)} %get-tuple-element.98.refs_2_.refs_6_.refs_8_, ...), custom_call_target="tpu_custom_call" | custom-call | flops 1000000 | bytes 100000 | tf_op jit(solution)/shard_map/pallas_call | solution.py:183
  67.5 1.6 %shard_map.126.refs_14_ = f32[2,128,512]{2,1,0:T(8,128)S(1)} custom-call(bf16[512,512]{1,0:T(8,128)(2,1)S(1)} %get-tuple-element.96.refs_0_.key, bf16[512,1024]{1,0:T(8,128)(2,1)S(1)} %get-tuple-element.97.refs_1_.value, bf16[2,128,512]{2,1,0:T(8,128)(2,1)S(1)} %get-tuple-element.98.refs_2_.refs_6_.refs_8_, ...), custom_call_target="tpu_custom_call" | custom-call | flops 1000000 | bytes 100000 | tf_op jit(solution)/shard_map/pallas_call | solution.py:411
  69.1 1.7 %shard_map.127 = (bf16[2,128,512]{2,1,0:T(8,128)(2,1)S(1)}, bf16[2,128,512]{2,1,0:T(8,128)(2,1)S(1)}, f32[2,256]{1,0:T(2,128)S(1)}, f32[2,128]{1,0:T(2,128)S(1)}) custom-call(bf16[512,512]{1,0:T(8,128)(2,1)S(1)} %get-tuple-element.96.refs_0_.key, bf16[512,1024]{1,0:T(8,128)(2,1)S(1)} %get-tuple-element.97.refs_1_.value, ...), custom_call_target="tpu_custom_call" | custom-call | flops 1000000 | bytes 100000 | tf_op jit(solution)/shard_map/pallas_call | solution.py:427
  70.9 1.6 %collective-permute-start.13 = (bf16[2,128,512]{2,1,0:T(8,128)(2,1)S(1)}, bf16[2,128,512]{2,1,0:T(8,128)(2,1)S(1)}, u32[]{:S(2)}, u32[]{:S(2)}) collective-permute-start(bf16[2,128,512]{2,1,0:T(8,128)(2,1)S(1)} %get-tuple-element.129), channel_id=1, source_target_pairs={{0,4},{4,0},{8,12},{12,8},{16,20},{20,16},{24,28},{28,24},{1,5},{5... | collective-permute-start | bytes 786440 | tf_op jit(solution)/shard_map/ppermute | solution.py:27
  72.4 4.2 %shard_map.128 = (f32[512,1024]{1,0:T(8,128)S(1)}, f32[512,1024]{1,0:T(8,128)S(1)}, bf16[1024,4096]{1,0:T(8,128)(2,1)S(1)}) custom-call(s32[3]{0:T(128)S(1)} %pad_add_fusion.info.refs_3_.refs_2_.refs_4_, s32[4]{0:T(128)S(1)} %copy-done.14, f32[2,128]{1,0:T(2,128)S(1)} %get-tuple-element.130.top_in, bf16[512,512]{1,0:T(8,128)(2,1)S(1)} %get-tuple-element.122.refs_2_.query, ...), custom_call_target="tpu_custom_call" | custom-call | flops 1000000 | bytes 100000 | tf_op jit(solution)/shard_map/pallas_call | solution.py:499
  76.6 1.0 collective-permute-done.13.other
  77.6 2.2 %shard_map.129 = (bf16[512,1024]{1,0:T(8,128)(2,1)S(1)}, bf16[512,512]{1,0:T(8,128)(2,1)S(1)}, bf16[512,512]{1,0:T(8,128)(2,1)S(1)}) custom-call(s32[3]{0:T(128)S(1)} %pad_add_fusion.info.refs_3_.refs_2_.refs_4_, bf16[512,512]{1,0:T(8,128)(2,1)S(1)} %get-tuple-element.122.refs_2_.query, bf16[2,128,512]{2,1,0:T(8,128)(2,1)S(1)} %get-tuple-element.128.own, ...), custom_call_target="tpu_custom_call" | custom-call | flops 3000000000 | bytes 8000000 | tf_op jit(solution)/shard_map/pallas_call | solution.py:543
  79.8 0.1 collective-permute-start.14
  79.9 1.8 %shard_map.130 = (bf16[512,512]{1,0:T(8,128)(2,1)S(1)}, bf16[512,512]{1,0:T(8,128)(2,1)S(1)}) custom-call(s32[3]{0:T(128)S(1)} %pad_add_fusion.info.refs_3_.refs_2_.refs_4_, bf16[512,1024]{1,0:T(8,128)(2,1)S(1)} %get-tuple-element.144.hidden, bf16[1024,4096]{1,0:T(8,128)(2,1)S(1)} %get-tuple-element.135.w), custom_call_target="tpu_custom_call" | custom-call | flops 1000000 | bytes 100000 | tf_op jit(solution)/shard_map/pallas_call | solution.py:564
  81.7 0.6 collective-permute-start.16
  82.4 0.1 convert_add_fusion.3
  82.6 1.6 %collective-permute-start.15 = (bf16[512,256]{1,0:T(8,128)(2,1)S(1)}, bf16[512,256]{1,0:T(8,128)(2,1)S(1)}, u32[]{:S(2)}, u32[]{:S(2)}) collective-permute-start(bf16[512,256]{1,0:T(8,128)(2,1)S(1)} %slice.99), channel_id=1, source_target_pairs={{0,2},{1,3},{2,0},{3,1},{4,6},{5,7},{6,4},{7,5},{8,10},{9,11},{10,... | collective-permute-start | bytes 786440 | tf_op jit(solution)/shard_map/ppermute | solution.py:27
  84.2 1.8 %shard_map.131 = (bf16[512,512]{1,0:T(8,128)(2,1)S(1)}, bf16[512,512]{1,0:T(8,128)(2,1)S(1)}) custom-call(s32[3]{0:T(128)S(1)} %pad_add_fusion.info.refs_3_.refs_2_.refs_4_, bf16[512,1024]{1,0:T(8,128)(2,1)S(1)} %get-tuple-element.144.hidden, bf16[1024,4096]{1,0:T(8,128)(2,1)S(1)} %get-tuple-element.135.w), custom_call_target="tpu_custom_call" | custom-call | flops 1000000 | bytes 100000 | tf_op jit(solution)/shard_map/pallas_call | solution.py:564
  86.1 0.1 convert_add_fusion.2
  86.3 0.6 collective-permute-start.17
  86.8 1.8 %shard_map.132 = (bf16[512,512]{1,0:T(8,128)(2,1)S(1)}, bf16[512,512]{1,0:T(8,128)(2,1)S(1)}) custom-call(s32[3]{0:T(128)S(1)} %pad_add_fusion.info.refs_3_.refs_2_.refs_4_, bf16[512,1024]{1,0:T(8,128)(2,1)S(1)} %get-tuple-element.144.hidden, bf16[1024,4096]{1,0:T(8,128)(2,1)S(1)} %get-tuple-element.135.w), custom_call_target="tpu_custom_call" | custom-call | flops 1000000 | bytes 100000 | tf_op jit(solution)/shard_map/pallas_call | solution.py:564
  88.7 0.3 collective-permute-start.20
  88.9 2.9 %collective-permute-done.15 = bf16[512,256]{1,0:T(8,128)(2,1)S(1)} collective-permute-done((bf16[512,256]{1,0:T(8,128)(2,1)S(1)}, bf16[512,256]{1,0:T(8,128)(2,1)S(1)}, u32[]{:S(2)}, u32[]{:S(2)}) %collective-permute-start.15) | collective-permute-done | bytes 262176 | tf_op jit(solution)/shard_map/ppermute | solution.py:27
  91.8 0.2 fusion.8
  92.0 0.1 convert_add_fusion.1
  92.2 1.6 %collective-permute-start.19 = (bf16[512,256]{1,0:T(8,128)(2,1)S(1)}, bf16[512,256]{1,0:T(8,128)(2,1)S(1)}, u32[]{:S(2)}, u32[]{:S(2)}) collective-permute-start(bf16[512,256]{1,0:T(8,128)(2,1)S(1)} %slice.97), channel_id=1, source_target_pairs={{0,2},{1,3},{2,0},{3,1},{4,6},{5,7},{6,4},{7,5},{8,10},{9,11},{10,... | collective-permute-start | bytes 786440 | tf_op jit(solution)/shard_map/ppermute | solution.py:27
  93.8 0.1 convert_add_fusion
  94.0 0.6 collective-permute-start.21
  94.6 2.9 %collective-permute-done.17 = bf16[512,256]{1,0:T(8,128)(2,1)S(1)} collective-permute-done((bf16[512,256]{1,0:T(8,128)(2,1)S(1)}, bf16[512,256]{1,0:T(8,128)(2,1)S(1)}, u32[]{:S(2)}, u32[]{:S(2)}) %collective-permute-start.17) | collective-permute-done | bytes 262176 | tf_op jit(solution)/shard_map/ppermute | solution.py:27
  97.4 0.1 fusion.9
  97.5 5.5 %collective-permute-done.19 = bf16[512,256]{1,0:T(8,128)(2,1)S(1)} collective-permute-done((bf16[512,256]{1,0:T(8,128)(2,1)S(1)}, bf16[512,256]{1,0:T(8,128)(2,1)S(1)}, u32[]{:S(2)}, u32[]{:S(2)}) %collective-permute-start.19) | collective-permute-done | bytes 262176 | tf_op jit(solution)/shard_map/ppermute | solution.py:27
  103.0 0.1 fusion.10
  103.2 4.6 %collective-permute-done.21 = bf16[512,256]{1,0:T(8,128)(2,1)S(1)} collective-permute-done((bf16[512,256]{1,0:T(8,128)(2,1)S(1)}, bf16[512,256]{1,0:T(8,128)(2,1)S(1)}, u32[]{:S(2)}, u32[]{:S(2)}) %collective-permute-start.21) | collective-permute-done | bytes 262176 | tf_op jit(solution)/shard_map/ppermute | solution.py:27
  107.7 0.8 fusion.11
  (49 shorter events, 0.4 us)
Async XLA Ops:
  0.0 7.2 %collective-permute-start.3 = (bf16[512,1024]{1,0:T(8,128)(2,1)}, bf16[512,1024]{1,0:T(8,128)(2,1)S(1)}, u32[]{:S(2)}, u32[]{:S(2)}) collective-permute-start(bf16[512,1024]{1,0:T(8,128)(2,1)} %refs_5_.4), channel_id=1, source_target_pairs={{0,1},{1,0},{2,3},{3,2},{4,5},{5,4},{6,7},{7,6},{8,9},{9,8},{10,11... | collective-permute-start | bytes 3145736 | tf_op jit(solution)/shard_map/ppermute | solution.py:27
  1.7 13.2 %collective-permute-start.1 = (bf16[512,256]{1,0:T(8,128)(2,1)S(1)}, bf16[512,256]{1,0:T(8,128)(2,1)S(1)}, u32[]{:S(2)}, u32[]{:S(2)}) collective-permute-start(bf16[512,256]{1,0:T(8,128)(2,1)S(1)} %get-tuple-element.77), channel_id=1, source_target_pairs={{0,2},{1,3},{2,0},{3,1},{4,6},{5,7},{6,4},{7,5},{8,10},{9,11},{10,... | collective-permute-start | bytes 786440 | tf_op jit(solution)/shard_map/ppermute | solution.py:27
  4.3 12.8 %collective-permute-start.2 = (bf16[512,256]{1,0:T(8,128)(2,1)S(1)}, bf16[512,256]{1,0:T(8,128)(2,1)S(1)}, u32[]{:S(2)}, u32[]{:S(2)}) collective-permute-start(bf16[512,256]{1,0:T(8,128)(2,1)S(1)} %get-tuple-element.78), channel_id=1, source_target_pairs={{0,2},{1,3},{2,0},{3,1},{4,6},{5,7},{6,4},{7,5},{8,10},{9,11},{10,... | collective-permute-start | bytes 786440 | tf_op jit(solution)/shard_map/ppermute | solution.py:27
  4.4 23.8 %collective-permute-start = (bf16[512,512]{1,0:T(8,128)(2,1)S(1)}, bf16[512,512]{1,0:T(8,128)(2,1)S(1)}, u32[]{:S(2)}, u32[]{:S(2)}) collective-permute-start(bf16[512,512]{1,0:T(8,128)(2,1)S(1)} %get-tuple-element.76), channel_id=1, source_target_pairs={{0,2},{1,3},{2,0},{3,1},{4,6},{5,7},{6,4},{7,5},{8,10},{9,11},{10,... | collective-permute-start | bytes 1572872 | tf_op jit(solution)/shard_map/ppermute | solution.py:27
  7.2 1.2 %copy-start = (bf16[512,1024]{1,0:T(8,128)(2,1)S(1)}, bf16[512,1024]{1,0:T(8,128)(2,1)}, u32[]{:S(2)}) copy-start(bf16[512,1024]{1,0:T(8,128)(2,1)} %refs_5_.4) | copy-start | bytes 3145732
  8.4 6.5 %copy-start.4 = (bf16[512,1024]{1,0:T(8,128)(2,1)}, bf16[512,1024]{1,0:T(8,128)(2,1)S(1)}, u32[]{:S(2)}) copy-start(bf16[512,1024]{1,0:T(8,128)(2,1)S(1)} %collective-permute-done.3.refs_1_.refs_6_) | copy-start | bytes 3145732
  17.1 7.1 %copy-start.8 = (bf16[512,256]{1,0:T(8,128)(2,1)}, bf16[512,256]{1,0:T(8,128)(2,1)S(1)}, u32[]{:S(2)}) copy-start(bf16[512,256]{1,0:T(8,128)(2,1)S(1)} %collective-permute-done.2.refs_2_.refs_7_) | copy-start | bytes 786436
  17.1 13.0 %copy-start.14 = (s32[4]{0:T(128)S(1)}, s32[4]{0:T(128)}, u32[]{:S(2)}) copy-start(s32[4]{0:T(128)} %docs.3) | copy-start | bytes 52
  17.1 13.0 %copy-start.16 = (f32[2,2]{1,0:T(2,128)S(1)}, f32[2,2]{1,0:T(2,128)}, u32[]{:S(2)}) copy-start(f32[2,2]{1,0:T(2,128)} %bias.1) | copy-start | bytes 52
  17.1 1.5 %collective-permute-start.4 = (bf16[512,256]{1,0:T(8,128)(2,1)S(1)}, bf16[512,256]{1,0:T(8,128)(2,1)S(1)}, u32[]{:S(2)}, u32[]{:S(2)}) collective-permute-start(bf16[512,256]{1,0:T(8,128)(2,1)S(1)} %collective-permute-done.1.refs_0_.refs_5_), channel_id=1, source_target_pairs={{0,1},{1,0},{2,3},{3,2},{4,5},{5,4},{6,7},{7,6},{8,9},{9,8},{10,11... | collective-permute-start | bytes 786440 | tf_op jit(solution)/shard_map/ppermute | solution.py:27
  17.1 1.9 %collective-permute-start.5 = (bf16[512,256]{1,0:T(8,128)(2,1)S(1)}, bf16[512,256]{1,0:T(8,128)(2,1)S(1)}, u32[]{:S(2)}, u32[]{:S(2)}) collective-permute-start(bf16[512,256]{1,0:T(8,128)(2,1)S(1)} %collective-permute-done.2.refs_2_.refs_7_), channel_id=1, source_target_pairs={{0,1},{1,0},{2,3},{3,2},{4,5},{5,4},{6,7},{7,6},{8,9},{9,8},{10,11... | collective-permute-start | bytes 786440 | tf_op jit(solution)/shard_map/ppermute | solution.py:27
  18.6 5.6 %copy-start.10 = (bf16[512,256]{1,0:T(8,128)(2,1)}, bf16[512,256]{1,0:T(8,128)(2,1)S(1)}, u32[]{:S(2)}) copy-start(bf16[512,256]{1,0:T(8,128)(2,1)S(1)} %collective-permute-done.4.refs_1_.refs_6_) | copy-start | bytes 786436
  19.0 5.2 %copy-start.12 = (bf16[512,256]{1,0:T(8,128)(2,1)}, bf16[512,256]{1,0:T(8,128)(2,1)S(1)}, u32[]{:S(2)}) copy-start(bf16[512,256]{1,0:T(8,128)(2,1)S(1)} %collective-permute-done.5.refs_3_.refs_8_) | copy-start | bytes 786436
  28.1 1.9 %collective-permute-start.6 = (bf16[512,512]{1,0:T(8,128)(2,1)S(1)}, bf16[512,512]{1,0:T(8,128)(2,1)S(1)}, u32[]{:S(2)}, u32[]{:S(2)}) collective-permute-start(bf16[512,512]{1,0:T(8,128)(2,1)S(1)} %collective-permute-done.refs_0_.refs_4_), channel_id=1, source_target_pairs={{0,1},{1,0},{2,3},{3,2},{4,5},{5,4},{6,7},{7,6},{8,9},{9,8},{10,11... | collective-permute-start | bytes 1572872 | tf_op jit(solution)/shard_map/ppermute | solution.py:27
  33.7 8.5 %collective-permute-start.8 = (bf16[2,128,512]{2,1,0:T(8,128)(2,1)S(1)}, bf16[2,128,512]{2,1,0:T(8,128)(2,1)S(1)}, u32[]{:S(2)}, u32[]{:S(2)}) collective-permute-start(bf16[2,128,512]{2,1,0:T(8,128)(2,1)S(1)} %get-tuple-element.100), channel_id=1, source_target_pairs={{0,4},{4,0},{8,12},{12,8},{16,20},{20,16},{24,28},{28,24},{1,5},{5... | collective-permute-start | bytes 786440 | tf_op jit(solution)/shard_map/ppermute | solution.py:27
  35.5 6.7 %collective-permute-start.7 = (f32[2,384]{1,0:T(2,128)S(1)}, f32[2,384]{1,0:T(2,128)S(1)}, u32[]{:S(2)}, u32[]{:S(2)}) collective-permute-start(f32[2,384]{1,0:T(2,128)S(1)} %get-tuple-element.99.refs_4_.refs_6_), channel_id=1, source_target_pairs={{0,4},{4,0},{8,12},{12,8},{16,20},{20,16},{24,28},{28,24},{1,5},{5... | collective-permute-start | bytes 9224 | tf_op jit(solution)/shard_map/ppermute | solution.py:27
  40.3 6.2 %copy-start.1 = (bf16[512,1024]{1,0:T(8,128)(2,1)S(1)}, bf16[512,1024]{1,0:T(8,128)(2,1)}, u32[]{:S(2)}) copy-start(bf16[512,1024]{1,0:T(8,128)(2,1)} %refs_5_.4) | copy-start | bytes 3145732
  40.3 6.1 %copy-start.5 = (bf16[512,1024]{1,0:T(8,128)(2,1)S(1)}, bf16[512,1024]{1,0:T(8,128)(2,1)}, u32[]{:S(2)}) copy-start(bf16[512,1024]{1,0:T(8,128)(2,1)} %copy-done.4) | copy-start | bytes 3145732
  43.0 12.4 %collective-permute-start.10 = (bf16[2,128,512]{2,1,0:T(8,128)(2,1)S(1)}, bf16[2,128,512]{2,1,0:T(8,128)(2,1)}, u32[]{:S(2)}, u32[]{:S(2)}) collective-permute-start(bf16[2,128,512]{2,1,0:T(8,128)(2,1)S(1)} %get-tuple-element.108), channel_id=1, source_target_pairs={{0,8},{4,12},{8,16},{12,20},{16,24},{20,28},{24,0},{28,4},{1,9},{5... | collective-permute-start | bytes 786440 | tf_op jit(solution)/shard_map/ppermute | solution.py:32
  44.8 12.3 %copy-start.18 = (f32[2]{0:T(128)S(1)}, f32[2]{0:T(128)}, u32[]{:S(2)}) copy-start(f32[2]{0:T(128)} %param.22) | copy-start | bytes 28
  44.8 10.5 %collective-permute-start.9 = (f32[2,384]{1,0:T(2,128)S(1)}, f32[2,384]{1,0:T(2,128)S(1)}, u32[]{:S(2)}, u32[]{:S(2)}) collective-permute-start(f32[2,384]{1,0:T(2,128)S(1)} %get-tuple-element.107), channel_id=1, source_target_pairs={{0,8},{4,12},{8,16},{12,20},{16,24},{20,28},{24,0},{28,4},{1,9},{5... | collective-permute-start | bytes 9224 | tf_op jit(solution)/shard_map/ppermute | solution.py:32
  53.0 1.3 %copy-start.2 = (f32[512,1024]{1,0:T(8,128)}, f32[512,1024]{1,0:T(8,128)S(1)}, u32[]{:S(2)}) copy-start(f32[512,1024]{1,0:T(8,128)S(1)} %get-tuple-element.121.refs_12_) | copy-start | bytes 6291460
  54.4 1.0 copy-start.6
  55.4 13.8 %collective-permute-start.12 = (bf16[2,128,512]{2,1,0:T(8,128)(2,1)}, bf16[2,128,512]{2,1,0:T(8,128)(2,1)}, u32[]{:S(2)}, u32[]{:S(2)}) collective-permute-start(bf16[2,128,512]{2,1,0:T(8,128)(2,1)} %collective-permute-done.10.refs_12_), channel_id=1, source_target_pairs={{0,8},{4,12},{8,16},{12,20},{16,24},{20,28},{24,0},{28,4},{1,9},{5... | collective-permute-start | bytes 786440 | tf_op jit(solution)/shard_map/ppermute | solution.py:32
  56.9 12.2 %collective-permute-start.11 = (f32[2,384]{1,0:T(2,128)S(1)}, f32[2,384]{1,0:T(2,128)S(1)}, u32[]{:S(2)}, u32[]{:S(2)}) collective-permute-start(f32[2,384]{1,0:T(2,128)S(1)} %collective-permute-done.9.refs_10_), channel_id=1, source_target_pairs={{0,8},{4,12},{8,16},{12,20},{16,24},{20,28},{24,0},{28,4},{1,9},{5... | collective-permute-start | bytes 9224 | tf_op jit(solution)/shard_map/ppermute | solution.py:32
  57.3 1.6 %copy-start.3 = (f32[512,1024]{1,0:T(8,128)S(1)}, f32[512,1024]{1,0:T(8,128)}, u32[]{:S(2)}) copy-start(f32[512,1024]{1,0:T(8,128)} %copy-done.2) | copy-start | bytes 6291460
  58.9 1.2 %copy-start.7 = (f32[512,512]{1,0:T(8,128)S(1)}, f32[512,512]{1,0:T(8,128)}, u32[]{:S(2)}) copy-start(f32[512,512]{1,0:T(8,128)} %copy-done.6) | copy-start | bytes 3145732
  60.1 0.9 copy-start.9
  61.0 0.9 copy-start.11
  62.0 0.9 copy-start.13
  67.5 1.6 %copy-start.15 = (f32[2,256]{1,0:T(2,128)S(1)}, f32[2,256]{1,0:T(2,128)}, u32[]{:S(2)}) copy-start(f32[2,256]{1,0:T(2,128)} %refs_15_.1) | copy-start | bytes 6148
  70.9 6.7 %collective-permute-start.13 = (bf16[2,128,512]{2,1,0:T(8,128)(2,1)S(1)}, bf16[2,128,512]{2,1,0:T(8,128)(2,1)S(1)}, u32[]{:S(2)}, u32[]{:S(2)}) collective-permute-start(bf16[2,128,512]{2,1,0:T(8,128)(2,1)S(1)} %get-tuple-element.129), channel_id=1, source_target_pairs={{0,4},{4,0},{8,12},{12,8},{16,20},{20,16},{24,28},{28,24},{1,5},{5... | collective-permute-start | bytes 786440 | tf_op jit(solution)/shard_map/ppermute | solution.py:27
  79.8 2.6 %collective-permute-start.14 = (bf16[512,512]{1,0:T(8,128)(2,1)S(1)}, bf16[512,512]{1,0:T(8,128)(2,1)S(1)}, u32[]{:S(2)}, u32[]{:S(2)}) collective-permute-start(bf16[512,512]{1,0:T(8,128)(2,1)S(1)} %get-tuple-element.137), channel_id=1, source_target_pairs={{0,1},{1,0},{2,3},{3,2},{4,5},{5,4},{6,7},{7,6},{8,9},{9,8},{10,11... | collective-permute-start | bytes 1572872 | tf_op jit(solution)/shard_map/ppermute | solution.py:27
  81.7 4.3 %collective-permute-start.16 = (bf16[512,512]{1,0:T(8,128)(2,1)S(1)}, bf16[512,512]{1,0:T(8,128)(2,1)S(1)}, u32[]{:S(2)}, u32[]{:S(2)}) collective-permute-start(bf16[512,512]{1,0:T(8,128)(2,1)S(1)} %get-tuple-element.140), channel_id=1, source_target_pairs={{0,1},{1,0},{2,3},{3,2},{4,5},{5,4},{6,7},{7,6},{8,9},{9,8},{10,11... | collective-permute-start | bytes 1572872 | tf_op jit(solution)/shard_map/ppermute | solution.py:27
  82.6 9.2 %collective-permute-start.15 = (bf16[512,256]{1,0:T(8,128)(2,1)S(1)}, bf16[512,256]{1,0:T(8,128)(2,1)S(1)}, u32[]{:S(2)}, u32[]{:S(2)}) collective-permute-start(bf16[512,256]{1,0:T(8,128)(2,1)S(1)} %slice.99), channel_id=1, source_target_pairs={{0,2},{1,3},{2,0},{3,1},{4,6},{5,7},{6,4},{7,5},{8,10},{9,11},{10,... | collective-permute-start | bytes 786440 | tf_op jit(solution)/shard_map/ppermute | solution.py:27
  86.0 6.0 %collective-permute-start.18 = (bf16[512,512]{1,0:T(8,128)(2,1)S(1)}, bf16[512,512]{1,0:T(8,128)(2,1)S(1)}, u32[]{:S(2)}, u32[]{:S(2)}) collective-permute-start(bf16[512,512]{1,0:T(8,128)(2,1)S(1)} %get-tuple-element.143), channel_id=1, source_target_pairs={{0,1},{1,0},{2,3},{3,2},{4,5},{5,4},{6,7},{7,6},{8,9},{9,8},{10,11... | collective-permute-start | bytes 1572872 | tf_op jit(solution)/shard_map/ppermute | solution.py:27
  86.3 11.1 %collective-permute-start.17 = (bf16[512,256]{1,0:T(8,128)(2,1)S(1)}, bf16[512,256]{1,0:T(8,128)(2,1)S(1)}, u32[]{:S(2)}, u32[]{:S(2)}) collective-permute-start(bf16[512,256]{1,0:T(8,128)(2,1)S(1)} %slice.98), channel_id=1, source_target_pairs={{0,2},{1,3},{2,0},{3,1},{4,6},{5,7},{6,4},{7,5},{8,10},{9,11},{10,... | collective-permute-start | bytes 786440 | tf_op jit(solution)/shard_map/ppermute | solution.py:27
  88.7 5.1 %collective-permute-start.20 = (bf16[512,512]{1,0:T(8,128)(2,1)S(1)}, bf16[512,512]{1,0:T(8,128)(2,1)S(1)}, u32[]{:S(2)}, u32[]{:S(2)}) collective-permute-start(bf16[512,512]{1,0:T(8,128)(2,1)S(1)} %get-tuple-element.146), channel_id=1, source_target_pairs={{0,1},{1,0},{2,3},{3,2},{4,5},{5,4},{6,7},{7,6},{8,9},{9,8},{10,11... | collective-permute-start | bytes 1572872 | tf_op jit(solution)/shard_map/ppermute | solution.py:27
  92.2 10.8 %collective-permute-start.19 = (bf16[512,256]{1,0:T(8,128)(2,1)S(1)}, bf16[512,256]{1,0:T(8,128)(2,1)S(1)}, u32[]{:S(2)}, u32[]{:S(2)}) collective-permute-start(bf16[512,256]{1,0:T(8,128)(2,1)S(1)} %slice.97), channel_id=1, source_target_pairs={{0,2},{1,3},{2,0},{3,1},{4,6},{5,7},{6,4},{7,5},{8,10},{9,11},{10,... | collective-permute-start | bytes 786440 | tf_op jit(solution)/shard_map/ppermute | solution.py:27
  94.0 13.7 %collective-permute-start.21 = (bf16[512,256]{1,0:T(8,128)(2,1)S(1)}, bf16[512,256]{1,0:T(8,128)(2,1)S(1)}, u32[]{:S(2)}, u32[]{:S(2)}) collective-permute-start(bf16[512,256]{1,0:T(8,128)(2,1)S(1)} %slice.96), channel_id=1, source_target_pairs={{0,2},{1,3},{2,0},{3,1},{4,6},{5,7},{6,4},{7,5},{8,10},{9,11},{10,... | collective-permute-start | bytes 786440 | tf_op jit(solution)/shard_map/ppermute | solution.py:27
  103.1 4.6 %copy-start.17 = (bf16[512,1024]{1,0:T(8,128)(2,1)}, bf16[512,1024]{1,0:T(8,128)(2,1)S(1)}, u32[]{:S(2)}) copy-start(bf16[512,1024]{1,0:T(8,128)(2,1)S(1)} %fusion.10) | copy-start | bytes 3145732

commit v7 on v6

--- a/solution.py
+++ b/solution.py
@@ -111,7 +111,7 @@
     gate_w = take(1)[0] if gated else None
     sums = take(count_w + gated) if with_sum else None
     outs = take(count_w + gated)
-    ahead = take(count_w) if ahead_at else []
+    ahead = take(2) if ahead_at else []
     held = take(count_w)
     sems = take(1)[0]
     place = info[0]
@@ -167,8 +167,8 @@
     scratch.append(pltpu.SemaphoreType.DMA((len(weights), len(xs_at))))
     if ahead_at:
         rows = sum(c for _, _, c in ahead_at)
-        shapes += [pltpu.VMEM((rows, w.shape[1]), BF) for w in weights]
-        scratch.append(pltpu.SemaphoreType.DMA((len(weights), len(ahead_at))))
+        shapes += [pltpu.VMEM((rows, w.shape[1]), BF) for w in weights[:2]]
+        scratch.append(pltpu.SemaphoreType.DMA((2, len(ahead_at))))
     operands = [*in_vmem(*held), info, *in_vmem(*xs), *[in_hbm(w) for w in weights]]
     specs = [VMEM_SPEC] * len(held) + [SMEM_SPEC] + [VMEM_SPEC] * len(xs) + [HBM_SPEC] * len(weights)
     if gated:
@@ -612,8 +612,8 @@
     info = jnp.stack([place, side, offset]).astype(jnp.int32)
     at = [[(o, s, c) for s, c, _ in group for o in (2, 3)] for group in groups]
     near_at = [(0, 0, share), (1, 0, share)]
-    key_value, query_gate = (w_key, w_value), (w_query, w_outgate)
-    sums = stage(info, [source, beside], near_at, key_value, share, gate_w)
+    first_three = (w_key, w_value, w_query)
+    sums = stage(info, [source, beside], near_at, first_three, share, gate_w)
     far = []
     for i, group in enumerate(groups):
         xs = lax.optimization_barrier((*[x for _, _, x in group], *sums))
@@ -623,43 +623,49 @@
         if i < len(groups) - 1:
             last = i == len(groups) - 2
             out = stage(
-                info, xs, at[i], key_value, share, gate_w, sums, at[-1] if last else None
+                info, xs, at[i], first_three, share, gate_w, sums, at[-1] if last else None
             )
-            sums = out[:3]
+            sums = out[:4]
             if last:
-                w_key_last, w_value_last = out[3:]
+                w_key_last, w_value_last = out[4:]
     keys, values, kept, sent, small, u = block_summary(
         info, doc_lengths, gate_bias, xs, at[-1], w_key_last, w_value_last, gate_w,
-        sums[0], sums[1], sums[2], share, heads,
+        sums[0], sums[1], sums[3], share, heads,
     )
 
     small_other = pair(small)
     got = pair(sent)
     held = (keys, values, kept)
-    later_xs = after(keys, *[x for xs in far[1:] for x in xs])
-    later = stage(info, later_xs, sum(at[1:], []), query_gate, share, held=held)
-    small_other, got, *later = lax.optimization_barrier((small_other, got, *later))
+    far_xs = after(keys, *[x for xs in far for x in xs])
+    (queries,) = stage(
+        info, far_xs[-len(far[-1]) :], at[-1], (w_query,), share, None, [sums[2]],
+        finishes=((unchanged, BF),), held=held,
+    )
+    gate = stage(info, far_xs, sum(at, []), (w_outgate,), share, held=held)
+    small_other, got, queries, *gate = lax.optimization_barrier(
+        (small_other, got, queries, *gate)
+    )
     state_pair, travel = pair_summary(
-        info, doc_lengths, small, small_other, kept, got, length, (keys, values)
+        info, doc_lengths, small, small_other, kept, got, length, (keys, values, queries)
     )
     smalls, states = [], []
-    held = (keys, values, kept, got)
+    held = (keys, values, kept, got, queries)
     for step in range(blocks // 4):
         before = state_pair
         travel, state_pair = down(travel), down(state_pair)
         if step == 0:
             near_xs = after(before, source, beside)
-            later = stage(info, near_xs, near_at, query_gate, share, None, later, held=held)
+            gate = stage(
+                info, near_xs, near_at, (w_outgate,), share, None, gate,
+                finishes=((jax.nn.sigmoid, F32),), held=held,
+            )
+            travel, state_pair, *gate = lax.optimization_barrier((travel, state_pair, *gate))
         elif step == 1:
-            last_xs = after(before, *far[0])
-            queries, gate = stage(
-                info, last_xs, at[0], query_gate, share, None, later,
-                finishes=((unchanged, BF), (jax.nn.sigmoid, F32)), held=held,
-            )
-            carry = carry_half(after(queries, info), carry_matrix, held)
-        travel, state_pair, *later = lax.optimization_barrier((travel, state_pair, *later))
+            carry = carry_half(after(before, info), carry_matrix, (*held, *gate))
+            travel, state_pair, carry = lax.optimization_barrier((travel, state_pair, carry))
         smalls.append(travel)
         states.append(state_pair)
+    (gate,) = gate
     state_own, state_other, norm_in, top_own = incoming_state(
         info, doc_lengths, small, small_other, kept, got, smalls, states,
         carry, carry_norm, carry_max, length, (keys, values, queries, gate),

time: 109 us -> 105 us (0.963)
  local copies, waits for them, and re-layouts: 10.3 us -> 5.42 us
  Pallas kernels: 48.2 us -> 49.5 us
    unnamed x39 -> x47, local copies, waits for them, and re-layouts: 9.32 us -> 4.41 us
    ppermute x4, waiting for transfers between devices: 0.01 us -> 4.18 us  [shifted(): return lax.ppermute(x, axis, [(i, (i + by) % size) for i in range(size)])]
    ppermute x18, waiting for transfers between devices: 28 us -> 24.3 us  [swapped(): return lax.ppermute(x, axis, [(i, i ^ mask) for i in range(size)])]
  transfers between devices with their start and end apart: 22 -> 22, of which waited for: 11 -> 12; matrix products, arithmetic and copies ran while one was open for 2% -> 2% of each run, Pallas kernels for 37% -> 39%
where the time goes in v7:
time: 105 us
  Pallas kernels  49.5 us (47%)
  waiting for transfers between devices  28.4 us (27%)
  starting transfers between devices  18.9 us (18%)
  local copies, waits for them, and re-layouts  5.42 us (5%)
  other arithmetic  1.86 us (2%)
    pallas_call x5, Pallas kernels, stage(): pl.pallas_call(holding(functools.partial(stage_kernel, xs_at, ahead_at, s...  27.9 us
    ppermute x18, waiting for transfers between devices, swapped(): return lax.ppermute(x, axis, [(i, i ^ mask) for i in range(size)])  24.3 us
    ppermute x18, starting transfers between devices, swapped(): return lax.ppermute(x, axis, [(i, i ^ mask) for i in range(size)])  14.2 us
    pallas_call x3, Pallas kernels, next_columns(): pl.pallas_call(functools.partial(columns_kernel, start), out_shape=(pltpu...  5.47 us
    ppermute x4, starting transfers between devices, shifted(): return lax.ppermute(x, axis, [(i, (i + by) % size) for i in range(size)])  4.71 us
    unnamed x47, local copies, waits for them, and re-layouts  4.41 us
    pallas_call x1, Pallas kernels, inner(): pl.pallas_call(functools.partial(inner_kernel, heads), out_shape=(pltpu.V...  4.19 us
    ppermute x4, waiting for transfers between devices, shifted(): return lax.ppermute(x, axis, [(i, (i + by) % size) for i in range(size)])  4.18 us
  transfers between devices with their start and end apart: 22, of which 12 were waited for; matrix products, arithmetic and copies ran while one was open for 2% of the time, Pallas kernels for 39%

profile of v7, /device:TPU:0, one launch (start us, length us, event | category | flops | bytes accessed | tf_op | source)
XLA Modules:
  0.0 104.7 jit_solution(14936532660502737603)
XLA Ops:
  0.0 0.5 collective-permute-start.3
  0.5 2.1 %shard_map.118 = (bf16[512,256]{1,0:T(8,128)(2,1)}, bf16[512,256]{1,0:T(8,128)(2,1)S(1)}, bf16[512,512]{1,0:T(8,128)(2,1)}) custom-call(bf16[512,1024]{1,0:T(8,128)(2,1)} %refs_6_.4), custom_call_target="tpu_custom_call" | custom-call | flops 1000000 | bytes 100000 | tf_op jit(solution)/shard_map/pallas_call | solution.py:70
  2.6 2.6 %collective-permute-start.1 = (bf16[512,256]{1,0:T(8,128)(2,1)}, bf16[512,256]{1,0:T(8,128)(2,1)S(1)}, u32[]{:S(2)}, u32[]{:S(2)}) collective-permute-start(bf16[512,256]{1,0:T(8,128)(2,1)} %get-tuple-element.75), channel_id=1, source_target_pairs={{0,2},{1,3},{2,0},{3,1},{4,6},{5,7},{6,4},{7,5},{8,10},{9,11},{10,... | collective-permute-start | bytes 786440 | tf_op jit(solution)/shard_map/ppermute | solution.py:27
  5.2 0.1 collective-permute-start.2
  5.2 1.9 %collective-permute-start = (bf16[512,512]{1,0:T(8,128)(2,1)}, bf16[512,512]{1,0:T(8,128)(2,1)S(1)}, u32[]{:S(2)}, u32[]{:S(2)}) collective-permute-start(bf16[512,512]{1,0:T(8,128)(2,1)} %get-tuple-element.74), channel_id=1, source_target_pairs={{0,2},{1,3},{2,0},{3,1},{4,6},{5,7},{6,4},{7,5},{8,10},{9,11},{10,... | collective-permute-start | bytes 1572872 | tf_op jit(solution)/shard_map/ppermute | solution.py:27
  7.2 0.8 reshape.3.refs_5_.refs_7_.refs_4_
  8.0 0.1 pad_add_fusion.info.refs_3_.refs_5_.refs_6_.refs_4_
  8.1 1.2 %copy-done.6 = bf16[512,1024]{1,0:T(8,128)(2,1)S(1)} copy-done((bf16[512,1024]{1,0:T(8,128)(2,1)S(1)}, bf16[512,1024]{1,0:T(8,128)(2,1)}, u32[]{:S(2)}) %copy-start.6) | copy-done | bytes 1048600
  9.3 8.0 %shard_map.119 = (f32[512,512]{1,0:T(8,128)S(1)}, f32[512,1024]{1,0:T(8,128)S(1)}, f32[512,512]{1,0:T(8,128)S(1)}, f32[4,512]{1,0:T(4,128)S(1)}) custom-call(s32[3]{0:T(128)S(1)} %pad_add_fusion.info.refs_3_.refs_5_.refs_6_.refs_4_, bf16[512,1024]{1,0:T(8,128)(2,1)S(1)} %copy-done.6, bf16[512,1024]{1,0:T(8,128)(2,1)S(1)} %collective-permute-done.3.refs_1_.refs_7_, ...), custom_call_target="tpu_custom_call" | custom-call | flops 1000000 | bytes 100000 | tf_op jit(solution)/shard_map/pallas_call | solution.py:183
  17.3 0.8 collective-permute-done.2.refs_2_.refs_6_
  18.2 0.5 collective-permute-start.5
  18.7 1.0 collective-permute-done.4.refs_1_.refs_5_
  19.7 0.4 collective-permute-done.5.refs_3_.refs_7_
  20.1 5.7 %shard_map.120 = (f32[512,512]{1,0:T(8,128)S(1)}, f32[512,1024]{1,0:T(8,128)S(1)}, f32[512,512]{1,0:T(8,128)S(1)}, f32[4,512]{1,0:T(4,128)S(1)}, bf16[1024,512]{...) custom-call(s32[3]{0:T(128)S(1)} %pad_add_fusion.info.refs_3_.refs_5, ...), custom_call_target="tpu_custom_call", output_to_operand_aliasing={{0}: (9, {}), {1}: (10, {}), {2}: (11, {}), {3}: (12, {})} | custom-call | flops 1000000 | bytes 100000 | tf_op jit(solution)/shard_map/pallas_call | solution.py:183
  25.8 3.4 %collective-permute-done.refs_0_.refs_4_.refs_8_ = bf16[512,512]{1,0:T(8,128)(2,1)S(1)} collective-permute-done((bf16[512,512]{1,0:T(8,128)(2,1)}, bf16[512,512]{1,0:T(8,128)(2,1)S(1)}, u32[]{:S(2)}, u32[]{:S(2)}) %collective-permute-start) | collective-permute-done | bytes 524320 | tf_op jit(solution)/shard_map/ppermute | solution.py:27
  29.2 1.9 %collective-permute-done.6.refs_1_.refs_5_.refs_9_ = bf16[512,512]{1,0:T(8,128)(2,1)S(1)} collective-permute-done((bf16[512,512]{1,0:T(8,128)(2,1)S(1)}, bf16[512,512]{1,0:T(8,128)(2,1)S(1)}, u32[]{:S(2)}, u32[]{:S(2)}) %collective-permute-start.6) | collective-permute-done | bytes 524320 | tf_op jit(solution)/shard_map/ppermute | solution.py:27
  31.1 3.7 %shard_map.121 = (bf16[512,512]{1,0:T(8,128)(2,1)S(1)}, bf16[512,1024]{1,0:T(8,128)(2,1)S(1)}, bf16[2,128,512]{2,1,0:T(8,128)(2,1)S(1)}, bf16[2,128,512]{2,1,0:T...) custom-call(s32[3]{0:T(128)S(1)} %pad_add_fusion.info.refs_3_.refs_5_.refs_6_.refs_4_, s32[4]{0:T(128)S(1)} %copy-done.18, ...), custom_call_target="tpu_custom_call" | custom-call | flops 4000000000 | bytes 4000000 | tf_op jit(solution)/shard_map/pallas_call | solution.py:281
  34.8 1.8 %collective-permute-start.8 = (bf16[2,128,512]{2,1,0:T(8,128)(2,1)S(1)}, bf16[2,128,512]{2,1,0:T(8,128)(2,1)S(1)}, u32[]{:S(2)}, u32[]{:S(2)}) collective-permute-start(bf16[2,128,512]{2,1,0:T(8,128)(2,1)S(1)} %get-tuple-element.98), channel_id=1, source_target_pairs={{0,4},{4,0},{8,12},{12,8},{16,20},{20,16},{24,28},{28,24},{1,5},{5... | collective-permute-start | bytes 786440 | tf_op jit(solution)/shard_map/ppermute | solution.py:27
  36.6 0.3 collective-permute-start.7
  36.9 2.6 %shard_map.122.refs_2_.refs_4_.query = bf16[512,512]{1,0:T(8,128)(2,1)S(1)} custom-call(bf16[512,512]{1,0:T(8,128)(2,1)S(1)} %get-tuple-element.99.refs_0_.key, bf16[512,1024]{1,0:T(8,128)(2,1)S(1)} %get-tuple-element.100.refs_1_.value, bf16[2,128,512]{2,1,0:T(8,128)(2,1)S(1)} %get-tuple-element.101.refs_2_.refs_7_.refs_8_, ...), custom_call_target="tpu_custom_call" | custom-call | flops 1000000 | bytes 100000 | tf_op jit(solution)/shard_map/pallas_call | solution.py:183
  39.6 5.7 %shard_map.123.refs_9_ = f32[512,1024]{1,0:T(8,128)S(1)} custom-call(bf16[512,512]{1,0:T(8,128)(2,1)S(1)} %get-tuple-element.99.refs_0_.key, bf16[512,1024]{1,0:T(8,128)(2,1)S(1)} %get-tuple-element.100.refs_1_.value, bf16[2,128,512]{2,1,0:T(8,128)(2,1)S(1)} %get-tuple-element.101.refs_2_.refs_7_.refs_8_, ...), custom_call_target="tpu_custom_call" | custom-call | flops 1000000 | bytes 100000 | tf_op jit(solution)/shard_map/pallas_call | solution.py:183
  45.3 0.0 copy-start.13
  45.4 0.8 shard_map.124
  46.2 1.8 %collective-permute-start.10 = (bf16[2,128,512]{2,1,0:T(8,128)(2,1)S(1)}, bf16[2,128,512]{2,1,0:T(8,128)(2,1)}, u32[]{:S(2)}, u32[]{:S(2)}) collective-permute-start(bf16[2,128,512]{2,1,0:T(8,128)(2,1)S(1)} %get-tuple-element.113), channel_id=1, source_target_pairs={{0,8},{4,12},{8,16},{12,20},{16,24},{20,28},{24,0},{28,4},{1,9},{5... | collective-permute-start | bytes 786440 | tf_op jit(solution)/shard_map/ppermute | solution.py:32
  48.0 1.6 %collective-permute-start.9 = (f32[2,384]{1,0:T(2,128)S(1)}, f32[2,384]{1,0:T(2,128)S(1)}, u32[]{:S(2)}, u32[]{:S(2)}) collective-permute-start(f32[2,384]{1,0:T(2,128)S(1)} %get-tuple-element.112), channel_id=1, source_target_pairs={{0,8},{4,12},{8,16},{12,20},{16,24},{20,28},{24,0},{28,4},{1,9},{5... | collective-permute-start | bytes 9224 | tf_op jit(solution)/shard_map/ppermute | solution.py:32
  49.6 5.8 %shard_map.125.refs_5_.refs_3_.gate = f32[512,1024]{1,0:T(8,128)S(1)} custom-call(bf16[512,512]{1,0:T(8,128)(2,1)S(1)} %get-tuple-element.99.refs_0_.key, bf16[512,1024]{1,0:T(8,128)(2,1)S(1)} %get-tuple-element.100.refs_1_.value, bf16[2,128,512]{2,1,0:T(8,128)(2,1)S(1)} %get-tuple-element.101.refs_2_.refs_7_.refs_8_, ...), custom_call_target="tpu_custom_call" | custom-call | flops 1000000 | bytes 100000 | tf_op jit(solution)/shard_map/pallas_call | solution.py:183
  55.4 0.8 collective-permute-done.9.refs_10_
  56.3 0.8 collective-permute-start.12
  57.1 0.5 collective-permute-start.11
  57.5 0.1 copy.17.refs_16_
  57.6 1.0 copy-done.1
  58.7 1.0 copy-done.4
  59.7 0.9 copy-done.10
  60.7 1.6 %shard_map.126.refs_14_ = f32[2,128,512]{2,1,0:T(8,128)S(1)} custom-call(bf16[512,512]{1,0:T(8,128)(2,1)S(1)} %copy-done.1, bf16[512,1024]{1,0:T(8,128)(2,1)S(1)} %get-tuple-element.100.refs_1_.value, bf16[2,128,512]{2,1,0:T(8,128)(2,1)S(1)} %get-tuple-element.101.refs_2_.refs_7_.refs_8_, bf16[2,128,512]{2,1,0:T(8,128)(2,1)S(1)} %copy-done.10, ...), custom_call_target="tpu_custom_call" | custom-call | flops 1000000 | bytes 100000 | tf_op jit(solution)/shard_map/pallas_call | solution.py:411
  62.3 3.3 %collective-permute-done.11.refs_11_ = f32[2,384]{1,0:T(2,128)S(1)} collective-permute-done((f32[2,384]{1,0:T(2,128)S(1)}, f32[2,384]{1,0:T(2,128)S(1)}, u32[]{:S(2)}, u32[]{:S(2)}) %collective-permute-start.11) | collective-permute-done | bytes 3104 | tf_op jit(solution)/shard_map/ppermute | solution.py:32
  65.7 1.7 %shard_map.127 = (bf16[2,128,512]{2,1,0:T(8,128)(2,1)S(1)}, bf16[2,128,512]{2,1,0:T(8,128)(2,1)S(1)}, f32[2,256]{1,0:T(2,128)S(1)}, f32[2,128]{1,0:T(2,128)S(1)}) custom-call(bf16[512,512]{1,0:T(8,128)(2,1)S(1)} %copy-done.2, bf16[512,1024]{1,0:T(8,128)(2,1)S(1)} %get-tuple-element.100.refs_1_.value, bf16[512,512]{1,0:T(8,128)(2,1)S(1)} %copy-done.5, ...), custom_call_target="tpu_custom_call" | custom-call | flops 1000000 | bytes 100000 | tf_op jit(solution)/shard_map/pallas_call | solution.py:427
  67.4 1.3 %collective-permute-start.13 = (bf16[2,128,512]{2,1,0:T(8,128)(2,1)S(1)}, bf16[2,128,512]{2,1,0:T(8,128)(2,1)S(1)}, u32[]{:S(2)}, u32[]{:S(2)}) collective-permute-start(bf16[2,128,512]{2,1,0:T(8,128)(2,1)S(1)} %get-tuple-element.125), channel_id=1, source_target_pairs={{0,4},{4,0},{8,12},{12,8},{16,20},{20,16},{24,28},{28,24},{1,5},{5... | collective-permute-start | bytes 786440 | tf_op jit(solution)/shard_map/ppermute | solution.py:27
  68.7 4.2 %shard_map.128 = (f32[512,1024]{1,0:T(8,128)S(1)}, f32[512,1024]{1,0:T(8,128)S(1)}, bf16[1024,4096]{1,0:T(8,128)(2,1)S(1)}) custom-call(s32[3]{0:T(128)S(1)} %pad_add_fusion.info.refs_3_.refs_5_.refs_6_.refs_4_, s32[4]{0:T(128)S(1)} %copy-done.18, f32[2,128]{1,0:T(2,128)S(1)} %get-tuple-element.126.top_in, bf16[512,512]{1,0:T(8,128)(2,1)S(1)} %copy-done.5, ...), custom_call_target="tpu_custom_call" | custom-call | flops 1000000 | bytes 100000 | tf_op jit(solution)/shard_map/pallas_call | solution.py:499
  72.9 0.9 collective-permute-done.13.other
  73.8 2.1 %shard_map.129 = (bf16[512,1024]{1,0:T(8,128)(2,1)S(1)}, bf16[512,512]{1,0:T(8,128)(2,1)S(1)}, bf16[512,512]{1,0:T(8,128)(2,1)S(1)}) custom-call(s32[3]{0:T(128)S(1)} %pad_add_fusion.info.refs_3_.refs_5_.refs_6_.refs_4_, bf16[512,512]{1,0:T(8,128)(2,1)S(1)} %copy-done.5, bf16[2,128,512]{2,1,0:T(8,128)(2,1)S(1)} %get-tuple-element.124.own, ...), custom_call_target="tpu_custom_call" | custom-call | flops 3000000000 | bytes 8000000 | tf_op jit(solution)/shard_map/pallas_call | solution.py:543
  75.9 0.1 collective-permute-start.14
  76.0 1.8 %shard_map.130 = (bf16[512,512]{1,0:T(8,128)(2,1)S(1)}, bf16[512,512]{1,0:T(8,128)(2,1)S(1)}) custom-call(s32[3]{0:T(128)S(1)} %pad_add_fusion.info.refs_3_.refs_5_.refs_6_.refs_4_, bf16[512,1024]{1,0:T(8,128)(2,1)S(1)} %get-tuple-element.140.hidden, bf16[1024,4096]{1,0:T(8,128)(2,1)S(1)} %get-tuple-element.131.w), custom_call_target="tpu_custom_call" | custom-call | flops 1000000 | bytes 100000 | tf_op jit(solution)/shard_map/pallas_call | solution.py:564
  77.9 0.5 collective-permute-start.16
  78.4 0.1 copy.22
  78.5 0.1 convert_add_fusion.3
  78.7 1.3 %collective-permute-start.15 = (bf16[512,256]{1,0:T(8,128)(2,1)S(1)}, bf16[512,256]{1,0:T(8,128)(2,1)S(1)}, u32[]{:S(2)}, u32[]{:S(2)}) collective-permute-start(bf16[512,256]{1,0:T(8,128)(2,1)S(1)} %slice.99), channel_id=1, source_target_pairs={{0,2},{1,3},{2,0},{3,1},{4,6},{5,7},{6,4},{7,5},{8,10},{9,11},{10,... | collective-permute-start | bytes 786440 | tf_op jit(solution)/shard_map/ppermute | solution.py:27
  80.0 1.8 %shard_map.131 = (bf16[512,512]{1,0:T(8,128)(2,1)S(1)}, bf16[512,512]{1,0:T(8,128)(2,1)S(1)}) custom-call(s32[3]{0:T(128)S(1)} %pad_add_fusion.info.refs_3_.refs_5_.refs_6_.refs_4_, bf16[512,1024]{1,0:T(8,128)(2,1)S(1)} %get-tuple-element.140.hidden, bf16[1024,4096]{1,0:T(8,128)(2,1)S(1)} %get-tuple-element.131.w), custom_call_target="tpu_custom_call" | custom-call | flops 1000000 | bytes 100000 | tf_op jit(solution)/shard_map/pallas_call | solution.py:564
  81.9 0.1 collective-permute-start.18
  81.9 0.1 convert_add_fusion.2
  82.1 0.8 collective-permute-start.17
  83.0 1.8 %shard_map.132 = (bf16[512,512]{1,0:T(8,128)(2,1)S(1)}, bf16[512,512]{1,0:T(8,128)(2,1)S(1)}) custom-call(s32[3]{0:T(128)S(1)} %pad_add_fusion.info.refs_3_.refs_5_.refs_6_.refs_4_, bf16[512,1024]{1,0:T(8,128)(2,1)S(1)} %get-tuple-element.140.hidden, bf16[1024,4096]{1,0:T(8,128)(2,1)S(1)} %get-tuple-element.131.w), custom_call_target="tpu_custom_call" | custom-call | flops 1000000 | bytes 100000 | tf_op jit(solution)/shard_map/pallas_call | solution.py:564
  84.8 0.3 collective-permute-start.20
  85.1 2.9 %collective-permute-done.15 = bf16[512,256]{1,0:T(8,128)(2,1)S(1)} collective-permute-done((bf16[512,256]{1,0:T(8,128)(2,1)S(1)}, bf16[512,256]{1,0:T(8,128)(2,1)S(1)}, u32[]{:S(2)}, u32[]{:S(2)}) %collective-permute-start.15) | collective-permute-done | bytes 262176 | tf_op jit(solution)/shard_map/ppermute | solution.py:27
  87.9 0.2 fusion.8
  88.1 0.1 convert_add_fusion.1
  88.3 1.3 %collective-permute-start.19 = (bf16[512,256]{1,0:T(8,128)(2,1)S(1)}, bf16[512,256]{1,0:T(8,128)(2,1)S(1)}, u32[]{:S(2)}, u32[]{:S(2)}) collective-permute-start(bf16[512,256]{1,0:T(8,128)(2,1)S(1)} %slice.97), channel_id=1, source_target_pairs={{0,2},{1,3},{2,0},{3,1},{4,6},{5,7},{6,4},{7,5},{8,10},{9,11},{10,... | collective-permute-start | bytes 786440 | tf_op jit(solution)/shard_map/ppermute | solution.py:27
  89.7 0.1 convert_add_fusion
  89.9 0.8 collective-permute-start.21
  90.7 2.9 %collective-permute-done.17 = bf16[512,256]{1,0:T(8,128)(2,1)S(1)} collective-permute-done((bf16[512,256]{1,0:T(8,128)(2,1)S(1)}, bf16[512,256]{1,0:T(8,128)(2,1)S(1)}, u32[]{:S(2)}, u32[]{:S(2)}) %collective-permute-start.17) | collective-permute-done | bytes 262176 | tf_op jit(solution)/shard_map/ppermute | solution.py:27
  93.6 0.1 fusion.9
  93.7 5.5 %collective-permute-done.19 = bf16[512,256]{1,0:T(8,128)(2,1)S(1)} collective-permute-done((bf16[512,256]{1,0:T(8,128)(2,1)S(1)}, bf16[512,256]{1,0:T(8,128)(2,1)S(1)}, u32[]{:S(2)}, u32[]{:S(2)}) %collective-permute-start.19) | collective-permute-done | bytes 262176 | tf_op jit(solution)/shard_map/ppermute | solution.py:27
  99.2 0.1 fusion.10
  99.3 4.6 %collective-permute-done.21 = bf16[512,256]{1,0:T(8,128)(2,1)S(1)} collective-permute-done((bf16[512,256]{1,0:T(8,128)(2,1)S(1)}, bf16[512,256]{1,0:T(8,128)(2,1)S(1)}, u32[]{:S(2)}, u32[]{:S(2)}) %collective-permute-start.21) | collective-permute-done | bytes 262176 | tf_op jit(solution)/shard_map/ppermute | solution.py:27
  103.9 0.8 fusion.11
  (57 shorter events, 0.3 us)
Async XLA Ops:
  0.0 8.1 %collective-permute-start.3 = (bf16[512,1024]{1,0:T(8,128)(2,1)}, bf16[512,1024]{1,0:T(8,128)(2,1)S(1)}, u32[]{:S(2)}, u32[]{:S(2)}) collective-permute-start(bf16[512,1024]{1,0:T(8,128)(2,1)} %refs_6_.4), channel_id=1, source_target_pairs={{0,1},{1,0},{2,3},{3,2},{4,5},{5,4},{6,7},{7,6},{8,9},{9,8},{10,11... | collective-permute-start | bytes 3145736 | tf_op jit(solution)/shard_map/ppermute | solution.py:27
  2.6 14.7 %collective-permute-start.1 = (bf16[512,256]{1,0:T(8,128)(2,1)}, bf16[512,256]{1,0:T(8,128)(2,1)S(1)}, u32[]{:S(2)}, u32[]{:S(2)}) collective-permute-start(bf16[512,256]{1,0:T(8,128)(2,1)} %get-tuple-element.75), channel_id=1, source_target_pairs={{0,2},{1,3},{2,0},{3,1},{4,6},{5,7},{6,4},{7,5},{8,10},{9,11},{10,... | collective-permute-start | bytes 786440 | tf_op jit(solution)/shard_map/ppermute | solution.py:27
  5.2 13.0 %collective-permute-start.2 = (bf16[512,256]{1,0:T(8,128)(2,1)S(1)}, bf16[512,256]{1,0:T(8,128)(2,1)S(1)}, u32[]{:S(2)}, u32[]{:S(2)}) collective-permute-start(bf16[512,256]{1,0:T(8,128)(2,1)S(1)} %get-tuple-element.76), channel_id=1, source_target_pairs={{0,2},{1,3},{2,0},{3,1},{4,6},{5,7},{6,4},{7,5},{8,10},{9,11},{10,... | collective-permute-start | bytes 786440 | tf_op jit(solution)/shard_map/ppermute | solution.py:27
  5.2 24.0 %collective-permute-start = (bf16[512,512]{1,0:T(8,128)(2,1)}, bf16[512,512]{1,0:T(8,128)(2,1)S(1)}, u32[]{:S(2)}, u32[]{:S(2)}) collective-permute-start(bf16[512,512]{1,0:T(8,128)(2,1)} %get-tuple-element.74), channel_id=1, source_target_pairs={{0,2},{1,3},{2,0},{3,1},{4,6},{5,7},{6,4},{7,5},{8,10},{9,11},{10,... | collective-permute-start | bytes 1572872 | tf_op jit(solution)/shard_map/ppermute | solution.py:27
  8.1 1.2 %copy-start.6 = (bf16[512,1024]{1,0:T(8,128)(2,1)S(1)}, bf16[512,1024]{1,0:T(8,128)(2,1)}, u32[]{:S(2)}) copy-start(bf16[512,1024]{1,0:T(8,128)(2,1)} %refs_6_.4) | copy-start | bytes 3145732
  9.3 8.0 %copy-start.12 = (bf16[512,1024]{1,0:T(8,128)(2,1)}, bf16[512,1024]{1,0:T(8,128)(2,1)S(1)}, u32[]{:S(2)}) copy-start(bf16[512,1024]{1,0:T(8,128)(2,1)S(1)} %collective-permute-done.3.refs_1_.refs_7_) | copy-start | bytes 3145732
  17.3 8.5 %copy-start.14 = (bf16[512,256]{1,0:T(8,128)(2,1)}, bf16[512,256]{1,0:T(8,128)(2,1)S(1)}, u32[]{:S(2)}) copy-start(bf16[512,256]{1,0:T(8,128)(2,1)S(1)} %collective-permute-done.1.refs_0_.refs_4_) | copy-start | bytes 786436
  18.2 7.7 %copy-start.16 = (bf16[512,256]{1,0:T(8,128)(2,1)}, bf16[512,256]{1,0:T(8,128)(2,1)S(1)}, u32[]{:S(2)}) copy-start(bf16[512,256]{1,0:T(8,128)(2,1)S(1)} %collective-permute-done.2.refs_2_.refs_6_) | copy-start | bytes 786436
  18.2 13.0 %copy-start.18 = (s32[4]{0:T(128)S(1)}, s32[4]{0:T(128)}, u32[]{:S(2)}) copy-start(s32[4]{0:T(128)} %docs.3) | copy-start | bytes 52
  18.2 13.0 %copy-start.20 = (f32[2,2]{1,0:T(2,128)S(1)}, f32[2,2]{1,0:T(2,128)}, u32[]{:S(2)}) copy-start(f32[2,2]{1,0:T(2,128)} %bias.1) | copy-start | bytes 52
  18.2 1.5 %collective-permute-start.4 = (bf16[512,256]{1,0:T(8,128)(2,1)S(1)}, bf16[512,256]{1,0:T(8,128)(2,1)S(1)}, u32[]{:S(2)}, u32[]{:S(2)}) collective-permute-start(bf16[512,256]{1,0:T(8,128)(2,1)S(1)} %collective-permute-done.1.refs_0_.refs_4_), channel_id=1, source_target_pairs={{0,1},{1,0},{2,3},{3,2},{4,5},{5,4},{6,7},{7,6},{8,9},{9,8},{10,11... | collective-permute-start | bytes 786440 | tf_op jit(solution)/shard_map/ppermute | solution.py:27
  18.2 1.9 %collective-permute-start.5 = (bf16[512,256]{1,0:T(8,128)(2,1)S(1)}, bf16[512,256]{1,0:T(8,128)(2,1)S(1)}, u32[]{:S(2)}, u32[]{:S(2)}) collective-permute-start(bf16[512,256]{1,0:T(8,128)(2,1)S(1)} %collective-permute-done.2.refs_2_.refs_6_), channel_id=1, source_target_pairs={{0,1},{1,0},{2,3},{3,2},{4,5},{5,4},{6,7},{7,6},{8,9},{9,8},{10,11... | collective-permute-start | bytes 786440 | tf_op jit(solution)/shard_map/ppermute | solution.py:27
  29.2 1.9 %collective-permute-start.6 = (bf16[512,512]{1,0:T(8,128)(2,1)S(1)}, bf16[512,512]{1,0:T(8,128)(2,1)S(1)}, u32[]{:S(2)}, u32[]{:S(2)}) collective-permute-start(bf16[512,512]{1,0:T(8,128)(2,1)S(1)} %collective-permute-done.refs_0_.refs_4_.refs_8_), channel_id=1, source_target_pairs={{0,1},{1,0},{2,3},{3,2},{4,5},{5,4},{6,7},{7,6},{8,9},{9,8},{10,11... | collective-permute-start | bytes 1572872 | tf_op jit(solution)/shard_map/ppermute | solution.py:27
  34.8 14.8 %copy-start = (bf16[512,512]{1,0:T(8,128)(2,1)}, bf16[512,512]{1,0:T(8,128)(2,1)S(1)}, u32[]{:S(2)}) copy-start(bf16[512,512]{1,0:T(8,128)(2,1)S(1)} %get-tuple-element.99.refs_0_.key) | copy-start | bytes 1572868
  34.8 10.5 %collective-permute-start.8 = (bf16[2,128,512]{2,1,0:T(8,128)(2,1)S(1)}, bf16[2,128,512]{2,1,0:T(8,128)(2,1)S(1)}, u32[]{:S(2)}, u32[]{:S(2)}) collective-permute-start(bf16[2,128,512]{2,1,0:T(8,128)(2,1)S(1)} %get-tuple-element.98), channel_id=1, source_target_pairs={{0,4},{4,0},{8,12},{12,8},{16,20},{20,16},{24,28},{28,24},{1,5},{5... | collective-permute-start | bytes 786440 | tf_op jit(solution)/shard_map/ppermute | solution.py:27
  36.6 8.7 %collective-permute-start.7 = (f32[2,384]{1,0:T(2,128)S(1)}, f32[2,384]{1,0:T(2,128)S(1)}, u32[]{:S(2)}, u32[]{:S(2)}) collective-permute-start(f32[2,384]{1,0:T(2,128)S(1)} %get-tuple-element.97.refs_5_.refs_6_), channel_id=1, source_target_pairs={{0,4},{4,0},{8,12},{12,8},{16,20},{20,16},{24,28},{28,24},{1,5},{5... | collective-permute-start | bytes 9224 | tf_op jit(solution)/shard_map/ppermute | solution.py:27
  36.9 2.7 %copy-start.15 = (bf16[512,256]{1,0:T(8,128)(2,1)S(1)}, bf16[512,256]{1,0:T(8,128)(2,1)}, u32[]{:S(2)}) copy-start(bf16[512,256]{1,0:T(8,128)(2,1)} %copy-done.14) | copy-start | bytes 786436
  36.9 2.7 %copy-start.17 = (bf16[512,256]{1,0:T(8,128)(2,1)S(1)}, bf16[512,256]{1,0:T(8,128)(2,1)}, u32[]{:S(2)}) copy-start(bf16[512,256]{1,0:T(8,128)(2,1)} %copy-done.16) | copy-start | bytes 786436
  39.6 10.0 %copy-start.3 = (bf16[512,512]{1,0:T(8,128)(2,1)}, bf16[512,512]{1,0:T(8,128)(2,1)S(1)}, u32[]{:S(2)}) copy-start(bf16[512,512]{1,0:T(8,128)(2,1)S(1)} %shard_map.122.refs_2_.refs_4_.query) | copy-start | bytes 1572868
  45.3 4.3 %copy-start.7 = (bf16[512,1024]{1,0:T(8,128)(2,1)S(1)}, bf16[512,1024]{1,0:T(8,128)(2,1)}, u32[]{:S(2)}) copy-start(bf16[512,1024]{1,0:T(8,128)(2,1)} %refs_6_.4) | copy-start | bytes 3145732
  45.3 4.3 %copy-start.13 = (bf16[512,1024]{1,0:T(8,128)(2,1)S(1)}, bf16[512,1024]{1,0:T(8,128)(2,1)}, u32[]{:S(2)}) copy-start(bf16[512,1024]{1,0:T(8,128)(2,1)} %copy-done.12) | copy-start | bytes 3145732
  45.4 10.0 %copy-start.9 = (bf16[2,128,512]{2,1,0:T(8,128)(2,1)}, bf16[2,128,512]{2,1,0:T(8,128)(2,1)S(1)}, u32[]{:S(2)}) copy-start(bf16[2,128,512]{2,1,0:T(8,128)(2,1)S(1)} %collective-permute-done.8.refs_8_.refs_3_.refs_9_) | copy-start | bytes 786436
  46.2 10.1 %collective-permute-start.10 = (bf16[2,128,512]{2,1,0:T(8,128)(2,1)S(1)}, bf16[2,128,512]{2,1,0:T(8,128)(2,1)}, u32[]{:S(2)}, u32[]{:S(2)}) collective-permute-start(bf16[2,128,512]{2,1,0:T(8,128)(2,1)S(1)} %get-tuple-element.113), channel_id=1, source_target_pairs={{0,8},{4,12},{8,16},{12,20},{16,24},{20,28},{24,0},{28,4},{1,9},{5... | collective-permute-start | bytes 786440 | tf_op jit(solution)/shard_map/ppermute | solution.py:32
  48.0 9.5 %copy-start.22 = (f32[2]{0:T(128)S(1)}, f32[2]{0:T(128)}, u32[]{:S(2)}) copy-start(f32[2]{0:T(128)} %param.22) | copy-start | bytes 28
  48.0 8.2 %collective-permute-start.9 = (f32[2,384]{1,0:T(2,128)S(1)}, f32[2,384]{1,0:T(2,128)S(1)}, u32[]{:S(2)}, u32[]{:S(2)}) collective-permute-start(f32[2,384]{1,0:T(2,128)S(1)} %get-tuple-element.112), channel_id=1, source_target_pairs={{0,8},{4,12},{8,16},{12,20},{16,24},{20,28},{24,0},{28,4},{1,9},{5... | collective-permute-start | bytes 9224 | tf_op jit(solution)/shard_map/ppermute | solution.py:32
  56.3 9.4 %collective-permute-start.12 = (bf16[2,128,512]{2,1,0:T(8,128)(2,1)}, bf16[2,128,512]{2,1,0:T(8,128)(2,1)}, u32[]{:S(2)}, u32[]{:S(2)}) collective-permute-start(bf16[2,128,512]{2,1,0:T(8,128)(2,1)} %collective-permute-done.10.refs_12_), channel_id=1, source_target_pairs={{0,8},{4,12},{8,16},{12,20},{16,24},{20,28},{24,0},{28,4},{1,9},{5... | collective-permute-start | bytes 786440 | tf_op jit(solution)/shard_map/ppermute | solution.py:32
  57.1 8.5 %collective-permute-start.11 = (f32[2,384]{1,0:T(2,128)S(1)}, f32[2,384]{1,0:T(2,128)S(1)}, u32[]{:S(2)}, u32[]{:S(2)}) collective-permute-start(f32[2,384]{1,0:T(2,128)S(1)} %collective-permute-done.9.refs_10_), channel_id=1, source_target_pairs={{0,8},{4,12},{8,16},{12,20},{16,24},{20,28},{24,0},{28,4},{1,9},{5... | collective-permute-start | bytes 9224 | tf_op jit(solution)/shard_map/ppermute | solution.py:32
  57.6 1.0 copy-start.1
  58.7 1.0 copy-start.4
  59.7 0.9 copy-start.10
  60.7 5.0 %copy-start.2 = (bf16[512,512]{1,0:T(8,128)(2,1)S(1)}, bf16[512,512]{1,0:T(8,128)(2,1)}, u32[]{:S(2)}) copy-start(bf16[512,512]{1,0:T(8,128)(2,1)} %copy-done) | copy-start | bytes 1572868
  60.7 5.0 %copy-start.5 = (bf16[512,512]{1,0:T(8,128)(2,1)S(1)}, bf16[512,512]{1,0:T(8,128)(2,1)}, u32[]{:S(2)}) copy-start(bf16[512,512]{1,0:T(8,128)(2,1)} %copy-done.3) | copy-start | bytes 1572868
  60.7 5.0 %copy-start.11 = (bf16[2,128,512]{2,1,0:T(8,128)(2,1)S(1)}, bf16[2,128,512]{2,1,0:T(8,128)(2,1)}, u32[]{:S(2)}) copy-start(bf16[2,128,512]{2,1,0:T(8,128)(2,1)} %copy-done.9) | copy-start | bytes 786436
  60.7 5.0 %copy-start.19 = (f32[2,256]{1,0:T(2,128)S(1)}, f32[2,256]{1,0:T(2,128)}, u32[]{:S(2)}) copy-start(f32[2,256]{1,0:T(2,128)} %refs_15_.1) | copy-start | bytes 6148
  67.4 6.4 %collective-permute-start.13 = (bf16[2,128,512]{2,1,0:T(8,128)(2,1)S(1)}, bf16[2,128,512]{2,1,0:T(8,128)(2,1)S(1)}, u32[]{:S(2)}, u32[]{:S(2)}) collective-permute-start(bf16[2,128,512]{2,1,0:T(8,128)(2,1)S(1)} %get-tuple-element.125), channel_id=1, source_target_pairs={{0,4},{4,0},{8,12},{12,8},{16,20},{20,16},{24,28},{28,24},{1,5},{5... | collective-permute-start | bytes 786440 | tf_op jit(solution)/shard_map/ppermute | solution.py:27
  75.9 2.6 %collective-permute-start.14 = (bf16[512,512]{1,0:T(8,128)(2,1)S(1)}, bf16[512,512]{1,0:T(8,128)(2,1)S(1)}, u32[]{:S(2)}, u32[]{:S(2)}) collective-permute-start(bf16[512,512]{1,0:T(8,128)(2,1)S(1)} %get-tuple-element.133), channel_id=1, source_target_pairs={{0,1},{1,0},{2,3},{3,2},{4,5},{5,4},{6,7},{7,6},{8,9},{9,8},{10,11... | collective-permute-start | bytes 1572872 | tf_op jit(solution)/shard_map/ppermute | solution.py:27
  76.0 2.4 %copy-start.8 = (bf16[512,1024]{1,0:T(8,128)(2,1)S(1)}, bf16[512,1024]{1,0:T(8,128)(2,1)}, u32[]{:S(2)}) copy-start(bf16[512,1024]{1,0:T(8,128)(2,1)} %refs_6_.4) | copy-start | bytes 3145732
  77.9 4.1 %collective-permute-start.16 = (bf16[512,512]{1,0:T(8,128)(2,1)S(1)}, bf16[512,512]{1,0:T(8,128)(2,1)S(1)}, u32[]{:S(2)}, u32[]{:S(2)}) collective-permute-start(bf16[512,512]{1,0:T(8,128)(2,1)S(1)} %get-tuple-element.136), channel_id=1, source_target_pairs={{0,1},{1,0},{2,3},{3,2},{4,5},{5,4},{6,7},{7,6},{8,9},{9,8},{10,11... | collective-permute-start | bytes 1572872 | tf_op jit(solution)/shard_map/ppermute | solution.py:27
  78.7 9.2 %collective-permute-start.15 = (bf16[512,256]{1,0:T(8,128)(2,1)S(1)}, bf16[512,256]{1,0:T(8,128)(2,1)S(1)}, u32[]{:S(2)}, u32[]{:S(2)}) collective-permute-start(bf16[512,256]{1,0:T(8,128)(2,1)S(1)} %slice.99), channel_id=1, source_target_pairs={{0,2},{1,3},{2,0},{3,1},{4,6},{5,7},{6,4},{7,5},{8,10},{9,11},{10,... | collective-permute-start | bytes 786440 | tf_op jit(solution)/shard_map/ppermute | solution.py:27
  81.9 6.3 %collective-permute-start.18 = (bf16[512,512]{1,0:T(8,128)(2,1)S(1)}, bf16[512,512]{1,0:T(8,128)(2,1)S(1)}, u32[]{:S(2)}, u32[]{:S(2)}) collective-permute-start(bf16[512,512]{1,0:T(8,128)(2,1)S(1)} %get-tuple-element.139), channel_id=1, source_target_pairs={{0,1},{1,0},{2,3},{3,2},{4,5},{5,4},{6,7},{7,6},{8,9},{9,8},{10,11... | collective-permute-start | bytes 1572872 | tf_op jit(solution)/shard_map/ppermute | solution.py:27
  82.1 11.4 %collective-permute-start.17 = (bf16[512,256]{1,0:T(8,128)(2,1)S(1)}, bf16[512,256]{1,0:T(8,128)(2,1)S(1)}, u32[]{:S(2)}, u32[]{:S(2)}) collective-permute-start(bf16[512,256]{1,0:T(8,128)(2,1)S(1)} %slice.98), channel_id=1, source_target_pairs={{0,2},{1,3},{2,0},{3,1},{4,6},{5,7},{6,4},{7,5},{8,10},{9,11},{10,... | collective-permute-start | bytes 786440 | tf_op jit(solution)/shard_map/ppermute | solution.py:27
  84.8 4.9 %collective-permute-start.20 = (bf16[512,512]{1,0:T(8,128)(2,1)S(1)}, bf16[512,512]{1,0:T(8,128)(2,1)S(1)}, u32[]{:S(2)}, u32[]{:S(2)}) collective-permute-start(bf16[512,512]{1,0:T(8,128)(2,1)S(1)} %get-tuple-element.142), channel_id=1, source_target_pairs={{0,1},{1,0},{2,3},{3,2},{4,5},{5,4},{6,7},{7,6},{8,9},{9,8},{10,11... | collective-permute-start | bytes 1572872 | tf_op jit(solution)/shard_map/ppermute | solution.py:27
  88.3 10.8 %collective-permute-start.19 = (bf16[512,256]{1,0:T(8,128)(2,1)S(1)}, bf16[512,256]{1,0:T(8,128)(2,1)S(1)}, u32[]{:S(2)}, u32[]{:S(2)}) collective-permute-start(bf16[512,256]{1,0:T(8,128)(2,1)S(1)} %slice.97), channel_id=1, source_target_pairs={{0,2},{1,3},{2,0},{3,1},{4,6},{5,7},{6,4},{7,5},{8,10},{9,11},{10,... | collective-permute-start | bytes 786440 | tf_op jit(solution)/shard_map/ppermute | solution.py:27
  89.9 14.0 %collective-permute-start.21 = (bf16[512,256]{1,0:T(8,128)(2,1)S(1)}, bf16[512,256]{1,0:T(8,128)(2,1)S(1)}, u32[]{:S(2)}, u32[]{:S(2)}) collective-permute-start(bf16[512,256]{1,0:T(8,128)(2,1)S(1)} %slice.96), channel_id=1, source_target_pairs={{0,2},{1,3},{2,0},{3,1},{4,6},{5,7},{6,4},{7,5},{8,10},{9,11},{10,... | collective-permute-start | bytes 786440 | tf_op jit(solution)/shard_map/ppermute | solution.py:27
  99.3 4.6 %copy-start.21 = (bf16[512,1024]{1,0:T(8,128)(2,1)}, bf16[512,1024]{1,0:T(8,128)(2,1)S(1)}, u32[]{:S(2)}) copy-start(bf16[512,1024]{1,0:T(8,128)(2,1)S(1)} %fusion.10) | copy-start | bytes 3145732

commit v8 on v7

--- a/solution.py
+++ b/solution.py
@@ -90,7 +90,7 @@
     result = []
     for i, (w, target) in enumerate(zip(weights, targets)):
         low, group = 0, []
-        for p, (owner, first, count) in enumerate(at):
+        for p, (owner, first, count) in enumerate(at[i]):
             group.append(
                 pltpu.make_async_copy(
                     w.at[pl.ds(row_start(place, share, owner, first), count)],
@@ -103,20 +103,21 @@
     return result
 
 
-def stage_kernel(xs_at, ahead_at, share, names, with_sum, finishes, gated, info, *refs):
+def stage_kernel(xs_at, skips, ahead_at, share, summed, finishes, gated, info, *refs):
     refs = list(refs)
     take = lambda n: [refs.pop(0) for _ in range(n)]
-    count_w = names
+    count_w, with_sum = len(skips), bool(summed)
     xs, ws = take(len(xs_at)), take(count_w)
     gate_w = take(1)[0] if gated else None
-    sums = take(count_w + gated) if with_sum else None
+    sums = [take(1)[0] if i in summed else None for i in range(count_w + gated)]
     outs = take(count_w + gated)
     ahead = take(2) if ahead_at else []
     held = take(count_w)
     sems = take(1)[0]
     place = info[0]
-    now = copies_of(ws, held, sems, xs_at, place, share)
-    later = copies_of(ws, ahead, take(1)[0], ahead_at, place, share) if ahead_at else []
+    at = [xs_at[skip:] for skip in skips]
+    now = copies_of(ws, held, sems, at, place, share)
+    later = copies_of(ws, ahead, take(1)[0], [ahead_at] * 2, place, share) if ahead_at else []
     for group in now + later:
         for copy in group:
             copy.start()
@@ -133,9 +134,9 @@
 
         def body(j, _, i=i):
             columns = pl.ds(pl.multiple_of(j * 256, 256), 256)
-            total = sums[i][:, columns] if with_sum else None
+            total = None if sums[i] is None else sums[i][:, columns]
             low = 0
-            for (_, _, count), x in zip(xs_at, xs):
+            for (_, _, count), x in zip(at[i], xs[skips[i] :]):
                 part = jnp.dot(
                     x[...], held[i][low : low + count, columns], preferred_element_type=F32
                 )
@@ -154,7 +155,7 @@
     return x
 
 
-def stage(info, xs, xs_at, weights, share, gate_w=None, sums=None, ahead_at=None, finishes=None, held=()):
+def stage(info, xs, xs_at, weights, share, gate_w=None, sums=None, ahead_at=None, finishes=None, held=(), skips=None):
     length = xs[0].shape[0]
     count = sum(c for _, _, c in xs_at)
     gated = int(gate_w is not None)
@@ -174,16 +175,18 @@
     if gated:
         operands.append(gate_w)
         specs.append(VMEM_SPEC)
-    aliases = {}
+    aliases, summed = {}, ()
     if sums is not None:
+        summed = tuple(i for i, x in enumerate(sums) if x is not None)
         if finishes is None:
             aliases = {len(operands) + i: i for i in range(len(sums))}
-        operands += in_vmem(*sums)
-        specs += [VMEM_SPEC] * len(sums)
+        operands += in_vmem(*[x for x in sums if x is not None])
+        specs += [VMEM_SPEC] * len(summed)
     return pl.pallas_call(
         holding(
             functools.partial(
-                stage_kernel, xs_at, ahead_at, share, len(weights), sums is not None, calls, gated
+                stage_kernel, xs_at, skips or [0] * len(weights), ahead_at, share, summed, calls,
+                gated,
             ),
             held,
         ),
@@ -511,19 +514,16 @@
     )(info, docs, *in_vmem(top, query, key, value, u, norm, gate), in_hbm(w_out))
 
 
-def some_columns(info, hidden, w, send, keep, start):
-    place = info[0]
-    wide = send.shape[1] // 2
+def some_columns(info, hidden, w, out, owners, start):
     share = w.shape[1] // 4
-    for step, owner in enumerate((1, 3, 0, 2)):
-        columns = pl.ds(pl.multiple_of((place ^ owner) * share + start, 128), wide)
-        part = jnp.dot(hidden[...], w[:, columns], preferred_element_type=F32).astype(BF)
-        out = (send, keep)[step // 2]
-        low = (step % 2) * wide
-        out[:, low : low + wide] = part
-
-
-def hidden_kernel(heads, info, query, own, other, base, slope, w, hidden, send, keep, state):
+    wide = out.shape[1] // 2
+    for step, owner in enumerate(owners):
+        columns = pl.ds(pl.multiple_of((info[0] ^ owner) * share + start, 128), wide)
+        part = jnp.dot(hidden[...], w[:, columns], preferred_element_type=F32)
+        out[:, step * wide : (step + 1) * wide] = part.astype(BF)
+
+
+def hidden_kernel(heads, info, query, own, other, base, slope, w, hidden, send, state):
     half = own.shape[1]
     side = info[1]
     size, wide = 2 * half, own.shape[2]
@@ -535,37 +535,38 @@
         )
         columns = slice(h * wide, (h + 1) * wide)
         hidden[:, columns] = (base[:, columns] + slope[:, columns] * outer).astype(BF)
-    some_columns(info, hidden, w, send, keep, 0)
+    some_columns(info, hidden, w, send, (1, 3), 0)
 
 
 def hidden_and_first(info, query, own, other, base, slope, w_here, wide, heads):
     length, depth = base.shape
     return pl.pallas_call(
         functools.partial(hidden_kernel, heads),
-        out_shape=(
-            pltpu.VMEM((length, depth), BF),
-            pltpu.VMEM((length, 2 * wide), BF),
-            pltpu.VMEM((length, 2 * wide), BF),
-        ),
+        out_shape=(pltpu.VMEM((length, depth), BF), pltpu.VMEM((length, 2 * wide), BF)),
         in_specs=[SMEM_SPEC] + [VMEM_SPEC] * 6,
-        out_specs=(VMEM_SPEC,) * 3,
+        out_specs=(VMEM_SPEC,) * 2,
         scratch_shapes=[pltpu.VMEM((2 * own.shape[1], own.shape[2]), BF)],
         compiler_params=params(12),
         cost_estimate=cost(3e9, 8e6),
     )(info, *in_vmem(query, own, other, base, slope, w_here))
 
 
-def columns_kernel(start, info, hidden, w, send, keep):
-    some_columns(info, hidden, w, send, keep, start)
-
-
-def next_columns(info, hidden, w_here, wide, start):
+def columns_kernel(start, following, info, hidden, w, keep, *send):
+    if send:
+        some_columns(info, hidden, w, send[0], (1, 3), following)
+    some_columns(info, hidden, w, keep, (0, 2), start)
+
+
+def next_columns(info, hidden, w_here, start, wide, following):
     length = hidden.shape[0]
+    shapes = [pltpu.VMEM((length, 2 * wide), BF)]
+    if following:
+        shapes.append(pltpu.VMEM((length, 2 * following), BF))
     return pl.pallas_call(
-        functools.partial(columns_kernel, start),
-        out_shape=(pltpu.VMEM((length, 2 * wide), BF),) * 2,
+        functools.partial(columns_kernel, start, start + wide),
+        out_shape=tuple(shapes),
         in_specs=[SMEM_SPEC, VMEM_SPEC, VMEM_SPEC],
-        out_specs=(VMEM_SPEC,) * 2,
+        out_specs=(VMEM_SPEC,) * len(shapes),
         compiler_params=params(12),
         cost_estimate=cost(1e6, 1e5),
     )(info, *in_vmem(hidden, w_here))
@@ -599,7 +600,9 @@
     beside = tensor(tokens, 1)
     sizes = [c for chunks in TOKEN_CHUNKS for c in chunks]
     starts = [sum(sizes[:i]) for i in range(len(sizes))]
-    pieces = split_tokens(tokens, starts, sizes)
+    first = split_tokens(tokens, starts[:1], sizes[:1])
+    others = split_tokens(after(beside, tokens), starts[1:], sizes[1:])
+    pieces = [*first, *others]
     source = tokens
     pieces = [(s, c, tensor(x, 2)) for s, c, x in zip(starts, sizes, pieces)]
     groups = []
@@ -637,11 +640,11 @@
     got = pair(sent)
     held = (keys, values, kept)
     far_xs = after(keys, *[x for xs in far for x in xs])
-    (queries,) = stage(
-        info, far_xs[-len(far[-1]) :], at[-1], (w_query,), share, None, [sums[2]],
-        finishes=((unchanged, BF),), held=held,
-    )
-    gate = stage(info, far_xs, sum(at, []), (w_outgate,), share, held=held)
+    queries, *gate = stage(
+        info, far_xs, sum(at, []), (w_query, w_outgate), share, None, [sums[2], None],
+        finishes=((unchanged, BF), (unchanged, F32)), held=held,
+        skips=[len(far_xs) - len(far[-1]), 0],
+    )
     small_other, got, queries, *gate = lax.optimization_barrier(
         (small_other, got, queries, *gate)
     )
@@ -675,17 +678,17 @@
         info, doc_lengths, top_own, queries, keys, values, u, norm_in, gate, w_out, heads
     )
 
+    hidden, send = hidden_and_first(
+        info, queries, state_own, state_got, base, slope, w_here, OUT_CHUNKS[0], heads
+    )
     start = 0
     leaving, arriving = [], []
-    for wide in OUT_CHUNKS:
-        if start == 0:
-            hidden, send, keep = hidden_and_first(
-                info, queries, state_own, state_got, base, slope, w_here, wide, heads
-            )
-        else:
-            now = after(leaving[-2], hidden) if len(leaving) > 1 else hidden
-            send, keep = next_columns(info, now, w_here, wide, start)
-        both = keep.astype(F32) + tensor(send, 1).astype(F32)
+    for wide, following in zip(OUT_CHUNKS, OUT_CHUNKS[1:] + (0,)):
+        came = tensor(send, 1)
+        now = after(leaving[max(len(leaving) - 1, 0)], hidden) if leaving else hidden
+        keep, *send = next_columns(info, now, w_here, start, wide, following)
+        send = send[0] if send else None
+        both = keep.astype(F32) + came.astype(F32)
         leaving.append(both[:, wide:].astype(BF))
         arriving.append((start, wide, both[:, :wide], tensor(leaving[-1], 2)))
         start += wide

time: 105 us -> 102 us (0.971)
  waiting for transfers between devices: 28.4 us -> 25 us
  starting transfers between devices: 18.9 us -> 20 us
    ppermute x18, waiting for transfers between devices: 24.3 us -> 21.9 us  [swapped(): return lax.ppermute(x, axis, [(i, i ^ mask) for i in range(size)])]
    pallas_call x1 -> x2, Pallas kernels: 2.12 us -> 3.35 us  [split_tokens(): pl.pallas_call(functools.partial(split_kernel, starts), out_shape=tuple((...]
    ppermute x4, waiting for transfers between devices: 4.18 us -> 3.13 us  [shifted(): return lax.ppermute(x, axis, [(i, (i + by) % size) for i in range(size)])]
    unnamed x47 -> x43, local copies, waits for them, and re-layouts: 4.41 us -> 5.06 us
  transfers between devices with their start and end apart: 22 -> 22, of which waited for: 12 -> 11; matrix products, arithmetic and copies ran while one was open for 2% -> 1% of each run, Pallas kernels for 39% -> 41%
where the time goes in v8:
time: 102 us
  Pallas kernels  49.5 us (49%)
  waiting for transfers between devices  25 us (25%)
  starting transfers between devices  20 us (20%)
  local copies, waits for them, and re-layouts  5.31 us (5%)
  other arithmetic  1.86 us (2%)
    pallas_call x4, Pallas kernels, stage(): pl.pallas_call(holding(functools.partial(stage_kernel, xs_at, skips or [0...  25.6 us
    ppermute x18, waiting for transfers between devices, swapped(): return lax.ppermute(x, axis, [(i, i ^ mask) for i in range(size)])  21.9 us
    ppermute x18, starting transfers between devices, swapped(): return lax.ppermute(x, axis, [(i, i ^ mask) for i in range(size)])  14.7 us
    pallas_call x4, Pallas kernels, next_columns(): pl.pallas_call(functools.partial(columns_kernel, start, start + wide), ou...  6.72 us
    ppermute x4, starting transfers between devices, shifted(): return lax.ppermute(x, axis, [(i, (i + by) % size) for i in range(size)])  5.28 us
    unnamed x43, local copies, waits for them, and re-layouts  5.06 us
    pallas_call x1, Pallas kernels, inner(): pl.pallas_call(functools.partial(inner_kernel, heads), out_shape=(pltpu.V...  4.19 us
    pallas_call x1, Pallas kernels, block_summary(): pl.pallas_call(functools.partial(summary_kernel, xs_at, share, heads), ou...  3.69 us
  transfers between devices with their start and end apart: 22, of which 11 were waited for; matrix products, arithmetic and copies ran while one was open for 1% of the time, Pallas kernels for 41%

profile of v8, /device:TPU:0, one launch (start us, length us, event | category | flops | bytes accessed | tf_op | source)
XLA Modules:
  0.0 102.0 jit_solution(8393059262197388019)
XLA Ops:
  0.0 0.5 collective-permute-start
  0.5 1.0 shard_map.119
  1.4 2.7 %collective-permute-start.2 = (bf16[512,256]{1,0:T(8,128)(2,1)S(1)}, bf16[512,256]{1,0:T(8,128)(2,1)S(1)}, u32[]{:S(2)}, u32[]{:S(2)}) collective-permute-start(bf16[512,256]{1,0:T(8,128)(2,1)S(1)} %shard_map.119), channel_id=1, source_target_pairs={{0,2},{1,3},{2,0},{3,1},{4,6},{5,7},{6,4},{7,5},{8,10},{9,11},{10,... | collective-permute-start | bytes 786440 | tf_op jit(solution)/shard_map/ppermute | solution.py:27
  4.1 2.4 %shard_map.118 = (bf16[512,256]{1,0:T(8,128)(2,1)}, bf16[512,512]{1,0:T(8,128)(2,1)}) custom-call(bf16[512,1024]{1,0:T(8,128)(2,1)} %refs_6_.2), custom_call_target="tpu_custom_call" | custom-call | flops 1000000 | bytes 100000 | tf_op jit(solution)/shard_map/pallas_call | solution.py:70
  6.5 1.8 %collective-permute-start.3 = (bf16[512,256]{1,0:T(8,128)(2,1)}, bf16[512,256]{1,0:T(8,128)(2,1)S(1)}, u32[]{:S(2)}, u32[]{:S(2)}) collective-permute-start(bf16[512,256]{1,0:T(8,128)(2,1)} %get-tuple-element.78), channel_id=1, source_target_pairs={{0,2},{1,3},{2,0},{3,1},{4,6},{5,7},{6,4},{7,5},{8,10},{9,11},{10,... | collective-permute-start | bytes 786440 | tf_op jit(solution)/shard_map/ppermute | solution.py:27
  8.3 0.3 collective-permute-start.1
  8.6 0.1 pad_add_fusion.info.refs_3_.refs_5_.refs_6_.refs_4_
  8.7 8.0 %shard_map.120 = (f32[512,512]{1,0:T(8,128)S(1)}, f32[512,1024]{1,0:T(8,128)S(1)}, f32[512,512]{1,0:T(8,128)S(1)}, f32[4,512]{1,0:T(4,128)S(1)}) custom-call(s32[3]{0:T(128)S(1)} %pad_add_fusion.info.refs_3_.refs_5_.refs_6_.refs_4_, bf16[512,1024]{1,0:T(8,128)(2,1)S(1)} %copy-done, bf16[512,1024]{1,0:T(8,128)(2,1)S(1)} %collective-permute-done.refs_1_.refs_7_, ...), custom_call_target="tpu_custom_call" | custom-call | flops 1000000 | bytes 100000 | tf_op jit(solution)/shard_map/pallas_call | solution.py:185
  16.7 0.1 collective-permute-done.3.refs_2_.refs_6_
  16.9 0.0 collective-permute-start.4
  16.9 0.5 collective-permute-start.5
  17.4 1.0 %collective-permute-done.4.refs_1_.refs_5_ = bf16[512,256]{1,0:T(8,128)(2,1)S(1)} collective-permute-done((bf16[512,256]{1,0:T(8,128)(2,1)S(1)}, bf16[512,256]{1,0:T(8,128)(2,1)S(1)}, u32[]{:S(2)}, u32[]{:S(2)}) %collective-permute-start.4) | collective-permute-done | bytes 262176 | tf_op jit(solution)/shard_map/ppermute | solution.py:27
  18.4 0.4 collective-permute-done.5.refs_3_.refs_7_
  18.8 5.7 %shard_map.121 = (f32[512,512]{1,0:T(8,128)S(1)}, f32[512,1024]{1,0:T(8,128)S(1)}, f32[512,512]{1,0:T(8,128)S(1)}, f32[4,512]{1,0:T(4,128)S(1)}, bf16[1024,512]{...) custom-call(s32[3]{0:T(128)S(1)} %pad_add_fusion.info.refs_3_.refs_5, ...), custom_call_target="tpu_custom_call", output_to_operand_aliasing={{0}: (9, {}), {1}: (10, {}), {2}: (11, {}), {3}: (12, {})} | custom-call | flops 1000000 | bytes 100000 | tf_op jit(solution)/shard_map/pallas_call | solution.py:185
  24.6 3.3 %collective-permute-done.1.refs_0_.refs_8_ = bf16[512,512]{1,0:T(8,128)(2,1)S(1)} collective-permute-done((bf16[512,512]{1,0:T(8,128)(2,1)}, bf16[512,512]{1,0:T(8,128)(2,1)S(1)}, u32[]{:S(2)}, u32[]{:S(2)}) %collective-permute-start.1) | collective-permute-done | bytes 524320 | tf_op jit(solution)/shard_map/ppermute | solution.py:27
  27.8 1.9 %collective-permute-done.6.refs_1_.refs_9_ = bf16[512,512]{1,0:T(8,128)(2,1)S(1)} collective-permute-done((bf16[512,512]{1,0:T(8,128)(2,1)S(1)}, bf16[512,512]{1,0:T(8,128)(2,1)S(1)}, u32[]{:S(2)}, u32[]{:S(2)}) %collective-permute-start.6) | collective-permute-done | bytes 524320 | tf_op jit(solution)/shard_map/ppermute | solution.py:27
  29.8 3.7 %shard_map.122 = (bf16[512,512]{1,0:T(8,128)(2,1)S(1)}, bf16[512,1024]{1,0:T(8,128)(2,1)S(1)}, bf16[2,128,512]{2,1,0:T(8,128)(2,1)S(1)}, bf16[2,128,512]{2,1,0:T...) custom-call(s32[3]{0:T(128)S(1)} %pad_add_fusion.info.refs_3_.refs_5_.refs_6_.refs_4_, s32[4]{0:T(128)S(1)} %copy-done.15, ...), custom_call_target="tpu_custom_call" | custom-call | flops 4000000000 | bytes 4000000 | tf_op jit(solution)/shard_map/pallas_call | solution.py:284
  33.5 1.8 %collective-permute-start.8 = (bf16[2,128,512]{2,1,0:T(8,128)(2,1)S(1)}, bf16[2,128,512]{2,1,0:T(8,128)(2,1)S(1)}, u32[]{:S(2)}, u32[]{:S(2)}) collective-permute-start(bf16[2,128,512]{2,1,0:T(8,128)(2,1)S(1)} %get-tuple-element.100), channel_id=1, source_target_pairs={{0,4},{4,0},{8,12},{12,8},{16,20},{20,16},{24,28},{28,24},{1,5},{5... | collective-permute-start | bytes 786440 | tf_op jit(solution)/shard_map/ppermute | solution.py:27
  35.3 0.3 collective-permute-start.7
  35.6 1.0 %copy-done.14 = bf16[512,512]{1,0:T(8,128)(2,1)S(1)} copy-done((bf16[512,512]{1,0:T(8,128)(2,1)S(1)}, bf16[512,512]{1,0:T(8,128)(2,1)}, u32[]{:S(2)}) %copy-start.14) | copy-done | bytes 524312
  36.6 6.1 %shard_map.123 = (bf16[512,512]{1,0:T(8,128)(2,1)S(1)}, f32[512,1024]{1,0:T(8,128)S(1)}) custom-call(bf16[512,512]{1,0:T(8,128)(2,1)S(1)} %get-tuple-element.101.refs_0_.key, bf16[512,1024]{1,0:T(8,128)(2,1)S(1)} %get-tuple-element.102.refs_1_.value, bf16[2,128,512]{2,1,0:T(8,128)(2,1)S(1)} %get-tuple-element.103.refs_2_.refs_7_.refs_8_, ...), custom_call_target="tpu_custom_call" | custom-call | flops 1000000 | bytes 100000 | tf_op jit(solution)/shard_map/pallas_call | solution.py:185
  42.7 0.0 copy-start.8
  42.7 0.8 shard_map.124
  43.5 1.9 %collective-permute-start.10 = (bf16[2,128,512]{2,1,0:T(8,128)(2,1)S(1)}, bf16[2,128,512]{2,1,0:T(8,128)(2,1)}, u32[]{:S(2)}, u32[]{:S(2)}) collective-permute-start(bf16[2,128,512]{2,1,0:T(8,128)(2,1)S(1)} %get-tuple-element.117), channel_id=1, source_target_pairs={{0,8},{4,12},{8,16},{12,20},{16,24},{20,28},{24,0},{28,4},{1,9},{5... | collective-permute-start | bytes 786440 | tf_op jit(solution)/shard_map/ppermute | solution.py:32
  45.4 1.6 %collective-permute-start.9 = (f32[2,384]{1,0:T(2,128)S(1)}, f32[2,384]{1,0:T(2,128)S(1)}, u32[]{:S(2)}, u32[]{:S(2)}) collective-permute-start(f32[2,384]{1,0:T(2,128)S(1)} %get-tuple-element.116), channel_id=1, source_target_pairs={{0,8},{4,12},{8,16},{12,20},{16,24},{20,28},{24,0},{28,4},{1,9},{5... | collective-permute-start | bytes 9224 | tf_op jit(solution)/shard_map/ppermute | solution.py:32
  47.0 5.8 %shard_map.125.refs_5_.refs_3_.gate = f32[512,1024]{1,0:T(8,128)S(1)} custom-call(bf16[512,512]{1,0:T(8,128)(2,1)S(1)} %get-tuple-element.101.refs_0_.key, bf16[512,1024]{1,0:T(8,128)(2,1)S(1)} %get-tuple-element.102.refs_1_.value, bf16[2,128,512]{2,1,0:T(8,128)(2,1)S(1)} %get-tuple-element.103.refs_2_.refs_7_.refs_8_, ...), custom_call_target="tpu_custom_call" | custom-call | flops 1000000 | bytes 100000 | tf_op jit(solution)/shard_map/pallas_call | solution.py:185
  52.8 1.3 %copy-done.1 = f32[512,1024]{1,0:T(8,128)} copy-done((f32[512,1024]{1,0:T(8,128)}, f32[512,1024]{1,0:T(8,128)S(1)}, u32[]{:S(2)}) %copy-start.1) | copy-done | bytes 2097176
  54.1 1.6 %collective-permute-start.12 = (bf16[2,128,512]{2,1,0:T(8,128)(2,1)}, bf16[2,128,512]{2,1,0:T(8,128)(2,1)}, u32[]{:S(2)}, u32[]{:S(2)}) collective-permute-start(bf16[2,128,512]{2,1,0:T(8,128)(2,1)} %collective-permute-done.10.refs_12_), channel_id=1, source_target_pairs={{0,8},{4,12},{8,16},{12,20},{16,24},{20,28},{24,0},{28,4},{1,9},{5... | collective-permute-start | bytes 786440 | tf_op jit(solution)/shard_map/ppermute | solution.py:32
  55.7 0.2 collective-permute-start.11
  55.9 0.1 copy.17.refs_16_
  56.0 1.6 %copy-done.2 = f32[512,1024]{1,0:T(8,128)S(1)} copy-done((f32[512,1024]{1,0:T(8,128)S(1)}, f32[512,1024]{1,0:T(8,128)}, u32[]{:S(2)}) %copy-start.2) | copy-done | bytes 2097176
  57.6 0.9 copy-done.5
  58.6 1.8 %shard_map.126.refs_14_ = f32[2,128,512]{2,1,0:T(8,128)S(1)} custom-call(bf16[512,512]{1,0:T(8,128)(2,1)S(1)} %get-tuple-element.101.refs_0_.key, bf16[512,1024]{1,0:T(8,128)(2,1)S(1)} %get-tuple-element.102.refs_1_.value, bf16[2,128,512]{2,1,0:T(8,128)(2,1)S(1)} %get-tuple-element.103.refs_2_.refs_7_.refs_8_, bf16[2,128,512]{2,1,0:T(8,128)(2,1)S(1)} %copy-done.5, ...), custom_call_target="tpu_custom_call" | custom-call | flops 1000000 | bytes 100000 | tf_op jit(solution)/shard_map/pallas_call | solution.py:414
  60.4 3.1 %collective-permute-done.11.refs_11_ = f32[2,384]{1,0:T(2,128)S(1)} collective-permute-done((f32[2,384]{1,0:T(2,128)S(1)}, f32[2,384]{1,0:T(2,128)S(1)}, u32[]{:S(2)}, u32[]{:S(2)}) %collective-permute-start.11) | collective-permute-done | bytes 3104 | tf_op jit(solution)/shard_map/ppermute | solution.py:32
  63.5 1.7 %shard_map.127 = (bf16[2,128,512]{2,1,0:T(8,128)(2,1)S(1)}, bf16[2,128,512]{2,1,0:T(8,128)(2,1)S(1)}, f32[2,256]{1,0:T(2,128)S(1)}, f32[2,128]{1,0:T(2,128)S(1)}) custom-call(bf16[512,512]{1,0:T(8,128)(2,1)S(1)} %get-tuple-element.101.refs_0_.key, bf16[512,1024]{1,0:T(8,128)(2,1)S(1)} %get-tuple-element.102.refs_1_.value, ...), custom_call_target="tpu_custom_call" | custom-call | flops 1000000 | bytes 100000 | tf_op jit(solution)/shard_map/pallas_call | solution.py:430
  65.2 1.6 %collective-permute-start.13 = (bf16[2,128,512]{2,1,0:T(8,128)(2,1)S(1)}, bf16[2,128,512]{2,1,0:T(8,128)(2,1)S(1)}, u32[]{:S(2)}, u32[]{:S(2)}) collective-permute-start(bf16[2,128,512]{2,1,0:T(8,128)(2,1)S(1)} %get-tuple-element.129), channel_id=1, source_target_pairs={{0,4},{4,0},{8,12},{12,8},{16,20},{20,16},{24,28},{28,24},{1,5},{5... | collective-permute-start | bytes 786440 | tf_op jit(solution)/shard_map/ppermute | solution.py:27
  66.8 4.2 %shard_map.128 = (f32[512,1024]{1,0:T(8,128)S(1)}, f32[512,1024]{1,0:T(8,128)S(1)}, bf16[1024,4096]{1,0:T(8,128)(2,1)S(1)}) custom-call(s32[3]{0:T(128)S(1)} %pad_add_fusion.info.refs_3_.refs_5_.refs_6_.refs_4_, s32[4]{0:T(128)S(1)} %copy-done.15, f32[2,128]{1,0:T(2,128)S(1)} %get-tuple-element.130.top_in, ...), custom_call_target="tpu_custom_call" | custom-call | flops 1000000 | bytes 100000 | tf_op jit(solution)/shard_map/pallas_call | solution.py:502
  71.0 0.7 collective-permute-done.13.other
  71.7 1.6 %shard_map.129 = (bf16[512,1024]{1,0:T(8,128)(2,1)S(1)}, bf16[512,512]{1,0:T(8,128)(2,1)S(1)}) custom-call(s32[3]{0:T(128)S(1)} %pad_add_fusion.info.refs_3_.refs_5_.refs_6_.refs_4_, bf16[512,512]{1,0:T(8,128)(2,1)S(1)} %get-tuple-element.113.refs_2_.refs_4_.query, bf16[2,128,512]{2,1,0:T(8,128)(2,1)S(1)} %get-tuple-element.128.own, ...), custom_call_target="tpu_custom_call" | custom-call | flops 3000000000 | bytes 8000000 | tf_op jit(solution)/shard_map/pallas_call | solution.py:543
  73.3 0.1 collective-permute-start.14
  73.4 1.8 %shard_map.130 = (bf16[512,512]{1,0:T(8,128)(2,1)S(1)}, bf16[512,512]{1,0:T(8,128)(2,1)S(1)}) custom-call(s32[3]{0:T(128)S(1)} %pad_add_fusion.info.refs_3_.refs_5_.refs_6_.refs_4_, bf16[512,1024]{1,0:T(8,128)(2,1)S(1)} %get-tuple-element.145.hidden, bf16[1024,4096]{1,0:T(8,128)(2,1)S(1)} %get-tuple-element.135.w), custom_call_target="tpu_custom_call" | custom-call | flops 1000000 | bytes 100000 | tf_op jit(solution)/shard_map/pallas_call | solution.py:565
  75.2 0.6 collective-permute-start.16
  75.8 0.1 copy.22
  75.9 0.1 convert_add_fusion.3
  76.1 1.6 %collective-permute-start.15 = (bf16[512,256]{1,0:T(8,128)(2,1)S(1)}, bf16[512,256]{1,0:T(8,128)(2,1)S(1)}, u32[]{:S(2)}, u32[]{:S(2)}) collective-permute-start(bf16[512,256]{1,0:T(8,128)(2,1)S(1)} %slice.99), channel_id=1, source_target_pairs={{0,2},{1,3},{2,0},{3,1},{4,6},{5,7},{6,4},{7,5},{8,10},{9,11},{10,... | collective-permute-start | bytes 786440 | tf_op jit(solution)/shard_map/ppermute | solution.py:27
  77.7 1.8 %shard_map.131 = (bf16[512,512]{1,0:T(8,128)(2,1)S(1)}, bf16[512,512]{1,0:T(8,128)(2,1)S(1)}) custom-call(s32[3]{0:T(128)S(1)} %pad_add_fusion.info.refs_3_.refs_5_.refs_6_.refs_4_, bf16[512,1024]{1,0:T(8,128)(2,1)S(1)} %get-tuple-element.145.hidden, bf16[1024,4096]{1,0:T(8,128)(2,1)S(1)} %get-tuple-element.135.w), custom_call_target="tpu_custom_call" | custom-call | flops 1000000 | bytes 100000 | tf_op jit(solution)/shard_map/pallas_call | solution.py:565
  79.5 0.1 collective-permute-start.18
  79.6 0.1 convert_add_fusion.2
  79.8 0.6 collective-permute-start.17
  80.4 1.8 %shard_map.132 = (bf16[512,512]{1,0:T(8,128)(2,1)S(1)}, bf16[512,512]{1,0:T(8,128)(2,1)S(1)}) custom-call(s32[3]{0:T(128)S(1)} %pad_add_fusion.info.refs_3_.refs_5_.refs_6_.refs_4_, bf16[512,1024]{1,0:T(8,128)(2,1)S(1)} %get-tuple-element.145.hidden, bf16[1024,4096]{1,0:T(8,128)(2,1)S(1)} %get-tuple-element.135.w), custom_call_target="tpu_custom_call" | custom-call | flops 1000000 | bytes 100000 | tf_op jit(solution)/shard_map/pallas_call | solution.py:565
  82.2 0.3 collective-permute-start.20
  82.5 2.9 %collective-permute-done.15 = bf16[512,256]{1,0:T(8,128)(2,1)S(1)} collective-permute-done((bf16[512,256]{1,0:T(8,128)(2,1)S(1)}, bf16[512,256]{1,0:T(8,128)(2,1)S(1)}, u32[]{:S(2)}, u32[]{:S(2)}) %collective-permute-start.15) | collective-permute-done | bytes 262176 | tf_op jit(solution)/shard_map/ppermute | solution.py:27
  85.3 0.2 fusion.8
  85.5 0.1 convert_add_fusion.1
  85.7 1.6 %collective-permute-start.19 = (bf16[512,256]{1,0:T(8,128)(2,1)S(1)}, bf16[512,256]{1,0:T(8,128)(2,1)S(1)}, u32[]{:S(2)}, u32[]{:S(2)}) collective-permute-start(bf16[512,256]{1,0:T(8,128)(2,1)S(1)} %slice.97), channel_id=1, source_target_pairs={{0,2},{1,3},{2,0},{3,1},{4,6},{5,7},{6,4},{7,5},{8,10},{9,11},{10,... | collective-permute-start | bytes 786440 | tf_op jit(solution)/shard_map/ppermute | solution.py:27
  87.3 1.3 %shard_map.133 = bf16[512,512]{1,0:T(8,128)(2,1)S(1)} custom-call(s32[3]{0:T(128)S(1)} %pad_add_fusion.info.refs_3_.refs_5_.refs_6_.refs_4_, bf16[512,1024]{1,0:T(8,128)(2,1)S(1)} %get-tuple-element.145.hidden, bf16[1024,4096]{1,0:T(8,128)(2,1)S(1)} %get-tuple-element.135.w), custom_call_target="tpu_custom_call" | custom-call | flops 1000000 | bytes 100000 | tf_op jit(solution)/shard_map/pallas_call | solution.py:565
  88.6 0.1 convert_add_fusion
  88.8 0.6 collective-permute-start.21
  89.4 1.6 %collective-permute-done.17 = bf16[512,256]{1,0:T(8,128)(2,1)S(1)} collective-permute-done((bf16[512,256]{1,0:T(8,128)(2,1)S(1)}, bf16[512,256]{1,0:T(8,128)(2,1)S(1)}, u32[]{:S(2)}, u32[]{:S(2)}) %collective-permute-start.17) | collective-permute-done | bytes 262176 | tf_op jit(solution)/shard_map/ppermute | solution.py:27
  90.9 0.1 fusion.9
  91.0 5.5 %collective-permute-done.19 = bf16[512,256]{1,0:T(8,128)(2,1)S(1)} collective-permute-done((bf16[512,256]{1,0:T(8,128)(2,1)S(1)}, bf16[512,256]{1,0:T(8,128)(2,1)S(1)}, u32[]{:S(2)}, u32[]{:S(2)}) %collective-permute-start.19) | collective-permute-done | bytes 262176 | tf_op jit(solution)/shard_map/ppermute | solution.py:27
  96.5 0.1 fusion.10
  96.7 4.6 %collective-permute-done.21 = bf16[512,256]{1,0:T(8,128)(2,1)S(1)} collective-permute-done((bf16[512,256]{1,0:T(8,128)(2,1)S(1)}, bf16[512,256]{1,0:T(8,128)(2,1)S(1)}, u32[]{:S(2)}, u32[]{:S(2)}) %collective-permute-start.21) | collective-permute-done | bytes 262176 | tf_op jit(solution)/shard_map/ppermute | solution.py:27
  101.2 0.8 fusion.11
  (54 shorter events, 0.3 us)
Async XLA Ops:
  0.0 8.7 %copy-start = (bf16[512,1024]{1,0:T(8,128)(2,1)S(1)}, bf16[512,1024]{1,0:T(8,128)(2,1)}, u32[]{:S(2)}) copy-start(bf16[512,1024]{1,0:T(8,128)(2,1)} %refs_6_.2) | copy-start | bytes 3145732
  0.0 8.6 %copy-start.19 = (bf16[2,4096,2]{1,2,0:T(2,128)(2,1)S(1)}, bf16[2,4096,2]{1,2,0:T(2,128)(2,1)}, u32[]{:S(2)}) copy-start(bf16[2,4096,2]{1,2,0:T(2,128)(2,1)} %param.17) | copy-start | bytes 98308
  0.0 4.1 %collective-permute-start = (bf16[512,1024]{1,0:T(8,128)(2,1)}, bf16[512,1024]{1,0:T(8,128)(2,1)S(1)}, u32[]{:S(2)}, u32[]{:S(2)}) collective-permute-start(bf16[512,1024]{1,0:T(8,128)(2,1)} %refs_6_.2), channel_id=1, source_target_pairs={{0,1},{1,0},{2,3},{3,2},{4,5},{5,4},{6,7},{7,6},{8,9},{9,8},{10,11... | collective-permute-start | bytes 3145736 | tf_op jit(solution)/shard_map/ppermute | solution.py:27
  1.4 15.3 %collective-permute-start.2 = (bf16[512,256]{1,0:T(8,128)(2,1)S(1)}, bf16[512,256]{1,0:T(8,128)(2,1)S(1)}, u32[]{:S(2)}, u32[]{:S(2)}) collective-permute-start(bf16[512,256]{1,0:T(8,128)(2,1)S(1)} %shard_map.119), channel_id=1, source_target_pairs={{0,2},{1,3},{2,0},{3,1},{4,6},{5,7},{6,4},{7,5},{8,10},{9,11},{10,... | collective-permute-start | bytes 786440 | tf_op jit(solution)/shard_map/ppermute | solution.py:27
  4.1 12.6 %copy-start.7 = (bf16[512,1024]{1,0:T(8,128)(2,1)}, bf16[512,1024]{1,0:T(8,128)(2,1)S(1)}, u32[]{:S(2)}) copy-start(bf16[512,1024]{1,0:T(8,128)(2,1)S(1)} %collective-permute-done.refs_1_.refs_7_) | copy-start | bytes 3145732
  6.5 10.4 %collective-permute-start.3 = (bf16[512,256]{1,0:T(8,128)(2,1)}, bf16[512,256]{1,0:T(8,128)(2,1)S(1)}, u32[]{:S(2)}, u32[]{:S(2)}) collective-permute-start(bf16[512,256]{1,0:T(8,128)(2,1)} %get-tuple-element.78), channel_id=1, source_target_pairs={{0,2},{1,3},{2,0},{3,1},{4,6},{5,7},{6,4},{7,5},{8,10},{9,11},{10,... | collective-permute-start | bytes 786440 | tf_op jit(solution)/shard_map/ppermute | solution.py:27
  8.3 19.5 %collective-permute-start.1 = (bf16[512,512]{1,0:T(8,128)(2,1)}, bf16[512,512]{1,0:T(8,128)(2,1)S(1)}, u32[]{:S(2)}, u32[]{:S(2)}) collective-permute-start(bf16[512,512]{1,0:T(8,128)(2,1)} %get-tuple-element.77), channel_id=1, source_target_pairs={{0,2},{1,3},{2,0},{3,1},{4,6},{5,7},{6,4},{7,5},{8,10},{9,11},{10,... | collective-permute-start | bytes 1572872 | tf_op jit(solution)/shard_map/ppermute | solution.py:27
  16.7 7.8 %copy-start.9 = (bf16[512,256]{1,0:T(8,128)(2,1)}, bf16[512,256]{1,0:T(8,128)(2,1)S(1)}, u32[]{:S(2)}) copy-start(bf16[512,256]{1,0:T(8,128)(2,1)S(1)} %collective-permute-done.2.refs_0_.refs_4_) | copy-start | bytes 786436
  16.9 7.7 %copy-start.11 = (bf16[512,256]{1,0:T(8,128)(2,1)}, bf16[512,256]{1,0:T(8,128)(2,1)S(1)}, u32[]{:S(2)}) copy-start(bf16[512,256]{1,0:T(8,128)(2,1)S(1)} %collective-permute-done.3.refs_2_.refs_6_) | copy-start | bytes 786436
  16.9 12.9 %copy-start.15 = (s32[4]{0:T(128)S(1)}, s32[4]{0:T(128)}, u32[]{:S(2)}) copy-start(s32[4]{0:T(128)} %docs.3) | copy-start | bytes 52
  16.9 12.9 %copy-start.17 = (f32[2,2]{1,0:T(2,128)S(1)}, f32[2,2]{1,0:T(2,128)}, u32[]{:S(2)}) copy-start(f32[2,2]{1,0:T(2,128)} %bias.1) | copy-start | bytes 52
  16.9 1.5 %collective-permute-start.4 = (bf16[512,256]{1,0:T(8,128)(2,1)S(1)}, bf16[512,256]{1,0:T(8,128)(2,1)S(1)}, u32[]{:S(2)}, u32[]{:S(2)}) collective-permute-start(bf16[512,256]{1,0:T(8,128)(2,1)S(1)} %collective-permute-done.2.refs_0_.refs_4_), channel_id=1, source_target_pairs={{0,1},{1,0},{2,3},{3,2},{4,5},{5,4},{6,7},{7,6},{8,9},{9,8},{10,11... | collective-permute-start | bytes 786440 | tf_op jit(solution)/shard_map/ppermute | solution.py:27
  16.9 1.9 %collective-permute-start.5 = (bf16[512,256]{1,0:T(8,128)(2,1)S(1)}, bf16[512,256]{1,0:T(8,128)(2,1)S(1)}, u32[]{:S(2)}, u32[]{:S(2)}) collective-permute-start(bf16[512,256]{1,0:T(8,128)(2,1)S(1)} %collective-permute-done.3.refs_2_.refs_6_), channel_id=1, source_target_pairs={{0,1},{1,0},{2,3},{3,2},{4,5},{5,4},{6,7},{7,6},{8,9},{9,8},{10,11... | collective-permute-start | bytes 786440 | tf_op jit(solution)/shard_map/ppermute | solution.py:27
  27.8 5.6 %copy-start.13 = (bf16[512,512]{1,0:T(8,128)(2,1)}, bf16[512,512]{1,0:T(8,128)(2,1)S(1)}, u32[]{:S(2)}) copy-start(bf16[512,512]{1,0:T(8,128)(2,1)S(1)} %collective-permute-done.1.refs_0_.refs_8_) | copy-start | bytes 1572868
  27.8 1.9 %collective-permute-start.6 = (bf16[512,512]{1,0:T(8,128)(2,1)S(1)}, bf16[512,512]{1,0:T(8,128)(2,1)S(1)}, u32[]{:S(2)}, u32[]{:S(2)}) collective-permute-start(bf16[512,512]{1,0:T(8,128)(2,1)S(1)} %collective-permute-done.1.refs_0_.refs_8_), channel_id=1, source_target_pairs={{0,1},{1,0},{2,3},{3,2},{4,5},{5,4},{6,7},{7,6},{8,9},{9,8},{10,11... | collective-permute-start | bytes 1572872 | tf_op jit(solution)/shard_map/ppermute | solution.py:27
  29.8 5.8 %copy-start.10 = (bf16[512,256]{1,0:T(8,128)(2,1)S(1)}, bf16[512,256]{1,0:T(8,128)(2,1)}, u32[]{:S(2)}) copy-start(bf16[512,256]{1,0:T(8,128)(2,1)} %copy-done.9) | copy-start | bytes 786436
  29.8 5.8 %copy-start.12 = (bf16[512,256]{1,0:T(8,128)(2,1)S(1)}, bf16[512,256]{1,0:T(8,128)(2,1)}, u32[]{:S(2)}) copy-start(bf16[512,256]{1,0:T(8,128)(2,1)} %copy-done.11) | copy-start | bytes 786436
  33.5 9.2 %collective-permute-start.8 = (bf16[2,128,512]{2,1,0:T(8,128)(2,1)S(1)}, bf16[2,128,512]{2,1,0:T(8,128)(2,1)S(1)}, u32[]{:S(2)}, u32[]{:S(2)}) collective-permute-start(bf16[2,128,512]{2,1,0:T(8,128)(2,1)S(1)} %get-tuple-element.100), channel_id=1, source_target_pairs={{0,4},{4,0},{8,12},{12,8},{16,20},{20,16},{24,28},{28,24},{1,5},{5... | collective-permute-start | bytes 786440 | tf_op jit(solution)/shard_map/ppermute | solution.py:27
  35.3 7.4 %collective-permute-start.7 = (f32[2,384]{1,0:T(2,128)S(1)}, f32[2,384]{1,0:T(2,128)S(1)}, u32[]{:S(2)}, u32[]{:S(2)}) collective-permute-start(f32[2,384]{1,0:T(2,128)S(1)} %get-tuple-element.99.refs_5_.refs_6_), channel_id=1, source_target_pairs={{0,4},{4,0},{8,12},{12,8},{16,20},{20,16},{24,28},{28,24},{1,5},{5... | collective-permute-start | bytes 9224 | tf_op jit(solution)/shard_map/ppermute | solution.py:27
  35.6 1.0 %copy-start.14 = (bf16[512,512]{1,0:T(8,128)(2,1)S(1)}, bf16[512,512]{1,0:T(8,128)(2,1)}, u32[]{:S(2)}) copy-start(bf16[512,512]{1,0:T(8,128)(2,1)} %copy-done.13) | copy-start | bytes 1572868
  42.7 4.3 %copy-start.8 = (bf16[512,1024]{1,0:T(8,128)(2,1)S(1)}, bf16[512,1024]{1,0:T(8,128)(2,1)}, u32[]{:S(2)}) copy-start(bf16[512,1024]{1,0:T(8,128)(2,1)} %copy-done.7) | copy-start | bytes 3145732
  42.7 10.0 %copy-start.4 = (bf16[2,128,512]{2,1,0:T(8,128)(2,1)}, bf16[2,128,512]{2,1,0:T(8,128)(2,1)S(1)}, u32[]{:S(2)}) copy-start(bf16[2,128,512]{2,1,0:T(8,128)(2,1)S(1)} %collective-permute-done.8.refs_8_.refs_3_.refs_9_) | copy-start | bytes 786436
  43.5 10.6 %collective-permute-start.10 = (bf16[2,128,512]{2,1,0:T(8,128)(2,1)S(1)}, bf16[2,128,512]{2,1,0:T(8,128)(2,1)}, u32[]{:S(2)}, u32[]{:S(2)}) collective-permute-start(bf16[2,128,512]{2,1,0:T(8,128)(2,1)S(1)} %get-tuple-element.117), channel_id=1, source_target_pairs={{0,8},{4,12},{8,16},{12,20},{16,24},{20,28},{24,0},{28,4},{1,9},{5... | collective-permute-start | bytes 786440 | tf_op jit(solution)/shard_map/ppermute | solution.py:32
  45.4 10.5 %copy-start.20 = (f32[2]{0:T(128)S(1)}, f32[2]{0:T(128)}, u32[]{:S(2)}) copy-start(f32[2]{0:T(128)} %param.22) | copy-start | bytes 28
  45.4 8.7 %collective-permute-start.9 = (f32[2,384]{1,0:T(2,128)S(1)}, f32[2,384]{1,0:T(2,128)S(1)}, u32[]{:S(2)}, u32[]{:S(2)}) collective-permute-start(f32[2,384]{1,0:T(2,128)S(1)} %get-tuple-element.116), channel_id=1, source_target_pairs={{0,8},{4,12},{8,16},{12,20},{16,24},{20,28},{24,0},{28,4},{1,9},{5... | collective-permute-start | bytes 9224 | tf_op jit(solution)/shard_map/ppermute | solution.py:32
  52.8 1.3 %copy-start.1 = (f32[512,1024]{1,0:T(8,128)}, f32[512,1024]{1,0:T(8,128)S(1)}, u32[]{:S(2)}) copy-start(f32[512,1024]{1,0:T(8,128)S(1)} %shard_map.125.refs_5_.refs_3_.gate) | copy-start | bytes 6291460
  54.1 9.4 %collective-permute-start.12 = (bf16[2,128,512]{2,1,0:T(8,128)(2,1)}, bf16[2,128,512]{2,1,0:T(8,128)(2,1)}, u32[]{:S(2)}, u32[]{:S(2)}) collective-permute-start(bf16[2,128,512]{2,1,0:T(8,128)(2,1)} %collective-permute-done.10.refs_12_), channel_id=1, source_target_pairs={{0,8},{4,12},{8,16},{12,20},{16,24},{20,28},{24,0},{28,4},{1,9},{5... | collective-permute-start | bytes 786440 | tf_op jit(solution)/shard_map/ppermute | solution.py:32
  55.7 7.8 %collective-permute-start.11 = (f32[2,384]{1,0:T(2,128)S(1)}, f32[2,384]{1,0:T(2,128)S(1)}, u32[]{:S(2)}, u32[]{:S(2)}) collective-permute-start(f32[2,384]{1,0:T(2,128)S(1)} %collective-permute-done.9.refs_10_), channel_id=1, source_target_pairs={{0,8},{4,12},{8,16},{12,20},{16,24},{20,28},{24,0},{28,4},{1,9},{5... | collective-permute-start | bytes 9224 | tf_op jit(solution)/shard_map/ppermute | solution.py:32
  56.0 1.6 %copy-start.2 = (f32[512,1024]{1,0:T(8,128)S(1)}, f32[512,1024]{1,0:T(8,128)}, u32[]{:S(2)}) copy-start(f32[512,1024]{1,0:T(8,128)} %copy-done.1) | copy-start | bytes 6291460
  57.6 0.9 copy-start.5
  58.6 4.9 %copy-start.3 = (f32[512,1024]{1,0:T(8,128)S(1)}, f32[512,1024]{1,0:T(8,128)}, u32[]{:S(2)}) copy-start(f32[512,1024]{1,0:T(8,128)} %copy-done.1) | copy-start | bytes 6291460
  58.6 4.9 %copy-start.6 = (bf16[2,128,512]{2,1,0:T(8,128)(2,1)S(1)}, bf16[2,128,512]{2,1,0:T(8,128)(2,1)}, u32[]{:S(2)}) copy-start(bf16[2,128,512]{2,1,0:T(8,128)(2,1)} %copy-done.4) | copy-start | bytes 786436
  58.6 4.9 %copy-start.16 = (f32[2,256]{1,0:T(2,128)S(1)}, f32[2,256]{1,0:T(2,128)}, u32[]{:S(2)}) copy-start(f32[2,256]{1,0:T(2,128)} %refs_15_.1) | copy-start | bytes 6148
  65.2 6.4 %collective-permute-start.13 = (bf16[2,128,512]{2,1,0:T(8,128)(2,1)S(1)}, bf16[2,128,512]{2,1,0:T(8,128)(2,1)S(1)}, u32[]{:S(2)}, u32[]{:S(2)}) collective-permute-start(bf16[2,128,512]{2,1,0:T(8,128)(2,1)S(1)} %get-tuple-element.129), channel_id=1, source_target_pairs={{0,4},{4,0},{8,12},{12,8},{16,20},{20,16},{24,28},{28,24},{1,5},{5... | collective-permute-start | bytes 786440 | tf_op jit(solution)/shard_map/ppermute | solution.py:27
  73.3 2.5 %collective-permute-start.14 = (bf16[512,512]{1,0:T(8,128)(2,1)S(1)}, bf16[512,512]{1,0:T(8,128)(2,1)S(1)}, u32[]{:S(2)}, u32[]{:S(2)}) collective-permute-start(bf16[512,512]{1,0:T(8,128)(2,1)S(1)} %get-tuple-element.138), channel_id=1, source_target_pairs={{0,1},{1,0},{2,3},{3,2},{4,5},{5,4},{6,7},{7,6},{8,9},{9,8},{10,11... | collective-permute-start | bytes 1572872 | tf_op jit(solution)/shard_map/ppermute | solution.py:27
  75.2 4.3 %collective-permute-start.16 = (bf16[512,512]{1,0:T(8,128)(2,1)S(1)}, bf16[512,512]{1,0:T(8,128)(2,1)S(1)}, u32[]{:S(2)}, u32[]{:S(2)}) collective-permute-start(bf16[512,512]{1,0:T(8,128)(2,1)S(1)} %get-tuple-element.141), channel_id=1, source_target_pairs={{0,1},{1,0},{2,3},{3,2},{4,5},{5,4},{6,7},{7,6},{8,9},{9,8},{10,11... | collective-permute-start | bytes 1572872 | tf_op jit(solution)/shard_map/ppermute | solution.py:27
  76.1 9.2 %collective-permute-start.15 = (bf16[512,256]{1,0:T(8,128)(2,1)S(1)}, bf16[512,256]{1,0:T(8,128)(2,1)S(1)}, u32[]{:S(2)}, u32[]{:S(2)}) collective-permute-start(bf16[512,256]{1,0:T(8,128)(2,1)S(1)} %slice.99), channel_id=1, source_target_pairs={{0,2},{1,3},{2,0},{3,1},{4,6},{5,7},{6,4},{7,5},{8,10},{9,11},{10,... | collective-permute-start | bytes 786440 | tf_op jit(solution)/shard_map/ppermute | solution.py:27
  79.5 6.0 %collective-permute-start.18 = (bf16[512,512]{1,0:T(8,128)(2,1)S(1)}, bf16[512,512]{1,0:T(8,128)(2,1)S(1)}, u32[]{:S(2)}, u32[]{:S(2)}) collective-permute-start(bf16[512,512]{1,0:T(8,128)(2,1)S(1)} %get-tuple-element.144), channel_id=1, source_target_pairs={{0,1},{1,0},{2,3},{3,2},{4,5},{5,4},{6,7},{7,6},{8,9},{9,8},{10,11... | collective-permute-start | bytes 1572872 | tf_op jit(solution)/shard_map/ppermute | solution.py:27
  79.8 11.1 %collective-permute-start.17 = (bf16[512,256]{1,0:T(8,128)(2,1)S(1)}, bf16[512,256]{1,0:T(8,128)(2,1)S(1)}, u32[]{:S(2)}, u32[]{:S(2)}) collective-permute-start(bf16[512,256]{1,0:T(8,128)(2,1)S(1)} %slice.98), channel_id=1, source_target_pairs={{0,2},{1,3},{2,0},{3,1},{4,6},{5,7},{6,4},{7,5},{8,10},{9,11},{10,... | collective-permute-start | bytes 786440 | tf_op jit(solution)/shard_map/ppermute | solution.py:27
  82.2 6.4 %collective-permute-start.20 = (bf16[512,512]{1,0:T(8,128)(2,1)S(1)}, bf16[512,512]{1,0:T(8,128)(2,1)S(1)}, u32[]{:S(2)}, u32[]{:S(2)}) collective-permute-start(bf16[512,512]{1,0:T(8,128)(2,1)S(1)} %get-tuple-element.146), channel_id=1, source_target_pairs={{0,1},{1,0},{2,3},{3,2},{4,5},{5,4},{6,7},{7,6},{8,9},{9,8},{10,11... | collective-permute-start | bytes 1572872 | tf_op jit(solution)/shard_map/ppermute | solution.py:27
  85.7 10.8 %collective-permute-start.19 = (bf16[512,256]{1,0:T(8,128)(2,1)S(1)}, bf16[512,256]{1,0:T(8,128)(2,1)S(1)}, u32[]{:S(2)}, u32[]{:S(2)}) collective-permute-start(bf16[512,256]{1,0:T(8,128)(2,1)S(1)} %slice.97), channel_id=1, source_target_pairs={{0,2},{1,3},{2,0},{3,1},{4,6},{5,7},{6,4},{7,5},{8,10},{9,11},{10,... | collective-permute-start | bytes 786440 | tf_op jit(solution)/shard_map/ppermute | solution.py:27
  88.8 12.4 %collective-permute-start.21 = (bf16[512,256]{1,0:T(8,128)(2,1)S(1)}, bf16[512,256]{1,0:T(8,128)(2,1)S(1)}, u32[]{:S(2)}, u32[]{:S(2)}) collective-permute-start(bf16[512,256]{1,0:T(8,128)(2,1)S(1)} %slice.96), channel_id=1, source_target_pairs={{0,2},{1,3},{2,0},{3,1},{4,6},{5,7},{6,4},{7,5},{8,10},{9,11},{10,... | collective-permute-start | bytes 786440 | tf_op jit(solution)/shard_map/ppermute | solution.py:27
  96.6 4.6 %copy-start.18 = (bf16[512,1024]{1,0:T(8,128)(2,1)}, bf16[512,1024]{1,0:T(8,128)(2,1)S(1)}, u32[]{:S(2)}) copy-start(bf16[512,1024]{1,0:T(8,128)(2,1)S(1)} %fusion.10) | copy-start | bytes 3145732

commit v9 on v8

--- a/solution.py
+++ b/solution.py
@@ -106,7 +106,7 @@
 def stage_kernel(xs_at, skips, ahead_at, share, summed, finishes, gated, info, *refs):
     refs = list(refs)
     take = lambda n: [refs.pop(0) for _ in range(n)]
-    count_w, with_sum = len(skips), bool(summed)
+    count_w = len(skips)
     xs, ws = take(len(xs_at)), take(count_w)
     gate_w = take(1)[0] if gated else None
     sums = [take(1)[0] if i in summed else None for i in range(count_w + gated)]
@@ -122,7 +122,7 @@
         for copy in group:
             copy.start()
     if gated:
-        gates = sums[count_w][...] if with_sum else 0.0
+        gates = 0.0 if sums[count_w] is None else sums[count_w][...]
         for (owner, first, count), x in zip(xs_at, xs):
             gates = gates + across_tokens(
                 gate_w[:, pl.ds(row_start(place, share, owner, first), count)], x[...]
@@ -153,6 +153,29 @@
 
 def unchanged(x):
     return x
+
+
+def twin_kernel(at, share, info, x, key_w, value_w, gate_w, *refs):
+    owner, first, count = at
+    for w, total, out in zip((key_w, value_w), refs[:2], refs[3:5]):
+        for low in range(0, out.shape[1], 512):
+            columns = slice(low, low + 512)
+            part = jnp.dot(x[...], w[:count, columns], preferred_element_type=F32)
+            out[:, columns] = total[:, columns] + part
+    rows = gate_w[:, pl.ds(row_start(info[0], share, owner, first), count)]
+    refs[5][...] = refs[2][...] + across_tokens(rows, x[...])
+
+
+def twin_stage(info, x, at, key_w, value_w, gate_w, sums, share):
+    return pl.pallas_call(
+        functools.partial(twin_kernel, at, share),
+        out_shape=tuple(pltpu.VMEM(y.shape, F32) for y in sums),
+        in_specs=[SMEM_SPEC] + [VMEM_SPEC] * 7,
+        out_specs=(VMEM_SPEC,) * 3,
+        input_output_aliases={5 + i: i for i in range(3)},
+        compiler_params=params(8),
+        cost_estimate=cost(1e6, 1e5),
+    )(info, *in_vmem(x, key_w, value_w), gate_w, *in_vmem(*sums))
 
 
 def stage(info, xs, xs_at, weights, share, gate_w=None, sums=None, ahead_at=None, finishes=None, held=(), skips=None):
@@ -179,7 +202,7 @@
     if sums is not None:
         summed = tuple(i for i, x in enumerate(sums) if x is not None)
         if finishes is None:
-            aliases = {len(operands) + i: i for i in range(len(sums))}
+            aliases = {len(operands) + n: i for n, i in enumerate(summed)}
         operands += in_vmem(*[x for x in sums if x is not None])
         specs += [VMEM_SPEC] * len(summed)
     return pl.pallas_call(
@@ -237,7 +260,7 @@
     return u, weight, stats
 
 
-def summary_kernel(xs_at, share, heads, info, docs, bias, *refs):
+def summary_kernel(xs_at, skip, share, heads, info, docs, bias, *refs):
     xs = refs[: len(xs_at)]
     key_w, value_w, gate_w, key_sum, value_sum, gate_sum = refs[len(xs_at) : len(xs_at) + 6]
     key_out, value_out, keep_out, send_out, small_out, u_out, state = refs[len(xs_at) + 6 :]
@@ -256,7 +279,7 @@
     half = size // 2
     for h in range(heads):
         key_at, value_at = slice(h * size, (h + 1) * size), slice(h * wide, (h + 1) * wide)
-        key, value, low = key_sum[:, key_at], value_sum[:, value_at], 0
+        key, value, low = key_sum[:, key_at], value_sum[:, value_at], skip
         for x in xs:
             count = x.shape[1]
             rows = slice(low, low + count)
@@ -277,12 +300,13 @@
 
 
 def block_summary(
-    info, docs, bias, xs, xs_at, key_w, value_w, gate_w, key_sum, value_sum, gates, share, heads
+    info, docs, bias, xs, xs_at, skip, key_w, value_w, gate_w, key_sum, value_sum, gates, share,
+    heads,
 ):
     length = xs[0].shape[0]
     size, wide = key_w.shape[1] // heads, value_w.shape[1] // heads
     return pl.pallas_call(
-        functools.partial(summary_kernel, xs_at, share, heads),
+        functools.partial(summary_kernel, xs_at, skip, share, heads),
         out_shape=(
             pltpu.VMEM((length, heads * size), BF),
             pltpu.VMEM((length, heads * wide), BF),
@@ -621,29 +645,34 @@
     for i, group in enumerate(groups):
         xs = lax.optimization_barrier((*[x for _, _, x in group], *sums))
         xs, sums = xs[: len(group)], xs[len(group) :]
+        if i == 0:
+            sums = [*sums[:3], None, sums[3]]
         xs = [y for x in xs for y in (x, tensor(x, 1))]
         far.append(xs)
         if i < len(groups) - 1:
             last = i == len(groups) - 2
             out = stage(
-                info, xs, at[i], first_three, share, gate_w, sums, at[-1] if last else None
+                info, xs, at[i], (*first_three, w_outgate), share, gate_w, sums,
+                at[-1] if last else None,
             )
-            sums = out[:4]
+            sums = out[:5]
             if last:
-                w_key_last, w_value_last = out[4:]
+                w_key_last, w_value_last = out[5:]
+    kv_sums = twin_stage(
+        info, xs[0], at[-1][0], w_key_last, w_value_last, gate_w, (*sums[:2], sums[4]), share
+    )
     keys, values, kept, sent, small, u = block_summary(
-        info, doc_lengths, gate_bias, xs, at[-1], w_key_last, w_value_last, gate_w,
-        sums[0], sums[1], sums[3], share, heads,
+        info, doc_lengths, gate_bias, xs[1:], at[-1][1:], at[-1][0][2], w_key_last, w_value_last,
+        gate_w, *kv_sums, share, heads,
     )
 
     small_other = pair(small)
     got = pair(sent)
     held = (keys, values, kept)
-    far_xs = after(keys, *[x for xs in far for x in xs])
+    now_xs = after(keys, beside, *far[-1])
     queries, *gate = stage(
-        info, far_xs, sum(at, []), (w_query, w_outgate), share, None, [sums[2], None],
-        finishes=((unchanged, BF), (unchanged, F32)), held=held,
-        skips=[len(far_xs) - len(far[-1]), 0],
+        info, now_xs, near_at[1:] + at[-1], (w_query, w_outgate), share, None, [sums[2], sums[3]],
+        finishes=((unchanged, BF), (unchanged, F32)), held=held, skips=[1, 0],
     )
     small_other, got, queries, *gate = lax.optimization_barrier(
         (small_other, got, queries, *gate)
@@ -657,9 +686,9 @@
         before = state_pair
         travel, state_pair = down(travel), down(state_pair)
         if step == 0:
-            near_xs = after(before, source, beside)
+            near_xs = [after(before, source)]
             gate = stage(
-                info, near_xs, near_at, (w_outgate,), share, None, gate,
+                info, near_xs, near_at[:1], (w_outgate,), share, None, gate,
                 finishes=((jax.nn.sigmoid, F32),), held=held,
             )
             travel, state_pair, *gate = lax.optimization_barrier((travel, state_pair, *gate))

time: 102 us -> 100 us (0.980)
  local copies, waits for them, and re-layouts: 5.31 us -> 4.25 us
    ppermute x18, waiting for transfers between devices: 21.9 us -> 19.2 us  [swapped(): return lax.ppermute(x, axis, [(i, i ^ mask) for i in range(size)])]
    ppermute x4, waiting for transfers between devices: 3.13 us -> 4.82 us  [shifted(): return lax.ppermute(x, axis, [(i, (i + by) % size) for i in range(size)])]
    unnamed x43 -> x35, local copies, waits for them, and re-layouts: 5.06 us -> 4 us
    pallas_call x1 -> x2, Pallas kernels: 3.69 us -> 4.51 us  [the longest x1 2.84 us: block_summary(): pl.pallas_call(functools.partial(summary_kernel, xs_at, skip, share, head...]
  transfers between devices with their start and end apart: 22 -> 22, of which waited for: 11 -> 13; matrix products, arithmetic and copies ran while one was open for 1% -> 1% of each run, Pallas kernels for 41% -> 43%
where the time goes in v9:
time: 100 us; the launch traced here: 99.9 us
  Pallas kernels  50.3 us (50%)
  waiting for transfers between devices  24 us (24%)
  starting transfers between devices  19.1 us (19%)
  local copies, waits for them, and re-layouts  4.25 us (4%)
  other arithmetic  1.86 us (2%)
    pallas_call x4, Pallas kernels, stage(): pl.pallas_call(holding(functools.partial(stage_kernel, xs_at, skips or [0...  25.6 us
    ppermute x18, waiting for transfers between devices, swapped(): return lax.ppermute(x, axis, [(i, i ^ mask) for i in range(size)])  19.2 us
    ppermute x18, starting transfers between devices, swapped(): return lax.ppermute(x, axis, [(i, i ^ mask) for i in range(size)])  14.4 us
    pallas_call x4, Pallas kernels, next_columns(): pl.pallas_call(functools.partial(columns_kernel, start, start + wide), ou...  6.72 us
    ppermute x4, waiting for transfers between devices, shifted(): return lax.ppermute(x, axis, [(i, (i + by) % size) for i in range(size)])  4.82 us
    ppermute x4, starting transfers between devices, shifted(): return lax.ppermute(x, axis, [(i, (i + by) % size) for i in range(size)])  4.74 us
    pallas_call x1, Pallas kernels, inner(): pl.pallas_call(functools.partial(inner_kernel, heads), out_shape=(pltpu.V...  4.19 us
    unnamed x35, local copies, waits for them, and re-layouts  4 us
  transfers between devices with their start and end apart: 22, of which 13 were waited for; matrix products, arithmetic and copies ran while one was open for 1% of the time, Pallas kernels for 43%

profile of v9, /device:TPU:0, one launch (start us, length us, event | category | flops | bytes accessed | tf_op | source)
XLA Modules:
  0.0 99.9 jit_solution(15542270989604099328)
XLA Ops:
  0.0 0.5 collective-permute-start
  0.5 1.0 shard_map.119
  1.4 2.7 %collective-permute-start.2 = (bf16[512,256]{1,0:T(8,128)(2,1)S(1)}, bf16[512,256]{1,0:T(8,128)(2,1)S(1)}, u32[]{:S(2)}, u32[]{:S(2)}) collective-permute-start(bf16[512,256]{1,0:T(8,128)(2,1)S(1)} %shard_map.119), channel_id=1, source_target_pairs={{0,2},{1,3},{2,0},{3,1},{4,6},{5,7},{6,4},{7,5},{8,10},{9,11},{10,... | collective-permute-start | bytes 786440 | tf_op jit(solution)/shard_map/ppermute | solution.py:27
  4.1 2.4 %shard_map.118 = (bf16[512,256]{1,0:T(8,128)(2,1)}, bf16[512,512]{1,0:T(8,128)(2,1)}) custom-call(bf16[512,1024]{1,0:T(8,128)(2,1)} %refs_6_.2), custom_call_target="tpu_custom_call" | custom-call | flops 1000000 | bytes 100000 | tf_op jit(solution)/shard_map/pallas_call | solution.py:70
  6.5 1.8 %collective-permute-start.3 = (bf16[512,256]{1,0:T(8,128)(2,1)}, bf16[512,256]{1,0:T(8,128)(2,1)S(1)}, u32[]{:S(2)}, u32[]{:S(2)}) collective-permute-start(bf16[512,256]{1,0:T(8,128)(2,1)} %get-tuple-element.79), channel_id=1, source_target_pairs={{0,2},{1,3},{2,0},{3,1},{4,6},{5,7},{6,4},{7,5},{8,10},{9,11},{10,... | collective-permute-start | bytes 786440 | tf_op jit(solution)/shard_map/ppermute | solution.py:27
  8.3 0.3 collective-permute-start.1
  8.6 0.1 pad_add_fusion.info.refs_3_.refs_5_.refs_6_.refs_4_
  8.7 8.0 %shard_map.120 = (f32[512,512]{1,0:T(8,128)S(1)}, f32[512,1024]{1,0:T(8,128)S(1)}, f32[512,512]{1,0:T(8,128)S(1)}, f32[4,512]{1,0:T(4,128)S(1)}) custom-call(s32[3]{0:T(128)S(1)} %pad_add_fusion.info.refs_3_.refs_5_.refs_6_.refs_4_, bf16[512,1024]{1,0:T(8,128)(2,1)S(1)} %copy-done, bf16[512,1024]{1,0:T(8,128)(2,1)S(1)} %collective-permute-done.refs_1_.refs_4_, ...), custom_call_target="tpu_custom_call" | custom-call | flops 1000000 | bytes 100000 | tf_op jit(solution)/shard_map/pallas_call | solution.py:208
  16.7 0.1 collective-permute-done.3.refs_2_
  16.9 0.5 collective-permute-start.5
  17.4 1.0 %collective-permute-done.4.refs_1_ = bf16[512,256]{1,0:T(8,128)(2,1)S(1)} collective-permute-done((bf16[512,256]{1,0:T(8,128)(2,1)S(1)}, bf16[512,256]{1,0:T(8,128)(2,1)S(1)}, u32[]{:S(2)}, u32[]{:S(2)}) %collective-permute-start.4) | collective-permute-done | bytes 262176 | tf_op jit(solution)/shard_map/ppermute | solution.py:27
  18.4 0.4 collective-permute-done.5.refs_3_
  18.8 7.6 %shard_map.121 = (f32[512,512]{1,0:T(8,128)S(1)}, f32[512,1024]{1,0:T(8,128)S(1)}, f32[512,512]{1,0:T(8,128)S(1)}, f32[512,1024]{1,0:T(8,128)S(1)}, f32[4,512]{1...) custom-call(s32[3]{0:T(128)S(1)} %pad_add_fusion.info.refs_3_.refs_5, ...), custom_call_target="tpu_custom_call", output_to_operand_aliasing={{0}: (10, {}), {1}: (11, {}), {2}: (12, {}), {4}: (13, {})} | custom-call | flops 1000000 | bytes 100000 | tf_op jit(solution)/shard_map/pallas_call | solution.py:208
  26.4 1.4 %collective-permute-done.1.x.refs_5_ = bf16[512,512]{1,0:T(8,128)(2,1)S(1)} collective-permute-done((bf16[512,512]{1,0:T(8,128)(2,1)}, bf16[512,512]{1,0:T(8,128)(2,1)S(1)}, u32[]{:S(2)}, u32[]{:S(2)}) %collective-permute-start.1) | collective-permute-done | bytes 524320 | tf_op jit(solution)/shard_map/ppermute | solution.py:27
  27.9 1.7 %shard_map.122 = (f32[512,512]{1,0:T(8,128)S(1)}, f32[512,1024]{1,0:T(8,128)S(1)}, f32[4,512]{1,0:T(4,128)S(1)}) custom-call(s32[3]{0:T(128)S(1)} %pad_add_fusion.info.refs_3_.refs_5_.refs_6_.refs_4_, bf16[512,512]{1,0:T(8,128)(2,1)S(1)} %collective-permute-done.1.x.refs_5_, ...), custom_call_target="tpu_custom_call", output_to_operand_aliasing={{0}: (5, {}), {1}: (6, {}), {2}: (7, {})} | custom-call | flops 1000000 | bytes 100000 | tf_op jit(solution)/shard_map/pallas_call | solution.py:170
  29.5 0.2 collective-permute-done.6.refs_0_.refs_6_
  29.8 2.8 %shard_map.123 = (bf16[512,512]{1,0:T(8,128)(2,1)S(1)}, bf16[512,1024]{1,0:T(8,128)(2,1)S(1)}, bf16[2,128,512]{2,1,0:T(8,128)(2,1)S(1)}, bf16[2,128,512]{2,1,0:T...) custom-call(s32[3]{0:T(128)S(1)} %pad_add_fusion.info.refs_3_.refs_5_.refs_6_.refs_4_, s32[4]{0:T(128)S(1)} %copy-done.11, ...), custom_call_target="tpu_custom_call" | custom-call | flops 4000000000 | bytes 4000000 | tf_op jit(solution)/shard_map/pallas_call | solution.py:308
  32.6 1.8 %collective-permute-start.8 = (bf16[2,128,512]{2,1,0:T(8,128)(2,1)S(1)}, bf16[2,128,512]{2,1,0:T(8,128)(2,1)S(1)}, u32[]{:S(2)}, u32[]{:S(2)}) collective-permute-start(bf16[2,128,512]{2,1,0:T(8,128)(2,1)S(1)} %get-tuple-element.105), channel_id=1, source_target_pairs={{0,4},{4,0},{8,12},{12,8},{16,20},{20,16},{24,28},{28,24},{1,5},{5... | collective-permute-start | bytes 786440 | tf_op jit(solution)/shard_map/ppermute | solution.py:27
  34.4 0.3 collective-permute-start.7
  34.7 6.0 %shard_map.124 = (bf16[512,512]{1,0:T(8,128)(2,1)S(1)}, f32[512,1024]{1,0:T(8,128)S(1)}) custom-call(bf16[512,512]{1,0:T(8,128)(2,1)S(1)} %get-tuple-element.106.refs_0_.key, bf16[512,1024]{1,0:T(8,128)(2,1)S(1)} %get-tuple-element.107.refs_1_.value, bf16[2,128,512]{2,1,0:T(8,128)(2,1)S(1)} %get-tuple-element.108.refs_2_.refs_7_.refs_8_, ...), custom_call_target="tpu_custom_call" | custom-call | flops 1000000 | bytes 100000 | tf_op jit(solution)/shard_map/pallas_call | solution.py:208
  40.7 0.5 collective-permute-done.7.refs_6_.refs_7_
  41.3 0.8 shard_map.125
  42.1 1.9 %collective-permute-start.10 = (bf16[2,128,512]{2,1,0:T(8,128)(2,1)S(1)}, bf16[2,128,512]{2,1,0:T(8,128)(2,1)}, u32[]{:S(2)}, u32[]{:S(2)}) collective-permute-start(bf16[2,128,512]{2,1,0:T(8,128)(2,1)S(1)} %get-tuple-element.120), channel_id=1, source_target_pairs={{0,8},{4,12},{8,16},{12,20},{16,24},{20,28},{24,0},{28,4},{1,9},{5... | collective-permute-start | bytes 786440 | tf_op jit(solution)/shard_map/ppermute | solution.py:32
  43.9 1.6 %collective-permute-start.9 = (f32[2,384]{1,0:T(2,128)S(1)}, f32[2,384]{1,0:T(2,128)S(1)}, u32[]{:S(2)}, u32[]{:S(2)}) collective-permute-start(f32[2,384]{1,0:T(2,128)S(1)} %get-tuple-element.119), channel_id=1, source_target_pairs={{0,8},{4,12},{8,16},{12,20},{16,24},{20,28},{24,0},{28,4},{1,9},{5... | collective-permute-start | bytes 9224 | tf_op jit(solution)/shard_map/ppermute | solution.py:32
  45.5 4.0 %shard_map.126.refs_5_.refs_3_.gate = f32[512,1024]{1,0:T(8,128)S(1)} custom-call(bf16[512,512]{1,0:T(8,128)(2,1)S(1)} %get-tuple-element.106.refs_0_.key, bf16[512,1024]{1,0:T(8,128)(2,1)S(1)} %get-tuple-element.107.refs_1_.value, bf16[2,128,512]{2,1,0:T(8,128)(2,1)S(1)} %get-tuple-element.108.refs_2_.refs_7_.refs_8_, ...), custom_call_target="tpu_custom_call" | custom-call | flops 1000000 | bytes 100000 | tf_op jit(solution)/shard_map/pallas_call | solution.py:208
  49.5 1.3 %copy-done.1 = f32[512,1024]{1,0:T(8,128)} copy-done((f32[512,1024]{1,0:T(8,128)}, f32[512,1024]{1,0:T(8,128)S(1)}, u32[]{:S(2)}) %copy-start.1) | copy-done | bytes 2097176
  50.8 1.2 %collective-permute-done.9.refs_10_ = f32[2,384]{1,0:T(2,128)S(1)} collective-permute-done((f32[2,384]{1,0:T(2,128)S(1)}, f32[2,384]{1,0:T(2,128)S(1)}, u32[]{:S(2)}, u32[]{:S(2)}) %collective-permute-start.9) | collective-permute-done | bytes 3104 | tf_op jit(solution)/shard_map/ppermute | solution.py:32
  52.1 0.4 collective-permute-start.12
  52.4 0.9 collective-permute-start.11
  53.4 0.1 copy.20.refs_16_
  53.5 1.6 %copy-done.2 = f32[512,1024]{1,0:T(8,128)S(1)} copy-done((f32[512,1024]{1,0:T(8,128)S(1)}, f32[512,1024]{1,0:T(8,128)}, u32[]{:S(2)}) %copy-start.2) | copy-done | bytes 2097176
  55.1 0.9 copy-done.5
  56.0 1.8 %shard_map.127.refs_14_ = f32[2,128,512]{2,1,0:T(8,128)S(1)} custom-call(bf16[512,512]{1,0:T(8,128)(2,1)S(1)} %get-tuple-element.106.refs_0_.key, bf16[512,1024]{1,0:T(8,128)(2,1)S(1)} %get-tuple-element.107.refs_1_.value, bf16[2,128,512]{2,1,0:T(8,128)(2,1)S(1)} %get-tuple-element.108.refs_2_.refs_7_.refs_8_, bf16[2,128,512]{2,1,0:T(8,128)(2,1)S(1)} %copy-done.5, ...), custom_call_target="tpu_custom_call" | custom-call | flops 1000000 | bytes 100000 | tf_op jit(solution)/shard_map/pallas_call | solution.py:438
  57.8 3.6 %collective-permute-done.11.refs_11_ = f32[2,384]{1,0:T(2,128)S(1)} collective-permute-done((f32[2,384]{1,0:T(2,128)S(1)}, f32[2,384]{1,0:T(2,128)S(1)}, u32[]{:S(2)}, u32[]{:S(2)}) %collective-permute-start.11) | collective-permute-done | bytes 3104 | tf_op jit(solution)/shard_map/ppermute | solution.py:32
  61.4 1.7 %shard_map.128 = (bf16[2,128,512]{2,1,0:T(8,128)(2,1)S(1)}, bf16[2,128,512]{2,1,0:T(8,128)(2,1)S(1)}, f32[2,256]{1,0:T(2,128)S(1)}, f32[2,128]{1,0:T(2,128)S(1)}) custom-call(bf16[512,512]{1,0:T(8,128)(2,1)S(1)} %get-tuple-element.106.refs_0_.key, bf16[512,1024]{1,0:T(8,128)(2,1)S(1)} %get-tuple-element.107.refs_1_.value, ...), custom_call_target="tpu_custom_call" | custom-call | flops 1000000 | bytes 100000 | tf_op jit(solution)/shard_map/pallas_call | solution.py:454
  63.1 1.3 %collective-permute-start.13 = (bf16[2,128,512]{2,1,0:T(8,128)(2,1)S(1)}, bf16[2,128,512]{2,1,0:T(8,128)(2,1)S(1)}, u32[]{:S(2)}, u32[]{:S(2)}) collective-permute-start(bf16[2,128,512]{2,1,0:T(8,128)(2,1)S(1)} %get-tuple-element.131), channel_id=1, source_target_pairs={{0,4},{4,0},{8,12},{12,8},{16,20},{20,16},{24,28},{28,24},{1,5},{5... | collective-permute-start | bytes 786440 | tf_op jit(solution)/shard_map/ppermute | solution.py:27
  64.4 4.2 %shard_map.129 = (f32[512,1024]{1,0:T(8,128)S(1)}, f32[512,1024]{1,0:T(8,128)S(1)}, bf16[1024,4096]{1,0:T(8,128)(2,1)S(1)}) custom-call(s32[3]{0:T(128)S(1)} %pad_add_fusion.info.refs_3_.refs_5_.refs_6_.refs_4_, s32[4]{0:T(128)S(1)} %copy-done.11, f32[2,128]{1,0:T(2,128)S(1)} %get-tuple-element.132.top_in, ...), custom_call_target="tpu_custom_call" | custom-call | flops 1000000 | bytes 100000 | tf_op jit(solution)/shard_map/pallas_call | solution.py:526
  68.6 0.9 collective-permute-done.13.other
  69.6 1.6 %shard_map.130 = (bf16[512,1024]{1,0:T(8,128)(2,1)S(1)}, bf16[512,512]{1,0:T(8,128)(2,1)S(1)}) custom-call(s32[3]{0:T(128)S(1)} %pad_add_fusion.info.refs_3_.refs_5_.refs_6_.refs_4_, bf16[512,512]{1,0:T(8,128)(2,1)S(1)} %get-tuple-element.116.refs_2_.refs_4_.query, bf16[2,128,512]{2,1,0:T(8,128)(2,1)S(1)} %get-tuple-element.130.own, ...), custom_call_target="tpu_custom_call" | custom-call | flops 3000000000 | bytes 8000000 | tf_op jit(solution)/shard_map/pallas_call | solution.py:567
  71.2 0.1 collective-permute-start.14
  71.3 1.8 %shard_map.131 = (bf16[512,512]{1,0:T(8,128)(2,1)S(1)}, bf16[512,512]{1,0:T(8,128)(2,1)S(1)}) custom-call(s32[3]{0:T(128)S(1)} %pad_add_fusion.info.refs_3_.refs_5_.refs_6_.refs_4_, bf16[512,1024]{1,0:T(8,128)(2,1)S(1)} %get-tuple-element.147.hidden, bf16[1024,4096]{1,0:T(8,128)(2,1)S(1)} %get-tuple-element.137.w), custom_call_target="tpu_custom_call" | custom-call | flops 1000000 | bytes 100000 | tf_op jit(solution)/shard_map/pallas_call | solution.py:589
  73.1 0.6 collective-permute-start.16
  73.7 0.1 copy.28
  73.8 0.1 convert_add_fusion.3
  74.0 1.3 %collective-permute-start.15 = (bf16[512,256]{1,0:T(8,128)(2,1)S(1)}, bf16[512,256]{1,0:T(8,128)(2,1)S(1)}, u32[]{:S(2)}, u32[]{:S(2)}) collective-permute-start(bf16[512,256]{1,0:T(8,128)(2,1)S(1)} %slice.99), channel_id=1, source_target_pairs={{0,2},{1,3},{2,0},{3,1},{4,6},{5,7},{6,4},{7,5},{8,10},{9,11},{10,... | collective-permute-start | bytes 786440 | tf_op jit(solution)/shard_map/ppermute | solution.py:27
  75.3 1.8 %shard_map.132 = (bf16[512,512]{1,0:T(8,128)(2,1)S(1)}, bf16[512,512]{1,0:T(8,128)(2,1)S(1)}) custom-call(s32[3]{0:T(128)S(1)} %pad_add_fusion.info.refs_3_.refs_5_.refs_6_.refs_4_, bf16[512,1024]{1,0:T(8,128)(2,1)S(1)} %get-tuple-element.147.hidden, bf16[1024,4096]{1,0:T(8,128)(2,1)S(1)} %get-tuple-element.137.w), custom_call_target="tpu_custom_call" | custom-call | flops 1000000 | bytes 100000 | tf_op jit(solution)/shard_map/pallas_call | solution.py:589
  77.2 0.1 collective-permute-start.18
  77.2 0.1 convert_add_fusion.2
  77.4 0.8 collective-permute-start.17
  78.3 1.8 %shard_map.133 = (bf16[512,512]{1,0:T(8,128)(2,1)S(1)}, bf16[512,512]{1,0:T(8,128)(2,1)S(1)}) custom-call(s32[3]{0:T(128)S(1)} %pad_add_fusion.info.refs_3_.refs_5_.refs_6_.refs_4_, bf16[512,1024]{1,0:T(8,128)(2,1)S(1)} %get-tuple-element.147.hidden, bf16[1024,4096]{1,0:T(8,128)(2,1)S(1)} %get-tuple-element.137.w), custom_call_target="tpu_custom_call" | custom-call | flops 1000000 | bytes 100000 | tf_op jit(solution)/shard_map/pallas_call | solution.py:589
  80.1 0.3 collective-permute-start.20
  80.3 2.9 %collective-permute-done.15 = bf16[512,256]{1,0:T(8,128)(2,1)S(1)} collective-permute-done((bf16[512,256]{1,0:T(8,128)(2,1)S(1)}, bf16[512,256]{1,0:T(8,128)(2,1)S(1)}, u32[]{:S(2)}, u32[]{:S(2)}) %collective-permute-start.15) | collective-permute-done | bytes 262176 | tf_op jit(solution)/shard_map/ppermute | solution.py:27
  83.2 0.2 fusion.8
  83.4 0.1 convert_add_fusion.1
  83.6 1.3 %collective-permute-start.19 = (bf16[512,256]{1,0:T(8,128)(2,1)S(1)}, bf16[512,256]{1,0:T(8,128)(2,1)S(1)}, u32[]{:S(2)}, u32[]{:S(2)}) collective-permute-start(bf16[512,256]{1,0:T(8,128)(2,1)S(1)} %slice.97), channel_id=1, source_target_pairs={{0,2},{1,3},{2,0},{3,1},{4,6},{5,7},{6,4},{7,5},{8,10},{9,11},{10,... | collective-permute-start | bytes 786440 | tf_op jit(solution)/shard_map/ppermute | solution.py:27
  85.0 1.3 %shard_map.134 = bf16[512,512]{1,0:T(8,128)(2,1)S(1)} custom-call(s32[3]{0:T(128)S(1)} %pad_add_fusion.info.refs_3_.refs_5_.refs_6_.refs_4_, bf16[512,1024]{1,0:T(8,128)(2,1)S(1)} %get-tuple-element.147.hidden, bf16[1024,4096]{1,0:T(8,128)(2,1)S(1)} %get-tuple-element.137.w), custom_call_target="tpu_custom_call" | custom-call | flops 1000000 | bytes 100000 | tf_op jit(solution)/shard_map/pallas_call | solution.py:589
  86.2 0.1 convert_add_fusion
  86.4 0.8 collective-permute-start.21
  87.2 1.6 %collective-permute-done.17 = bf16[512,256]{1,0:T(8,128)(2,1)S(1)} collective-permute-done((bf16[512,256]{1,0:T(8,128)(2,1)S(1)}, bf16[512,256]{1,0:T(8,128)(2,1)S(1)}, u32[]{:S(2)}, u32[]{:S(2)}) %collective-permute-start.17) | collective-permute-done | bytes 262176 | tf_op jit(solution)/shard_map/ppermute | solution.py:27
  88.8 0.1 fusion.9
  88.9 5.5 %collective-permute-done.19 = bf16[512,256]{1,0:T(8,128)(2,1)S(1)} collective-permute-done((bf16[512,256]{1,0:T(8,128)(2,1)S(1)}, bf16[512,256]{1,0:T(8,128)(2,1)S(1)}, u32[]{:S(2)}, u32[]{:S(2)}) %collective-permute-start.19) | collective-permute-done | bytes 262176 | tf_op jit(solution)/shard_map/ppermute | solution.py:27
  94.4 0.1 fusion.10
  94.6 4.6 %collective-permute-done.21 = bf16[512,256]{1,0:T(8,128)(2,1)S(1)} collective-permute-done((bf16[512,256]{1,0:T(8,128)(2,1)S(1)}, bf16[512,256]{1,0:T(8,128)(2,1)S(1)}, u32[]{:S(2)}, u32[]{:S(2)}) %collective-permute-start.21) | collective-permute-done | bytes 262176 | tf_op jit(solution)/shard_map/ppermute | solution.py:27
  99.1 0.8 fusion.11
  (47 shorter events, 0.3 us)
Async XLA Ops:
  0.0 8.7 %copy-start = (bf16[512,1024]{1,0:T(8,128)(2,1)S(1)}, bf16[512,1024]{1,0:T(8,128)(2,1)}, u32[]{:S(2)}) copy-start(bf16[512,1024]{1,0:T(8,128)(2,1)} %refs_6_.2) | copy-start | bytes 3145732
  0.0 8.6 %copy-start.15 = (bf16[2,4096,2]{1,2,0:T(2,128)(2,1)S(1)}, bf16[2,4096,2]{1,2,0:T(2,128)(2,1)}, u32[]{:S(2)}) copy-start(bf16[2,4096,2]{1,2,0:T(2,128)(2,1)} %param.17) | copy-start | bytes 98308
  0.0 4.1 %collective-permute-start = (bf16[512,1024]{1,0:T(8,128)(2,1)}, bf16[512,1024]{1,0:T(8,128)(2,1)S(1)}, u32[]{:S(2)}, u32[]{:S(2)}) collective-permute-start(bf16[512,1024]{1,0:T(8,128)(2,1)} %refs_6_.2), channel_id=1, source_target_pairs={{0,1},{1,0},{2,3},{3,2},{4,5},{5,4},{6,7},{7,6},{8,9},{9,8},{10,11... | collective-permute-start | bytes 3145736 | tf_op jit(solution)/shard_map/ppermute | solution.py:27
  1.4 15.3 %collective-permute-start.2 = (bf16[512,256]{1,0:T(8,128)(2,1)S(1)}, bf16[512,256]{1,0:T(8,128)(2,1)S(1)}, u32[]{:S(2)}, u32[]{:S(2)}) collective-permute-start(bf16[512,256]{1,0:T(8,128)(2,1)S(1)} %shard_map.119), channel_id=1, source_target_pairs={{0,2},{1,3},{2,0},{3,1},{4,6},{5,7},{6,4},{7,5},{8,10},{9,11},{10,... | collective-permute-start | bytes 786440 | tf_op jit(solution)/shard_map/ppermute | solution.py:27
  4.1 12.6 %copy-start.7 = (bf16[512,1024]{1,0:T(8,128)(2,1)}, bf16[512,1024]{1,0:T(8,128)(2,1)S(1)}, u32[]{:S(2)}) copy-start(bf16[512,1024]{1,0:T(8,128)(2,1)S(1)} %collective-permute-done.refs_1_.refs_4_) | copy-start | bytes 3145732
  6.5 10.4 %collective-permute-start.3 = (bf16[512,256]{1,0:T(8,128)(2,1)}, bf16[512,256]{1,0:T(8,128)(2,1)S(1)}, u32[]{:S(2)}, u32[]{:S(2)}) collective-permute-start(bf16[512,256]{1,0:T(8,128)(2,1)} %get-tuple-element.79), channel_id=1, source_target_pairs={{0,2},{1,3},{2,0},{3,1},{4,6},{5,7},{6,4},{7,5},{8,10},{9,11},{10,... | collective-permute-start | bytes 786440 | tf_op jit(solution)/shard_map/ppermute | solution.py:27
  8.3 19.5 %collective-permute-start.1 = (bf16[512,512]{1,0:T(8,128)(2,1)}, bf16[512,512]{1,0:T(8,128)(2,1)S(1)}, u32[]{:S(2)}, u32[]{:S(2)}) collective-permute-start(bf16[512,512]{1,0:T(8,128)(2,1)} %get-tuple-element.78), channel_id=1, source_target_pairs={{0,2},{1,3},{2,0},{3,1},{4,6},{5,7},{6,4},{7,5},{8,10},{9,11},{10,... | collective-permute-start | bytes 1572872 | tf_op jit(solution)/shard_map/ppermute | solution.py:27
  16.9 1.5 %collective-permute-start.4 = (bf16[512,256]{1,0:T(8,128)(2,1)S(1)}, bf16[512,256]{1,0:T(8,128)(2,1)S(1)}, u32[]{:S(2)}, u32[]{:S(2)}) collective-permute-start(bf16[512,256]{1,0:T(8,128)(2,1)S(1)} %collective-permute-done.2.refs_0_), channel_id=1, source_target_pairs={{0,1},{1,0},{2,3},{3,2},{4,5},{5,4},{6,7},{7,6},{8,9},{9,8},{10,11... | collective-permute-start | bytes 786440 | tf_op jit(solution)/shard_map/ppermute | solution.py:27
  16.9 1.9 %collective-permute-start.5 = (bf16[512,256]{1,0:T(8,128)(2,1)S(1)}, bf16[512,256]{1,0:T(8,128)(2,1)S(1)}, u32[]{:S(2)}, u32[]{:S(2)}) collective-permute-start(bf16[512,256]{1,0:T(8,128)(2,1)S(1)} %collective-permute-done.3.refs_2_), channel_id=1, source_target_pairs={{0,1},{1,0},{2,3},{3,2},{4,5},{5,4},{6,7},{7,6},{8,9},{9,8},{10,11... | collective-permute-start | bytes 786440 | tf_op jit(solution)/shard_map/ppermute | solution.py:27
  27.8 1.7 %copy-start.9 = (bf16[512,512]{1,0:T(8,128)(2,1)}, bf16[512,512]{1,0:T(8,128)(2,1)S(1)}, u32[]{:S(2)}) copy-start(bf16[512,512]{1,0:T(8,128)(2,1)S(1)} %collective-permute-done.1.x.refs_5_) | copy-start | bytes 1572868
  27.8 1.9 %collective-permute-start.6 = (bf16[512,512]{1,0:T(8,128)(2,1)S(1)}, bf16[512,512]{1,0:T(8,128)(2,1)S(1)}, u32[]{:S(2)}, u32[]{:S(2)}) collective-permute-start(bf16[512,512]{1,0:T(8,128)(2,1)S(1)} %collective-permute-done.1.x.refs_5_), channel_id=1, source_target_pairs={{0,1},{1,0},{2,3},{3,2},{4,5},{5,4},{6,7},{7,6},{8,9},{9,8},{10,11... | collective-permute-start | bytes 1572872 | tf_op jit(solution)/shard_map/ppermute | solution.py:27
  27.8 1.9 %copy-start.11 = (s32[4]{0:T(128)S(1)}, s32[4]{0:T(128)}, u32[]{:S(2)}) copy-start(s32[4]{0:T(128)} %docs.3) | copy-start | bytes 52
  27.8 1.9 %copy-start.13 = (f32[2,2]{1,0:T(2,128)S(1)}, f32[2,2]{1,0:T(2,128)}, u32[]{:S(2)}) copy-start(f32[2,2]{1,0:T(2,128)} %bias.1) | copy-start | bytes 52
  29.8 5.0 %copy-start.8 = (bf16[512,1024]{1,0:T(8,128)(2,1)S(1)}, bf16[512,1024]{1,0:T(8,128)(2,1)}, u32[]{:S(2)}) copy-start(bf16[512,1024]{1,0:T(8,128)(2,1)} %copy-done.7) | copy-start | bytes 3145732
  29.8 5.0 %copy-start.10 = (bf16[512,512]{1,0:T(8,128)(2,1)S(1)}, bf16[512,512]{1,0:T(8,128)(2,1)}, u32[]{:S(2)}) copy-start(bf16[512,512]{1,0:T(8,128)(2,1)} %copy-done.9) | copy-start | bytes 1572868
  32.6 8.7 %collective-permute-start.8 = (bf16[2,128,512]{2,1,0:T(8,128)(2,1)S(1)}, bf16[2,128,512]{2,1,0:T(8,128)(2,1)S(1)}, u32[]{:S(2)}, u32[]{:S(2)}) collective-permute-start(bf16[2,128,512]{2,1,0:T(8,128)(2,1)S(1)} %get-tuple-element.105), channel_id=1, source_target_pairs={{0,4},{4,0},{8,12},{12,8},{16,20},{20,16},{24,28},{28,24},{1,5},{5... | collective-permute-start | bytes 786440 | tf_op jit(solution)/shard_map/ppermute | solution.py:27
  34.4 6.8 %collective-permute-start.7 = (f32[2,384]{1,0:T(2,128)S(1)}, f32[2,384]{1,0:T(2,128)S(1)}, u32[]{:S(2)}, u32[]{:S(2)}) collective-permute-start(f32[2,384]{1,0:T(2,128)S(1)} %get-tuple-element.104.refs_5_.refs_6_), channel_id=1, source_target_pairs={{0,4},{4,0},{8,12},{12,8},{16,20},{20,16},{24,28},{28,24},{1,5},{5... | collective-permute-start | bytes 9224 | tf_op jit(solution)/shard_map/ppermute | solution.py:27
  41.3 8.2 %copy-start.4 = (bf16[2,128,512]{2,1,0:T(8,128)(2,1)}, bf16[2,128,512]{2,1,0:T(8,128)(2,1)S(1)}, u32[]{:S(2)}) copy-start(bf16[2,128,512]{2,1,0:T(8,128)(2,1)S(1)} %collective-permute-done.8.refs_8_.refs_3_.refs_9_) | copy-start | bytes 786436
  42.1 10.0 %collective-permute-start.10 = (bf16[2,128,512]{2,1,0:T(8,128)(2,1)S(1)}, bf16[2,128,512]{2,1,0:T(8,128)(2,1)}, u32[]{:S(2)}, u32[]{:S(2)}) collective-permute-start(bf16[2,128,512]{2,1,0:T(8,128)(2,1)S(1)} %get-tuple-element.120), channel_id=1, source_target_pairs={{0,8},{4,12},{8,16},{12,20},{16,24},{20,28},{24,0},{28,4},{1,9},{5... | collective-permute-start | bytes 786440 | tf_op jit(solution)/shard_map/ppermute | solution.py:32
  43.9 9.4 %copy-start.16 = (f32[2]{0:T(128)S(1)}, f32[2]{0:T(128)}, u32[]{:S(2)}) copy-start(f32[2]{0:T(128)} %param.22) | copy-start | bytes 28
  43.9 8.1 %collective-permute-start.9 = (f32[2,384]{1,0:T(2,128)S(1)}, f32[2,384]{1,0:T(2,128)S(1)}, u32[]{:S(2)}, u32[]{:S(2)}) collective-permute-start(f32[2,384]{1,0:T(2,128)S(1)} %get-tuple-element.119), channel_id=1, source_target_pairs={{0,8},{4,12},{8,16},{12,20},{16,24},{20,28},{24,0},{28,4},{1,9},{5... | collective-permute-start | bytes 9224 | tf_op jit(solution)/shard_map/ppermute | solution.py:32
  49.5 1.3 %copy-start.1 = (f32[512,1024]{1,0:T(8,128)}, f32[512,1024]{1,0:T(8,128)S(1)}, u32[]{:S(2)}) copy-start(f32[512,1024]{1,0:T(8,128)S(1)} %shard_map.126.refs_5_.refs_3_.gate) | copy-start | bytes 6291460
  52.1 9.3 %collective-permute-start.12 = (bf16[2,128,512]{2,1,0:T(8,128)(2,1)}, bf16[2,128,512]{2,1,0:T(8,128)(2,1)}, u32[]{:S(2)}, u32[]{:S(2)}) collective-permute-start(bf16[2,128,512]{2,1,0:T(8,128)(2,1)} %collective-permute-done.10.refs_12_), channel_id=1, source_target_pairs={{0,8},{4,12},{8,16},{12,20},{16,24},{20,28},{24,0},{28,4},{1,9},{5... | collective-permute-start | bytes 786440 | tf_op jit(solution)/shard_map/ppermute | solution.py:32
  52.4 8.9 %collective-permute-start.11 = (f32[2,384]{1,0:T(2,128)S(1)}, f32[2,384]{1,0:T(2,128)S(1)}, u32[]{:S(2)}, u32[]{:S(2)}) collective-permute-start(f32[2,384]{1,0:T(2,128)S(1)} %collective-permute-done.9.refs_10_), channel_id=1, source_target_pairs={{0,8},{4,12},{8,16},{12,20},{16,24},{20,28},{24,0},{28,4},{1,9},{5... | collective-permute-start | bytes 9224 | tf_op jit(solution)/shard_map/ppermute | solution.py:32
  53.5 1.6 %copy-start.2 = (f32[512,1024]{1,0:T(8,128)S(1)}, f32[512,1024]{1,0:T(8,128)}, u32[]{:S(2)}) copy-start(f32[512,1024]{1,0:T(8,128)} %copy-done.1) | copy-start | bytes 6291460
  55.1 0.9 copy-start.5
  56.0 5.4 %copy-start.3 = (f32[512,1024]{1,0:T(8,128)S(1)}, f32[512,1024]{1,0:T(8,128)}, u32[]{:S(2)}) copy-start(f32[512,1024]{1,0:T(8,128)} %copy-done.1) | copy-start | bytes 6291460
  56.0 5.4 %copy-start.6 = (bf16[2,128,512]{2,1,0:T(8,128)(2,1)S(1)}, bf16[2,128,512]{2,1,0:T(8,128)(2,1)}, u32[]{:S(2)}) copy-start(bf16[2,128,512]{2,1,0:T(8,128)(2,1)} %copy-done.4) | copy-start | bytes 786436
  56.0 5.4 %copy-start.12 = (f32[2,256]{1,0:T(2,128)S(1)}, f32[2,256]{1,0:T(2,128)}, u32[]{:S(2)}) copy-start(f32[2,256]{1,0:T(2,128)} %refs_15_.1) | copy-start | bytes 6148
  63.1 6.4 %collective-permute-start.13 = (bf16[2,128,512]{2,1,0:T(8,128)(2,1)S(1)}, bf16[2,128,512]{2,1,0:T(8,128)(2,1)S(1)}, u32[]{:S(2)}, u32[]{:S(2)}) collective-permute-start(bf16[2,128,512]{2,1,0:T(8,128)(2,1)S(1)} %get-tuple-element.131), channel_id=1, source_target_pairs={{0,4},{4,0},{8,12},{12,8},{16,20},{20,16},{24,28},{28,24},{1,5},{5... | collective-permute-start | bytes 786440 | tf_op jit(solution)/shard_map/ppermute | solution.py:27
  71.2 2.5 %collective-permute-start.14 = (bf16[512,512]{1,0:T(8,128)(2,1)S(1)}, bf16[512,512]{1,0:T(8,128)(2,1)S(1)}, u32[]{:S(2)}, u32[]{:S(2)}) collective-permute-start(bf16[512,512]{1,0:T(8,128)(2,1)S(1)} %get-tuple-element.140), channel_id=1, source_target_pairs={{0,1},{1,0},{2,3},{3,2},{4,5},{5,4},{6,7},{7,6},{8,9},{9,8},{10,11... | collective-permute-start | bytes 1572872 | tf_op jit(solution)/shard_map/ppermute | solution.py:27
  73.1 4.1 %collective-permute-start.16 = (bf16[512,512]{1,0:T(8,128)(2,1)S(1)}, bf16[512,512]{1,0:T(8,128)(2,1)S(1)}, u32[]{:S(2)}, u32[]{:S(2)}) collective-permute-start(bf16[512,512]{1,0:T(8,128)(2,1)S(1)} %get-tuple-element.143), channel_id=1, source_target_pairs={{0,1},{1,0},{2,3},{3,2},{4,5},{5,4},{6,7},{7,6},{8,9},{9,8},{10,11... | collective-permute-start | bytes 1572872 | tf_op jit(solution)/shard_map/ppermute | solution.py:27
  74.0 9.2 %collective-permute-start.15 = (bf16[512,256]{1,0:T(8,128)(2,1)S(1)}, bf16[512,256]{1,0:T(8,128)(2,1)S(1)}, u32[]{:S(2)}, u32[]{:S(2)}) collective-permute-start(bf16[512,256]{1,0:T(8,128)(2,1)S(1)} %slice.99), channel_id=1, source_target_pairs={{0,2},{1,3},{2,0},{3,1},{4,6},{5,7},{6,4},{7,5},{8,10},{9,11},{10,... | collective-permute-start | bytes 786440 | tf_op jit(solution)/shard_map/ppermute | solution.py:27
  77.2 6.2 %collective-permute-start.18 = (bf16[512,512]{1,0:T(8,128)(2,1)S(1)}, bf16[512,512]{1,0:T(8,128)(2,1)S(1)}, u32[]{:S(2)}, u32[]{:S(2)}) collective-permute-start(bf16[512,512]{1,0:T(8,128)(2,1)S(1)} %get-tuple-element.146), channel_id=1, source_target_pairs={{0,1},{1,0},{2,3},{3,2},{4,5},{5,4},{6,7},{7,6},{8,9},{9,8},{10,11... | collective-permute-start | bytes 1572872 | tf_op jit(solution)/shard_map/ppermute | solution.py:27
  77.4 11.4 %collective-permute-start.17 = (bf16[512,256]{1,0:T(8,128)(2,1)S(1)}, bf16[512,256]{1,0:T(8,128)(2,1)S(1)}, u32[]{:S(2)}, u32[]{:S(2)}) collective-permute-start(bf16[512,256]{1,0:T(8,128)(2,1)S(1)} %slice.98), channel_id=1, source_target_pairs={{0,2},{1,3},{2,0},{3,1},{4,6},{5,7},{6,4},{7,5},{8,10},{9,11},{10,... | collective-permute-start | bytes 786440 | tf_op jit(solution)/shard_map/ppermute | solution.py:27
  80.1 6.1 %collective-permute-start.20 = (bf16[512,512]{1,0:T(8,128)(2,1)S(1)}, bf16[512,512]{1,0:T(8,128)(2,1)S(1)}, u32[]{:S(2)}, u32[]{:S(2)}) collective-permute-start(bf16[512,512]{1,0:T(8,128)(2,1)S(1)} %get-tuple-element.148), channel_id=1, source_target_pairs={{0,1},{1,0},{2,3},{3,2},{4,5},{5,4},{6,7},{7,6},{8,9},{9,8},{10,11... | collective-permute-start | bytes 1572872 | tf_op jit(solution)/shard_map/ppermute | solution.py:27
  83.6 10.8 %collective-permute-start.19 = (bf16[512,256]{1,0:T(8,128)(2,1)S(1)}, bf16[512,256]{1,0:T(8,128)(2,1)S(1)}, u32[]{:S(2)}, u32[]{:S(2)}) collective-permute-start(bf16[512,256]{1,0:T(8,128)(2,1)S(1)} %slice.97), channel_id=1, source_target_pairs={{0,2},{1,3},{2,0},{3,1},{4,6},{5,7},{6,4},{7,5},{8,10},{9,11},{10,... | collective-permute-start | bytes 786440 | tf_op jit(solution)/shard_map/ppermute | solution.py:27
  86.4 12.7 %collective-permute-start.21 = (bf16[512,256]{1,0:T(8,128)(2,1)S(1)}, bf16[512,256]{1,0:T(8,128)(2,1)S(1)}, u32[]{:S(2)}, u32[]{:S(2)}) collective-permute-start(bf16[512,256]{1,0:T(8,128)(2,1)S(1)} %slice.96), channel_id=1, source_target_pairs={{0,2},{1,3},{2,0},{3,1},{4,6},{5,7},{6,4},{7,5},{8,10},{9,11},{10,... | collective-permute-start | bytes 786440 | tf_op jit(solution)/shard_map/ppermute | solution.py:27
  94.5 4.6 %copy-start.14 = (bf16[512,1024]{1,0:T(8,128)(2,1)}, bf16[512,1024]{1,0:T(8,128)(2,1)S(1)}, u32[]{:S(2)}) copy-start(bf16[512,1024]{1,0:T(8,128)(2,1)S(1)} %fusion.10) | copy-start | bytes 3145732

commit v10 on v9

--- a/solution.py
+++ b/solution.py
@@ -343,7 +343,7 @@
     return m_even, g_even, g_odd, m_pair, weights
 
 
-def pair_kernel(length, info, docs, own, other, kept, got, state_out, small_out):
+def pair_kernel(length, info, docs, own, other, kept, got, small_out, *state_out):
     heads = own.shape[0]
     size = own.shape[1] - 128
     _, g_even, g_odd, m_pair, (w_own, w_other) = pair_scales(
@@ -357,25 +357,26 @@
     for h in range(heads):
         at = slice(h, h + 1)
         state = w_own[at] * kept[h].astype(F32) + w_other[at] * got[h].astype(F32)
-        state_out[h] = state.astype(BF)
+        state_out[h][0] = state.astype(BF)
 
 
 def pair_summary(info, docs, small, small_other, kept, got, length, held):
     return pl.pallas_call(
         holding(functools.partial(pair_kernel, length), held),
-        out_shape=(pltpu.VMEM(kept.shape, BF), pltpu.VMEM(small.shape, F32)),
+        out_shape=(pltpu.VMEM(small.shape, F32),)
+        + (pltpu.VMEM((1,) + kept.shape[1:], BF),) * kept.shape[0],
         in_specs=[VMEM_SPEC] * len(held) + [SMEM_SPEC] * 2 + [VMEM_SPEC] * 4,
-        out_specs=(VMEM_SPEC,) * 2,
+        out_specs=(VMEM_SPEC,) * (1 + kept.shape[0]),
         compiler_params=params(4),
         cost_estimate=cost(1e6, 1e5),
     )(*in_vmem(*held), info, docs, *in_vmem(small, small_other, kept, got))
 
 
 def incoming_kernel(length, reach, info, docs, own, other, kept, got, *refs):
-    smalls, states = refs[:reach], refs[reach : 2 * reach]
-    carry, carry_norm, carry_max = refs[2 * reach : 2 * reach + 3]
-    own_out, other_out, norm_out, top_out = refs[2 * reach + 3 :]
     heads = own.shape[0]
+    smalls, refs = refs[:reach], refs[reach:]
+    states = [refs[k * heads : (k + 1) * heads] for k in range(reach)]
+    carry, carry_norm, carry_max, own_out, other_out, norm_out, top_out = refs[reach * heads :]
     size = own.shape[1] - 128
     side = info[1]
     even = side == 0
@@ -418,7 +419,7 @@
         mine = w_own[reach][at] * base + direct_own[at] * here
         theirs = w_other[reach][at] * base + direct_other[at] * here
         for k in range(reach):
-            state = states[k][h].astype(F32)
+            state = states[k][h][0].astype(F32)
             mine = mine + w_own[k][at] * state
             theirs = theirs + w_other[k][at] * state
         own_out[h] = mine.astype(BF)
@@ -461,13 +462,13 @@
         ),
         in_specs=[VMEM_SPEC] * len(held)
         + [SMEM_SPEC] * 2
-        + [VMEM_SPEC] * (7 + 2 * len(smalls)),
+        + [VMEM_SPEC] * (7 + (1 + heads) * len(smalls)),
         out_specs=(VMEM_SPEC,) * 4,
         compiler_params=params(6),
         cost_estimate=cost(1e6, 1e5),
     )(
         *in_vmem(*held), info, docs,
-        *in_vmem(small, small_other, kept, got, *smalls, *states, carry),
+        *in_vmem(small, small_other, kept, got, *smalls, *sum(states, []), carry),
         carry_norm, carry_max[:, None],
     )
 
@@ -668,7 +669,7 @@
 
     small_other = pair(small)
     got = pair(sent)
-    held = (keys, values, kept)
+    held = (keys, values, kept, u)
     now_xs = after(keys, beside, *far[-1])
     queries, *gate = stage(
         info, now_xs, near_at[1:] + at[-1], (w_query, w_outgate), share, None, [sums[2], sums[3]],
@@ -677,30 +678,33 @@
     small_other, got, queries, *gate = lax.optimization_barrier(
         (small_other, got, queries, *gate)
     )
-    state_pair, travel = pair_summary(
-        info, doc_lengths, small, small_other, kept, got, length, (keys, values, queries)
+    travel, *state_pair = pair_summary(
+        info, doc_lengths, small, small_other, kept, got, length, (keys, values, queries, u)
     )
     smalls, states = [], []
-    held = (keys, values, kept, got, queries)
+    held = (keys, values, kept, got, queries, u)
     for step in range(blocks // 4):
-        before = state_pair
-        travel, state_pair = down(travel), down(state_pair)
+        before = state_pair[0]
+        first = down(state_pair[0])
+        travel = down(travel)
+        state_pair = [first] + [down(x) for x in state_pair[1:]]
         if step == 0:
             near_xs = [after(before, source)]
             gate = stage(
                 info, near_xs, near_at[:1], (w_outgate,), share, None, gate,
                 finishes=((jax.nn.sigmoid, F32),), held=held,
             )
-            travel, state_pair, *gate = lax.optimization_barrier((travel, state_pair, *gate))
+            travel, first, *gate = lax.optimization_barrier((travel, state_pair[0], *gate))
+            state_pair[0] = first
         elif step == 1:
             carry = carry_half(after(before, info), carry_matrix, (*held, *gate))
-            travel, state_pair, carry = lax.optimization_barrier((travel, state_pair, carry))
+            travel, carry, *state_pair = lax.optimization_barrier((travel, carry, *state_pair))
         smalls.append(travel)
         states.append(state_pair)
     (gate,) = gate
     state_own, state_other, norm_in, top_own = incoming_state(
         info, doc_lengths, small, small_other, kept, got, smalls, states,
-        carry, carry_norm, carry_max, length, (keys, values, queries, gate),
+        carry, carry_norm, carry_max, length, (keys, values, queries, gate, u),
     )
     state_got = pair(state_other)
     base, slope, w_here = inner(

time: 100 us -> 100 us (level)
  waiting for transfers between devices: 24 us -> 18.9 us
  starting transfers between devices: 19.1 us -> 23.1 us
  local copies, waits for them, and re-layouts: 4.25 us -> 5.49 us
    ppermute x4 -> x6, waiting for transfers between devices: 4.82 us -> 0.02 us  [shifted(): return lax.ppermute(x, axis, [(i, (i + by) % size) for i in range(size)])]
    ppermute x4 -> x6, starting transfers between devices: 4.74 us -> 8.4 us  [shifted(): return lax.ppermute(x, axis, [(i, (i + by) % size) for i in range(size)])]
    broadcast_in_dim x1, local copies, waits for them, and re-layouts: 0.09 us -> 1.32 us  [incoming_state(): carry_max[:, None]]
    unnamed x35 -> x37, local copies, waits for them, and re-layouts: 4 us -> 4 us
  transfers between devices with their start and end apart: 22 -> 24, of which waited for: 13 -> 11; matrix products, arithmetic and copies ran while one was open for 1% -> 3% of each run, Pallas kernels for 43% -> 43%
where the time goes in v10:
time: 100 us
  Pallas kernels  50.2 us (50%)
  starting transfers between devices  23.1 us (23%)
  waiting for transfers between devices  18.9 us (19%)
  local copies, waits for them, and re-layouts  5.49 us (5%)
  other arithmetic  1.94 us (2%)
    pallas_call x4, Pallas kernels, stage(): pl.pallas_call(holding(functools.partial(stage_kernel, xs_at, skips or [0...  25.6 us
    ppermute x18, waiting for transfers between devices, swapped(): return lax.ppermute(x, axis, [(i, i ^ mask) for i in range(size)])  18.9 us
    ppermute x18, starting transfers between devices, swapped(): return lax.ppermute(x, axis, [(i, i ^ mask) for i in range(size)])  14.7 us
    ppermute x6, starting transfers between devices, shifted(): return lax.ppermute(x, axis, [(i, (i + by) % size) for i in range(size)])  8.4 us
    pallas_call x4, Pallas kernels, next_columns(): pl.pallas_call(functools.partial(columns_kernel, start, start + wide), ou...  6.72 us
    pallas_call x1, Pallas kernels, inner(): pl.pallas_call(functools.partial(inner_kernel, heads), out_shape=(pltpu.V...  4.19 us
    unnamed x37, local copies, waits for them, and re-layouts  4 us
    pallas_call x2, Pallas kernels, split_tokens(): pl.pallas_call(functools.partial(split_kernel, starts), out_shape=tuple((...  3.35 us
  transfers between devices with their start and end apart: 24, of which 11 were waited for; matrix products, arithmetic and copies ran while one was open for 3% of the time, Pallas kernels for 43%

profile of v10, /device:TPU:0, one launch (start us, length us, event | category | flops | bytes accessed | tf_op | source)
XLA Modules:
  0.0 100.0 jit_solution(2024180700035894873)
XLA Ops:
  0.0 0.5 collective-permute-start
  0.5 1.0 shard_map.119
  1.4 2.7 %collective-permute-start.2 = (bf16[512,256]{1,0:T(8,128)(2,1)S(1)}, bf16[512,256]{1,0:T(8,128)(2,1)S(1)}, u32[]{:S(2)}, u32[]{:S(2)}) collective-permute-start(bf16[512,256]{1,0:T(8,128)(2,1)S(1)} %shard_map.119), channel_id=1, source_target_pairs={{0,2},{1,3},{2,0},{3,1},{4,6},{5,7},{6,4},{7,5},{8,10},{9,11},{10,... | collective-permute-start | bytes 786440 | tf_op jit(solution)/shard_map/ppermute | solution.py:27
  4.1 2.4 %shard_map.118 = (bf16[512,256]{1,0:T(8,128)(2,1)}, bf16[512,512]{1,0:T(8,128)(2,1)}) custom-call(bf16[512,1024]{1,0:T(8,128)(2,1)} %refs_7_.2), custom_call_target="tpu_custom_call" | custom-call | flops 1000000 | bytes 100000 | tf_op jit(solution)/shard_map/pallas_call | solution.py:70
  6.5 1.8 %collective-permute-start.3 = (bf16[512,256]{1,0:T(8,128)(2,1)}, bf16[512,256]{1,0:T(8,128)(2,1)S(1)}, u32[]{:S(2)}, u32[]{:S(2)}) collective-permute-start(bf16[512,256]{1,0:T(8,128)(2,1)} %get-tuple-element.81), channel_id=1, source_target_pairs={{0,2},{1,3},{2,0},{3,1},{4,6},{5,7},{6,4},{7,5},{8,10},{9,11},{10,... | collective-permute-start | bytes 786440 | tf_op jit(solution)/shard_map/ppermute | solution.py:27
  8.3 0.3 collective-permute-start.1
  8.6 0.1 pad_add_fusion.info.refs_4_.refs_6_.refs_7_.refs_5_
  8.7 8.0 %shard_map.120 = (f32[512,512]{1,0:T(8,128)S(1)}, f32[512,1024]{1,0:T(8,128)S(1)}, f32[512,512]{1,0:T(8,128)S(1)}, f32[4,512]{1,0:T(4,128)S(1)}) custom-call(s32[3]{0:T(128)S(1)} %pad_add_fusion.info.refs_4_.refs_6_.refs_7_.refs_5_, bf16[512,1024]{1,0:T(8,128)(2,1)S(1)} %copy-done, bf16[512,1024]{1,0:T(8,128)(2,1)S(1)} %collective-permute-done.refs_1_.refs_5_, ...), custom_call_target="tpu_custom_call" | custom-call | flops 1000000 | bytes 100000 | tf_op jit(solution)/shard_map/pallas_call | solution.py:208
  16.7 0.1 collective-permute-done.3.refs_2_
  16.9 0.5 collective-permute-start.5
  17.4 1.0 %collective-permute-done.4.refs_1_ = bf16[512,256]{1,0:T(8,128)(2,1)S(1)} collective-permute-done((bf16[512,256]{1,0:T(8,128)(2,1)S(1)}, bf16[512,256]{1,0:T(8,128)(2,1)S(1)}, u32[]{:S(2)}, u32[]{:S(2)}) %collective-permute-start.4) | collective-permute-done | bytes 262176 | tf_op jit(solution)/shard_map/ppermute | solution.py:27
  18.4 0.4 collective-permute-done.5.refs_3_
  18.8 7.6 %shard_map.121 = (f32[512,512]{1,0:T(8,128)S(1)}, f32[512,1024]{1,0:T(8,128)S(1)}, f32[512,512]{1,0:T(8,128)S(1)}, f32[512,1024]{1,0:T(8,128)S(1)}, f32[4,512]{1...) custom-call(s32[3]{0:T(128)S(1)} %pad_add_fusion.info.refs_4_.refs_6, ...), custom_call_target="tpu_custom_call", output_to_operand_aliasing={{0}: (10, {}), {1}: (11, {}), {2}: (12, {}), {4}: (13, {})} | custom-call | flops 1000000 | bytes 100000 | tf_op jit(solution)/shard_map/pallas_call | solution.py:208
  26.4 1.4 %collective-permute-done.1.x.refs_6_ = bf16[512,512]{1,0:T(8,128)(2,1)S(1)} collective-permute-done((bf16[512,512]{1,0:T(8,128)(2,1)}, bf16[512,512]{1,0:T(8,128)(2,1)S(1)}, u32[]{:S(2)}, u32[]{:S(2)}) %collective-permute-start.1) | collective-permute-done | bytes 524320 | tf_op jit(solution)/shard_map/ppermute | solution.py:27
  27.9 1.7 %shard_map.122 = (f32[512,512]{1,0:T(8,128)S(1)}, f32[512,1024]{1,0:T(8,128)S(1)}, f32[4,512]{1,0:T(4,128)S(1)}) custom-call(s32[3]{0:T(128)S(1)} %pad_add_fusion.info.refs_4_.refs_6_.refs_7_.refs_5_, bf16[512,512]{1,0:T(8,128)(2,1)S(1)} %collective-permute-done.1.x.refs_6_, ...), custom_call_target="tpu_custom_call", output_to_operand_aliasing={{0}: (5, {}), {1}: (6, {}), {2}: (7, {})} | custom-call | flops 1000000 | bytes 100000 | tf_op jit(solution)/shard_map/pallas_call | solution.py:170
  29.5 0.2 collective-permute-done.6.refs_0_.refs_7_
  29.8 2.8 %shard_map.123 = (bf16[512,512]{1,0:T(8,128)(2,1)S(1)}, bf16[512,1024]{1,0:T(8,128)(2,1)S(1)}, bf16[2,128,512]{2,1,0:T(8,128)(2,1)S(1)}, bf16[2,128,512]{2,1,0:T...) custom-call(s32[3]{0:T(128)S(1)} %pad_add_fusion.info.refs_4_.refs_6_.refs_7_.refs_5_, s32[4]{0:T(128)S(1)} %copy-done.11, ...), custom_call_target="tpu_custom_call" | custom-call | flops 4000000000 | bytes 4000000 | tf_op jit(solution)/shard_map/pallas_call | solution.py:308
  32.6 1.8 %collective-permute-start.8 = (bf16[2,128,512]{2,1,0:T(8,128)(2,1)S(1)}, bf16[2,128,512]{2,1,0:T(8,128)(2,1)S(1)}, u32[]{:S(2)}, u32[]{:S(2)}) collective-permute-start(bf16[2,128,512]{2,1,0:T(8,128)(2,1)S(1)} %get-tuple-element.107), channel_id=1, source_target_pairs={{0,4},{4,0},{8,12},{12,8},{16,20},{20,16},{24,28},{28,24},{1,5},{5... | collective-permute-start | bytes 786440 | tf_op jit(solution)/shard_map/ppermute | solution.py:27
  34.4 0.3 collective-permute-start.7
  34.7 6.0 %shard_map.124 = (bf16[512,512]{1,0:T(8,128)(2,1)S(1)}, f32[512,1024]{1,0:T(8,128)S(1)}) custom-call(bf16[512,512]{1,0:T(8,128)(2,1)S(1)} %get-tuple-element.108.refs_0_.key, bf16[512,1024]{1,0:T(8,128)(2,1)S(1)} %get-tuple-element.109.refs_1_.value, bf16[2,128,512]{2,1,0:T(8,128)(2,1)S(1)} %get-tuple-element.110.refs_2_.refs_8_.refs_9_, ...), custom_call_target="tpu_custom_call" | custom-call | flops 1000000 | bytes 100000 | tf_op jit(solution)/shard_map/pallas_call | solution.py:208
  40.7 0.5 collective-permute-done.7.refs_7_.refs_8_
  41.2 0.8 shard_map.125
  42.0 1.9 %collective-permute-start.10 = (bf16[1,128,512]{2,1,0:T(8,128)(2,1)S(1)}, bf16[1,128,512]{2,1,0:T(8,128)(2,1)S(1)}, u32[]{:S(2)}, u32[]{:S(2)}) collective-permute-start(bf16[1,128,512]{2,1,0:T(8,128)(2,1)S(1)} %get-tuple-element.123), channel_id=1, source_target_pairs={{0,8},{4,12},{8,16},{12,20},{16,24},{20,28},{24,0},{28,4},{1,9},{5... | collective-permute-start | bytes 393224 | tf_op jit(solution)/shard_map/ppermute | solution.py:32
  43.9 1.6 %collective-permute-start.13 = (bf16[1,128,512]{2,1,0:T(8,128)(2,1)S(1)}, bf16[1,128,512]{2,1,0:T(8,128)(2,1)}, u32[]{:S(2)}, u32[]{:S(2)}) collective-permute-start(bf16[1,128,512]{2,1,0:T(8,128)(2,1)S(1)} %get-tuple-element.130), channel_id=1, source_target_pairs={{0,8},{4,12},{8,16},{12,20},{16,24},{20,28},{24,0},{28,4},{1,9},{5... | collective-permute-start | bytes 393224 | tf_op jit(solution)/shard_map/ppermute | solution.py:32
  45.5 1.6 %collective-permute-start.9 = (f32[2,384]{1,0:T(2,128)S(1)}, f32[2,384]{1,0:T(2,128)}, u32[]{:S(2)}, u32[]{:S(2)}) collective-permute-start(f32[2,384]{1,0:T(2,128)S(1)} %get-tuple-element.122), channel_id=1, source_target_pairs={{0,8},{4,12},{8,16},{12,20},{16,24},{20,28},{24,0},{28,4},{1,9},{5... | collective-permute-start | bytes 9224 | tf_op jit(solution)/shard_map/ppermute | solution.py:32
  47.1 4.0 %shard_map.126.refs_6_.refs_3_.gate = f32[512,1024]{1,0:T(8,128)S(1)} custom-call(bf16[512,512]{1,0:T(8,128)(2,1)S(1)} %get-tuple-element.108.refs_0_.key, bf16[512,1024]{1,0:T(8,128)(2,1)S(1)} %get-tuple-element.109.refs_1_.value, bf16[2,128,512]{2,1,0:T(8,128)(2,1)S(1)} %get-tuple-element.110.refs_2_.refs_8_.refs_9_, ...), custom_call_target="tpu_custom_call" | custom-call | flops 1000000 | bytes 100000 | tf_op jit(solution)/shard_map/pallas_call | solution.py:208
  51.1 1.3 %copy-done.1 = f32[512,1024]{1,0:T(8,128)} copy-done((f32[512,1024]{1,0:T(8,128)}, f32[512,1024]{1,0:T(8,128)S(1)}, u32[]{:S(2)}) %copy-start.1) | copy-done | bytes 2097176
  52.4 0.1 collective-permute-start.12
  52.5 1.7 %collective-permute-start.14 = (bf16[1,128,512]{2,1,0:T(8,128)(2,1)}, bf16[1,128,512]{2,1,0:T(8,128)(2,1)}, u32[]{:S(2)}, u32[]{:S(2)}) collective-permute-start(bf16[1,128,512]{2,1,0:T(8,128)(2,1)} %collective-permute-done.13.refs_14_), channel_id=1, source_target_pairs={{0,8},{4,12},{8,16},{12,20},{16,24},{20,28},{24,0},{28,4},{1,9},{5... | collective-permute-start | bytes 393224 | tf_op jit(solution)/shard_map/ppermute | solution.py:32
  54.2 1.6 %collective-permute-start.11 = (f32[2,384]{1,0:T(2,128)}, f32[2,384]{1,0:T(2,128)}, u32[]{:S(2)}, u32[]{:S(2)}) collective-permute-start(f32[2,384]{1,0:T(2,128)} %collective-permute-done.9.refs_11_), channel_id=1, source_target_pairs={{0,8},{4,12},{8,16},{12,20},{16,24},{20,28},{24,0},{28,4},{1,9},{5... | collective-permute-start | bytes 9224 | tf_op jit(solution)/shard_map/ppermute | solution.py:32
  55.8 1.3 %copy.20.refs_19_ = f32[2,1]{1,0:T(2,128)} copy(f32[2,1]{0,1:T(1,128)} %bitcast.6) | data formatting | bytes 16 | tf_op jit(solution)/shard_map/broadcast_in_dim | solution.py:472
  57.1 1.6 %copy-done.2 = f32[512,1024]{1,0:T(8,128)S(1)} copy-done((f32[512,1024]{1,0:T(8,128)S(1)}, f32[512,1024]{1,0:T(8,128)}, u32[]{:S(2)}) %copy-start.2) | copy-done | bytes 2097176
  58.7 0.9 copy-done.5
  59.7 1.8 %shard_map.127.refs_17_ = f32[2,128,512]{2,1,0:T(8,128)S(1)} custom-call(bf16[512,512]{1,0:T(8,128)(2,1)S(1)} %get-tuple-element.108.refs_0_.key, bf16[512,1024]{1,0:T(8,128)(2,1)S(1)} %get-tuple-element.109.refs_1_.value, bf16[2,128,512]{2,1,0:T(8,128)(2,1)S(1)} %get-tuple-element.110.refs_2_.refs_8_.refs_9_, bf16[2,128,512]{2,1,0:T(8,128)(2,1)S(1)} %copy-done.5, ...), custom_call_target="tpu_custom_call" | custom-call | flops 1000000 | bytes 100000 | tf_op jit(solution)/shard_map/pallas_call | solution.py:439
  61.5 1.7 %shard_map.128 = (bf16[2,128,512]{2,1,0:T(8,128)(2,1)S(1)}, bf16[2,128,512]{2,1,0:T(8,128)(2,1)S(1)}, f32[2,256]{1,0:T(2,128)S(1)}, f32[2,128]{1,0:T(2,128)S(1)}) custom-call(bf16[512,512]{1,0:T(8,128)(2,1)S(1)} %get-tuple-element.108.refs_0_.key, bf16[512,1024]{1,0:T(8,128)(2,1)S(1)} %get-tuple-element.109.refs_1_.value, ...), custom_call_target="tpu_custom_call" | custom-call | flops 1000000 | bytes 100000 | tf_op jit(solution)/shard_map/pallas_call | solution.py:455
  63.3 1.6 %collective-permute-start.15 = (bf16[2,128,512]{2,1,0:T(8,128)(2,1)S(1)}, bf16[2,128,512]{2,1,0:T(8,128)(2,1)S(1)}, u32[]{:S(2)}, u32[]{:S(2)}) collective-permute-start(bf16[2,128,512]{2,1,0:T(8,128)(2,1)S(1)} %get-tuple-element.136), channel_id=1, source_target_pairs={{0,4},{4,0},{8,12},{12,8},{16,20},{20,16},{24,28},{28,24},{1,5},{5... | collective-permute-start | bytes 786440 | tf_op jit(solution)/shard_map/ppermute | solution.py:27
  64.8 4.2 %shard_map.129 = (f32[512,1024]{1,0:T(8,128)S(1)}, f32[512,1024]{1,0:T(8,128)S(1)}, bf16[1024,4096]{1,0:T(8,128)(2,1)S(1)}) custom-call(s32[3]{0:T(128)S(1)} %pad_add_fusion.info.refs_4_.refs_6_.refs_7_.refs_5_, s32[4]{0:T(128)S(1)} %copy-done.12, f32[2,128]{1,0:T(2,128)S(1)} %get-tuple-element.137.top_in, ...), custom_call_target="tpu_custom_call" | custom-call | flops 1000000 | bytes 100000 | tf_op jit(solution)/shard_map/pallas_call | solution.py:527
  69.0 0.7 collective-permute-done.15.other
  69.7 1.6 %shard_map.130 = (bf16[512,1024]{1,0:T(8,128)(2,1)S(1)}, bf16[512,512]{1,0:T(8,128)(2,1)S(1)}) custom-call(s32[3]{0:T(128)S(1)} %pad_add_fusion.info.refs_4_.refs_6_.refs_7_.refs_5_, bf16[512,512]{1,0:T(8,128)(2,1)S(1)} %get-tuple-element.119.refs_2_.refs_4_.query, bf16[2,128,512]{2,1,0:T(8,128)(2,1)S(1)} %get-tuple-element.135.own, ...), custom_call_target="tpu_custom_call" | custom-call | flops 3000000000 | bytes 8000000 | tf_op jit(solution)/shard_map/pallas_call | solution.py:568
  71.3 0.1 collective-permute-start.16
  71.4 1.8 %shard_map.131 = (bf16[512,512]{1,0:T(8,128)(2,1)S(1)}, bf16[512,512]{1,0:T(8,128)(2,1)S(1)}) custom-call(s32[3]{0:T(128)S(1)} %pad_add_fusion.info.refs_4_.refs_6_.refs_7_.refs_5_, bf16[512,1024]{1,0:T(8,128)(2,1)S(1)} %get-tuple-element.151.hidden, bf16[1024,4096]{1,0:T(8,128)(2,1)S(1)} %get-tuple-element.141.w), custom_call_target="tpu_custom_call" | custom-call | flops 1000000 | bytes 100000 | tf_op jit(solution)/shard_map/pallas_call | solution.py:590
  73.2 0.6 collective-permute-start.18
  73.8 0.1 copy.28
  73.8 0.1 convert_add_fusion.3
  74.0 1.6 %collective-permute-start.17 = (bf16[512,256]{1,0:T(8,128)(2,1)S(1)}, bf16[512,256]{1,0:T(8,128)(2,1)S(1)}, u32[]{:S(2)}, u32[]{:S(2)}) collective-permute-start(bf16[512,256]{1,0:T(8,128)(2,1)S(1)} %slice.99), channel_id=1, source_target_pairs={{0,2},{1,3},{2,0},{3,1},{4,6},{5,7},{6,4},{7,5},{8,10},{9,11},{10,... | collective-permute-start | bytes 786440 | tf_op jit(solution)/shard_map/ppermute | solution.py:27
  75.6 1.8 %shard_map.132 = (bf16[512,512]{1,0:T(8,128)(2,1)S(1)}, bf16[512,512]{1,0:T(8,128)(2,1)S(1)}) custom-call(s32[3]{0:T(128)S(1)} %pad_add_fusion.info.refs_4_.refs_6_.refs_7_.refs_5_, bf16[512,1024]{1,0:T(8,128)(2,1)S(1)} %get-tuple-element.151.hidden, bf16[1024,4096]{1,0:T(8,128)(2,1)S(1)} %get-tuple-element.141.w), custom_call_target="tpu_custom_call" | custom-call | flops 1000000 | bytes 100000 | tf_op jit(solution)/shard_map/pallas_call | solution.py:590
  77.5 0.1 collective-permute-start.20
  77.6 0.1 convert_add_fusion.2
  77.8 0.6 collective-permute-start.19
  78.3 1.8 %shard_map.133 = (bf16[512,512]{1,0:T(8,128)(2,1)S(1)}, bf16[512,512]{1,0:T(8,128)(2,1)S(1)}) custom-call(s32[3]{0:T(128)S(1)} %pad_add_fusion.info.refs_4_.refs_6_.refs_7_.refs_5_, bf16[512,1024]{1,0:T(8,128)(2,1)S(1)} %get-tuple-element.151.hidden, bf16[1024,4096]{1,0:T(8,128)(2,1)S(1)} %get-tuple-element.141.w), custom_call_target="tpu_custom_call" | custom-call | flops 1000000 | bytes 100000 | tf_op jit(solution)/shard_map/pallas_call | solution.py:590
  80.2 0.3 collective-permute-start.22
  80.4 2.9 %collective-permute-done.17 = bf16[512,256]{1,0:T(8,128)(2,1)S(1)} collective-permute-done((bf16[512,256]{1,0:T(8,128)(2,1)S(1)}, bf16[512,256]{1,0:T(8,128)(2,1)S(1)}, u32[]{:S(2)}, u32[]{:S(2)}) %collective-permute-start.17) | collective-permute-done | bytes 262176 | tf_op jit(solution)/shard_map/ppermute | solution.py:27
  83.3 0.2 fusion.8
  83.5 0.1 convert_add_fusion.1
  83.7 1.6 %collective-permute-start.21 = (bf16[512,256]{1,0:T(8,128)(2,1)S(1)}, bf16[512,256]{1,0:T(8,128)(2,1)S(1)}, u32[]{:S(2)}, u32[]{:S(2)}) collective-permute-start(bf16[512,256]{1,0:T(8,128)(2,1)S(1)} %slice.97), channel_id=1, source_target_pairs={{0,2},{1,3},{2,0},{3,1},{4,6},{5,7},{6,4},{7,5},{8,10},{9,11},{10,... | collective-permute-start | bytes 786440 | tf_op jit(solution)/shard_map/ppermute | solution.py:27
  85.3 1.3 %shard_map.134 = bf16[512,512]{1,0:T(8,128)(2,1)S(1)} custom-call(s32[3]{0:T(128)S(1)} %pad_add_fusion.info.refs_4_.refs_6_.refs_7_.refs_5_, bf16[512,1024]{1,0:T(8,128)(2,1)S(1)} %get-tuple-element.151.hidden, bf16[1024,4096]{1,0:T(8,128)(2,1)S(1)} %get-tuple-element.141.w), custom_call_target="tpu_custom_call" | custom-call | flops 1000000 | bytes 100000 | tf_op jit(solution)/shard_map/pallas_call | solution.py:590
  86.5 0.1 convert_add_fusion
  86.7 0.6 collective-permute-start.23
  87.3 1.6 %collective-permute-done.19 = bf16[512,256]{1,0:T(8,128)(2,1)S(1)} collective-permute-done((bf16[512,256]{1,0:T(8,128)(2,1)S(1)}, bf16[512,256]{1,0:T(8,128)(2,1)S(1)}, u32[]{:S(2)}, u32[]{:S(2)}) %collective-permute-start.19) | collective-permute-done | bytes 262176 | tf_op jit(solution)/shard_map/ppermute | solution.py:27
  88.9 0.1 fusion.9
  89.1 5.5 %collective-permute-done.21 = bf16[512,256]{1,0:T(8,128)(2,1)S(1)} collective-permute-done((bf16[512,256]{1,0:T(8,128)(2,1)S(1)}, bf16[512,256]{1,0:T(8,128)(2,1)S(1)}, u32[]{:S(2)}, u32[]{:S(2)}) %collective-permute-start.21) | collective-permute-done | bytes 262176 | tf_op jit(solution)/shard_map/ppermute | solution.py:27
  94.5 0.1 fusion.10
  94.7 4.5 %collective-permute-done.23 = bf16[512,256]{1,0:T(8,128)(2,1)S(1)} collective-permute-done((bf16[512,256]{1,0:T(8,128)(2,1)S(1)}, bf16[512,256]{1,0:T(8,128)(2,1)S(1)}, u32[]{:S(2)}, u32[]{:S(2)}) %collective-permute-start.23) | collective-permute-done | bytes 262176 | tf_op jit(solution)/shard_map/ppermute | solution.py:27
  99.2 0.8 fusion.11
  (53 shorter events, 0.3 us)
Async XLA Ops:
  0.0 8.7 %copy-start = (bf16[512,1024]{1,0:T(8,128)(2,1)S(1)}, bf16[512,1024]{1,0:T(8,128)(2,1)}, u32[]{:S(2)}) copy-start(bf16[512,1024]{1,0:T(8,128)(2,1)} %refs_7_.2) | copy-start | bytes 3145732
  0.0 8.6 %copy-start.17 = (bf16[2,4096,2]{1,2,0:T(2,128)(2,1)S(1)}, bf16[2,4096,2]{1,2,0:T(2,128)(2,1)}, u32[]{:S(2)}) copy-start(bf16[2,4096,2]{1,2,0:T(2,128)(2,1)} %param.17) | copy-start | bytes 98308
  0.0 4.1 %collective-permute-start = (bf16[512,1024]{1,0:T(8,128)(2,1)}, bf16[512,1024]{1,0:T(8,128)(2,1)S(1)}, u32[]{:S(2)}, u32[]{:S(2)}) collective-permute-start(bf16[512,1024]{1,0:T(8,128)(2,1)} %refs_7_.2), channel_id=1, source_target_pairs={{0,1},{1,0},{2,3},{3,2},{4,5},{5,4},{6,7},{7,6},{8,9},{9,8},{10,11... | collective-permute-start | bytes 3145736 | tf_op jit(solution)/shard_map/ppermute | solution.py:27
  1.4 15.3 %collective-permute-start.2 = (bf16[512,256]{1,0:T(8,128)(2,1)S(1)}, bf16[512,256]{1,0:T(8,128)(2,1)S(1)}, u32[]{:S(2)}, u32[]{:S(2)}) collective-permute-start(bf16[512,256]{1,0:T(8,128)(2,1)S(1)} %shard_map.119), channel_id=1, source_target_pairs={{0,2},{1,3},{2,0},{3,1},{4,6},{5,7},{6,4},{7,5},{8,10},{9,11},{10,... | collective-permute-start | bytes 786440 | tf_op jit(solution)/shard_map/ppermute | solution.py:27
  4.1 12.6 %copy-start.7 = (bf16[512,1024]{1,0:T(8,128)(2,1)}, bf16[512,1024]{1,0:T(8,128)(2,1)S(1)}, u32[]{:S(2)}) copy-start(bf16[512,1024]{1,0:T(8,128)(2,1)S(1)} %collective-permute-done.refs_1_.refs_5_) | copy-start | bytes 3145732
  6.5 10.4 %collective-permute-start.3 = (bf16[512,256]{1,0:T(8,128)(2,1)}, bf16[512,256]{1,0:T(8,128)(2,1)S(1)}, u32[]{:S(2)}, u32[]{:S(2)}) collective-permute-start(bf16[512,256]{1,0:T(8,128)(2,1)} %get-tuple-element.81), channel_id=1, source_target_pairs={{0,2},{1,3},{2,0},{3,1},{4,6},{5,7},{6,4},{7,5},{8,10},{9,11},{10,... | collective-permute-start | bytes 786440 | tf_op jit(solution)/shard_map/ppermute | solution.py:27
  8.3 19.5 %collective-permute-start.1 = (bf16[512,512]{1,0:T(8,128)(2,1)}, bf16[512,512]{1,0:T(8,128)(2,1)S(1)}, u32[]{:S(2)}, u32[]{:S(2)}) collective-permute-start(bf16[512,512]{1,0:T(8,128)(2,1)} %get-tuple-element.80), channel_id=1, source_target_pairs={{0,2},{1,3},{2,0},{3,1},{4,6},{5,7},{6,4},{7,5},{8,10},{9,11},{10,... | collective-permute-start | bytes 1572872 | tf_op jit(solution)/shard_map/ppermute | solution.py:27
  16.9 1.5 %collective-permute-start.4 = (bf16[512,256]{1,0:T(8,128)(2,1)S(1)}, bf16[512,256]{1,0:T(8,128)(2,1)S(1)}, u32[]{:S(2)}, u32[]{:S(2)}) collective-permute-start(bf16[512,256]{1,0:T(8,128)(2,1)S(1)} %collective-permute-done.2.refs_0_), channel_id=1, source_target_pairs={{0,1},{1,0},{2,3},{3,2},{4,5},{5,4},{6,7},{7,6},{8,9},{9,8},{10,11... | collective-permute-start | bytes 786440 | tf_op jit(solution)/shard_map/ppermute | solution.py:27
  16.9 1.9 %collective-permute-start.5 = (bf16[512,256]{1,0:T(8,128)(2,1)S(1)}, bf16[512,256]{1,0:T(8,128)(2,1)S(1)}, u32[]{:S(2)}, u32[]{:S(2)}) collective-permute-start(bf16[512,256]{1,0:T(8,128)(2,1)S(1)} %collective-permute-done.3.refs_2_), channel_id=1, source_target_pairs={{0,1},{1,0},{2,3},{3,2},{4,5},{5,4},{6,7},{7,6},{8,9},{9,8},{10,11... | collective-permute-start | bytes 786440 | tf_op jit(solution)/shard_map/ppermute | solution.py:27
  27.8 1.7 %copy-start.9 = (bf16[512,512]{1,0:T(8,128)(2,1)}, bf16[512,512]{1,0:T(8,128)(2,1)S(1)}, u32[]{:S(2)}) copy-start(bf16[512,512]{1,0:T(8,128)(2,1)S(1)} %collective-permute-done.1.x.refs_6_) | copy-start | bytes 1572868
  27.8 1.9 %collective-permute-start.6 = (bf16[512,512]{1,0:T(8,128)(2,1)S(1)}, bf16[512,512]{1,0:T(8,128)(2,1)S(1)}, u32[]{:S(2)}, u32[]{:S(2)}) collective-permute-start(bf16[512,512]{1,0:T(8,128)(2,1)S(1)} %collective-permute-done.1.x.refs_6_), channel_id=1, source_target_pairs={{0,1},{1,0},{2,3},{3,2},{4,5},{5,4},{6,7},{7,6},{8,9},{9,8},{10,11... | collective-permute-start | bytes 1572872 | tf_op jit(solution)/shard_map/ppermute | solution.py:27
  27.8 1.9 %copy-start.11 = (s32[4]{0:T(128)S(1)}, s32[4]{0:T(128)}, u32[]{:S(2)}) copy-start(s32[4]{0:T(128)} %docs.3) | copy-start | bytes 52
  27.8 1.9 %copy-start.15 = (f32[2,2]{1,0:T(2,128)S(1)}, f32[2,2]{1,0:T(2,128)}, u32[]{:S(2)}) copy-start(f32[2,2]{1,0:T(2,128)} %bias.1) | copy-start | bytes 52
  29.8 4.9 %copy-start.8 = (bf16[512,1024]{1,0:T(8,128)(2,1)S(1)}, bf16[512,1024]{1,0:T(8,128)(2,1)}, u32[]{:S(2)}) copy-start(bf16[512,1024]{1,0:T(8,128)(2,1)} %copy-done.7) | copy-start | bytes 3145732
  29.8 4.9 %copy-start.10 = (bf16[512,512]{1,0:T(8,128)(2,1)S(1)}, bf16[512,512]{1,0:T(8,128)(2,1)}, u32[]{:S(2)}) copy-start(bf16[512,512]{1,0:T(8,128)(2,1)} %copy-done.9) | copy-start | bytes 1572868
  32.6 8.6 %collective-permute-start.8 = (bf16[2,128,512]{2,1,0:T(8,128)(2,1)S(1)}, bf16[2,128,512]{2,1,0:T(8,128)(2,1)S(1)}, u32[]{:S(2)}, u32[]{:S(2)}) collective-permute-start(bf16[2,128,512]{2,1,0:T(8,128)(2,1)S(1)} %get-tuple-element.107), channel_id=1, source_target_pairs={{0,4},{4,0},{8,12},{12,8},{16,20},{20,16},{24,28},{28,24},{1,5},{5... | collective-permute-start | bytes 786440 | tf_op jit(solution)/shard_map/ppermute | solution.py:27
  34.4 6.8 %collective-permute-start.7 = (f32[2,384]{1,0:T(2,128)S(1)}, f32[2,384]{1,0:T(2,128)S(1)}, u32[]{:S(2)}, u32[]{:S(2)}) collective-permute-start(f32[2,384]{1,0:T(2,128)S(1)} %get-tuple-element.106.refs_6_.refs_7_), channel_id=1, source_target_pairs={{0,4},{4,0},{8,12},{12,8},{16,20},{20,16},{24,28},{28,24},{1,5},{5... | collective-permute-start | bytes 9224 | tf_op jit(solution)/shard_map/ppermute | solution.py:27
  41.2 9.8 %copy-start.4 = (bf16[2,128,512]{2,1,0:T(8,128)(2,1)}, bf16[2,128,512]{2,1,0:T(8,128)(2,1)S(1)}, u32[]{:S(2)}) copy-start(bf16[2,128,512]{2,1,0:T(8,128)(2,1)S(1)} %collective-permute-done.8.refs_9_.refs_3_.refs_10_) | copy-start | bytes 786436
  42.0 10.4 %collective-permute-start.10 = (bf16[1,128,512]{2,1,0:T(8,128)(2,1)S(1)}, bf16[1,128,512]{2,1,0:T(8,128)(2,1)S(1)}, u32[]{:S(2)}, u32[]{:S(2)}) collective-permute-start(bf16[1,128,512]{2,1,0:T(8,128)(2,1)S(1)} %get-tuple-element.123), channel_id=1, source_target_pairs={{0,8},{4,12},{8,16},{12,20},{16,24},{20,28},{24,0},{28,4},{1,9},{5... | collective-permute-start | bytes 393224 | tf_op jit(solution)/shard_map/ppermute | solution.py:32
  43.9 8.6 %collective-permute-start.13 = (bf16[1,128,512]{2,1,0:T(8,128)(2,1)S(1)}, bf16[1,128,512]{2,1,0:T(8,128)(2,1)}, u32[]{:S(2)}, u32[]{:S(2)}) collective-permute-start(bf16[1,128,512]{2,1,0:T(8,128)(2,1)S(1)} %get-tuple-element.130), channel_id=1, source_target_pairs={{0,8},{4,12},{8,16},{12,20},{16,24},{20,28},{24,0},{28,4},{1,9},{5... | collective-permute-start | bytes 393224 | tf_op jit(solution)/shard_map/ppermute | solution.py:32
  45.5 6.9 %collective-permute-start.9 = (f32[2,384]{1,0:T(2,128)S(1)}, f32[2,384]{1,0:T(2,128)}, u32[]{:S(2)}, u32[]{:S(2)}) collective-permute-start(f32[2,384]{1,0:T(2,128)S(1)} %get-tuple-element.122), channel_id=1, source_target_pairs={{0,8},{4,12},{8,16},{12,20},{16,24},{20,28},{24,0},{28,4},{1,9},{5... | collective-permute-start | bytes 9224 | tf_op jit(solution)/shard_map/ppermute | solution.py:32
  51.1 1.3 %copy-start.1 = (f32[512,1024]{1,0:T(8,128)}, f32[512,1024]{1,0:T(8,128)S(1)}, u32[]{:S(2)}) copy-start(f32[512,1024]{1,0:T(8,128)S(1)} %shard_map.126.refs_6_.refs_3_.gate) | copy-start | bytes 6291460
  52.4 9.1 %collective-permute-start.12 = (bf16[1,128,512]{2,1,0:T(8,128)(2,1)S(1)}, bf16[1,128,512]{2,1,0:T(8,128)(2,1)}, u32[]{:S(2)}, u32[]{:S(2)}) collective-permute-start(bf16[1,128,512]{2,1,0:T(8,128)(2,1)S(1)} %collective-permute-done.10.refs_13_), channel_id=1, source_target_pairs={{0,8},{4,12},{8,16},{12,20},{16,24},{20,28},{24,0},{28,4},{1,9},{5... | collective-permute-start | bytes 393224 | tf_op jit(solution)/shard_map/ppermute | solution.py:32
  52.5 9.0 %collective-permute-start.14 = (bf16[1,128,512]{2,1,0:T(8,128)(2,1)}, bf16[1,128,512]{2,1,0:T(8,128)(2,1)}, u32[]{:S(2)}, u32[]{:S(2)}) collective-permute-start(bf16[1,128,512]{2,1,0:T(8,128)(2,1)} %collective-permute-done.13.refs_14_), channel_id=1, source_target_pairs={{0,8},{4,12},{8,16},{12,20},{16,24},{20,28},{24,0},{28,4},{1,9},{5... | collective-permute-start | bytes 393224 | tf_op jit(solution)/shard_map/ppermute | solution.py:32
  54.2 7.2 %collective-permute-start.11 = (f32[2,384]{1,0:T(2,128)}, f32[2,384]{1,0:T(2,128)}, u32[]{:S(2)}, u32[]{:S(2)}) collective-permute-start(f32[2,384]{1,0:T(2,128)} %collective-permute-done.9.refs_11_), channel_id=1, source_target_pairs={{0,8},{4,12},{8,16},{12,20},{16,24},{20,28},{24,0},{28,4},{1,9},{5... | collective-permute-start | bytes 9224 | tf_op jit(solution)/shard_map/ppermute | solution.py:32
  57.1 1.6 %copy-start.2 = (f32[512,1024]{1,0:T(8,128)S(1)}, f32[512,1024]{1,0:T(8,128)}, u32[]{:S(2)}) copy-start(f32[512,1024]{1,0:T(8,128)} %copy-done.1) | copy-start | bytes 6291460
  58.7 0.9 copy-start.5
  59.7 1.8 %copy-start.3 = (f32[512,1024]{1,0:T(8,128)S(1)}, f32[512,1024]{1,0:T(8,128)}, u32[]{:S(2)}) copy-start(f32[512,1024]{1,0:T(8,128)} %copy-done.1) | copy-start | bytes 6291460
  59.7 1.8 %copy-start.6 = (bf16[2,128,512]{2,1,0:T(8,128)(2,1)S(1)}, bf16[2,128,512]{2,1,0:T(8,128)(2,1)}, u32[]{:S(2)}) copy-start(bf16[2,128,512]{2,1,0:T(8,128)(2,1)} %copy-done.4) | copy-start | bytes 786436
  59.7 1.9 %copy-start.12 = (s32[4]{0:T(128)S(1)}, s32[4]{0:T(128)}, u32[]{:S(2)}) copy-start(s32[4]{0:T(128)} %docs.3) | copy-start | bytes 52
  59.7 1.9 %copy-start.13 = (f32[2,256]{1,0:T(2,128)S(1)}, f32[2,256]{1,0:T(2,128)}, u32[]{:S(2)}) copy-start(f32[2,256]{1,0:T(2,128)} %refs_18_.1) | copy-start | bytes 6148
  59.7 1.9 %copy-start.14 = (f32[2,1]{1,0:T(2,128)S(1)}, f32[2,1]{1,0:T(2,128)}, u32[]{:S(2)}) copy-start(f32[2,1]{1,0:T(2,128)} %copy.20.refs_19_) | copy-start | bytes 28
  63.3 6.4 %collective-permute-start.15 = (bf16[2,128,512]{2,1,0:T(8,128)(2,1)S(1)}, bf16[2,128,512]{2,1,0:T(8,128)(2,1)S(1)}, u32[]{:S(2)}, u32[]{:S(2)}) collective-permute-start(bf16[2,128,512]{2,1,0:T(8,128)(2,1)S(1)} %get-tuple-element.136), channel_id=1, source_target_pairs={{0,4},{4,0},{8,12},{12,8},{16,20},{20,16},{24,28},{28,24},{1,5},{5... | collective-permute-start | bytes 786440 | tf_op jit(solution)/shard_map/ppermute | solution.py:27
  71.3 2.5 %collective-permute-start.16 = (bf16[512,512]{1,0:T(8,128)(2,1)S(1)}, bf16[512,512]{1,0:T(8,128)(2,1)S(1)}, u32[]{:S(2)}, u32[]{:S(2)}) collective-permute-start(bf16[512,512]{1,0:T(8,128)(2,1)S(1)} %get-tuple-element.144), channel_id=1, source_target_pairs={{0,1},{1,0},{2,3},{3,2},{4,5},{5,4},{6,7},{7,6},{8,9},{9,8},{10,11... | collective-permute-start | bytes 1572872 | tf_op jit(solution)/shard_map/ppermute | solution.py:27
  73.2 4.4 %collective-permute-start.18 = (bf16[512,512]{1,0:T(8,128)(2,1)S(1)}, bf16[512,512]{1,0:T(8,128)(2,1)S(1)}, u32[]{:S(2)}, u32[]{:S(2)}) collective-permute-start(bf16[512,512]{1,0:T(8,128)(2,1)S(1)} %get-tuple-element.147), channel_id=1, source_target_pairs={{0,1},{1,0},{2,3},{3,2},{4,5},{5,4},{6,7},{7,6},{8,9},{9,8},{10,11... | collective-permute-start | bytes 1572872 | tf_op jit(solution)/shard_map/ppermute | solution.py:27
  74.0 9.2 %collective-permute-start.17 = (bf16[512,256]{1,0:T(8,128)(2,1)S(1)}, bf16[512,256]{1,0:T(8,128)(2,1)S(1)}, u32[]{:S(2)}, u32[]{:S(2)}) collective-permute-start(bf16[512,256]{1,0:T(8,128)(2,1)S(1)} %slice.99), channel_id=1, source_target_pairs={{0,2},{1,3},{2,0},{3,1},{4,6},{5,7},{6,4},{7,5},{8,10},{9,11},{10,... | collective-permute-start | bytes 786440 | tf_op jit(solution)/shard_map/ppermute | solution.py:27
  77.5 6.0 %collective-permute-start.20 = (bf16[512,512]{1,0:T(8,128)(2,1)S(1)}, bf16[512,512]{1,0:T(8,128)(2,1)S(1)}, u32[]{:S(2)}, u32[]{:S(2)}) collective-permute-start(bf16[512,512]{1,0:T(8,128)(2,1)S(1)} %get-tuple-element.150), channel_id=1, source_target_pairs={{0,1},{1,0},{2,3},{3,2},{4,5},{5,4},{6,7},{7,6},{8,9},{9,8},{10,11... | collective-permute-start | bytes 1572872 | tf_op jit(solution)/shard_map/ppermute | solution.py:27
  77.8 11.1 %collective-permute-start.19 = (bf16[512,256]{1,0:T(8,128)(2,1)S(1)}, bf16[512,256]{1,0:T(8,128)(2,1)S(1)}, u32[]{:S(2)}, u32[]{:S(2)}) collective-permute-start(bf16[512,256]{1,0:T(8,128)(2,1)S(1)} %slice.98), channel_id=1, source_target_pairs={{0,2},{1,3},{2,0},{3,1},{4,6},{5,7},{6,4},{7,5},{8,10},{9,11},{10,... | collective-permute-start | bytes 786440 | tf_op jit(solution)/shard_map/ppermute | solution.py:27
  80.2 6.4 %collective-permute-start.22 = (bf16[512,512]{1,0:T(8,128)(2,1)S(1)}, bf16[512,512]{1,0:T(8,128)(2,1)S(1)}, u32[]{:S(2)}, u32[]{:S(2)}) collective-permute-start(bf16[512,512]{1,0:T(8,128)(2,1)S(1)} %get-tuple-element.152), channel_id=1, source_target_pairs={{0,1},{1,0},{2,3},{3,2},{4,5},{5,4},{6,7},{7,6},{8,9},{9,8},{10,11... | collective-permute-start | bytes 1572872 | tf_op jit(solution)/shard_map/ppermute | solution.py:27
  83.7 10.8 %collective-permute-start.21 = (bf16[512,256]{1,0:T(8,128)(2,1)S(1)}, bf16[512,256]{1,0:T(8,128)(2,1)S(1)}, u32[]{:S(2)}, u32[]{:S(2)}) collective-permute-start(bf16[512,256]{1,0:T(8,128)(2,1)S(1)} %slice.97), channel_id=1, source_target_pairs={{0,2},{1,3},{2,0},{3,1},{4,6},{5,7},{6,4},{7,5},{8,10},{9,11},{10,... | collective-permute-start | bytes 786440 | tf_op jit(solution)/shard_map/ppermute | solution.py:27
  86.7 12.5 %collective-permute-start.23 = (bf16[512,256]{1,0:T(8,128)(2,1)S(1)}, bf16[512,256]{1,0:T(8,128)(2,1)S(1)}, u32[]{:S(2)}, u32[]{:S(2)}) collective-permute-start(bf16[512,256]{1,0:T(8,128)(2,1)S(1)} %slice.96), channel_id=1, source_target_pairs={{0,2},{1,3},{2,0},{3,1},{4,6},{5,7},{6,4},{7,5},{8,10},{9,11},{10,... | collective-permute-start | bytes 786440 | tf_op jit(solution)/shard_map/ppermute | solution.py:27
  94.6 4.6 %copy-start.16 = (bf16[512,1024]{1,0:T(8,128)(2,1)}, bf16[512,1024]{1,0:T(8,128)(2,1)S(1)}, u32[]{:S(2)}) copy-start(bf16[512,1024]{1,0:T(8,128)(2,1)S(1)} %fusion.10) | copy-start | bytes 3145732

commit v11 on v10

--- a/solution.py
+++ b/solution.py
@@ -52,6 +52,21 @@
 
 def holding(kernel, held):
     return (lambda *refs: kernel(*refs[len(held) :])) if held else kernel
+
+
+def same_kernel(x, out):
+    out[...] = x[...]
+
+
+def hold(x, held):
+    return pl.pallas_call(
+        holding(same_kernel, held),
+        out_shape=pltpu.VMEM(x.shape, x.dtype),
+        in_specs=[VMEM_SPEC] * (len(held) + 1),
+        out_specs=VMEM_SPEC,
+        compiler_params=params(4),
+        cost_estimate=cost(1e6, 1e5),
+    )(*in_vmem(*held, x))
 
 
 def split_kernel(starts, tokens, *refs):
@@ -376,7 +391,13 @@
     heads = own.shape[0]
     smalls, refs = refs[:reach], refs[reach:]
     states = [refs[k * heads : (k + 1) * heads] for k in range(reach)]
-    carry, carry_norm, carry_max, own_out, other_out, norm_out, top_out = refs[reach * heads :]
+    carry, carry_norm, carry_max, own_out, other_out, norm_out, top_out, base, sem = refs[
+        reach * heads :
+    ]
+    half = base.shape[1]
+    rows = pl.ds(pl.multiple_of(info[1] * half, half), half)
+    fetch = pltpu.make_async_copy(carry.at[:, rows], base, sem)
+    fetch.start()
     size = own.shape[1] - 128
     side = info[1]
     even = side == 0
@@ -412,39 +433,18 @@
     for k in range(reach):
         norm = norm + w_own[k] * smalls[k][:, :size]
     norm_out[...] = norm
+    fetch.wait()
     for h in range(heads):
         at = slice(h, h + 1)
         here = jnp.where(even, kept[h].astype(F32), got[h].astype(F32))
-        base = carry[h]
-        mine = w_own[reach][at] * base + direct_own[at] * here
-        theirs = w_other[reach][at] * base + direct_other[at] * here
+        mine = w_own[reach][at] * base[h] + direct_own[at] * here
+        theirs = w_other[reach][at] * base[h] + direct_other[at] * here
         for k in range(reach):
             state = states[k][h][0].astype(F32)
             mine = mine + w_own[k][at] * state
             theirs = theirs + w_other[k][at] * state
         own_out[h] = mine.astype(BF)
         other_out[h] = theirs.astype(BF)
-
-
-def carry_kernel(info, carry, out, sem):
-    half = out.shape[1]
-    rows = pl.ds(pl.multiple_of(info[1] * half, half), half)
-    copy = pltpu.make_async_copy(carry.at[:, rows], out, sem)
-    copy.start()
-    copy.wait()
-
-
-def carry_half(info, carry, held):
-    heads, size, wide = carry.shape
-    return pl.pallas_call(
-        holding(carry_kernel, held),
-        out_shape=pltpu.VMEM((heads, size // 2, wide), F32),
-        in_specs=[VMEM_SPEC] * len(held) + [SMEM_SPEC, HBM_SPEC],
-        out_specs=VMEM_SPEC,
-        scratch_shapes=[pltpu.SemaphoreType.DMA],
-        compiler_params=params(4),
-        cost_estimate=cost(1e6, 1e5),
-    )(*in_vmem(*held), info, in_hbm(carry))
 
 
 def incoming_state(
@@ -462,14 +462,16 @@
         ),
         in_specs=[VMEM_SPEC] * len(held)
         + [SMEM_SPEC] * 2
-        + [VMEM_SPEC] * (7 + (1 + heads) * len(smalls)),
+        + [VMEM_SPEC] * (4 + (1 + heads) * len(smalls))
+        + [HBM_SPEC, VMEM_SPEC, VMEM_SPEC],
         out_specs=(VMEM_SPEC,) * 4,
+        scratch_shapes=[pltpu.VMEM(kept.shape, F32), pltpu.SemaphoreType.DMA],
         compiler_params=params(6),
         cost_estimate=cost(1e6, 1e5),
     )(
         *in_vmem(*held), info, docs,
-        *in_vmem(small, small_other, kept, got, *smalls, *sum(states, []), carry),
-        carry_norm, carry_max[:, None],
+        *in_vmem(small, small_other, kept, got, *smalls, *sum(states, [])),
+        in_hbm(carry), carry_norm, carry_max[:, None],
     )
 
 
@@ -689,22 +691,23 @@
         travel = down(travel)
         state_pair = [first] + [down(x) for x in state_pair[1:]]
         if step == 0:
+            small_here = hold(after(before, small), (*held, *gate))
+            travel, first, small = lax.optimization_barrier((travel, state_pair[0], small_here))
+            state_pair[0] = first
+        elif step == 1:
             near_xs = [after(before, source)]
             gate = stage(
                 info, near_xs, near_at[:1], (w_outgate,), share, None, gate,
                 finishes=((jax.nn.sigmoid, F32),), held=held,
             )
-            travel, first, *gate = lax.optimization_barrier((travel, state_pair[0], *gate))
-            state_pair[0] = first
-        elif step == 1:
-            carry = carry_half(after(before, info), carry_matrix, (*held, *gate))
-            travel, carry, *state_pair = lax.optimization_barrier((travel, carry, *state_pair))
+            travel, *rest = lax.optimization_barrier((travel, *gate, *state_pair))
+            gate, state_pair = rest[:1], rest[1:]
         smalls.append(travel)
         states.append(state_pair)
     (gate,) = gate
     state_own, state_other, norm_in, top_own = incoming_state(
         info, doc_lengths, small, small_other, kept, got, smalls, states,
-        carry, carry_norm, carry_max, length, (keys, values, queries, gate, u),
+        carry_matrix, carry_norm, carry_max, length, (keys, values, queries, gate, u),
     )
     state_got = pair(state_other)
     base, slope, w_here = inner(

time: 100 us -> 103 us (1.030)
  waiting for transfers between devices: 18.9 us -> 23.9 us
  local copies, waits for them, and re-layouts: 5.49 us -> 4.13 us
    ppermute x6, waiting for transfers between devices: 0.02 us -> 5.03 us  [shifted(): return lax.ppermute(x, axis, [(i, (i + by) % size) for i in range(size)])]
    pallas_call x1, Pallas kernels: 1.77 us -> 0.01 us  [hold(): pl.pallas_call(holding(same_kernel, held), out_shape=pltpu.VMEM(x.shape,...]
    unnamed x37 -> x33, local copies, waits for them, and re-layouts: 4 us -> 2.66 us
  transfers between devices with their start and end apart: 24 -> 24, of which waited for: 11 -> 12; matrix products, arithmetic and copies ran while one was open for 3% -> 3% of each run, Pallas kernels for 43% -> 41%
where the time goes in v11:
time: 103 us; the launch traced here: 102 us
  Pallas kernels  49.6 us (48%)
  waiting for transfers between devices  23.9 us (23%)
  starting transfers between devices  22.6 us (22%)
  local copies, waits for them, and re-layouts  4.13 us (4%)
  other arithmetic  1.86 us (2%)
    pallas_call x4, Pallas kernels, stage(): pl.pallas_call(holding(functools.partial(stage_kernel, xs_at, skips or [0...  25.6 us
    ppermute x18, waiting for transfers between devices, swapped(): return lax.ppermute(x, axis, [(i, i ^ mask) for i in range(size)])  18.9 us
    ppermute x18, starting transfers between devices, swapped(): return lax.ppermute(x, axis, [(i, i ^ mask) for i in range(size)])  14.7 us
    ppermute x6, starting transfers between devices, shifted(): return lax.ppermute(x, axis, [(i, (i + by) % size) for i in range(size)])  7.89 us
    pallas_call x4, Pallas kernels, next_columns(): pl.pallas_call(functools.partial(columns_kernel, start, start + wide), ou...  6.73 us
    ppermute x6, waiting for transfers between devices, shifted(): return lax.ppermute(x, axis, [(i, (i + by) % size) for i in range(size)])  5.03 us
    pallas_call x1, Pallas kernels, inner(): pl.pallas_call(functools.partial(inner_kernel, heads), out_shape=(pltpu.V...  4.19 us
    pallas_call x2, Pallas kernels, split_tokens(): pl.pallas_call(functools.partial(split_kernel, starts), out_shape=tuple((...  3.36 us
  transfers between devices with their start and end apart: 24, of which 12 were waited for; matrix products, arithmetic and copies ran while one was open for 3% of the time, Pallas kernels for 41%

profile of v11, /device:TPU:0, one launch (start us, length us, event | category | flops | bytes accessed | tf_op | source)
XLA Modules:
  0.0 102.4 jit_solution(14398291772264928325)
XLA Ops:
  0.0 0.5 collective-permute-start
  0.5 1.0 shard_map.119
  1.4 2.7 %collective-permute-start.2 = (bf16[512,256]{1,0:T(8,128)(2,1)S(1)}, bf16[512,256]{1,0:T(8,128)(2,1)S(1)}, u32[]{:S(2)}, u32[]{:S(2)}) collective-permute-start(bf16[512,256]{1,0:T(8,128)(2,1)S(1)} %shard_map.119), channel_id=1, source_target_pairs={{0,2},{1,3},{2,0},{3,1},{4,6},{5,7},{6,4},{7,5},{8,10},{9,11},{10,... | collective-permute-start | bytes 786440 | tf_op jit(solution)/shard_map/ppermute | solution.py:27
  4.1 2.4 %shard_map.118 = (bf16[512,256]{1,0:T(8,128)(2,1)}, bf16[512,512]{1,0:T(8,128)(2,1)}) custom-call(bf16[512,1024]{1,0:T(8,128)(2,1)} %refs_7_.2), custom_call_target="tpu_custom_call" | custom-call | flops 1000000 | bytes 100000 | tf_op jit(solution)/shard_map/pallas_call | solution.py:85
  6.5 1.8 %collective-permute-start.3 = (bf16[512,256]{1,0:T(8,128)(2,1)}, bf16[512,256]{1,0:T(8,128)(2,1)S(1)}, u32[]{:S(2)}, u32[]{:S(2)}) collective-permute-start(bf16[512,256]{1,0:T(8,128)(2,1)} %get-tuple-element.81), channel_id=1, source_target_pairs={{0,2},{1,3},{2,0},{3,1},{4,6},{5,7},{6,4},{7,5},{8,10},{9,11},{10,... | collective-permute-start | bytes 786440 | tf_op jit(solution)/shard_map/ppermute | solution.py:27
  8.3 0.3 collective-permute-start.1
  8.6 0.1 pad_add_fusion.info.refs_4_.refs_6_.refs_5_
  8.7 8.0 %shard_map.120 = (f32[512,512]{1,0:T(8,128)S(1)}, f32[512,1024]{1,0:T(8,128)S(1)}, f32[512,512]{1,0:T(8,128)S(1)}, f32[4,512]{1,0:T(4,128)S(1)}) custom-call(s32[3]{0:T(128)S(1)} %pad_add_fusion.info.refs_4_.refs_6_.refs_5_, bf16[512,1024]{1,0:T(8,128)(2,1)S(1)} %copy-done, bf16[512,1024]{1,0:T(8,128)(2,1)S(1)} %collective-permute-done.refs_1_.refs_5_, ...), custom_call_target="tpu_custom_call" | custom-call | flops 1000000 | bytes 100000 | tf_op jit(solution)/shard_map/pallas_call | solution.py:223
  16.7 0.0 collective-permute-done.2.refs_0_
  16.7 0.1 collective-permute-done.3.refs_2_
  16.9 0.5 collective-permute-start.5
  17.4 1.0 %collective-permute-done.4.refs_1_ = bf16[512,256]{1,0:T(8,128)(2,1)S(1)} collective-permute-done((bf16[512,256]{1,0:T(8,128)(2,1)S(1)}, bf16[512,256]{1,0:T(8,128)(2,1)S(1)}, u32[]{:S(2)}, u32[]{:S(2)}) %collective-permute-start.4) | collective-permute-done | bytes 262176 | tf_op jit(solution)/shard_map/ppermute | solution.py:27
  18.4 0.4 collective-permute-done.5.refs_3_
  18.8 7.6 %shard_map.121 = (f32[512,512]{1,0:T(8,128)S(1)}, f32[512,1024]{1,0:T(8,128)S(1)}, f32[512,512]{1,0:T(8,128)S(1)}, f32[512,1024]{1,0:T(8,128)S(1)}, f32[4,512]{1...) custom-call(s32[3]{0:T(128)S(1)} %pad_add_fusion.info.refs_4_.refs_6, ...), custom_call_target="tpu_custom_call", output_to_operand_aliasing={{0}: (10, {}), {1}: (11, {}), {2}: (12, {}), {4}: (13, {})} | custom-call | flops 1000000 | bytes 100000 | tf_op jit(solution)/shard_map/pallas_call | solution.py:223
  26.4 1.4 %collective-permute-done.1.x.refs_6_ = bf16[512,512]{1,0:T(8,128)(2,1)S(1)} collective-permute-done((bf16[512,512]{1,0:T(8,128)(2,1)}, bf16[512,512]{1,0:T(8,128)(2,1)S(1)}, u32[]{:S(2)}, u32[]{:S(2)}) %collective-permute-start.1) | collective-permute-done | bytes 524320 | tf_op jit(solution)/shard_map/ppermute | solution.py:27
  27.9 1.7 %shard_map.122 = (f32[512,512]{1,0:T(8,128)S(1)}, f32[512,1024]{1,0:T(8,128)S(1)}, f32[4,512]{1,0:T(4,128)S(1)}) custom-call(s32[3]{0:T(128)S(1)} %pad_add_fusion.info.refs_4_.refs_6_.refs_5_, bf16[512,512]{1,0:T(8,128)(2,1)S(1)} %collective-permute-done.1.x.refs_6_, ...), custom_call_target="tpu_custom_call", output_to_operand_aliasing={{0}: (5, {}), {1}: (6, {}), {2}: (7, {})} | custom-call | flops 1000000 | bytes 100000 | tf_op jit(solution)/shard_map/pallas_call | solution.py:185
  29.5 0.2 collective-permute-done.6.refs_0_.refs_7_
  29.8 2.8 %shard_map.123 = (bf16[512,512]{1,0:T(8,128)(2,1)S(1)}, bf16[512,1024]{1,0:T(8,128)(2,1)S(1)}, bf16[2,128,512]{2,1,0:T(8,128)(2,1)S(1)}, bf16[2,128,512]{2,1,0:T...) custom-call(s32[3]{0:T(128)S(1)} %pad_add_fusion.info.refs_4_.refs_6_.refs_5_, s32[4]{0:T(128)S(1)} %copy-done.9, ...), custom_call_target="tpu_custom_call" | custom-call | flops 4000000000 | bytes 4000000 | tf_op jit(solution)/shard_map/pallas_call | solution.py:323
  32.6 1.8 %collective-permute-start.8 = (bf16[2,128,512]{2,1,0:T(8,128)(2,1)S(1)}, bf16[2,128,512]{2,1,0:T(8,128)(2,1)S(1)}, u32[]{:S(2)}, u32[]{:S(2)}) collective-permute-start(bf16[2,128,512]{2,1,0:T(8,128)(2,1)S(1)} %get-tuple-element.107), channel_id=1, source_target_pairs={{0,4},{4,0},{8,12},{12,8},{16,20},{20,16},{24,28},{28,24},{1,5},{5... | collective-permute-start | bytes 786440 | tf_op jit(solution)/shard_map/ppermute | solution.py:27
  34.4 0.3 collective-permute-start.7
  34.7 6.0 %shard_map.124 = (bf16[512,512]{1,0:T(8,128)(2,1)S(1)}, f32[512,1024]{1,0:T(8,128)S(1)}) custom-call(bf16[512,512]{1,0:T(8,128)(2,1)S(1)} %get-tuple-element.108.refs_0_.key, bf16[512,1024]{1,0:T(8,128)(2,1)S(1)} %get-tuple-element.109.refs_1_.value, bf16[2,128,512]{2,1,0:T(8,128)(2,1)S(1)} %get-tuple-element.110.refs_2_.refs_8_.refs_9_, ...), custom_call_target="tpu_custom_call" | custom-call | flops 1000000 | bytes 100000 | tf_op jit(solution)/shard_map/pallas_call | solution.py:223
  40.7 0.5 collective-permute-done.7.refs_7_.refs_8_
  41.3 0.8 shard_map.125
  42.1 1.9 %collective-permute-start.10 = (bf16[1,128,512]{2,1,0:T(8,128)(2,1)S(1)}, bf16[1,128,512]{2,1,0:T(8,128)(2,1)S(1)}, u32[]{:S(2)}, u32[]{:S(2)}) collective-permute-start(bf16[1,128,512]{2,1,0:T(8,128)(2,1)S(1)} %get-tuple-element.123), channel_id=1, source_target_pairs={{0,8},{4,12},{8,16},{12,20},{16,24},{20,28},{24,0},{28,4},{1,9},{5... | collective-permute-start | bytes 393224 | tf_op jit(solution)/shard_map/ppermute | solution.py:32
  43.9 1.6 %collective-permute-start.13 = (bf16[1,128,512]{2,1,0:T(8,128)(2,1)S(1)}, bf16[1,128,512]{2,1,0:T(8,128)(2,1)}, u32[]{:S(2)}, u32[]{:S(2)}) collective-permute-start(bf16[1,128,512]{2,1,0:T(8,128)(2,1)S(1)} %get-tuple-element.129), channel_id=1, source_target_pairs={{0,8},{4,12},{8,16},{12,20},{16,24},{20,28},{24,0},{28,4},{1,9},{5... | collective-permute-start | bytes 393224 | tf_op jit(solution)/shard_map/ppermute | solution.py:32
  45.5 1.6 %collective-permute-start.9 = (f32[2,384]{1,0:T(2,128)S(1)}, f32[2,384]{1,0:T(2,128)}, u32[]{:S(2)}, u32[]{:S(2)}) collective-permute-start(f32[2,384]{1,0:T(2,128)S(1)} %get-tuple-element.122), channel_id=1, source_target_pairs={{0,8},{4,12},{8,16},{12,20},{16,24},{20,28},{24,0},{28,4},{1,9},{5... | collective-permute-start | bytes 9224 | tf_op jit(solution)/shard_map/ppermute | solution.py:32
  47.1 5.0 %collective-permute-done.9.refs_11_ = f32[2,384]{1,0:T(2,128)} collective-permute-done((f32[2,384]{1,0:T(2,128)S(1)}, f32[2,384]{1,0:T(2,128)}, u32[]{:S(2)}, u32[]{:S(2)}) %collective-permute-start.9) | collective-permute-done | bytes 3104 | tf_op jit(solution)/shard_map/ppermute | solution.py:32
  52.1 1.3 %collective-permute-start.14 = (bf16[1,128,512]{2,1,0:T(8,128)(2,1)}, bf16[1,128,512]{2,1,0:T(8,128)(2,1)}, u32[]{:S(2)}, u32[]{:S(2)}) collective-permute-start(bf16[1,128,512]{2,1,0:T(8,128)(2,1)} %collective-permute-done.13.refs_14_), channel_id=1, source_target_pairs={{0,8},{4,12},{8,16},{12,20},{16,24},{20,28},{24,0},{28,4},{1,9},{5... | collective-permute-start | bytes 393224 | tf_op jit(solution)/shard_map/ppermute | solution.py:32
  53.4 1.6 %collective-permute-start.11 = (f32[2,384]{1,0:T(2,128)}, f32[2,384]{1,0:T(2,128)}, u32[]{:S(2)}, u32[]{:S(2)}) collective-permute-start(f32[2,384]{1,0:T(2,128)} %collective-permute-done.9.refs_11_), channel_id=1, source_target_pairs={{0,8},{4,12},{8,16},{12,20},{16,24},{20,28},{24,0},{28,4},{1,9},{5... | collective-permute-start | bytes 9224 | tf_op jit(solution)/shard_map/ppermute | solution.py:32
  55.0 1.3 %copy.20.refs_19_ = f32[2,1]{1,0:T(2,128)} copy(f32[2,1]{0,1:T(1,128)} %bitcast.6) | data formatting | bytes 16 | tf_op jit(solution)/shard_map/broadcast_in_dim | solution.py:474
  56.3 1.6 %copy-done.2 = f32[512,1024]{1,0:T(8,128)S(1)} copy-done((f32[512,1024]{1,0:T(8,128)S(1)}, f32[512,1024]{1,0:T(8,128)}, u32[]{:S(2)}) %copy-start.2) | copy-done | bytes 2097176
  57.9 0.9 copy-done.4
  58.8 4.0 %shard_map.127.refs_3_.gate = f32[512,1024]{1,0:T(8,128)S(1)} custom-call(bf16[512,512]{1,0:T(8,128)(2,1)S(1)} %get-tuple-element.108.refs_0_.key, bf16[512,1024]{1,0:T(8,128)(2,1)S(1)} %get-tuple-element.109.refs_1_.value, bf16[2,128,512]{2,1,0:T(8,128)(2,1)S(1)} %get-tuple-element.110.refs_2_.refs_8_.refs_9_, bf16[2,128,512]{2,1,0:T(8,128)(2,1)S(1)} %copy-done.4, ...), custom_call_target="tpu_custom_call" | custom-call | flops 1000000 | bytes 100000 | tf_op jit(solution)/shard_map/pallas_call | solution.py:223
  62.9 2.8 %shard_map.128 = (bf16[2,128,512]{2,1,0:T(8,128)(2,1)S(1)}, bf16[2,128,512]{2,1,0:T(8,128)(2,1)S(1)}, f32[2,256]{1,0:T(2,128)S(1)}, f32[2,128]{1,0:T(2,128)S(1)}) custom-call(bf16[512,512]{1,0:T(8,128)(2,1)S(1)} %get-tuple-element.108.refs_0_.key, bf16[512,1024]{1,0:T(8,128)(2,1)S(1)} %get-tuple-element.109.refs_1_.value, ...), custom_call_target="tpu_custom_call" | custom-call | flops 1000000 | bytes 100000 | tf_op jit(solution)/shard_map/pallas_call | solution.py:455
  65.7 1.6 %collective-permute-start.15 = (bf16[2,128,512]{2,1,0:T(8,128)(2,1)S(1)}, bf16[2,128,512]{2,1,0:T(8,128)(2,1)S(1)}, u32[]{:S(2)}, u32[]{:S(2)}) collective-permute-start(bf16[2,128,512]{2,1,0:T(8,128)(2,1)S(1)} %get-tuple-element.136), channel_id=1, source_target_pairs={{0,4},{4,0},{8,12},{12,8},{16,20},{20,16},{24,28},{28,24},{1,5},{5... | collective-permute-start | bytes 786440 | tf_op jit(solution)/shard_map/ppermute | solution.py:27
  67.2 4.2 %shard_map.129 = (f32[512,1024]{1,0:T(8,128)S(1)}, f32[512,1024]{1,0:T(8,128)S(1)}, bf16[1024,4096]{1,0:T(8,128)(2,1)S(1)}) custom-call(s32[3]{0:T(128)S(1)} %pad_add_fusion.info.refs_4_.refs_6_.refs_5_, s32[4]{0:T(128)S(1)} %copy-done.10, f32[2,128]{1,0:T(2,128)S(1)} %get-tuple-element.137.top_in, ...), custom_call_target="tpu_custom_call" | custom-call | flops 1000000 | bytes 100000 | tf_op jit(solution)/shard_map/pallas_call | solution.py:529
  71.4 0.7 collective-permute-done.15.other
  72.1 1.6 %shard_map.130 = (bf16[512,1024]{1,0:T(8,128)(2,1)S(1)}, bf16[512,512]{1,0:T(8,128)(2,1)S(1)}) custom-call(s32[3]{0:T(128)S(1)} %pad_add_fusion.info.refs_4_.refs_6_.refs_5_, bf16[512,512]{1,0:T(8,128)(2,1)S(1)} %get-tuple-element.119.refs_2_.refs_4_.query, bf16[2,128,512]{2,1,0:T(8,128)(2,1)S(1)} %get-tuple-element.135.own, ...), custom_call_target="tpu_custom_call" | custom-call | flops 3000000000 | bytes 8000000 | tf_op jit(solution)/shard_map/pallas_call | solution.py:570
  73.7 0.1 collective-permute-start.16
  73.8 1.8 %shard_map.131 = (bf16[512,512]{1,0:T(8,128)(2,1)S(1)}, bf16[512,512]{1,0:T(8,128)(2,1)S(1)}) custom-call(s32[3]{0:T(128)S(1)} %pad_add_fusion.info.refs_4_.refs_6_.refs_5_, bf16[512,1024]{1,0:T(8,128)(2,1)S(1)} %get-tuple-element.151.hidden, bf16[1024,4096]{1,0:T(8,128)(2,1)S(1)} %get-tuple-element.141.w), custom_call_target="tpu_custom_call" | custom-call | flops 1000000 | bytes 100000 | tf_op jit(solution)/shard_map/pallas_call | solution.py:592
  75.7 0.6 collective-permute-start.18
  76.2 0.1 copy.28
  76.3 0.1 convert_add_fusion.3
  76.5 1.6 %collective-permute-start.17 = (bf16[512,256]{1,0:T(8,128)(2,1)S(1)}, bf16[512,256]{1,0:T(8,128)(2,1)S(1)}, u32[]{:S(2)}, u32[]{:S(2)}) collective-permute-start(bf16[512,256]{1,0:T(8,128)(2,1)S(1)} %slice.99), channel_id=1, source_target_pairs={{0,2},{1,3},{2,0},{3,1},{4,6},{5,7},{6,4},{7,5},{8,10},{9,11},{10,... | collective-permute-start | bytes 786440 | tf_op jit(solution)/shard_map/ppermute | solution.py:27
  78.1 1.8 %shard_map.132 = (bf16[512,512]{1,0:T(8,128)(2,1)S(1)}, bf16[512,512]{1,0:T(8,128)(2,1)S(1)}) custom-call(s32[3]{0:T(128)S(1)} %pad_add_fusion.info.refs_4_.refs_6_.refs_5_, bf16[512,1024]{1,0:T(8,128)(2,1)S(1)} %get-tuple-element.151.hidden, bf16[1024,4096]{1,0:T(8,128)(2,1)S(1)} %get-tuple-element.141.w), custom_call_target="tpu_custom_call" | custom-call | flops 1000000 | bytes 100000 | tf_op jit(solution)/shard_map/pallas_call | solution.py:592
  79.9 0.1 collective-permute-start.20
  80.0 0.1 convert_add_fusion.2
  80.2 0.6 collective-permute-start.19
  80.8 1.8 %shard_map.133 = (bf16[512,512]{1,0:T(8,128)(2,1)S(1)}, bf16[512,512]{1,0:T(8,128)(2,1)S(1)}) custom-call(s32[3]{0:T(128)S(1)} %pad_add_fusion.info.refs_4_.refs_6_.refs_5_, bf16[512,1024]{1,0:T(8,128)(2,1)S(1)} %get-tuple-element.151.hidden, bf16[1024,4096]{1,0:T(8,128)(2,1)S(1)} %get-tuple-element.141.w), custom_call_target="tpu_custom_call" | custom-call | flops 1000000 | bytes 100000 | tf_op jit(solution)/shard_map/pallas_call | solution.py:592
  82.6 0.3 collective-permute-start.22
  82.9 2.9 %collective-permute-done.17 = bf16[512,256]{1,0:T(8,128)(2,1)S(1)} collective-permute-done((bf16[512,256]{1,0:T(8,128)(2,1)S(1)}, bf16[512,256]{1,0:T(8,128)(2,1)S(1)}, u32[]{:S(2)}, u32[]{:S(2)}) %collective-permute-start.17) | collective-permute-done | bytes 262176 | tf_op jit(solution)/shard_map/ppermute | solution.py:27
  85.7 0.2 fusion.8
  85.9 0.1 convert_add_fusion.1
  86.1 1.6 %collective-permute-start.21 = (bf16[512,256]{1,0:T(8,128)(2,1)S(1)}, bf16[512,256]{1,0:T(8,128)(2,1)S(1)}, u32[]{:S(2)}, u32[]{:S(2)}) collective-permute-start(bf16[512,256]{1,0:T(8,128)(2,1)S(1)} %slice.97), channel_id=1, source_target_pairs={{0,2},{1,3},{2,0},{3,1},{4,6},{5,7},{6,4},{7,5},{8,10},{9,11},{10,... | collective-permute-start | bytes 786440 | tf_op jit(solution)/shard_map/ppermute | solution.py:27
  87.7 1.3 %shard_map.134 = bf16[512,512]{1,0:T(8,128)(2,1)S(1)} custom-call(s32[3]{0:T(128)S(1)} %pad_add_fusion.info.refs_4_.refs_6_.refs_5_, bf16[512,1024]{1,0:T(8,128)(2,1)S(1)} %get-tuple-element.151.hidden, bf16[1024,4096]{1,0:T(8,128)(2,1)S(1)} %get-tuple-element.141.w), custom_call_target="tpu_custom_call" | custom-call | flops 1000000 | bytes 100000 | tf_op jit(solution)/shard_map/pallas_call | solution.py:592
  89.0 0.1 convert_add_fusion
  89.2 0.6 collective-permute-start.23
  89.8 1.6 %collective-permute-done.19 = bf16[512,256]{1,0:T(8,128)(2,1)S(1)} collective-permute-done((bf16[512,256]{1,0:T(8,128)(2,1)S(1)}, bf16[512,256]{1,0:T(8,128)(2,1)S(1)}, u32[]{:S(2)}, u32[]{:S(2)}) %collective-permute-start.19) | collective-permute-done | bytes 262176 | tf_op jit(solution)/shard_map/ppermute | solution.py:27
  91.3 0.1 fusion.9
  91.5 5.5 %collective-permute-done.21 = bf16[512,256]{1,0:T(8,128)(2,1)S(1)} collective-permute-done((bf16[512,256]{1,0:T(8,128)(2,1)S(1)}, bf16[512,256]{1,0:T(8,128)(2,1)S(1)}, u32[]{:S(2)}, u32[]{:S(2)}) %collective-permute-start.21) | collective-permute-done | bytes 262176 | tf_op jit(solution)/shard_map/ppermute | solution.py:27
  97.0 0.1 fusion.10
  97.1 0.0 copy-start.14
  97.1 4.6 %collective-permute-done.23 = bf16[512,256]{1,0:T(8,128)(2,1)S(1)} collective-permute-done((bf16[512,256]{1,0:T(8,128)(2,1)S(1)}, bf16[512,256]{1,0:T(8,128)(2,1)S(1)}, u32[]{:S(2)}, u32[]{:S(2)}) %collective-permute-start.23) | collective-permute-done | bytes 262176 | tf_op jit(solution)/shard_map/ppermute | solution.py:27
  101.6 0.8 fusion.11
  (49 shorter events, 0.3 us)
Async XLA Ops:
  0.0 8.7 %copy-start = (bf16[512,1024]{1,0:T(8,128)(2,1)S(1)}, bf16[512,1024]{1,0:T(8,128)(2,1)}, u32[]{:S(2)}) copy-start(bf16[512,1024]{1,0:T(8,128)(2,1)} %refs_7_.2) | copy-start | bytes 3145732
  0.0 8.6 %copy-start.15 = (bf16[2,4096,2]{1,2,0:T(2,128)(2,1)S(1)}, bf16[2,4096,2]{1,2,0:T(2,128)(2,1)}, u32[]{:S(2)}) copy-start(bf16[2,4096,2]{1,2,0:T(2,128)(2,1)} %param.17) | copy-start | bytes 98308
  0.0 4.1 %collective-permute-start = (bf16[512,1024]{1,0:T(8,128)(2,1)}, bf16[512,1024]{1,0:T(8,128)(2,1)S(1)}, u32[]{:S(2)}, u32[]{:S(2)}) collective-permute-start(bf16[512,1024]{1,0:T(8,128)(2,1)} %refs_7_.2), channel_id=1, source_target_pairs={{0,1},{1,0},{2,3},{3,2},{4,5},{5,4},{6,7},{7,6},{8,9},{9,8},{10,11... | collective-permute-start | bytes 3145736 | tf_op jit(solution)/shard_map/ppermute | solution.py:27
  1.4 15.3 %collective-permute-start.2 = (bf16[512,256]{1,0:T(8,128)(2,1)S(1)}, bf16[512,256]{1,0:T(8,128)(2,1)S(1)}, u32[]{:S(2)}, u32[]{:S(2)}) collective-permute-start(bf16[512,256]{1,0:T(8,128)(2,1)S(1)} %shard_map.119), channel_id=1, source_target_pairs={{0,2},{1,3},{2,0},{3,1},{4,6},{5,7},{6,4},{7,5},{8,10},{9,11},{10,... | collective-permute-start | bytes 786440 | tf_op jit(solution)/shard_map/ppermute | solution.py:27
  4.1 12.6 %copy-start.5 = (bf16[512,1024]{1,0:T(8,128)(2,1)}, bf16[512,1024]{1,0:T(8,128)(2,1)S(1)}, u32[]{:S(2)}) copy-start(bf16[512,1024]{1,0:T(8,128)(2,1)S(1)} %collective-permute-done.refs_1_.refs_5_) | copy-start | bytes 3145732
  6.5 10.4 %collective-permute-start.3 = (bf16[512,256]{1,0:T(8,128)(2,1)}, bf16[512,256]{1,0:T(8,128)(2,1)S(1)}, u32[]{:S(2)}, u32[]{:S(2)}) collective-permute-start(bf16[512,256]{1,0:T(8,128)(2,1)} %get-tuple-element.81), channel_id=1, source_target_pairs={{0,2},{1,3},{2,0},{3,1},{4,6},{5,7},{6,4},{7,5},{8,10},{9,11},{10,... | collective-permute-start | bytes 786440 | tf_op jit(solution)/shard_map/ppermute | solution.py:27
  8.3 19.5 %collective-permute-start.1 = (bf16[512,512]{1,0:T(8,128)(2,1)}, bf16[512,512]{1,0:T(8,128)(2,1)S(1)}, u32[]{:S(2)}, u32[]{:S(2)}) collective-permute-start(bf16[512,512]{1,0:T(8,128)(2,1)} %get-tuple-element.80), channel_id=1, source_target_pairs={{0,2},{1,3},{2,0},{3,1},{4,6},{5,7},{6,4},{7,5},{8,10},{9,11},{10,... | collective-permute-start | bytes 1572872 | tf_op jit(solution)/shard_map/ppermute | solution.py:27
  16.9 1.5 %collective-permute-start.4 = (bf16[512,256]{1,0:T(8,128)(2,1)S(1)}, bf16[512,256]{1,0:T(8,128)(2,1)S(1)}, u32[]{:S(2)}, u32[]{:S(2)}) collective-permute-start(bf16[512,256]{1,0:T(8,128)(2,1)S(1)} %collective-permute-done.2.refs_0_), channel_id=1, source_target_pairs={{0,1},{1,0},{2,3},{3,2},{4,5},{5,4},{6,7},{7,6},{8,9},{9,8},{10,11... | collective-permute-start | bytes 786440 | tf_op jit(solution)/shard_map/ppermute | solution.py:27
  16.9 1.9 %collective-permute-start.5 = (bf16[512,256]{1,0:T(8,128)(2,1)S(1)}, bf16[512,256]{1,0:T(8,128)(2,1)S(1)}, u32[]{:S(2)}, u32[]{:S(2)}) collective-permute-start(bf16[512,256]{1,0:T(8,128)(2,1)S(1)} %collective-permute-done.3.refs_2_), channel_id=1, source_target_pairs={{0,1},{1,0},{2,3},{3,2},{4,5},{5,4},{6,7},{7,6},{8,9},{9,8},{10,11... | collective-permute-start | bytes 786440 | tf_op jit(solution)/shard_map/ppermute | solution.py:27
  27.8 1.7 %copy-start.7 = (bf16[512,512]{1,0:T(8,128)(2,1)}, bf16[512,512]{1,0:T(8,128)(2,1)S(1)}, u32[]{:S(2)}) copy-start(bf16[512,512]{1,0:T(8,128)(2,1)S(1)} %collective-permute-done.1.x.refs_6_) | copy-start | bytes 1572868
  27.8 1.9 %collective-permute-start.6 = (bf16[512,512]{1,0:T(8,128)(2,1)S(1)}, bf16[512,512]{1,0:T(8,128)(2,1)S(1)}, u32[]{:S(2)}, u32[]{:S(2)}) collective-permute-start(bf16[512,512]{1,0:T(8,128)(2,1)S(1)} %collective-permute-done.1.x.refs_6_), channel_id=1, source_target_pairs={{0,1},{1,0},{2,3},{3,2},{4,5},{5,4},{6,7},{7,6},{8,9},{9,8},{10,11... | collective-permute-start | bytes 1572872 | tf_op jit(solution)/shard_map/ppermute | solution.py:27
  27.8 1.9 %copy-start.9 = (s32[4]{0:T(128)S(1)}, s32[4]{0:T(128)}, u32[]{:S(2)}) copy-start(s32[4]{0:T(128)} %docs.3) | copy-start | bytes 52
  27.8 1.9 %copy-start.13 = (f32[2,2]{1,0:T(2,128)S(1)}, f32[2,2]{1,0:T(2,128)}, u32[]{:S(2)}) copy-start(f32[2,2]{1,0:T(2,128)} %bias.1) | copy-start | bytes 52
  29.8 5.0 %copy-start.6 = (bf16[512,1024]{1,0:T(8,128)(2,1)S(1)}, bf16[512,1024]{1,0:T(8,128)(2,1)}, u32[]{:S(2)}) copy-start(bf16[512,1024]{1,0:T(8,128)(2,1)} %copy-done.5) | copy-start | bytes 3145732
  29.8 5.0 %copy-start.8 = (bf16[512,512]{1,0:T(8,128)(2,1)S(1)}, bf16[512,512]{1,0:T(8,128)(2,1)}, u32[]{:S(2)}) copy-start(bf16[512,512]{1,0:T(8,128)(2,1)} %copy-done.7) | copy-start | bytes 1572868
  32.6 8.7 %collective-permute-start.8 = (bf16[2,128,512]{2,1,0:T(8,128)(2,1)S(1)}, bf16[2,128,512]{2,1,0:T(8,128)(2,1)S(1)}, u32[]{:S(2)}, u32[]{:S(2)}) collective-permute-start(bf16[2,128,512]{2,1,0:T(8,128)(2,1)S(1)} %get-tuple-element.107), channel_id=1, source_target_pairs={{0,4},{4,0},{8,12},{12,8},{16,20},{20,16},{24,28},{28,24},{1,5},{5... | collective-permute-start | bytes 786440 | tf_op jit(solution)/shard_map/ppermute | solution.py:27
  34.4 6.8 %collective-permute-start.7 = (f32[2,384]{1,0:T(2,128)S(1)}, f32[2,384]{1,0:T(2,128)S(1)}, u32[]{:S(2)}, u32[]{:S(2)}) collective-permute-start(f32[2,384]{1,0:T(2,128)S(1)} %get-tuple-element.125.refs_6_.refs_7_), channel_id=1, source_target_pairs={{0,4},{4,0},{8,12},{12,8},{16,20},{20,16},{24,28},{28,24},{1,5},{5... | collective-permute-start | bytes 9224 | tf_op jit(solution)/shard_map/ppermute | solution.py:27
  40.7 6.4 %copy-start.1 = (f32[512,1024]{1,0:T(8,128)}, f32[512,1024]{1,0:T(8,128)S(1)}, u32[]{:S(2)}) copy-start(f32[512,1024]{1,0:T(8,128)S(1)} %get-tuple-element.124.refs_6_.refs_9_) | copy-start | bytes 6291460
  41.3 5.8 %copy-start.3 = (bf16[2,128,512]{2,1,0:T(8,128)(2,1)}, bf16[2,128,512]{2,1,0:T(8,128)(2,1)S(1)}, u32[]{:S(2)}) copy-start(bf16[2,128,512]{2,1,0:T(8,128)(2,1)S(1)} %collective-permute-done.8.refs_9_.refs_3_.refs_10_) | copy-start | bytes 786436
  42.1 10.0 %collective-permute-start.10 = (bf16[1,128,512]{2,1,0:T(8,128)(2,1)S(1)}, bf16[1,128,512]{2,1,0:T(8,128)(2,1)S(1)}, u32[]{:S(2)}, u32[]{:S(2)}) collective-permute-start(bf16[1,128,512]{2,1,0:T(8,128)(2,1)S(1)} %get-tuple-element.123), channel_id=1, source_target_pairs={{0,8},{4,12},{8,16},{12,20},{16,24},{20,28},{24,0},{28,4},{1,9},{5... | collective-permute-start | bytes 393224 | tf_op jit(solution)/shard_map/ppermute | solution.py:32
  43.9 8.2 %collective-permute-start.13 = (bf16[1,128,512]{2,1,0:T(8,128)(2,1)S(1)}, bf16[1,128,512]{2,1,0:T(8,128)(2,1)}, u32[]{:S(2)}, u32[]{:S(2)}) collective-permute-start(bf16[1,128,512]{2,1,0:T(8,128)(2,1)S(1)} %get-tuple-element.129), channel_id=1, source_target_pairs={{0,8},{4,12},{8,16},{12,20},{16,24},{20,28},{24,0},{28,4},{1,9},{5... | collective-permute-start | bytes 393224 | tf_op jit(solution)/shard_map/ppermute | solution.py:32
  45.5 6.6 %collective-permute-start.9 = (f32[2,384]{1,0:T(2,128)S(1)}, f32[2,384]{1,0:T(2,128)}, u32[]{:S(2)}, u32[]{:S(2)}) collective-permute-start(f32[2,384]{1,0:T(2,128)S(1)} %get-tuple-element.122), channel_id=1, source_target_pairs={{0,8},{4,12},{8,16},{12,20},{16,24},{20,28},{24,0},{28,4},{1,9},{5... | collective-permute-start | bytes 9224 | tf_op jit(solution)/shard_map/ppermute | solution.py:32
  52.1 10.7 %collective-permute-start.12 = (bf16[1,128,512]{2,1,0:T(8,128)(2,1)S(1)}, bf16[1,128,512]{2,1,0:T(8,128)(2,1)}, u32[]{:S(2)}, u32[]{:S(2)}) collective-permute-start(bf16[1,128,512]{2,1,0:T(8,128)(2,1)S(1)} %collective-permute-done.10.refs_13_), channel_id=1, source_target_pairs={{0,8},{4,12},{8,16},{12,20},{16,24},{20,28},{24,0},{28,4},{1,9},{5... | collective-permute-start | bytes 393224 | tf_op jit(solution)/shard_map/ppermute | solution.py:32
  52.1 10.7 %collective-permute-start.14 = (bf16[1,128,512]{2,1,0:T(8,128)(2,1)}, bf16[1,128,512]{2,1,0:T(8,128)(2,1)}, u32[]{:S(2)}, u32[]{:S(2)}) collective-permute-start(bf16[1,128,512]{2,1,0:T(8,128)(2,1)} %collective-permute-done.13.refs_14_), channel_id=1, source_target_pairs={{0,8},{4,12},{8,16},{12,20},{16,24},{20,28},{24,0},{28,4},{1,9},{5... | collective-permute-start | bytes 393224 | tf_op jit(solution)/shard_map/ppermute | solution.py:32
  53.4 9.4 %collective-permute-start.11 = (f32[2,384]{1,0:T(2,128)}, f32[2,384]{1,0:T(2,128)}, u32[]{:S(2)}, u32[]{:S(2)}) collective-permute-start(f32[2,384]{1,0:T(2,128)} %collective-permute-done.9.refs_11_), channel_id=1, source_target_pairs={{0,8},{4,12},{8,16},{12,20},{16,24},{20,28},{24,0},{28,4},{1,9},{5... | collective-permute-start | bytes 9224 | tf_op jit(solution)/shard_map/ppermute | solution.py:32
  56.3 1.6 %copy-start.2 = (f32[512,1024]{1,0:T(8,128)S(1)}, f32[512,1024]{1,0:T(8,128)}, u32[]{:S(2)}) copy-start(f32[512,1024]{1,0:T(8,128)} %copy-done.1) | copy-start | bytes 6291460
  57.9 0.9 copy-start.4
  58.8 4.0 %copy-start.10 = (s32[4]{0:T(128)S(1)}, s32[4]{0:T(128)}, u32[]{:S(2)}) copy-start(s32[4]{0:T(128)} %docs.3) | copy-start | bytes 52
  58.8 4.0 %copy-start.11 = (f32[2,256]{1,0:T(2,128)S(1)}, f32[2,256]{1,0:T(2,128)}, u32[]{:S(2)}) copy-start(f32[2,256]{1,0:T(2,128)} %refs_18_.1) | copy-start | bytes 6148
  58.8 4.0 %copy-start.12 = (f32[2,1]{1,0:T(2,128)S(1)}, f32[2,1]{1,0:T(2,128)}, u32[]{:S(2)}) copy-start(f32[2,1]{1,0:T(2,128)} %copy.20.refs_19_) | copy-start | bytes 28
  65.7 6.4 %collective-permute-start.15 = (bf16[2,128,512]{2,1,0:T(8,128)(2,1)S(1)}, bf16[2,128,512]{2,1,0:T(8,128)(2,1)S(1)}, u32[]{:S(2)}, u32[]{:S(2)}) collective-permute-start(bf16[2,128,512]{2,1,0:T(8,128)(2,1)S(1)} %get-tuple-element.136), channel_id=1, source_target_pairs={{0,4},{4,0},{8,12},{12,8},{16,20},{20,16},{24,28},{28,24},{1,5},{5... | collective-permute-start | bytes 786440 | tf_op jit(solution)/shard_map/ppermute | solution.py:27
  73.7 2.5 %collective-permute-start.16 = (bf16[512,512]{1,0:T(8,128)(2,1)S(1)}, bf16[512,512]{1,0:T(8,128)(2,1)S(1)}, u32[]{:S(2)}, u32[]{:S(2)}) collective-permute-start(bf16[512,512]{1,0:T(8,128)(2,1)S(1)} %get-tuple-element.144), channel_id=1, source_target_pairs={{0,1},{1,0},{2,3},{3,2},{4,5},{5,4},{6,7},{7,6},{8,9},{9,8},{10,11... | collective-permute-start | bytes 1572872 | tf_op jit(solution)/shard_map/ppermute | solution.py:27
  75.7 4.4 %collective-permute-start.18 = (bf16[512,512]{1,0:T(8,128)(2,1)S(1)}, bf16[512,512]{1,0:T(8,128)(2,1)S(1)}, u32[]{:S(2)}, u32[]{:S(2)}) collective-permute-start(bf16[512,512]{1,0:T(8,128)(2,1)S(1)} %get-tuple-element.147), channel_id=1, source_target_pairs={{0,1},{1,0},{2,3},{3,2},{4,5},{5,4},{6,7},{7,6},{8,9},{9,8},{10,11... | collective-permute-start | bytes 1572872 | tf_op jit(solution)/shard_map/ppermute | solution.py:27
  76.5 9.2 %collective-permute-start.17 = (bf16[512,256]{1,0:T(8,128)(2,1)S(1)}, bf16[512,256]{1,0:T(8,128)(2,1)S(1)}, u32[]{:S(2)}, u32[]{:S(2)}) collective-permute-start(bf16[512,256]{1,0:T(8,128)(2,1)S(1)} %slice.99), channel_id=1, source_target_pairs={{0,2},{1,3},{2,0},{3,1},{4,6},{5,7},{6,4},{7,5},{8,10},{9,11},{10,... | collective-permute-start | bytes 786440 | tf_op jit(solution)/shard_map/ppermute | solution.py:27
  79.9 6.0 %collective-permute-start.20 = (bf16[512,512]{1,0:T(8,128)(2,1)S(1)}, bf16[512,512]{1,0:T(8,128)(2,1)S(1)}, u32[]{:S(2)}, u32[]{:S(2)}) collective-permute-start(bf16[512,512]{1,0:T(8,128)(2,1)S(1)} %get-tuple-element.150), channel_id=1, source_target_pairs={{0,1},{1,0},{2,3},{3,2},{4,5},{5,4},{6,7},{7,6},{8,9},{9,8},{10,11... | collective-permute-start | bytes 1572872 | tf_op jit(solution)/shard_map/ppermute | solution.py:27
  80.2 11.1 %collective-permute-start.19 = (bf16[512,256]{1,0:T(8,128)(2,1)S(1)}, bf16[512,256]{1,0:T(8,128)(2,1)S(1)}, u32[]{:S(2)}, u32[]{:S(2)}) collective-permute-start(bf16[512,256]{1,0:T(8,128)(2,1)S(1)} %slice.98), channel_id=1, source_target_pairs={{0,2},{1,3},{2,0},{3,1},{4,6},{5,7},{6,4},{7,5},{8,10},{9,11},{10,... | collective-permute-start | bytes 786440 | tf_op jit(solution)/shard_map/ppermute | solution.py:27
  82.6 6.4 %collective-permute-start.22 = (bf16[512,512]{1,0:T(8,128)(2,1)S(1)}, bf16[512,512]{1,0:T(8,128)(2,1)S(1)}, u32[]{:S(2)}, u32[]{:S(2)}) collective-permute-start(bf16[512,512]{1,0:T(8,128)(2,1)S(1)} %get-tuple-element.152), channel_id=1, source_target_pairs={{0,1},{1,0},{2,3},{3,2},{4,5},{5,4},{6,7},{7,6},{8,9},{9,8},{10,11... | collective-permute-start | bytes 1572872 | tf_op jit(solution)/shard_map/ppermute | solution.py:27
  86.1 10.8 %collective-permute-start.21 = (bf16[512,256]{1,0:T(8,128)(2,1)S(1)}, bf16[512,256]{1,0:T(8,128)(2,1)S(1)}, u32[]{:S(2)}, u32[]{:S(2)}) collective-permute-start(bf16[512,256]{1,0:T(8,128)(2,1)S(1)} %slice.97), channel_id=1, source_target_pairs={{0,2},{1,3},{2,0},{3,1},{4,6},{5,7},{6,4},{7,5},{8,10},{9,11},{10,... | collective-permute-start | bytes 786440 | tf_op jit(solution)/shard_map/ppermute | solution.py:27
  89.2 12.4 %collective-permute-start.23 = (bf16[512,256]{1,0:T(8,128)(2,1)S(1)}, bf16[512,256]{1,0:T(8,128)(2,1)S(1)}, u32[]{:S(2)}, u32[]{:S(2)}) collective-permute-start(bf16[512,256]{1,0:T(8,128)(2,1)S(1)} %slice.96), channel_id=1, source_target_pairs={{0,2},{1,3},{2,0},{3,1},{4,6},{5,7},{6,4},{7,5},{8,10},{9,11},{10,... | collective-permute-start | bytes 786440 | tf_op jit(solution)/shard_map/ppermute | solution.py:27
  97.1 4.6 %copy-start.14 = (bf16[512,1024]{1,0:T(8,128)(2,1)}, bf16[512,1024]{1,0:T(8,128)(2,1)S(1)}, u32[]{:S(2)}) copy-start(bf16[512,1024]{1,0:T(8,128)(2,1)S(1)} %fusion.10) | copy-start | bytes 3145732
